TPU v7x, 256 devices: a whole 4x4x8 slice. The times are simulated.
256 devices in a mesh: dp: 8 (over y, core), mp: 32 (over z, x).
Axes of the slice: x: 4, y: 4, z: 8, core: 2. Of those that a mesh axis runs over, the one named last changes fastest.
Arguments:
- tokens: bfloat16 [4096, 12288], P(('dp', 'mp')), may hold values from -6 to 6
- block_weights: float32 [384, 8, 128, 128], P('mp'), may hold values from -0.1875 to 0.1875
- block_rows: int32 [384, 8], P('mp'), may hold values from 0 to 95, all different within a row
- block_owners: int32 [384, 8, 1], P('mp'), may hold values from 0 to 7; in each aligned block of 96 rows (0 to 95, 96 to 191, ..., all dimensions but the last counted through in order) at most 18 rows name the same one
- factor_in: float32 [12288, 128], P('mp'), may hold values from -0.0546875 to 0.0546875
- factor_out: float32 [128, 49152], P(None, 'mp'), may hold values from -0.5 to 0.5
- upstream: bfloat16 [4096, 49152], P('dp', 'mp'), may hold values from -0.09375 to 0.09375
Outputs:
- hidden: bfloat16 [4096, 49152], P('dp', 'mp')
- block_grads: float32 [4608, 128, 128], P(('mp', 'dp'))
- factor_in_grad: float32 [12288, 128], P(('mp', 'dp'))
- factor_out_grad: float32 [128, 49152], P(None, ('mp', 'dp'))
Inputs may be any that keep to these rules, and one draw needn't show every extreme that they name: `block_rows`: each column block names 8 different row blocks. `block_owners`: among the 96 active blocks of one index of mp (aligned runs of 12 column blocks), one index of dp owns at most 18; in some runs one owns exactly 18.
All inputs are finite; a program needn't handle non-finite values.
Results may differ from a plain program's by a relative error of at most 0.001.
Values may be sent and summed in bfloat16 or wider, within the bound.
No kernel may reach another device: no remote copies, remote signals or barrier semaphores. Data moves between devices by JAX's collectives and lax.ppermute only.
A program may use at most 128 MiB of HBM per device.

v0:
```python
import functools

import jax
import jax.numpy as jnp
from jax import lax
from jax.experimental import pallas as pl
from jax.experimental.pallas import tpu as pltpu
from jax.sharding import Mesh
from jax.sharding import PartitionSpec as P

highest = lax.Precision.HIGHEST
BS = 128
ROWS = 16
NX, NZ, NY, NC = 4, 8, 4, 2
COLS = 12
PER_STEP = 2
KB = 8
RB = 96
CAP = 18
GROUPS = NY * NC
SLOT_ROWS = CAP * BS
FO_ROWS = COLS * BS // GROUPS
CODE_ROWS = SLOT_ROWS + FO_ROWS
PART_ROWS = CODE_ROWS + 32
FINE = 256.0
CUT = 10 * BS


def shift(axis, size, step):
    pairs = [(i, (i + step) % size) for i in range(size)]
    return lambda value: lax.ppermute(value, axis, pairs)


def flip(axis, size, bit):
    pairs = [(i, i ^ bit) for i in range(size)]
    return lambda value: lax.ppermute(value, axis, pairs)


def split_two(value):
    high = value.astype(jnp.bfloat16)
    low = (value - high.astype(jnp.float32)).astype(jnp.bfloat16)
    return high, low


def level_of(block):
    top = jnp.max(jnp.abs(block), axis=0, keepdims=True)
    return jnp.ceil(jnp.log2(jnp.maximum(top, 1e-30)) * FINE)


def encode(block, level):
    inverse = jnp.exp2(level * (-1.0 / FINE)) * 32700.0
    return jnp.floor(block * inverse + 0.5).astype(jnp.int32).astype(jnp.int16)


def decode(code, level):
    unit = jnp.exp2(level * (1.0 / FINE)) * (1.0 / 32700.0)
    return code.astype(jnp.int32).astype(jnp.float32) * unit


def main_kernel(
    counts, rows_ref, where_ref, place_ref, low_ref, weight_ref, factor_ref, up_ref, *rest
):
    arrays, rest = rest[: len(counts)], rest[len(counts) :]
    pieces = [ref.at[i] for ref, n in zip(arrays, counts) for i in range(n)]
    hidden_ref, send_ref, keep_ref, back_ref, cols_ref = rest[:5]
    tok, wide, low_two, codes, levels, sems = rest[5:]
    c = pl.program_id(0)
    tokens = NX * NZ * ROWS

    @pl.when(c == 0)
    def _():
        for j in range(NX * NZ):
            pltpu.make_async_copy(pieces[j], tok.at[place_ref[j]], sems.at[j]).start()
        for g in range(NZ):
            high, low = split_two(low_ref[place_ref[NX * NZ + g]])
            low_two[g * NX * ROWS : (g + 1) * NX * ROWS, :BS] = high
            low_two[g * NX * ROWS : (g + 1) * NX * ROWS, BS:] = low
        wide[(KB + 1) * BS :, BS:] = jnp.zeros((BS, BS), jnp.bfloat16)
        back_ref[...] = jnp.zeros_like(back_ref)
        for j in range(NX * NZ):
            pltpu.make_async_copy(pieces[j], tok.at[place_ref[j]], sems.at[j]).wait()
        for j in range(cols_ref.shape[0]):
            first = place_ref[NX * NZ + NZ]
            cols_ref[j] = tok[:, first + j].reshape(tokens, BS)

    for i in range(PER_STEP):
        col = c * PER_STEP + i
        here = slice(i * BS, (i + 1) * BS)
        for k in range(KB):
            high, low = split_two(weight_ref[i, k])
            wide[k * BS : (k + 1) * BS, :BS] = high
            wide[k * BS : (k + 1) * BS, BS:] = low
        f_high, f_low = split_two(factor_ref[:, here])
        wide[KB * BS : (KB + 1) * BS, :BS] = f_high
        wide[KB * BS : (KB + 1) * BS, BS:] = f_low
        wide[(KB + 1) * BS :, :BS] = f_high

        panel = jnp.concatenate(
            [tok[:, rows_ref[col * KB + k]].reshape(tokens, BS) for k in range(KB)]
            + [low_two[...]],
            axis=1,
        )
        both = jnp.dot(panel, wide[...], preferred_element_type=jnp.float32)
        v = both[:, :BS] + both[:, BS:]
        root = 0.7978845608028654
        square = v * v
        t = jnp.tanh(root * v * (1.0 + 0.044715 * square))
        half = 0.5 * (1.0 + t)
        hidden_ref[:, here] = (v * half).astype(jnp.bfloat16)
        slope = half + 0.5 * root * v * (1.0 - t * t) * (1.0 + 3.0 * 0.044715 * square)
        grad = up_ref[:, here].astype(jnp.float32) * slope

        g_high, g_low = split_two(grad)
        g_two = jnp.concatenate([g_high, g_low], axis=1)
        f_two = jnp.concatenate(
            [
                jnp.concatenate([f_high, f_high], axis=1),
                jnp.concatenate([f_low, jnp.zeros_like(f_low)], axis=1),
            ],
            axis=0,
        )
        back = lax.dot_general(
            g_two, f_two, (((1,), (1,)), ((), ())), preferred_element_type=jnp.float32
        )
        back_ref[...] += back[:, :BS] + back[:, BS:]

        grad_t = grad.T
        t_high, t_low = split_two(grad_t)
        gt_two = jnp.concatenate([t_high, t_low], axis=0)
        product = jnp.dot(gt_two, panel, preferred_element_type=jnp.float32)
        product = product[:BS] + product[BS:]
        for k in range(KB):
            block = product[:, k * BS : (k + 1) * BS]
            level = level_of(block)
            part = where_ref[0, col * KB + k]
            slot = where_ref[1, col * KB + k]
            codes[part, pl.ds(pl.multiple_of(slot * BS, BS), BS)] = encode(block, level)
            levels[part, pl.ds(slot, 1)] = level
        outer = product[:, KB * BS : (KB + 1) * BS] + product[:, (KB + 1) * BS :]
        for h in range(2):
            block = outer[h * 64 : (h + 1) * 64]
            level = level_of(block)
            part = where_ref[2, col * 2 + h]
            slot = where_ref[3, col * 2 + h]
            start = pl.multiple_of(SLOT_ROWS + slot * 64, 64)
            codes[part, pl.ds(start, 64)] = encode(block, level)
            levels[part, pl.ds(CAP + slot, 1)] = level

    @pl.when(c == COLS // PER_STEP - 1)
    def _():
        for part in range(2 * NY):
            codes[part, CODE_ROWS:] = levels[part].astype(jnp.int32).astype(jnp.int16)
        send = pltpu.make_async_copy(codes.at[pl.ds(0, NY)], send_ref, sems.at[0])
        keep = pltpu.make_async_copy(codes.at[pl.ds(NY, NY)], keep_ref, sems.at[1])
        send.start()
        keep.start()
        send.wait()
        keep.wait()


def blocks_of():
    spans = [(s * BS, BS, s) for s in range(CAP)]
    return spans + [(SLOT_ROWS + h * 64, 64, CAP + h) for h in range(FO_ROWS // 64)]


def pair_kernel(keep_ref, got_ref, out_ref):
    keep_levels = keep_ref[0, CODE_ROWS:].astype(jnp.int32).astype(jnp.float32)
    got_levels = got_ref[0, CODE_ROWS:].astype(jnp.int32).astype(jnp.float32)
    fresh = []
    for start, size, index in blocks_of():
        span = slice(start, start + size)
        total = decode(keep_ref[0, span], keep_levels[index : index + 1])
        total += decode(got_ref[0, span], got_levels[index : index + 1])
        level = level_of(total)
        out_ref[0, span] = encode(total, level)
        fresh.append(level)
    fresh.append(jnp.zeros((32 - len(fresh), BS), jnp.float32))
    fresh = jnp.concatenate(fresh, axis=0)
    out_ref[0, CODE_ROWS:] = fresh.astype(jnp.int32).astype(jnp.int16)


def final_kernel(count_ref, own_ref, *refs):
    firsts, seconds = refs[: NY - 1], refs[NY - 1 : 2 * NY - 2]
    slots_ref, outer_ref = refs[2 * NY - 2 :]
    tails = [own_ref[0, CODE_ROWS:]] + [r[CODE_ROWS - CUT :] for r in seconds]
    levels = [t.astype(jnp.int32).astype(jnp.float32) for t in tails]
    count = count_ref[0]
    for start, size, index in blocks_of():
        total = decode(own_ref[0, start : start + size], levels[0][index : index + 1])
        for i in range(NY - 1):
            if start < CUT:
                code = firsts[i][start : start + size]
            else:
                code = seconds[i][start - CUT : start - CUT + size]
            total += decode(code, levels[i + 1][index : index + 1])
        if index < CAP:
            slots_ref[index] = jnp.where(index < count, total.T, 0.0)
        else:
            h = index - CAP
            outer_ref[:, h * 64 : (h + 1) * 64] = total.T


def low_kernel(near_ref, factor_ref, *rest):
    pieces, (out_ref, tok, sems) = rest[:NX], rest[NX:]
    per = RB // (NX * NZ)
    copies = []
    for j in range(NX):
        source = pieces[j].at[:, pl.ds(near_ref[0] * per, per)]
        copies.append(pltpu.make_async_copy(source, tok.at[near_ref[j]], sems.at[j]))
        copies[j].start()
    high, low = split_two(factor_ref[...])
    wide = jnp.concatenate([high, low], axis=1)
    for copy in copies:
        copy.wait()
    panel = jnp.concatenate(
        [tok[:, g, j].reshape(NX * ROWS, BS) for g in range(NZ) for j in range(per)], axis=1
    )
    both = jnp.dot(panel, wide, preferred_element_type=jnp.float32)
    out_ref[...] = both[:, :BS] + both[:, BS:]


def low_partial(near, factor, pieces):
    per = RB // (NX * NZ)
    pieces = [p.reshape(NZ, NX * per, ROWS, BS) for p in pieces]
    return pl.pallas_call(
        low_kernel,
        in_specs=[
            pl.BlockSpec(memory_space=pltpu.SMEM),
            pl.BlockSpec(memory_space=pltpu.VMEM),
        ]
        + [pl.BlockSpec(memory_space=pl.ANY)] * NX,
        out_specs=pl.BlockSpec(memory_space=pltpu.VMEM),
        out_shape=jax.ShapeDtypeStruct((NX * ROWS, BS), jnp.float32),
        scratch_shapes=[
            pltpu.VMEM((NX, NZ, per, ROWS, BS), jnp.bfloat16),
            pltpu.SemaphoreType.DMA((NX,)),
        ],
        compiler_params=pltpu.CompilerParams(vmem_limit_bytes=30 * 1024 * 1024),
        name="low",
    )(near, factor, *pieces)


def in_kernel(near_ref, turns_ref, cols_ref, *rest):
    backs, (out_ref, full) = rest[:NX], rest[NX:]
    for j in range(NX):
        for g in range(NZ):
            full[g, near_ref[j]] = backs[j][g]
    total = NZ * NX * ROWS
    high, low = split_two(full[...].reshape(total, BS).T)
    two = jnp.concatenate([high, low], axis=0)
    panel = jnp.concatenate([cols_ref[j] for j in range(cols_ref.shape[0])], axis=1)
    both = jnp.dot(two, panel, preferred_element_type=jnp.float32)
    grad = (both[:BS] + both[BS:]).T
    size = grad.shape[0] // GROUPS
    for d in range(GROUPS):
        out_ref[turns_ref[d]] = grad[d * size : (d + 1) * size]


def in_partial(near, turns, cols, backs):
    small = pl.BlockSpec(memory_space=pltpu.SMEM)
    whole = pl.BlockSpec(memory_space=pltpu.VMEM)
    size = cols.shape[0] * BS // GROUPS
    return pl.pallas_call(
        in_kernel,
        in_specs=[small, small, whole] + [whole] * NX,
        out_specs=whole,
        out_shape=jax.ShapeDtypeStruct((GROUPS, size, BS), jnp.float32),
        scratch_shapes=[pltpu.VMEM((NZ, NX, ROWS, BS), jnp.float32)],
        compiler_params=pltpu.CompilerParams(vmem_limit_bytes=30 * 1024 * 1024),
        name="into",
    )(near, turns, cols, *backs)


def gather_tokens(own):
    z_up, z_down = shift("z", NZ, 1), shift("z", NZ, -1)
    x_up, x_down, across = shift("x", NX, 1), shift("x", NX, -1), shift("x", NX, 2)
    far = across(own)
    ring = {0: own}
    sides = {-1: x_up(own), 1: x_down(own)}
    sent = {(0,): (sides[-1][None], sides[1][None])}

    def step(a):
        ring[-a] = z_up(ring[1 - a])
        ring[a] = z_down(ring[a - 1])

    def batch(*which):
        block = jnp.stack([ring[a] for a in which])
        sent[which] = (x_up(block), x_down(block))
        return sent[which]

    step(1)
    first_ring = [ring[1], ring[-1]]
    step(2)
    first = batch(1, -1)
    ring[2], ring[-2], _ = lax.optimization_barrier((ring[2], ring[-2], (far, sides)))
    far_all = lax.all_gather(far, "z", axis=0)
    step(3)
    second = batch(2, -2)
    ring[3], ring[-3], _ = lax.optimization_barrier((ring[3], ring[-3], first))
    ring[4] = z_up(ring[-3])
    ring[4], _ = lax.optimization_barrier((ring[4], second))
    batch(3, -3, 4)
    arrays, keys = [far_all], [[(None, g, 2) for g in range(NZ)]]
    for a in ring:
        arrays.append(ring[a][None])
        keys.append([(a, None, 0)])
    for which, pair in sent.items():
        for b, value in zip((-1, 1), pair):
            arrays.append(value)
            keys.append([(a, None, b) for a in which])
    return arrays, keys, first_ring, [own, sides[-1], sides[1], far]


def per_device(tokens, block_weights, block_rows, block_owners, factor_in, factor_out, upstream):
    own = jnp.transpose(tokens.reshape(ROWS, RB, BS), (1, 0, 2))
    arrays, keys, first_ring, near_pieces = gather_tokens(own)
    z, x = lax.axis_index("z"), lax.axis_index("x")
    y, core = lax.axis_index("y"), lax.axis_index("core")
    place = []
    for group in keys:
        for a, g, b in group:
            row = g if a is None else (z + a) % NZ
            place.append(row * NX + (x + b) % NX)
    place += [z ^ g for g in range(NZ)] + [(z * NX + x) * (RB // (NX * NZ))]
    place = jnp.stack([jnp.asarray(p, jnp.int32) for p in place])

    span = NX * NZ
    per = RB // span
    turn_x = lambda step: jnp.asarray((x + step) % NX, jnp.int32)
    x_up, x_down, across = shift("x", NX, 1), shift("x", NX, -1), shift("x", NX, 2)
    factor_late, _ = lax.optimization_barrier((factor_in, (near_pieces, first_ring)))
    factor = lax.all_gather(factor_late, "z", axis=0, tiled=True)
    near = jnp.stack([turn_x(b) for b in (0, -1, 1, 2)])
    low_part = low_partial(near, factor, near_pieces)
    low = (low_part + across(low_part)) + (x_up(low_part) + x_down(low_part))
    low = low[None]
    for bit in (1, 2, 4):
        low = jnp.concatenate([low, flip("z", NZ, bit)(low)], axis=0)

    owners = block_owners.reshape(-1)
    count_all = owners.shape[0]
    marks = (owners[:, None] == jnp.arange(GROUPS, dtype=jnp.int32)[None, :]).astype(jnp.int32)
    before = (
        jnp.arange(count_all, dtype=jnp.int32)[:, None]
        > jnp.arange(count_all, dtype=jnp.int32)[None, :]
    ) & (owners[:, None] == owners[None, :])
    rank = jnp.sum(before.astype(jnp.int32), axis=1)

    def part_of(owner):
        turn = (owner // NC - y) % NY
        return turn + jnp.where(owner % NC == core, NY, 0)

    halves = jnp.arange(2 * COLS, dtype=jnp.int32)
    per_owner = FO_ROWS // 64
    pad = count_all - 2 * COLS
    where = jnp.stack(
        [
            part_of(owners),
            rank,
            jnp.pad(part_of(halves // per_owner), (0, pad)),
            jnp.pad(halves % per_owner, (0, pad)),
        ]
    ).astype(jnp.int32)
    counts = jnp.sum(marks, axis=0)
    mine = jnp.sum(
        jnp.where(jnp.arange(GROUPS) == y * NC + core, counts, 0), dtype=jnp.int32
    ).reshape(1)

    total = span * ROWS
    anywhere = pl.BlockSpec(memory_space=pl.ANY)
    hidden, send, keep, back, cols = pl.pallas_call(
        functools.partial(main_kernel, [len(g) for g in keys]),
        grid_spec=pltpu.PrefetchScalarGridSpec(
            num_scalar_prefetch=3,
            grid=(COLS // PER_STEP,),
            in_specs=[
                pl.BlockSpec((NZ, NX * ROWS, BS), lambda c, *_: (0, 0, 0)),
                pl.BlockSpec((PER_STEP, KB, BS, BS), lambda c, *_: (c, 0, 0, 0)),
                pl.BlockSpec((BS, PER_STEP * BS), lambda c, *_: (0, c)),
                pl.BlockSpec((total, PER_STEP * BS), lambda c, *_: (0, c)),
            ]
            + [anywhere] * len(arrays),
            out_specs=[
                pl.BlockSpec((total, PER_STEP * BS), lambda c, *_: (0, c)),
                anywhere,
                anywhere,
                pl.BlockSpec((total, BS), lambda c, *_: (0, 0)),
                pl.BlockSpec((per, total, BS), lambda c, *_: (0, 0, 0)),
            ],
            scratch_shapes=[
                pltpu.VMEM((span, RB, ROWS, BS), jnp.bfloat16),
                pltpu.VMEM(((KB + 2) * BS, 2 * BS), jnp.bfloat16),
                pltpu.VMEM((total, 2 * BS), jnp.bfloat16),
                pltpu.VMEM((2 * NY, PART_ROWS, BS), jnp.int16),
                pltpu.VMEM((2 * NY, 32, BS), jnp.float32),
                pltpu.SemaphoreType.DMA((span,)),
            ],
        ),
        out_shape=[
            jax.ShapeDtypeStruct((total, COLS * BS), jnp.bfloat16),
            jax.ShapeDtypeStruct((NY, PART_ROWS, BS), jnp.int16),
            jax.ShapeDtypeStruct((NY, PART_ROWS, BS), jnp.int16),
            jax.ShapeDtypeStruct((total, BS), jnp.float32),
            jax.ShapeDtypeStruct((per, total, BS), jnp.bfloat16),
        ],
        compiler_params=pltpu.CompilerParams(vmem_limit_bytes=50 * 1024 * 1024),
        name="columns",
    )(
        block_rows.reshape(-1), where, place,
        low, block_weights, factor_out, upstream, *arrays,
    )

    got = shift("core", NC, 1)(send)
    paired = pl.pallas_call(
        pair_kernel,
        grid=(NY,),
        in_specs=[pl.BlockSpec((1, PART_ROWS, BS), lambda i: (i, 0, 0))] * 2,
        out_specs=pl.BlockSpec((1, PART_ROWS, BS), lambda i: (i, 0, 0)),
        out_shape=jax.ShapeDtypeStruct((NY, PART_ROWS, BS), jnp.int16),
        compiler_params=pltpu.CompilerParams(vmem_limit_bytes=50 * 1024 * 1024),
        name="pairs",
    )(keep, got)
    first_y = [shift("y", NY, i)(paired[i, :CUT]) for i in (1, 2, 3)]

    back = back.reshape(NZ, NX, ROWS, BS)
    pick = lambda step: lax.dynamic_index_in_dim(back, turn_x(step), 1, keepdims=False)
    back_x = (pick(0) + across(pick(2))) + (x_up(pick(1)) + x_down(pick(-1)))
    back_x, _ = lax.optimization_barrier((back_x, paired))
    for bit in (1, 2, 4):
        back_x = back_x + flip("z", NZ, bit)(back_x)
    back_x, rest, _ = lax.optimization_barrier((back_x, paired[1:, CUT:], first_y))
    second_y = [shift("y", NY, i)(rest[i - 1]) for i in (1, 2, 3)]
    backs = [back_x, x_up(back_x), x_down(back_x), across(back_x)]
    turns = jnp.stack([part_of(jnp.int32(d)) for d in range(GROUPS)]).astype(jnp.int32)
    in_part = in_partial(near, turns, cols, backs)
    in_sum = in_part[NY:] + shift("core", NC, 1)(in_part[:NY])
    in_sum, _ = lax.optimization_barrier((in_sum, second_y))
    in_grad = in_sum[0]
    for step in (1, 2, 3):
        in_grad = in_grad + shift("y", NY, step)(in_sum[step])

    whole = pl.BlockSpec(memory_space=pltpu.VMEM)
    slots, out_grad = pl.pallas_call(
        final_kernel,
        in_specs=[pl.BlockSpec(memory_space=pltpu.SMEM)] + [whole] * (2 * NY - 1),
        out_specs=[whole, whole],
        out_shape=[
            jax.ShapeDtypeStruct((CAP, BS, BS), jnp.float32),
            jax.ShapeDtypeStruct((BS, FO_ROWS), jnp.float32),
        ],
        compiler_params=pltpu.CompilerParams(vmem_limit_bytes=50 * 1024 * 1024),
        name="slots",
    )(mine, paired, *first_y, *second_y)
    return hidden, slots, in_grad, out_grad


def solution(mesh):
    split = Mesh(mesh.devices.reshape(NY, NC, NZ, NX), ("y", "core", "z", "x"))
    dp, mp = ("y", "core"), ("z", "x")
    return jax.shard_map(
        per_device,
        mesh=split,
        in_specs=(
            P(dp + mp, None),
            P(mp, None, None, None),
            P(mp, None),
            P(mp, None, None),
            P(mp, None),
            P(None, mp),
            P(dp, mp),
        ),
        out_specs=(
            P(dp, mp),
            P(mp + dp, None, None),
            P(mp + dp, None),
            P(None, mp + dp),
        ),
        check_vma=False,
    )
```

profile of v0, /device:TPU:1, one launch (start us, length us, event | category | flops | bytes accessed | tf_op | source)
XLA Modules:
  0.0 242.5 jit_solution(15621813567852654796)
XLA Ops:
  8.3 2.5 %collective-permute-start.4 = (bf16[96,16,128]{2,1,0:T(8,128)(2,1)S(1)}, bf16[96,16,128]{2,1,0:T(8,128)(2,1)S(1)}, u32[]{:S(2)}, u32[]{:S(2)}) collective-permute-start(bf16[96,16,128]{2,1,0:T(8,128)(2,1)S(1)} %get-tuple-element.61), channel_id=1, source_target_pairs={{0,4},{4,8},{8,12},{12,16},{16,20},{20,24},{24,28},{28,0},{1,5},{5... | collective-permute-start | bytes 1179656 | tf_op jit(solution)/shard_map/ppermute | solution.py:31
  10.9 4.0 %collective-permute-start.3 = (bf16[96,16,128]{2,1,0:T(8,128)(2,1)S(1)}, bf16[96,16,128]{2,1,0:T(8,128)(2,1)S(1)}, u32[]{:S(2)}, u32[]{:S(2)}) collective-permute-start(bf16[96,16,128]{2,1,0:T(8,128)(2,1)S(1)} %get-tuple-element.61), channel_id=1, source_target_pairs={{0,28},{4,0},{8,4},{12,8},{16,12},{20,16},{24,20},{28,24},{1,29},{... | collective-permute-start | bytes 1179656 | tf_op jit(solution)/shard_map/ppermute | solution.py:31
  14.9 2.7 %collective-permute-start.2 = (bf16[96,16,128]{2,1,0:T(8,128)(2,1)S(1)}, bf16[96,16,128]{2,1,0:T(8,128)(2,1)S(1)}, u32[]{:S(2)}, u32[]{:S(2)}) collective-permute-start(bf16[96,16,128]{2,1,0:T(8,128)(2,1)S(1)} %get-tuple-element.61), channel_id=1, source_target_pairs={{0,2},{1,3},{2,0},{3,1},{4,6},{5,7},{6,4},{7,5},{8,10},{9,11},{10,... | collective-permute-start | bytes 1179656 | tf_op jit(solution)/shard_map/ppermute | solution.py:31
  19.1 4.5 %collective-permute-done.4 = bf16[96,16,128]{2,1,0:T(8,128)(2,1)S(1)} collective-permute-done((bf16[96,16,128]{2,1,0:T(8,128)(2,1)S(1)}, bf16[96,16,128]{2,1,0:T(8,128)(2,1)S(1)}, u32[]{:S(2)}, u32[]{:S(2)}) %collective-permute-start.4) | collective-permute-done | bytes 393248 | tf_op jit(solution)/shard_map/ppermute | solution.py:31
  23.6 2.5 %collective-permute-done.2 = bf16[96,16,128]{2,1,0:T(8,128)(2,1)S(1)} collective-permute-done((bf16[96,16,128]{2,1,0:T(8,128)(2,1)S(1)}, bf16[96,16,128]{2,1,0:T(8,128)(2,1)S(1)}, u32[]{:S(2)}, u32[]{:S(2)}) %collective-permute-start.2) | collective-permute-done | bytes 393248 | tf_op jit(solution)/shard_map/ppermute | solution.py:31
  26.1 8.8 %collective-permute-done.1 = bf16[96,16,128]{2,1,0:T(8,128)(2,1)S(1)} collective-permute-done((bf16[96,16,128]{2,1,0:T(8,128)(2,1)S(1)}, bf16[96,16,128]{2,1,0:T(8,128)(2,1)S(1)}, u32[]{:S(2)}, u32[]{:S(2)}) %collective-permute-start.1) | collective-permute-done | bytes 393248 | tf_op jit(solution)/shard_map/ppermute | solution.py:31
  36.7 2.7 %collective-permute-start.11 = (bf16[96,16,128]{2,1,0:T(8,128)(2,1)S(1)}, bf16[96,16,128]{2,1,0:T(8,128)(2,1)S(1)}, u32[]{:S(2)}, u32[]{:S(2)}) collective-permute-start(bf16[96,16,128]{2,1,0:T(8,128)(2,1)S(1)} %collective-permute-done.3), channel_id=1, source_target_pairs={{0,28},{4,0},{8,4},{12,8},{16,12},{20,16},{24,20},{28,24},{1,29},{... | collective-permute-start | bytes 1179656 | tf_op jit(solution)/shard_map/ppermute | solution.py:31
  39.5 2.6 %collective-permute-start.16 = (bf16[2,96,16,128]{3,2,1,0:T(8,128)(2,1)S(1)}, bf16[2,96,16,128]{3,2,1,0:T(8,128)(2,1)S(1)}, u32[]{:S(2)}, u32[]{:S(2)}) collective-permute-start(bf16[2,96,16,128]{3,2,1,0:T(8,128)(2,1)S(1)} %pad_maximum_fusion.1), channel_id=1, source_target_pairs={{0,3},{1,0},{2,1},{3,2},{4,7},{5,4},{6,5},{7,6},{8,11},{9,8},{10,9... | collective-permute-start | bytes 2359304 | tf_op jit(solution)/shard_map/ppermute | solution.py:31
  42.0 5.9 %collective-permute-done.12 = bf16[96,16,128]{2,1,0:T(8,128)(2,1)S(1)} collective-permute-done((bf16[96,16,128]{2,1,0:T(8,128)(2,1)S(1)}, bf16[96,16,128]{2,1,0:T(8,128)(2,1)S(1)}, u32[]{:S(2)}, u32[]{:S(2)}) %collective-permute-start.12) | collective-permute-done | bytes 393248 | tf_op jit(solution)/shard_map/ppermute | solution.py:31
  48.1 2.7 %collective-permute-start.13 = (bf16[96,16,128]{2,1,0:T(8,128)(2,1)S(1)}, bf16[96,16,128]{2,1,0:T(8,128)(2,1)S(1)}, u32[]{:S(2)}, u32[]{:S(2)}) collective-permute-start(bf16[96,16,128]{2,1,0:T(8,128)(2,1)S(1)} %collective-permute-done.11), channel_id=1, source_target_pairs={{0,28},{4,0},{8,4},{12,8},{16,12},{20,16},{24,20},{28,24},{1,29},{... | collective-permute-start | bytes 1179656 | tf_op jit(solution)/shard_map/ppermute | solution.py:31
  51.7 2.6 %collective-permute-start.19 = (bf16[2,96,16,128]{3,2,1,0:T(8,128)(2,1)}, bf16[2,96,16,128]{3,2,1,0:T(8,128)(2,1)}, u32[]{:S(2)}, u32[]{:S(2)}) collective-permute-start(bf16[2,96,16,128]{3,2,1,0:T(8,128)(2,1)} %pad_maximum_fusion.2), channel_id=1, source_target_pairs={{0,3},{1,0},{2,1},{3,2},{4,7},{5,4},{6,5},{7,6},{8,11},{9,8},{10,9... | collective-permute-start | bytes 2359304 | tf_op jit(solution)/shard_map/ppermute | solution.py:31
  54.3 11.0 %collective-permute-done.14 = bf16[96,16,128]{2,1,0:T(8,128)(2,1)S(1)} collective-permute-done((bf16[96,16,128]{2,1,0:T(8,128)(2,1)S(1)}, bf16[96,16,128]{2,1,0:T(8,128)(2,1)S(1)}, u32[]{:S(2)}, u32[]{:S(2)}) %collective-permute-start.14) | collective-permute-done | bytes 393248 | tf_op jit(solution)/shard_map/ppermute | solution.py:31
  69.0 12.1 %collective-permute-done.17 = bf16[96,16,128]{2,1,0:T(8,128)(2,1)S(1)} collective-permute-done((bf16[96,16,128]{2,1,0:T(8,128)(2,1)S(1)}, bf16[96,16,128]{2,1,0:T(8,128)(2,1)S(1)}, u32[]{:S(2)}, u32[]{:S(2)}) %collective-permute-start.17) | collective-permute-done | bytes 393248 | tf_op jit(solution)/shard_map/ppermute | solution.py:31
  89.9 2.7 %collective-permute-start.7 = (f32[64,128]{1,0:T(8,128)S(1)}, f32[64,128]{1,0:T(8,128)S(1)}, u32[]{:S(2)}, u32[]{:S(2)}) collective-permute-start(f32[64,128]{1,0:T(8,128)S(1)} %low.1), channel_id=1, source_target_pairs={{0,3},{1,0},{2,1},{3,2},{4,7},{5,4},{6,5},{7,6},{8,11},{9,8},{10,9... | collective-permute-start | bytes 98312 | tf_op jit(solution)/shard_map/ppermute | solution.py:31
  94.6 11.8 %collective-permute-done.7 = f32[64,128]{1,0:T(8,128)S(1)} collective-permute-done((f32[64,128]{1,0:T(8,128)S(1)}, f32[64,128]{1,0:T(8,128)S(1)}, u32[]{:S(2)}, u32[]{:S(2)}) %collective-permute-start.7) | collective-permute-done | bytes 32800 | tf_op jit(solution)/shard_map/ppermute | solution.py:31
  106.4 2.6 %collective-permute-done.6 = f32[64,128]{1,0:T(8,128)S(1)} collective-permute-done((f32[64,128]{1,0:T(8,128)S(1)}, f32[64,128]{1,0:T(8,128)S(1)}, u32[]{:S(2)}, u32[]{:S(2)}) %collective-permute-start.6) | collective-permute-done | bytes 32800 | tf_op jit(solution)/shard_map/ppermute | solution.py:31
  109.4 5.4 %collective-permute-start.8 = (f32[1,64,128]{2,1,0:T(8,128)S(1)}, f32[1,64,128]{2,1,0:T(8,128)S(1)}, u32[]{:S(2)}, u32[]{:S(2)}) collective-permute-start(f32[1,64,128]{2,1,0:T(8,128)S(1)} %add_bitcast_fusion), channel_id=1, source_target_pairs={{0,4},{4,0},{8,12},{12,8},{16,20},{20,16},{24,28},{28,24},{1,5},{5... | collective-permute-start | bytes 98312 | tf_op jit(solution)/shard_map/ppermute | solution.py:36
  119.7 3.3 %collective-permute-done.9 = f32[2,64,128]{2,1,0:T(8,128)S(1)} collective-permute-done((f32[2,64,128]{2,1,0:T(8,128)S(1)}, f32[2,64,128]{2,1,0:T(8,128)S(1)}, u32[]{:S(2)}, u32[]{:S(2)}) %collective-permute-start.9) | collective-permute-done | bytes 65568 | tf_op jit(solution)/shard_map/ppermute | solution.py:36
  123.7 4.8 %collective-permute-start.10 = (f32[4,64,128]{2,1,0:T(8,128)}, f32[4,64,128]{2,1,0:T(8,128)}, u32[]{:S(2)}, u32[]{:S(2)}) collective-permute-start(f32[4,64,128]{2,1,0:T(8,128)} %pad_maximum_fusion.4), channel_id=1, source_target_pairs={{0,16},{4,20},{8,24},{12,28},{16,0},{20,4},{24,8},{28,12},{1,17},{... | collective-permute-start | bytes 393224 | tf_op jit(solution)/shard_map/ppermute | solution.py:36
  134.3 29.5 %columns.1 = (bf16[512,1536]{1,0:T(8,128)(2,1)}, s16[4,2528,128]{2,1,0:T(8,128)(2,1)}, s16[4,2528,128]{2,1,0:T(8,128)(2,1)}, f32[512,128]{1,0:T(8,128)S(1)}, bf16[3,512,128]{2,1,0:T(8,128)(2,1)S(1)}) custom-call(s32[96]{0:T(128)S(1)} %reshape.177.rows_ref, s32[4,96]{1,0:T(4,128)S(1)} %pad_add_fusion.where_ref, s32[41]{0:T(128)S(1)} %stack.240.place_ref, ...), custom_call_target="tpu_custom_call" | custom-call | tf_op jit(solution)/shard_map/columns/pallas_call | solution.py:371
  165.3 6.1 %collective-permute-start.22 = (s16[4,2528,128]{2,1,0:T(8,128)(2,1)}, s16[4,2528,128]{2,1,0:T(8,128)(2,1)S(1)}, u32[]{:S(2)}, u32[]{:S(2)}) collective-permute-start(s16[4,2528,128]{2,1,0:T(8,128)(2,1)} %get-tuple-element.29), channel_id=1, source_target_pairs={{0,32},{32,0},{1,33},{33,1},{2,34},{34,2},{3,35},{35,3},{4,36},{36... | collective-permute-start | bytes 7766024 | tf_op jit(solution)/shard_map/ppermute | solution.py:31
  177.5 4.6 %pairs.1.own_ref = s16[4,2528,128]{2,1,0:T(8,128)(2,1)S(1)} custom-call(s16[4,2528,128]{2,1,0:T(8,128)(2,1)} %get-tuple-element.28.keep_ref, s16[4,2528,128]{2,1,0:T(8,128)(2,1)} %copy-done.17), custom_call_target="tpu_custom_call" | custom-call | tf_op jit(solution)/shard_map/pairs/pallas_call | solution.py:414
  183.1 3.5 %collective-permute-start.25 = (s16[1280,128]{1,0:T(8,128)(2,1)}, s16[1280,128]{1,0:T(8,128)(2,1)S(1)}, u32[]{:S(2)}, u32[]{:S(2)}) collective-permute-start(s16[1280,128]{1,0:T(8,128)(2,1)} %get-tuple-element.54), channel_id=1, source_target_pairs={{0,192},{64,0},{128,64},{192,128},{1,193},{65,1},{129,65},{193,129... | collective-permute-start | bytes 983048 | tf_op jit(solution)/shard_map/ppermute | solution.py:31
  188.8 2.8 %collective-permute-done.29 = f32[8,16,128]{2,1,0:T(8,128)S(1)} collective-permute-done((f32[8,16,128]{2,1,0:T(8,128)S(1)}, f32[8,16,128]{2,1,0:T(8,128)S(1)}, u32[]{:S(2)}, u32[]{:S(2)}) %collective-permute-start.29) | collective-permute-done | bytes 65568 | tf_op jit(solution)/shard_map/ppermute | solution.py:36
  191.6 2.9 %collective-permute-start.30 = (f32[8,16,128]{2,1,0:T(8,128)S(1)}, f32[8,16,128]{2,1,0:T(8,128)S(1)}, u32[]{:S(2)}, u32[]{:S(2)}) collective-permute-start(f32[8,16,128]{2,1,0:T(8,128)S(1)} %add.481), channel_id=1, source_target_pairs={{0,8},{4,12},{8,0},{12,4},{16,24},{20,28},{24,16},{28,20},{1,9},{5... | collective-permute-start | bytes 196616 | tf_op jit(solution)/shard_map/ppermute | solution.py:36
  196.6 3.8 %collective-permute-start.31 = (f32[8,16,128]{2,1,0:T(8,128)S(1)}, f32[8,16,128]{2,1,0:T(8,128)S(1)}, u32[]{:S(2)}, u32[]{:S(2)}) collective-permute-start(f32[8,16,128]{2,1,0:T(8,128)S(1)} %add.482), channel_id=1, source_target_pairs={{0,16},{4,20},{8,24},{12,28},{16,0},{20,4},{24,8},{28,12},{1,17},{... | collective-permute-start | bytes 196616 | tf_op jit(solution)/shard_map/ppermute | solution.py:36
  200.5 3.2 %collective-permute-done.31 = f32[8,16,128]{2,1,0:T(8,128)S(1)} collective-permute-done((f32[8,16,128]{2,1,0:T(8,128)S(1)}, f32[8,16,128]{2,1,0:T(8,128)S(1)}, u32[]{:S(2)}, u32[]{:S(2)}) %collective-permute-start.31) | collective-permute-done | bytes 65568 | tf_op jit(solution)/shard_map/ppermute | solution.py:36
  206.2 2.6 %collective-permute-start.36 = (f32[8,16,128]{2,1,0:T(8,128)S(1)}, f32[8,16,128]{2,1,0:T(8,128)S(1)}, u32[]{:S(2)}, u32[]{:S(2)}) collective-permute-start(f32[8,16,128]{2,1,0:T(8,128)S(1)} %add.483.rest_0_), channel_id=1, source_target_pairs={{0,3},{1,0},{2,1},{3,2},{4,7},{5,4},{6,5},{7,6},{8,11},{9,8},{10,9... | collective-permute-start | bytes 196616 | tf_op jit(solution)/shard_map/ppermute | solution.py:31
  215.0 4.4 %collective-permute-start.38 = (f32[4,48,128]{2,1,0:T(8,128)S(1)}, f32[4,48,128]{2,1,0:T(8,128)S(1)}, u32[]{:S(2)}, u32[]{:S(2)}) collective-permute-start(f32[4,48,128]{2,1,0:T(8,128)S(1)} %slice.57), channel_id=1, source_target_pairs={{0,32},{32,0},{1,33},{33,1},{2,34},{34,2},{3,35},{35,3},{4,36},{36... | collective-permute-start | bytes 294920 | tf_op jit(solution)/shard_map/ppermute | solution.py:31
  220.4 5.3 %collective-permute-done.32.refs_3_ = s16[1248,128]{1,0:T(8,128)(2,1)S(1)} collective-permute-done((s16[1248,128]{1,0:T(8,128)(2,1)S(1)}, s16[1248,128]{1,0:T(8,128)(2,1)S(1)}, u32[]{:S(2)}, u32[]{:S(2)}) %collective-permute-start.32) | collective-permute-done | bytes 319520 | tf_op jit(solution)/shard_map/ppermute | solution.py:31
  225.7 2.7 %collective-permute-start.41 = (f32[48,128]{1,0:T(8,128)S(1)}, f32[48,128]{1,0:T(8,128)S(1)}, u32[]{:S(2)}, u32[]{:S(2)}) collective-permute-start(f32[48,128]{1,0:T(8,128)S(1)} %get-tuple-element.67), channel_id=1, source_target_pairs={{0,192},{64,0},{128,64},{192,128},{1,193},{65,1},{129,65},{193,129... | collective-permute-start | bytes 73736 | tf_op jit(solution)/shard_map/ppermute | solution.py:31
  230.1 4.2 %slots.1 = (f32[18,128,128]{2,1,0:T(8,128)}, f32[128,192]{1,0:T(8,128)S(1)}) custom-call(s32[1]{0:T(128)} %bitcast.64.count_ref, s16[4,2528,128]{2,1,0:T(8,128)(2,1)} %copy-done.1, s16[1280,128]{1,0:T(8,128)(2,1)} %collective-permute-done.23.refs_0_, s16[1280,128]{1,0:T(8,128)(2,1)} %collective-permute-done.24.refs_1_, ...), custom_call_target="tpu_custom_call" | custom-call | tf_op jit(solution)/shard_map/slots/pallas_call | solution.py:443
  (154 shorter events, 57.3 us)
Async XLA Ops:
  7.2 78.0 %all-gather.4.cloned.1.call-start = ((), (), s32[]{:S(2)}) async-start(), calls=%async_computation | async-start | bytes 1769472 | tf_op jit(solution)/shard_map/all_gather | solution.py:332
  8.3 15.3 %collective-permute-start.4 = (bf16[96,16,128]{2,1,0:T(8,128)(2,1)S(1)}, bf16[96,16,128]{2,1,0:T(8,128)(2,1)S(1)}, u32[]{:S(2)}, u32[]{:S(2)}) collective-permute-start(bf16[96,16,128]{2,1,0:T(8,128)(2,1)S(1)} %get-tuple-element.61), channel_id=1, source_target_pairs={{0,4},{4,8},{8,12},{12,16},{16,20},{20,24},{24,28},{28,0},{1,5},{5... | collective-permute-start | bytes 1179656 | tf_op jit(solution)/shard_map/ppermute | solution.py:31
  10.9 12.8 %collective-permute-start.3 = (bf16[96,16,128]{2,1,0:T(8,128)(2,1)S(1)}, bf16[96,16,128]{2,1,0:T(8,128)(2,1)S(1)}, u32[]{:S(2)}, u32[]{:S(2)}) collective-permute-start(bf16[96,16,128]{2,1,0:T(8,128)(2,1)S(1)} %get-tuple-element.61), channel_id=1, source_target_pairs={{0,28},{4,0},{8,4},{12,8},{16,12},{20,16},{24,20},{28,24},{1,29},{... | collective-permute-start | bytes 1179656 | tf_op jit(solution)/shard_map/ppermute | solution.py:31
  14.9 11.2 %collective-permute-start.2 = (bf16[96,16,128]{2,1,0:T(8,128)(2,1)S(1)}, bf16[96,16,128]{2,1,0:T(8,128)(2,1)S(1)}, u32[]{:S(2)}, u32[]{:S(2)}) collective-permute-start(bf16[96,16,128]{2,1,0:T(8,128)(2,1)S(1)} %get-tuple-element.61), channel_id=1, source_target_pairs={{0,2},{1,3},{2,0},{3,1},{4,6},{5,7},{6,4},{7,5},{8,10},{9,11},{10,... | collective-permute-start | bytes 1179656 | tf_op jit(solution)/shard_map/ppermute | solution.py:31
  17.6 17.3 %collective-permute-start.1 = (bf16[96,16,128]{2,1,0:T(8,128)(2,1)S(1)}, bf16[96,16,128]{2,1,0:T(8,128)(2,1)S(1)}, u32[]{:S(2)}, u32[]{:S(2)}) collective-permute-start(bf16[96,16,128]{2,1,0:T(8,128)(2,1)S(1)} %get-tuple-element.61), channel_id=1, source_target_pairs={{0,3},{1,0},{2,1},{3,2},{4,7},{5,4},{6,5},{7,6},{8,11},{9,8},{10,9... | collective-permute-start | bytes 1179656 | tf_op jit(solution)/shard_map/ppermute | solution.py:31
  18.5 17.4 %collective-permute-start = (bf16[96,16,128]{2,1,0:T(8,128)(2,1)S(1)}, bf16[96,16,128]{2,1,0:T(8,128)(2,1)S(1)}, u32[]{:S(2)}, u32[]{:S(2)}) collective-permute-start(bf16[96,16,128]{2,1,0:T(8,128)(2,1)S(1)} %get-tuple-element.61), channel_id=1, source_target_pairs={{0,1},{1,2},{2,3},{3,0},{4,5},{5,6},{6,7},{7,4},{8,9},{9,10},{10,1... | collective-permute-start | bytes 1179656 | tf_op jit(solution)/shard_map/ppermute | solution.py:31
  35.9 97.5 %all-gather.6.cloned.1.call-start = ((), (), s32[]{:S(2)}) async-start(), calls=%async_computation.1 | async-start | bytes 3538944 | tf_op jit(solution)/shard_map/all_gather | solution.py:296
  36.6 11.3 %collective-permute-start.12 = (bf16[96,16,128]{2,1,0:T(8,128)(2,1)S(1)}, bf16[96,16,128]{2,1,0:T(8,128)(2,1)S(1)}, u32[]{:S(2)}, u32[]{:S(2)}) collective-permute-start(bf16[96,16,128]{2,1,0:T(8,128)(2,1)S(1)} %collective-permute-done.4), channel_id=1, source_target_pairs={{0,4},{4,8},{8,12},{12,16},{16,20},{20,24},{24,28},{28,0},{1,5},{5... | collective-permute-start | bytes 1179656 | tf_op jit(solution)/shard_map/ppermute | solution.py:31
  36.7 11.2 %collective-permute-start.11 = (bf16[96,16,128]{2,1,0:T(8,128)(2,1)S(1)}, bf16[96,16,128]{2,1,0:T(8,128)(2,1)S(1)}, u32[]{:S(2)}, u32[]{:S(2)}) collective-permute-start(bf16[96,16,128]{2,1,0:T(8,128)(2,1)S(1)} %collective-permute-done.3), channel_id=1, source_target_pairs={{0,28},{4,0},{8,4},{12,8},{16,12},{20,16},{24,20},{28,24},{1,29},{... | collective-permute-start | bytes 1179656 | tf_op jit(solution)/shard_map/ppermute | solution.py:31
  39.5 26.9 %collective-permute-start.16 = (bf16[2,96,16,128]{3,2,1,0:T(8,128)(2,1)S(1)}, bf16[2,96,16,128]{3,2,1,0:T(8,128)(2,1)S(1)}, u32[]{:S(2)}, u32[]{:S(2)}) collective-permute-start(bf16[2,96,16,128]{3,2,1,0:T(8,128)(2,1)S(1)} %pad_maximum_fusion.1), channel_id=1, source_target_pairs={{0,3},{1,0},{2,1},{3,2},{4,7},{5,4},{6,5},{7,6},{8,11},{9,8},{10,9... | collective-permute-start | bytes 2359304 | tf_op jit(solution)/shard_map/ppermute | solution.py:31
  42.0 24.4 %collective-permute-start.15 = (bf16[2,96,16,128]{3,2,1,0:T(8,128)(2,1)S(1)}, bf16[2,96,16,128]{3,2,1,0:T(8,128)(2,1)S(1)}, u32[]{:S(2)}, u32[]{:S(2)}) collective-permute-start(bf16[2,96,16,128]{3,2,1,0:T(8,128)(2,1)S(1)} %pad_maximum_fusion.1), channel_id=1, source_target_pairs={{0,1},{1,2},{2,3},{3,0},{4,5},{5,6},{6,7},{7,4},{8,9},{9,10},{10,1... | collective-permute-start | bytes 2359304 | tf_op jit(solution)/shard_map/ppermute | solution.py:31
  48.0 17.3 %collective-permute-start.14 = (bf16[96,16,128]{2,1,0:T(8,128)(2,1)S(1)}, bf16[96,16,128]{2,1,0:T(8,128)(2,1)S(1)}, u32[]{:S(2)}, u32[]{:S(2)}) collective-permute-start(bf16[96,16,128]{2,1,0:T(8,128)(2,1)S(1)} %collective-permute-done.12), channel_id=1, source_target_pairs={{0,4},{4,8},{8,12},{12,16},{16,20},{20,24},{24,28},{28,0},{1,5},{5... | collective-permute-start | bytes 1179656 | tf_op jit(solution)/shard_map/ppermute | solution.py:31
  48.1 18.3 %collective-permute-start.13 = (bf16[96,16,128]{2,1,0:T(8,128)(2,1)S(1)}, bf16[96,16,128]{2,1,0:T(8,128)(2,1)S(1)}, u32[]{:S(2)}, u32[]{:S(2)}) collective-permute-start(bf16[96,16,128]{2,1,0:T(8,128)(2,1)S(1)} %collective-permute-done.11), channel_id=1, source_target_pairs={{0,28},{4,0},{8,4},{12,8},{16,12},{20,16},{24,20},{28,24},{1,29},{... | collective-permute-start | bytes 1179656 | tf_op jit(solution)/shard_map/ppermute | solution.py:31
  51.7 29.4 %collective-permute-start.19 = (bf16[2,96,16,128]{3,2,1,0:T(8,128)(2,1)}, bf16[2,96,16,128]{3,2,1,0:T(8,128)(2,1)}, u32[]{:S(2)}, u32[]{:S(2)}) collective-permute-start(bf16[2,96,16,128]{3,2,1,0:T(8,128)(2,1)} %pad_maximum_fusion.2), channel_id=1, source_target_pairs={{0,3},{1,0},{2,1},{3,2},{4,7},{5,4},{6,5},{7,6},{8,11},{9,8},{10,9... | collective-permute-start | bytes 2359304 | tf_op jit(solution)/shard_map/ppermute | solution.py:31
  65.3 16.5 %collective-permute-start.18 = (bf16[2,96,16,128]{3,2,1,0:T(8,128)(2,1)}, bf16[2,96,16,128]{3,2,1,0:T(8,128)(2,1)}, u32[]{:S(2)}, u32[]{:S(2)}) collective-permute-start(bf16[2,96,16,128]{3,2,1,0:T(8,128)(2,1)} %pad_maximum_fusion.2), channel_id=1, source_target_pairs={{0,1},{1,2},{2,3},{3,0},{4,5},{5,6},{6,7},{7,4},{8,9},{9,10},{10,1... | collective-permute-start | bytes 2359304 | tf_op jit(solution)/shard_map/ppermute | solution.py:31
  66.4 14.6 %collective-permute-start.17 = (bf16[96,16,128]{2,1,0:T(8,128)(2,1)S(1)}, bf16[96,16,128]{2,1,0:T(8,128)(2,1)S(1)}, u32[]{:S(2)}, u32[]{:S(2)}) collective-permute-start(bf16[96,16,128]{2,1,0:T(8,128)(2,1)S(1)} %collective-permute-done.14), channel_id=1, source_target_pairs={{0,4},{4,8},{8,12},{12,16},{16,20},{20,24},{24,28},{28,0},{1,5},{5... | collective-permute-start | bytes 1179656 | tf_op jit(solution)/shard_map/ppermute | solution.py:31
  82.9 50.4 %collective-permute-start.21 = (bf16[3,96,16,128]{3,2,1,0:T(8,128)(2,1)}, bf16[3,96,16,128]{3,2,1,0:T(8,128)(2,1)}, u32[]{:S(2)}, u32[]{:S(2)}) collective-permute-start(bf16[3,96,16,128]{3,2,1,0:T(8,128)(2,1)} %pad_maximum_fusion), channel_id=1, source_target_pairs={{0,3},{1,0},{2,1},{3,2},{4,7},{5,4},{6,5},{7,6},{8,11},{9,8},{10,9... | collective-permute-start | bytes 3538952 | tf_op jit(solution)/shard_map/ppermute | solution.py:31
  84.4 49.0 %collective-permute-start.20 = (bf16[3,96,16,128]{3,2,1,0:T(8,128)(2,1)}, bf16[3,96,16,128]{3,2,1,0:T(8,128)(2,1)}, u32[]{:S(2)}, u32[]{:S(2)}) collective-permute-start(bf16[3,96,16,128]{3,2,1,0:T(8,128)(2,1)} %pad_maximum_fusion), channel_id=1, source_target_pairs={{0,1},{1,2},{2,3},{3,0},{4,5},{5,6},{6,7},{7,4},{8,9},{9,10},{10,1... | collective-permute-start | bytes 3538952 | tf_op jit(solution)/shard_map/ppermute | solution.py:31
  89.9 16.5 %collective-permute-start.7 = (f32[64,128]{1,0:T(8,128)S(1)}, f32[64,128]{1,0:T(8,128)S(1)}, u32[]{:S(2)}, u32[]{:S(2)}) collective-permute-start(f32[64,128]{1,0:T(8,128)S(1)} %low.1), channel_id=1, source_target_pairs={{0,3},{1,0},{2,1},{3,2},{4,7},{5,4},{6,5},{7,6},{8,11},{9,8},{10,9... | collective-permute-start | bytes 98312 | tf_op jit(solution)/shard_map/ppermute | solution.py:31
  92.6 16.4 %collective-permute-start.6 = (f32[64,128]{1,0:T(8,128)S(1)}, f32[64,128]{1,0:T(8,128)S(1)}, u32[]{:S(2)}, u32[]{:S(2)}) collective-permute-start(f32[64,128]{1,0:T(8,128)S(1)} %low.1), channel_id=1, source_target_pairs={{0,1},{1,2},{2,3},{3,0},{4,5},{5,6},{6,7},{7,4},{8,9},{9,10},{10,1... | collective-permute-start | bytes 98312 | tf_op jit(solution)/shard_map/ppermute | solution.py:31
  92.6 16.7 %collective-permute-start.5 = (f32[64,128]{1,0:T(8,128)S(1)}, f32[64,128]{1,0:T(8,128)S(1)}, u32[]{:S(2)}, u32[]{:S(2)}) collective-permute-start(f32[64,128]{1,0:T(8,128)S(1)} %low.1), channel_id=1, source_target_pairs={{0,2},{1,3},{2,0},{3,1},{4,6},{5,7},{6,4},{7,5},{8,10},{9,11},{10,... | collective-permute-start | bytes 98312 | tf_op jit(solution)/shard_map/ppermute | solution.py:31
  165.3 10.8 %collective-permute-start.22 = (s16[4,2528,128]{2,1,0:T(8,128)(2,1)}, s16[4,2528,128]{2,1,0:T(8,128)(2,1)S(1)}, u32[]{:S(2)}, u32[]{:S(2)}) collective-permute-start(s16[4,2528,128]{2,1,0:T(8,128)(2,1)} %get-tuple-element.29), channel_id=1, source_target_pairs={{0,32},{32,0},{1,33},{33,1},{2,34},{34,2},{3,35},{35,3},{4,36},{36... | collective-permute-start | bytes 7766024 | tf_op jit(solution)/shard_map/ppermute | solution.py:31
  172.3 14.4 %collective-permute-start.28 = (f32[8,16,128]{2,1,0:T(8,128)S(1)}, f32[8,16,128]{2,1,0:T(8,128)S(1)}, u32[]{:S(2)}, u32[]{:S(2)}) collective-permute-start(f32[8,16,128]{2,1,0:T(8,128)S(1)} %get-tuple-element.63), channel_id=1, source_target_pairs={{0,3},{1,0},{2,1},{3,2},{4,7},{5,4},{6,5},{7,6},{8,11},{9,8},{10,9... | collective-permute-start | bytes 196616 | tf_op jit(solution)/shard_map/ppermute | solution.py:31
  173.8 13.4 %collective-permute-start.27 = (f32[8,16,128]{2,1,0:T(8,128)S(1)}, f32[8,16,128]{2,1,0:T(8,128)S(1)}, u32[]{:S(2)}, u32[]{:S(2)}) collective-permute-start(f32[8,16,128]{2,1,0:T(8,128)S(1)} %get-tuple-element.64), channel_id=1, source_target_pairs={{0,1},{1,2},{2,3},{3,0},{4,5},{5,6},{6,7},{7,4},{8,9},{9,10},{10,1... | collective-permute-start | bytes 196616 | tf_op jit(solution)/shard_map/ppermute | solution.py:31
  174.2 13.1 %collective-permute-start.26 = (f32[8,16,128]{2,1,0:T(8,128)S(1)}, f32[8,16,128]{2,1,0:T(8,128)S(1)}, u32[]{:S(2)}, u32[]{:S(2)}) collective-permute-start(f32[8,16,128]{2,1,0:T(8,128)S(1)} %get-tuple-element.65), channel_id=1, source_target_pairs={{0,2},{1,3},{2,0},{3,1},{4,6},{5,7},{6,4},{7,5},{8,10},{9,11},{10,... | collective-permute-start | bytes 196616 | tf_op jit(solution)/shard_map/ppermute | solution.py:31
  183.1 20.6 %collective-permute-start.25 = (s16[1280,128]{1,0:T(8,128)(2,1)}, s16[1280,128]{1,0:T(8,128)(2,1)S(1)}, u32[]{:S(2)}, u32[]{:S(2)}) collective-permute-start(s16[1280,128]{1,0:T(8,128)(2,1)} %get-tuple-element.54), channel_id=1, source_target_pairs={{0,192},{64,0},{128,64},{192,128},{1,193},{65,1},{129,65},{193,129... | collective-permute-start | bytes 983048 | tf_op jit(solution)/shard_map/ppermute | solution.py:31
  186.7 17.1 %collective-permute-start.24 = (s16[1280,128]{1,0:T(8,128)(2,1)}, s16[1280,128]{1,0:T(8,128)(2,1)}, u32[]{:S(2)}, u32[]{:S(2)}) collective-permute-start(s16[1280,128]{1,0:T(8,128)(2,1)} %get-tuple-element.55), channel_id=1, source_target_pairs={{0,128},{64,192},{128,0},{192,64},{1,129},{65,193},{129,1},{193,65... | collective-permute-start | bytes 983048 | tf_op jit(solution)/shard_map/ppermute | solution.py:31
  186.7 17.9 %collective-permute-start.23 = (s16[1280,128]{1,0:T(8,128)(2,1)}, s16[1280,128]{1,0:T(8,128)(2,1)}, u32[]{:S(2)}, u32[]{:S(2)}) collective-permute-start(s16[1280,128]{1,0:T(8,128)(2,1)} %get-tuple-element.56), channel_id=1, source_target_pairs={{0,64},{64,128},{128,192},{192,0},{1,65},{65,129},{129,193},{193,1... | collective-permute-start | bytes 983048 | tf_op jit(solution)/shard_map/ppermute | solution.py:31
  208.9 11.5 %collective-permute-start.34 = (s16[1248,128]{1,0:T(8,128)(2,1)S(1)}, s16[1248,128]{1,0:T(8,128)(2,1)S(1)}, u32[]{:S(2)}, u32[]{:S(2)}) collective-permute-start(s16[1248,128]{1,0:T(8,128)(2,1)S(1)} %get-tuple-element.57), channel_id=1, source_target_pairs={{0,192},{64,0},{128,64},{192,128},{1,193},{65,1},{129,65},{193,129... | collective-permute-start | bytes 958472 | tf_op jit(solution)/shard_map/ppermute | solution.py:31
  210.7 9.8 %collective-permute-start.33 = (s16[1248,128]{1,0:T(8,128)(2,1)S(1)}, s16[1248,128]{1,0:T(8,128)(2,1)S(1)}, u32[]{:S(2)}, u32[]{:S(2)}) collective-permute-start(s16[1248,128]{1,0:T(8,128)(2,1)S(1)} %get-tuple-element.58), channel_id=1, source_target_pairs={{0,128},{64,192},{128,0},{192,64},{1,129},{65,193},{129,1},{193,65... | collective-permute-start | bytes 958472 | tf_op jit(solution)/shard_map/ppermute | solution.py:31
  212.2 13.5 %collective-permute-start.32 = (s16[1248,128]{1,0:T(8,128)(2,1)S(1)}, s16[1248,128]{1,0:T(8,128)(2,1)S(1)}, u32[]{:S(2)}, u32[]{:S(2)}) collective-permute-start(s16[1248,128]{1,0:T(8,128)(2,1)S(1)} %get-tuple-element.59), channel_id=1, source_target_pairs={{0,64},{64,128},{128,192},{192,0},{1,65},{65,129},{129,193},{193,1... | collective-permute-start | bytes 958472 | tf_op jit(solution)/shard_map/ppermute | solution.py:31
  225.7 9.3 %collective-permute-start.39 = (f32[48,128]{1,0:T(8,128)S(1)}, f32[48,128]{1,0:T(8,128)S(1)}, u32[]{:S(2)}, u32[]{:S(2)}) collective-permute-start(f32[48,128]{1,0:T(8,128)S(1)} %get-tuple-element.66), channel_id=1, source_target_pairs={{0,64},{64,128},{128,192},{192,0},{1,65},{65,129},{129,193},{193,1... | collective-permute-start | bytes 73736 | tf_op jit(solution)/shard_map/ppermute | solution.py:31
  (39 other events, 432.8 us)
Sparse Core Ops, SparseCore 0:
  36.0 41.8 all-gather.3
  80.2 44.9 all-gather.5
where the time goes:
time: 245 us; the launch traced here: 242 us
  waiting for transfers between devices  84.6 us (35%)
  starting transfers between devices  79.1 us (32%)
  Pallas kernels  40.6 us (17%)
  local copies, waits for them, and re-layouts  14.9 us (6%)
  between operations  14.4 us (6%)
  other arithmetic  8.85 us (4%)
    ppermute x36, waiting for transfers between devices, shift(): return lambda value: lax.ppermute(value, axis, pairs)  70.1 us
    ppermute x36, starting transfers between devices, shift(): return lambda value: lax.ppermute(value, axis, pairs)  59.2 us
    pallas_call x1, Pallas kernels, per_device(): pl.pallas_call(functools.partial(main_kernel, [len(g) for g in keys]), gr...  29.5 us
    ppermute x6, starting transfers between devices, flip(): return lambda value: lax.ppermute(value, axis, pairs)  19.8 us
    ppermute x6, waiting for transfers between devices, flip(): return lambda value: lax.ppermute(value, axis, pairs)  13.8 us
    unnamed x57, local copies, waits for them, and re-layouts  9.76 us
  transfers between devices with their start and end apart: 44, of which 22 were waited for; matrix products, arithmetic and copies ran while one was open for 6% of the time, Pallas kernels for 5%

commit v1 on v0

--- a/solution.py
+++ b/solution.py
@@ -23,7 +23,7 @@
 CODE_ROWS = SLOT_ROWS + FO_ROWS
 PART_ROWS = CODE_ROWS + 32
 FINE = 256.0
-CUT = 10 * BS
+CUT = 14 * BS
 
 
 def shift(axis, size, step):
@@ -62,8 +62,8 @@
 ):
     arrays, rest = rest[: len(counts)], rest[len(counts) :]
     pieces = [ref.at[i] for ref, n in zip(arrays, counts) for i in range(n)]
-    hidden_ref, send_ref, keep_ref, back_ref, cols_ref = rest[:5]
-    tok, wide, low_two, codes, levels, sems = rest[5:]
+    hidden_ref, send_ref, keep_ref, back_ref = rest[:4]
+    tok, wide, low_two, codes, levels, sems = rest[4:]
     c = pl.program_id(0)
     tokens = NX * NZ * ROWS
 
@@ -71,17 +71,13 @@
     def _():
         for j in range(NX * NZ):
             pltpu.make_async_copy(pieces[j], tok.at[place_ref[j]], sems.at[j]).start()
-        for g in range(NZ):
-            high, low = split_two(low_ref[place_ref[NX * NZ + g]])
-            low_two[g * NX * ROWS : (g + 1) * NX * ROWS, :BS] = high
-            low_two[g * NX * ROWS : (g + 1) * NX * ROWS, BS:] = low
+        high, low = split_two(low_ref[...])
+        low_two[:, :BS] = high
+        low_two[:, BS:] = low
         wide[(KB + 1) * BS :, BS:] = jnp.zeros((BS, BS), jnp.bfloat16)
         back_ref[...] = jnp.zeros_like(back_ref)
         for j in range(NX * NZ):
             pltpu.make_async_copy(pieces[j], tok.at[place_ref[j]], sems.at[j]).wait()
-        for j in range(cols_ref.shape[0]):
-            first = place_ref[NX * NZ + NZ]
-            cols_ref[j] = tok[:, first + j].reshape(tokens, BS)
 
     for i in range(PER_STEP):
         col = c * PER_STEP + i
@@ -200,46 +196,6 @@
             outer_ref[:, h * 64 : (h + 1) * 64] = total.T
 
 
-def low_kernel(near_ref, factor_ref, *rest):
-    pieces, (out_ref, tok, sems) = rest[:NX], rest[NX:]
-    per = RB // (NX * NZ)
-    copies = []
-    for j in range(NX):
-        source = pieces[j].at[:, pl.ds(near_ref[0] * per, per)]
-        copies.append(pltpu.make_async_copy(source, tok.at[near_ref[j]], sems.at[j]))
-        copies[j].start()
-    high, low = split_two(factor_ref[...])
-    wide = jnp.concatenate([high, low], axis=1)
-    for copy in copies:
-        copy.wait()
-    panel = jnp.concatenate(
-        [tok[:, g, j].reshape(NX * ROWS, BS) for g in range(NZ) for j in range(per)], axis=1
-    )
-    both = jnp.dot(panel, wide, preferred_element_type=jnp.float32)
-    out_ref[...] = both[:, :BS] + both[:, BS:]
-
-
-def low_partial(near, factor, pieces):
-    per = RB // (NX * NZ)
-    pieces = [p.reshape(NZ, NX * per, ROWS, BS) for p in pieces]
-    return pl.pallas_call(
-        low_kernel,
-        in_specs=[
-            pl.BlockSpec(memory_space=pltpu.SMEM),
-            pl.BlockSpec(memory_space=pltpu.VMEM),
-        ]
-        + [pl.BlockSpec(memory_space=pl.ANY)] * NX,
-        out_specs=pl.BlockSpec(memory_space=pltpu.VMEM),
-        out_shape=jax.ShapeDtypeStruct((NX * ROWS, BS), jnp.float32),
-        scratch_shapes=[
-            pltpu.VMEM((NX, NZ, per, ROWS, BS), jnp.bfloat16),
-            pltpu.SemaphoreType.DMA((NX,)),
-        ],
-        compiler_params=pltpu.CompilerParams(vmem_limit_bytes=30 * 1024 * 1024),
-        name="low",
-    )(near, factor, *pieces)
-
-
 def in_kernel(near_ref, turns_ref, cols_ref, *rest):
     backs, (out_ref, full) = rest[:NX], rest[NX:]
     for j in range(NX):
@@ -248,7 +204,9 @@
     total = NZ * NX * ROWS
     high, low = split_two(full[...].reshape(total, BS).T)
     two = jnp.concatenate([high, low], axis=0)
-    panel = jnp.concatenate([cols_ref[j] for j in range(cols_ref.shape[0])], axis=1)
+    panel = jnp.concatenate(
+        [cols_ref[:, j].reshape(total, BS) for j in range(cols_ref.shape[1])], axis=1
+    )
     both = jnp.dot(two, panel, preferred_element_type=jnp.float32)
     grad = (both[:BS] + both[BS:]).T
     size = grad.shape[0] // GROUPS
@@ -259,7 +217,7 @@
 def in_partial(near, turns, cols, backs):
     small = pl.BlockSpec(memory_space=pltpu.SMEM)
     whole = pl.BlockSpec(memory_space=pltpu.VMEM)
-    size = cols.shape[0] * BS // GROUPS
+    size = cols.shape[1] * BS // GROUPS
     return pl.pallas_call(
         in_kernel,
         in_specs=[small, small, whole] + [whole] * NX,
@@ -271,71 +229,69 @@
     )(near, turns, cols, *backs)
 
 
-def gather_tokens(own):
+def gather_tokens(own, factor):
     z_up, z_down = shift("z", NZ, 1), shift("z", NZ, -1)
     x_up, x_down, across = shift("x", NX, 1), shift("x", NX, -1), shift("x", NX, 2)
-    far = across(own)
-    ring = {0: own}
-    sides = {-1: x_up(own), 1: x_down(own)}
-    sent = {(0,): (sides[-1][None], sides[1][None])}
-
-    def step(a):
-        ring[-a] = z_up(ring[1 - a])
-        ring[a] = z_down(ring[a - 1])
-
-    def batch(*which):
-        block = jnp.stack([ring[a] for a in which])
+    after = lambda value, *others: lax.optimization_barrier((value, others))[0]
+    ring, far, sent = {0: own}, {}, {}
+
+    def step(part, a):
+        part[-a] = z_up(part[1 - a])
+        part[a] = z_down(part[a - 1])
+
+    def batch(*which, later=()):
+        block = after(jnp.stack([ring[a] for a in which]), *later)
         sent[which] = (x_up(block), x_down(block))
         return sent[which]
 
-    step(1)
-    first_ring = [ring[1], ring[-1]]
-    step(2)
+    step(ring, 1)
+    far[0] = across(own)
+    side = batch(0)
+    spread = lax.all_to_all(own.reshape(NX * NZ, -1, ROWS, BS), ("z", "x"), 0, 0)
+    step(ring, 2)
     first = batch(1, -1)
-    ring[2], ring[-2], _ = lax.optimization_barrier((ring[2], ring[-2], (far, sides)))
-    far_all = lax.all_gather(far, "z", axis=0)
-    step(3)
+    own_cols = after(spread, ring[2], ring[-2]).astype(jnp.float32)
+    partial = jnp.einsum("sbtf,bfr->str", own_cols, factor, precision=highest)
+    ring[2], ring[-2] = after((ring[2], ring[-2]), far[0], side, partial)
+    step(ring, 3)
+    step(far, 1)
     second = batch(2, -2)
-    ring[3], ring[-3], _ = lax.optimization_barrier((ring[3], ring[-3], first))
+    low_own = jnp.sum(after(lax.all_to_all(partial, ("z", "x"), 0, 0), first), axis=0)
+    ring[3], ring[-3] = after((ring[3], ring[-3]), first, far[1], far[-1], low_own)
     ring[4] = z_up(ring[-3])
-    ring[4], _ = lax.optimization_barrier((ring[4], second))
-    batch(3, -3, 4)
-    arrays, keys = [far_all], [[(None, g, 2) for g in range(NZ)]]
-    for a in ring:
-        arrays.append(ring[a][None])
-        keys.append([(a, None, 0)])
+    step(far, 2)
+    low = lax.all_to_all(
+        jnp.broadcast_to(low_own[None], (NX * NZ, ROWS, BS)), ("z", "x"), 0, 0
+    )
+    batch(3, -3, 4, later=(second, far[2], far[-2]))
+    step(far, 3)
+    low = after(low, far[3], far[-3])
+    far[4] = z_down(far[3])
+    arrays, keys = [], []
+    for b, part in ((0, ring), (2, far)):
+        for a in part:
+            arrays.append(part[a][None])
+            keys.append([(a, b)])
     for which, pair in sent.items():
         for b, value in zip((-1, 1), pair):
             arrays.append(value)
-            keys.append([(a, None, b) for a in which])
-    return arrays, keys, first_ring, [own, sides[-1], sides[1], far]
+            keys.append([(a, b) for a in which])
+    return arrays, keys, spread, low
 
 
 def per_device(tokens, block_weights, block_rows, block_owners, factor_in, factor_out, upstream):
     own = jnp.transpose(tokens.reshape(ROWS, RB, BS), (1, 0, 2))
-    arrays, keys, first_ring, near_pieces = gather_tokens(own)
+    span = NX * NZ
+    per = RB // span
+    arrays, keys, spread, low = gather_tokens(own, factor_in.reshape(per, BS, BS))
     z, x = lax.axis_index("z"), lax.axis_index("x")
     y, core = lax.axis_index("y"), lax.axis_index("core")
-    place = []
-    for group in keys:
-        for a, g, b in group:
-            row = g if a is None else (z + a) % NZ
-            place.append(row * NX + (x + b) % NX)
-    place += [z ^ g for g in range(NZ)] + [(z * NX + x) * (RB // (NX * NZ))]
-    place = jnp.stack([jnp.asarray(p, jnp.int32) for p in place])
-
-    span = NX * NZ
-    per = RB // span
+    place = [((z + a) % NZ) * NX + (x + b) % NX for group in keys for a, b in group]
+    place = jnp.stack(place).astype(jnp.int32)
     turn_x = lambda step: jnp.asarray((x + step) % NX, jnp.int32)
     x_up, x_down, across = shift("x", NX, 1), shift("x", NX, -1), shift("x", NX, 2)
-    factor_late, _ = lax.optimization_barrier((factor_in, (near_pieces, first_ring)))
-    factor = lax.all_gather(factor_late, "z", axis=0, tiled=True)
     near = jnp.stack([turn_x(b) for b in (0, -1, 1, 2)])
-    low_part = low_partial(near, factor, near_pieces)
-    low = (low_part + across(low_part)) + (x_up(low_part) + x_down(low_part))
-    low = low[None]
-    for bit in (1, 2, 4):
-        low = jnp.concatenate([low, flip("z", NZ, bit)(low)], axis=0)
+    low = low.reshape(span * ROWS, BS)
 
     owners = block_owners.reshape(-1)
     count_all = owners.shape[0]
@@ -368,13 +324,13 @@
 
     total = span * ROWS
     anywhere = pl.BlockSpec(memory_space=pl.ANY)
-    hidden, send, keep, back, cols = pl.pallas_call(
+    hidden, send, keep, back = pl.pallas_call(
         functools.partial(main_kernel, [len(g) for g in keys]),
         grid_spec=pltpu.PrefetchScalarGridSpec(
             num_scalar_prefetch=3,
             grid=(COLS // PER_STEP,),
             in_specs=[
-                pl.BlockSpec((NZ, NX * ROWS, BS), lambda c, *_: (0, 0, 0)),
+                pl.BlockSpec((total, BS), lambda c, *_: (0, 0)),
                 pl.BlockSpec((PER_STEP, KB, BS, BS), lambda c, *_: (c, 0, 0, 0)),
                 pl.BlockSpec((BS, PER_STEP * BS), lambda c, *_: (0, c)),
                 pl.BlockSpec((total, PER_STEP * BS), lambda c, *_: (0, c)),
@@ -385,7 +341,6 @@
                 anywhere,
                 anywhere,
                 pl.BlockSpec((total, BS), lambda c, *_: (0, 0)),
-                pl.BlockSpec((per, total, BS), lambda c, *_: (0, 0, 0)),
             ],
             scratch_shapes=[
                 pltpu.VMEM((span, RB, ROWS, BS), jnp.bfloat16),
@@ -401,7 +356,6 @@
             jax.ShapeDtypeStruct((NY, PART_ROWS, BS), jnp.int16),
             jax.ShapeDtypeStruct((NY, PART_ROWS, BS), jnp.int16),
             jax.ShapeDtypeStruct((total, BS), jnp.float32),
-            jax.ShapeDtypeStruct((per, total, BS), jnp.bfloat16),
         ],
         compiler_params=pltpu.CompilerParams(vmem_limit_bytes=50 * 1024 * 1024),
         name="columns",
@@ -425,14 +379,15 @@
     back = back.reshape(NZ, NX, ROWS, BS)
     pick = lambda step: lax.dynamic_index_in_dim(back, turn_x(step), 1, keepdims=False)
     back_x = (pick(0) + across(pick(2))) + (x_up(pick(1)) + x_down(pick(-1)))
+    back_x = back_x + flip("z", NZ, 1)(back_x)
     back_x, _ = lax.optimization_barrier((back_x, paired))
-    for bit in (1, 2, 4):
+    for bit in (2, 4):
         back_x = back_x + flip("z", NZ, bit)(back_x)
     back_x, rest, _ = lax.optimization_barrier((back_x, paired[1:, CUT:], first_y))
     second_y = [shift("y", NY, i)(rest[i - 1]) for i in (1, 2, 3)]
     backs = [back_x, x_up(back_x), x_down(back_x), across(back_x)]
     turns = jnp.stack([part_of(jnp.int32(d)) for d in range(GROUPS)]).astype(jnp.int32)
-    in_part = in_partial(near, turns, cols, backs)
+    in_part = in_partial(near, turns, spread, backs)
     in_sum = in_part[NY:] + shift("core", NC, 1)(in_part[:NY])
     in_sum, _ = lax.optimization_barrier((in_sum, second_y))
     in_grad = in_sum[0]

time: 245 us -> 254 us (1.037)
  starting transfers between devices: 79.1 us -> 93.8 us
  between operations: 14.4 us -> 1.19 us
  waiting for transfers between devices: 84.6 us -> 94.9 us
  local copies, waits for them, and re-layouts: 14.9 us -> 10.4 us
    all_to_all x0 -> x3, starting transfers between devices: none -> 22.8 us  [the longest x1 8.26 us: gather_tokens(): lax.all_to_all(own.reshape(NX * NZ, -1, ROWS, BS), ('z', 'x'), 0, 0)]
    ppermute x6 -> x3, starting transfers between devices: 19.8 us -> 3.15 us  [flip(): return lambda value: lax.ppermute(value, axis, pairs)]
    ppermute x36 -> x40, starting transfers between devices: 59.2 us -> 67.8 us  [shift(): return lambda value: lax.ppermute(value, axis, pairs)]
    ppermute x36 -> x40, waiting for transfers between devices: 70.1 us -> 76.8 us  [shift(): return lambda value: lax.ppermute(value, axis, pairs)]
    all_to_all x0 -> x3, waiting for transfers between devices: none -> 5.13 us  [the longest x1 5.13 us: gather_tokens(): lax.all_to_all(jnp.broadcast_to(low_own[None], (NX * NZ, ROWS, BS)), ('z'...]
    unnamed x57 -> x27, local copies, waits for them, and re-layouts: 9.76 us -> 6.09 us
    ppermute x6 -> x3, waiting for transfers between devices: 13.8 us -> 13 us  [flip(): return lambda value: lax.ppermute(value, axis, pairs)]
  transfers between devices with their start and end apart: 44 -> 46, of which waited for: 22 -> 19; matrix products, arithmetic and copies ran while one was open for 6% -> 5% of each run, Pallas kernels for 5% -> 4%
where the time goes in v1:
time: 254 us; the launch traced here: 249 us
  waiting for transfers between devices  94.9 us (37%)
  starting transfers between devices  93.8 us (37%)
  Pallas kernels  40.2 us (16%)
  local copies, waits for them, and re-layouts  10.4 us (4%)
  other arithmetic  7.63 us (3%)
    ppermute x40, waiting for transfers between devices, shift(): return lambda value: lax.ppermute(value, axis, pairs)  76.8 us
    ppermute x40, starting transfers between devices, shift(): return lambda value: lax.ppermute(value, axis, pairs)  67.8 us
    pallas_call x1, Pallas kernels, per_device(): pl.pallas_call(functools.partial(main_kernel, [len(g) for g in keys]), gr...  30.2 us
    ppermute x3, waiting for transfers between devices, flip(): return lambda value: lax.ppermute(value, axis, pairs)  13 us
    all_to_all x1, starting transfers between devices, gather_tokens(): lax.all_to_all(own.reshape(NX * NZ, -1, ROWS, BS), ('z', 'x'), 0, 0)  8.26 us
    all_to_all x1, starting transfers between devices, gather_tokens(): lax.all_to_all(partial, ('z', 'x'), 0, 0)  8.16 us
    all_to_all x1, starting transfers between devices, gather_tokens(): lax.all_to_all(jnp.broadcast_to(low_own[None], (NX * NZ, ROWS, BS)), ('z'...  6.37 us
    unnamed x27, local copies, waits for them, and re-layouts  6.09 us
  transfers between devices with their start and end apart: 46, of which 19 were waited for; matrix products, arithmetic and copies ran while one was open for 5% of the time, Pallas kernels for 4%

profile of v1, /device:TPU:1, one launch (start us, length us, event | category | flops | bytes accessed | tf_op | source)
XLA Modules:
  0.0 249.3 jit_solution(2124388022221700314)
XLA Ops:
  5.0 3.9 %collective-permute-start = (bf16[96,16,128]{2,1,0:T(8,128)(2,1)S(1)}, bf16[96,16,128]{2,1,0:T(8,128)(2,1)S(1)}, u32[]{:S(2)}, u32[]{:S(2)}) collective-permute-start(bf16[96,16,128]{2,1,0:T(8,128)(2,1)S(1)} %get-tuple-element.59), channel_id=1, source_target_pairs={{0,28},{4,0},{8,4},{12,8},{16,12},{20,16},{24,20},{28,24},{1,29},{... | collective-permute-start | bytes 1179656 | tf_op jit(solution)/shard_map/ppermute | solution.py:31
  8.9 8.3 %all-to-all-start = ((bf16[32,3,16,128]{3,2,1,0:T(8,128)(2,1)}), bf16[32,3,16,128]{3,2,1,0:T(8,128)(2,1)S(1)}, u32[]{:S(2)}, u32[]{:S(2)}) async-start(bf16[32,3,16,128]{3,2,1,0:T(8,128)(2,1)} %bitcast.36), calls=%async_computation | async-start | bytes 786432 | tf_op jit(solution)/shard_map/all_to_all | solution.py:250
  17.2 2.8 %collective-permute-start.6 = (bf16[96,16,128]{2,1,0:T(8,128)(2,1)S(1)}, bf16[96,16,128]{2,1,0:T(8,128)(2,1)}, u32[]{:S(2)}, u32[]{:S(2)}) collective-permute-start(bf16[96,16,128]{2,1,0:T(8,128)(2,1)S(1)} %get-tuple-element.59), channel_id=1, source_target_pairs={{0,2},{1,3},{2,0},{3,1},{4,6},{5,7},{6,4},{7,5},{8,10},{9,11},{10,... | collective-permute-start | bytes 1179656 | tf_op jit(solution)/shard_map/ppermute | solution.py:31
  25.1 6.6 %collective-permute-done.6 = bf16[96,16,128]{2,1,0:T(8,128)(2,1)} collective-permute-done((bf16[96,16,128]{2,1,0:T(8,128)(2,1)S(1)}, bf16[96,16,128]{2,1,0:T(8,128)(2,1)}, u32[]{:S(2)}, u32[]{:S(2)}) %collective-permute-start.6) | collective-permute-done | bytes 393248 | tf_op jit(solution)/shard_map/ppermute | solution.py:31
  31.8 3.0 %collective-permute-start.14 = (bf16[1,96,16,128]{3,2,1,0:T(8,128)(2,1)S(1)}, bf16[1,96,16,128]{3,2,1,0:T(8,128)(2,1)S(1)}, u32[]{:S(2)}, u32[]{:S(2)}) collective-permute-start(bf16[1,96,16,128]{3,2,1,0:T(8,128)(2,1)S(1)} %get-tuple-element.58.rest_0_), channel_id=1, source_target_pairs={{0,3},{1,0},{2,1},{3,2},{4,7},{5,4},{6,5},{7,6},{8,11},{9,8},{10,9... | collective-permute-start | bytes 1179656 | tf_op jit(solution)/shard_map/ppermute | solution.py:31
  39.1 8.2 %all-to-all-start.1 = ((f32[32,16,128]{2,1,0:T(8,128)}), f32[32,16,128]{2,1,0:T(8,128)}, u32[]{:S(2)}, u32[]{:S(2)}) async-start(f32[32,16,128]{2,1,0:T(8,128)} %convolution_bitcast_fusion), calls=%async_computation.1 | async-start | bytes 524288 | tf_op jit(solution)/shard_map/all_to_all | solution.py:259
  47.3 12.9 %collective-permute-done.14.rest_17_ = bf16[1,96,16,128]{3,2,1,0:T(8,128)(2,1)S(1)} collective-permute-done((bf16[1,96,16,128]{3,2,1,0:T(8,128)(2,1)S(1)}, bf16[1,96,16,128]{3,2,1,0:T(8,128)(2,1)S(1)}, u32[]{:S(2)}, u32[]{:S(2)}) %collective-permute-start.14) | collective-permute-done | bytes 393248 | tf_op jit(solution)/shard_map/ppermute | solution.py:31
  60.2 2.9 %collective-permute-start.7 = (bf16[96,16,128]{2,1,0:T(8,128)(2,1)}, bf16[96,16,128]{2,1,0:T(8,128)(2,1)}, u32[]{:S(2)}, u32[]{:S(2)}) collective-permute-start(bf16[96,16,128]{2,1,0:T(8,128)(2,1)} %collective-permute-done.6), channel_id=1, source_target_pairs={{0,28},{4,0},{8,4},{12,8},{16,12},{20,16},{24,20},{28,24},{1,29},{... | collective-permute-start | bytes 1179656 | tf_op jit(solution)/shard_map/ppermute | solution.py:31
  63.2 2.7 %collective-permute-start.15 = (bf16[96,16,128]{2,1,0:T(8,128)(2,1)}, bf16[96,16,128]{2,1,0:T(8,128)(2,1)S(1)}, u32[]{:S(2)}, u32[]{:S(2)}) collective-permute-start(bf16[96,16,128]{2,1,0:T(8,128)(2,1)} %copy-done.4), channel_id=1, source_target_pairs={{0,28},{4,0},{8,4},{12,8},{16,12},{20,16},{24,20},{28,24},{1,29},{... | collective-permute-start | bytes 1179656 | tf_op jit(solution)/shard_map/ppermute | solution.py:31
  67.8 3.2 %collective-permute-start.20 = (bf16[2,96,16,128]{3,2,1,0:T(8,128)(2,1)}, bf16[2,96,16,128]{3,2,1,0:T(8,128)(2,1)}, u32[]{:S(2)}, u32[]{:S(2)}) collective-permute-start(bf16[2,96,16,128]{3,2,1,0:T(8,128)(2,1)} %pad_maximum_fusion.2), channel_id=1, source_target_pairs={{0,3},{1,0},{2,1},{3,2},{4,7},{5,4},{6,5},{7,6},{8,11},{9,8},{10,9... | collective-permute-start | bytes 2359304 | tf_op jit(solution)/shard_map/ppermute | solution.py:31
  73.5 5.6 %collective-permute-done.15 = bf16[96,16,128]{2,1,0:T(8,128)(2,1)S(1)} collective-permute-done((bf16[96,16,128]{2,1,0:T(8,128)(2,1)}, bf16[96,16,128]{2,1,0:T(8,128)(2,1)S(1)}, u32[]{:S(2)}, u32[]{:S(2)}) %collective-permute-start.15) | collective-permute-done | bytes 393248 | tf_op jit(solution)/shard_map/ppermute | solution.py:31
  82.5 7.5 %collective-permute-done.17 = bf16[96,16,128]{2,1,0:T(8,128)(2,1)S(1)} collective-permute-done((bf16[96,16,128]{2,1,0:T(8,128)(2,1)S(1)}, bf16[96,16,128]{2,1,0:T(8,128)(2,1)S(1)}, u32[]{:S(2)}, u32[]{:S(2)}) %collective-permute-start.17) | collective-permute-done | bytes 393248 | tf_op jit(solution)/shard_map/ppermute | solution.py:31
  91.2 7.3 %collective-permute-done.11 = bf16[96,16,128]{2,1,0:T(8,128)(2,1)} collective-permute-done((bf16[96,16,128]{2,1,0:T(8,128)(2,1)}, bf16[96,16,128]{2,1,0:T(8,128)(2,1)}, u32[]{:S(2)}, u32[]{:S(2)}) %collective-permute-start.11) | collective-permute-done | bytes 393248 | tf_op jit(solution)/shard_map/ppermute | solution.py:31
  98.5 4.8 %collective-permute-start.22 = (bf16[3,96,16,128]{3,2,1,0:T(8,128)(2,1)}, bf16[3,96,16,128]{3,2,1,0:T(8,128)(2,1)}, u32[]{:S(2)}, u32[]{:S(2)}) collective-permute-start(bf16[3,96,16,128]{3,2,1,0:T(8,128)(2,1)} %pad_maximum_fusion), channel_id=1, source_target_pairs={{0,3},{1,0},{2,1},{3,2},{4,7},{5,4},{6,5},{7,6},{8,11},{9,8},{10,9... | collective-permute-start | bytes 3538952 | tf_op jit(solution)/shard_map/ppermute | solution.py:31
  105.9 6.4 %all-to-all-start.2 = ((f32[32,16,128]{2,1,0:T(8,128)}), f32[32,16,128]{2,1,0:T(8,128)}, u32[]{:S(2)}, u32[]{:S(2)}) async-start(f32[32,16,128]{2,1,0:T(8,128)} %broadcast_in_dim.65), calls=%async_computation.2 | async-start | bytes 524288 | tf_op jit(solution)/shard_map/all_to_all | solution.py:263
  115.1 12.6 %collective-permute-done.12 = bf16[96,16,128]{2,1,0:T(8,128)(2,1)} collective-permute-done((bf16[96,16,128]{2,1,0:T(8,128)(2,1)}, bf16[96,16,128]{2,1,0:T(8,128)(2,1)}, u32[]{:S(2)}, u32[]{:S(2)}) %collective-permute-start.12) | collective-permute-done | bytes 393248 | tf_op jit(solution)/shard_map/ppermute | solution.py:31
  127.7 5.1 %all-to-all-done.2 = f32[32,16,128]{2,1,0:T(8,128)} async-done(((f32[32,16,128]{2,1,0:T(8,128)}), f32[32,16,128]{2,1,0:T(8,128)}, u32[]{:S(2)}, u32[]{:S(2)}) %all-to-all-start.2) | async-done | bytes 262176 | tf_op jit(solution)/shard_map/all_to_all | solution.py:263
  134.9 30.2 %columns.1 = (bf16[512,1536]{1,0:T(8,128)(2,1)}, s16[4,2528,128]{2,1,0:T(8,128)(2,1)}, s16[4,2528,128]{2,1,0:T(8,128)(2,1)}, f32[512,128]{1,0:T(8,128)S(1)}) custom-call(s32[96]{0:T(128)S(1)} %reshape.175.rows_ref, s32[4,96]{1,0:T(4,128)S(1)} %pad_add_fusion.where_ref, s32[32]{0:T(128)S(1)} %stack.211.place_ref, f32[512,128]{1,0:T(8,128)} %bitcast.43.low_ref, ...), custom_call_target="tpu_custom_call" | custom-call | tf_op jit(solution)/shard_map/columns/pallas_call | solution.py:327
  165.8 3.1 %collective-permute-start.23 = (s16[4,2528,128]{2,1,0:T(8,128)(2,1)}, s16[4,2528,128]{2,1,0:T(8,128)(2,1)S(1)}, u32[]{:S(2)}, u32[]{:S(2)}) collective-permute-start(s16[4,2528,128]{2,1,0:T(8,128)(2,1)} %get-tuple-element.32), channel_id=1, source_target_pairs={{0,32},{32,0},{1,33},{33,1},{2,34},{34,2},{3,35},{35,3},{4,36},{36... | collective-permute-start | bytes 7766024 | tf_op jit(solution)/shard_map/ppermute | solution.py:31
  169.8 10.1 %collective-permute-start.29 = (f32[8,16,128]{2,1,0:T(8,128)S(1)}, f32[8,16,128]{2,1,0:T(8,128)S(1)}, u32[]{:S(2)}, u32[]{:S(2)}) collective-permute-start(f32[8,16,128]{2,1,0:T(8,128)S(1)} %get-tuple-element.61), channel_id=1, source_target_pairs={{0,3},{1,0},{2,1},{3,2},{4,7},{5,4},{6,5},{7,6},{8,11},{9,8},{10,9... | collective-permute-start | bytes 196616 | tf_op jit(solution)/shard_map/ppermute | solution.py:31
  183.1 4.6 %pairs.1.own_ref = s16[4,2528,128]{2,1,0:T(8,128)(2,1)S(1)} custom-call(s16[4,2528,128]{2,1,0:T(8,128)(2,1)} %get-tuple-element.31.keep_ref, s16[4,2528,128]{2,1,0:T(8,128)(2,1)} %copy-done.7), custom_call_target="tpu_custom_call" | custom-call | tf_op jit(solution)/shard_map/pairs/pallas_call | solution.py:368
  188.9 2.7 %collective-permute-start.26 = (s16[1792,128]{1,0:T(8,128)(2,1)}, s16[1792,128]{1,0:T(8,128)(2,1)}, u32[]{:S(2)}, u32[]{:S(2)}) collective-permute-start(s16[1792,128]{1,0:T(8,128)(2,1)} %get-tuple-element.52), channel_id=1, source_target_pairs={{0,192},{64,0},{128,64},{192,128},{1,193},{65,1},{129,65},{193,129... | collective-permute-start | bytes 1376264 | tf_op jit(solution)/shard_map/ppermute | solution.py:31
  193.7 3.5 %collective-permute-done.30 = f32[8,16,128]{2,1,0:T(8,128)S(1)} collective-permute-done((f32[8,16,128]{2,1,0:T(8,128)S(1)}, f32[8,16,128]{2,1,0:T(8,128)S(1)}, u32[]{:S(2)}, u32[]{:S(2)}) %collective-permute-start.30) | collective-permute-done | bytes 65568 | tf_op jit(solution)/shard_map/ppermute | solution.py:36
  197.5 4.7 %collective-permute-done.31 = f32[8,16,128]{2,1,0:T(8,128)S(1)} collective-permute-done((f32[8,16,128]{2,1,0:T(8,128)S(1)}, f32[8,16,128]{2,1,0:T(8,128)S(1)}, u32[]{:S(2)}, u32[]{:S(2)}) %collective-permute-start.31) | collective-permute-done | bytes 65568 | tf_op jit(solution)/shard_map/ppermute | solution.py:36
  202.1 3.0 %collective-permute-start.32 = (f32[8,16,128]{2,1,0:T(8,128)S(1)}, f32[8,16,128]{2,1,0:T(8,128)S(1)}, u32[]{:S(2)}, u32[]{:S(2)}) collective-permute-start(f32[8,16,128]{2,1,0:T(8,128)S(1)} %add.508), channel_id=1, source_target_pairs={{0,16},{4,20},{8,24},{12,28},{16,0},{20,4},{24,8},{28,12},{1,17},{... | collective-permute-start | bytes 196616 | tf_op jit(solution)/shard_map/ppermute | solution.py:36
  205.3 4.8 %collective-permute-done.32 = f32[8,16,128]{2,1,0:T(8,128)S(1)} collective-permute-done((f32[8,16,128]{2,1,0:T(8,128)S(1)}, f32[8,16,128]{2,1,0:T(8,128)S(1)}, u32[]{:S(2)}, u32[]{:S(2)}) %collective-permute-start.32) | collective-permute-done | bytes 65568 | tf_op jit(solution)/shard_map/ppermute | solution.py:36
  210.1 5.7 %collective-permute-done.24.refs_0_ = s16[1792,128]{1,0:T(8,128)(2,1)} collective-permute-done((s16[1792,128]{1,0:T(8,128)(2,1)}, s16[1792,128]{1,0:T(8,128)(2,1)}, u32[]{:S(2)}, u32[]{:S(2)}) %collective-permute-start.24) | collective-permute-done | bytes 458784 | tf_op jit(solution)/shard_map/ppermute | solution.py:31
  215.8 2.6 %collective-permute-start.38 = (f32[8,16,128]{2,1,0:T(8,128)S(1)}, f32[8,16,128]{2,1,0:T(8,128)S(1)}, u32[]{:S(2)}, u32[]{:S(2)}) collective-permute-start(f32[8,16,128]{2,1,0:T(8,128)S(1)} %add.509.rest_0_), channel_id=1, source_target_pairs={{0,2},{1,3},{2,0},{3,1},{4,6},{5,7},{6,4},{7,5},{8,10},{9,11},{10,... | collective-permute-start | bytes 196616 | tf_op jit(solution)/shard_map/ppermute | solution.py:31
  229.0 4.8 %collective-permute-done.35.refs_5_ = s16[736,128]{1,0:T(8,128)(2,1)S(1)} collective-permute-done((s16[736,128]{1,0:T(8,128)(2,1)S(1)}, s16[736,128]{1,0:T(8,128)(2,1)S(1)}, u32[]{:S(2)}, u32[]{:S(2)}) %collective-permute-start.35) | collective-permute-done | bytes 188448 | tf_op jit(solution)/shard_map/ppermute | solution.py:31
  235.4 4.6 %collective-permute-done.33.refs_3_ = s16[736,128]{1,0:T(8,128)(2,1)S(1)} collective-permute-done((s16[736,128]{1,0:T(8,128)(2,1)S(1)}, s16[736,128]{1,0:T(8,128)(2,1)S(1)}, u32[]{:S(2)}, u32[]{:S(2)}) %collective-permute-start.33) | collective-permute-done | bytes 188448 | tf_op jit(solution)/shard_map/ppermute | solution.py:31
  240.0 2.7 %collective-permute-start.42 = (f32[48,128]{1,0:T(8,128)S(1)}, f32[48,128]{1,0:T(8,128)S(1)}, u32[]{:S(2)}, u32[]{:S(2)}) collective-permute-start(f32[48,128]{1,0:T(8,128)S(1)} %get-tuple-element.65), channel_id=1, source_target_pairs={{0,192},{64,0},{128,64},{192,128},{1,193},{65,1},{129,65},{193,129... | collective-permute-start | bytes 73736 | tf_op jit(solution)/shard_map/ppermute | solution.py:31
  243.3 4.4 %slots.1 = (f32[18,128,128]{2,1,0:T(8,128)}, f32[128,192]{1,0:T(8,128)S(1)}) custom-call(s32[1]{0:T(128)} %bitcast.59.count_ref, s16[4,2528,128]{2,1,0:T(8,128)(2,1)} %copy-done.1, s16[1792,128]{1,0:T(8,128)(2,1)} %collective-permute-done.24.refs_0_, s16[1792,128]{1,0:T(8,128)(2,1)} %collective-permute-done.25.refs_1_, ...), custom_call_target="tpu_custom_call" | custom-call | tf_op jit(solution)/shard_map/slots/pallas_call | solution.py:398
  (124 shorter events, 52.8 us)
Async XLA Ops:
  2.5 17.5 %collective-permute-start.2 = (bf16[96,16,128]{2,1,0:T(8,128)(2,1)S(1)}, bf16[96,16,128]{2,1,0:T(8,128)(2,1)S(1)}, u32[]{:S(2)}, u32[]{:S(2)}) collective-permute-start(bf16[96,16,128]{2,1,0:T(8,128)(2,1)S(1)} %get-tuple-element.59), channel_id=1, source_target_pairs={{0,4},{4,8},{8,12},{12,16},{16,20},{20,24},{24,28},{28,0},{1,5},{5... | collective-permute-start | bytes 1179656 | tf_op jit(solution)/shard_map/ppermute | solution.py:31
  5.0 16.2 %collective-permute-start = (bf16[96,16,128]{2,1,0:T(8,128)(2,1)S(1)}, bf16[96,16,128]{2,1,0:T(8,128)(2,1)S(1)}, u32[]{:S(2)}, u32[]{:S(2)}) collective-permute-start(bf16[96,16,128]{2,1,0:T(8,128)(2,1)S(1)} %get-tuple-element.59), channel_id=1, source_target_pairs={{0,28},{4,0},{8,4},{12,8},{16,12},{20,16},{24,20},{28,24},{1,29},{... | collective-permute-start | bytes 1179656 | tf_op jit(solution)/shard_map/ppermute | solution.py:31
  8.9 29.0 %all-to-all-start = ((bf16[32,3,16,128]{3,2,1,0:T(8,128)(2,1)}), bf16[32,3,16,128]{3,2,1,0:T(8,128)(2,1)S(1)}, u32[]{:S(2)}, u32[]{:S(2)}) async-start(bf16[32,3,16,128]{3,2,1,0:T(8,128)(2,1)} %bitcast.36), calls=%async_computation | async-start | bytes 786432 | tf_op jit(solution)/shard_map/all_to_all | solution.py:250
  17.2 14.5 %collective-permute-start.6 = (bf16[96,16,128]{2,1,0:T(8,128)(2,1)S(1)}, bf16[96,16,128]{2,1,0:T(8,128)(2,1)}, u32[]{:S(2)}, u32[]{:S(2)}) collective-permute-start(bf16[96,16,128]{2,1,0:T(8,128)(2,1)S(1)} %get-tuple-element.59), channel_id=1, source_target_pairs={{0,2},{1,3},{2,0},{3,1},{4,6},{5,7},{6,4},{7,5},{8,10},{9,11},{10,... | collective-permute-start | bytes 1179656 | tf_op jit(solution)/shard_map/ppermute | solution.py:31
  20.0 16.7 %collective-permute-start.3 = (bf16[96,16,128]{2,1,0:T(8,128)(2,1)S(1)}, bf16[96,16,128]{2,1,0:T(8,128)(2,1)S(1)}, u32[]{:S(2)}, u32[]{:S(2)}) collective-permute-start(bf16[96,16,128]{2,1,0:T(8,128)(2,1)S(1)} %collective-permute-done.2), channel_id=1, source_target_pairs={{0,4},{4,8},{8,12},{12,16},{16,20},{20,24},{24,28},{28,0},{1,5},{5... | collective-permute-start | bytes 1179656 | tf_op jit(solution)/shard_map/ppermute | solution.py:31
  21.2 16.7 %collective-permute-start.1 = (bf16[96,16,128]{2,1,0:T(8,128)(2,1)S(1)}, bf16[96,16,128]{2,1,0:T(8,128)(2,1)S(1)}, u32[]{:S(2)}, u32[]{:S(2)}) collective-permute-start(bf16[96,16,128]{2,1,0:T(8,128)(2,1)S(1)} %collective-permute-done), channel_id=1, source_target_pairs={{0,28},{4,0},{8,4},{12,8},{16,12},{20,16},{24,20},{28,24},{1,29},{... | collective-permute-start | bytes 1179656 | tf_op jit(solution)/shard_map/ppermute | solution.py:31
  23.7 44.2 %collective-permute-start.5 = (bf16[2,96,16,128]{3,2,1,0:T(8,128)(2,1)}, bf16[2,96,16,128]{3,2,1,0:T(8,128)(2,1)}, u32[]{:S(2)}, u32[]{:S(2)}) collective-permute-start(bf16[2,96,16,128]{3,2,1,0:T(8,128)(2,1)} %pad_maximum_fusion.1), channel_id=1, source_target_pairs={{0,3},{1,0},{2,1},{3,2},{4,7},{5,4},{6,5},{7,6},{8,11},{9,8},{10,9... | collective-permute-start | bytes 2359304 | tf_op jit(solution)/shard_map/ppermute | solution.py:31
  24.6 46.5 %collective-permute-start.4 = (bf16[2,96,16,128]{3,2,1,0:T(8,128)(2,1)}, bf16[2,96,16,128]{3,2,1,0:T(8,128)(2,1)}, u32[]{:S(2)}, u32[]{:S(2)}) collective-permute-start(bf16[2,96,16,128]{3,2,1,0:T(8,128)(2,1)} %pad_maximum_fusion.1), channel_id=1, source_target_pairs={{0,1},{1,2},{2,3},{3,0},{4,5},{5,6},{6,7},{7,4},{8,9},{9,10},{10,1... | collective-permute-start | bytes 2359304 | tf_op jit(solution)/shard_map/ppermute | solution.py:31
  31.8 28.5 %collective-permute-start.14 = (bf16[1,96,16,128]{3,2,1,0:T(8,128)(2,1)S(1)}, bf16[1,96,16,128]{3,2,1,0:T(8,128)(2,1)S(1)}, u32[]{:S(2)}, u32[]{:S(2)}) collective-permute-start(bf16[1,96,16,128]{3,2,1,0:T(8,128)(2,1)S(1)} %get-tuple-element.58.rest_0_), channel_id=1, source_target_pairs={{0,3},{1,0},{2,1},{3,2},{4,7},{5,4},{6,5},{7,6},{8,11},{9,8},{10,9... | collective-permute-start | bytes 1179656 | tf_op jit(solution)/shard_map/ppermute | solution.py:31
  36.7 26.5 %collective-permute-start.13 = (bf16[1,96,16,128]{3,2,1,0:T(8,128)(2,1)S(1)}, bf16[1,96,16,128]{3,2,1,0:T(8,128)(2,1)}, u32[]{:S(2)}, u32[]{:S(2)}) collective-permute-start(bf16[1,96,16,128]{3,2,1,0:T(8,128)(2,1)S(1)} %get-tuple-element.58.rest_0_), channel_id=1, source_target_pairs={{0,1},{1,2},{2,3},{3,0},{4,5},{5,6},{6,7},{7,4},{8,9},{9,10},{10,1... | collective-permute-start | bytes 1179656 | tf_op jit(solution)/shard_map/ppermute | solution.py:31
  37.9 25.3 %collective-permute-start.10 = (bf16[96,16,128]{2,1,0:T(8,128)(2,1)}, bf16[96,16,128]{2,1,0:T(8,128)(2,1)}, u32[]{:S(2)}, u32[]{:S(2)}) collective-permute-start(bf16[96,16,128]{2,1,0:T(8,128)(2,1)} %collective-permute-done.6), channel_id=1, source_target_pairs={{0,4},{4,8},{8,12},{12,16},{16,20},{20,24},{24,28},{28,0},{1,5},{5... | collective-permute-start | bytes 1179656 | tf_op jit(solution)/shard_map/ppermute | solution.py:31
  39.1 31.9 %all-to-all-start.1 = ((f32[32,16,128]{2,1,0:T(8,128)}), f32[32,16,128]{2,1,0:T(8,128)}, u32[]{:S(2)}, u32[]{:S(2)}) async-start(f32[32,16,128]{2,1,0:T(8,128)} %convolution_bitcast_fusion), calls=%async_computation.1 | async-start | bytes 524288 | tf_op jit(solution)/shard_map/all_to_all | solution.py:259
  60.2 11.8 %collective-permute-start.7 = (bf16[96,16,128]{2,1,0:T(8,128)(2,1)}, bf16[96,16,128]{2,1,0:T(8,128)(2,1)}, u32[]{:S(2)}, u32[]{:S(2)}) collective-permute-start(bf16[96,16,128]{2,1,0:T(8,128)(2,1)} %collective-permute-done.6), channel_id=1, source_target_pairs={{0,28},{4,0},{8,4},{12,8},{16,12},{20,16},{24,20},{28,24},{1,29},{... | collective-permute-start | bytes 1179656 | tf_op jit(solution)/shard_map/ppermute | solution.py:31
  63.2 15.9 %collective-permute-start.15 = (bf16[96,16,128]{2,1,0:T(8,128)(2,1)}, bf16[96,16,128]{2,1,0:T(8,128)(2,1)S(1)}, u32[]{:S(2)}, u32[]{:S(2)}) collective-permute-start(bf16[96,16,128]{2,1,0:T(8,128)(2,1)} %copy-done.4), channel_id=1, source_target_pairs={{0,28},{4,0},{8,4},{12,8},{16,12},{20,16},{24,20},{28,24},{1,29},{... | collective-permute-start | bytes 1179656 | tf_op jit(solution)/shard_map/ppermute | solution.py:31
  67.8 30.6 %collective-permute-start.20 = (bf16[2,96,16,128]{3,2,1,0:T(8,128)(2,1)}, bf16[2,96,16,128]{3,2,1,0:T(8,128)(2,1)}, u32[]{:S(2)}, u32[]{:S(2)}) collective-permute-start(bf16[2,96,16,128]{3,2,1,0:T(8,128)(2,1)} %pad_maximum_fusion.2), channel_id=1, source_target_pairs={{0,3},{1,0},{2,1},{3,2},{4,7},{5,4},{6,5},{7,6},{8,11},{9,8},{10,9... | collective-permute-start | bytes 2359304 | tf_op jit(solution)/shard_map/ppermute | solution.py:31
  71.0 27.4 %collective-permute-start.19 = (bf16[2,96,16,128]{3,2,1,0:T(8,128)(2,1)}, bf16[2,96,16,128]{3,2,1,0:T(8,128)(2,1)}, u32[]{:S(2)}, u32[]{:S(2)}) collective-permute-start(bf16[2,96,16,128]{3,2,1,0:T(8,128)(2,1)} %pad_maximum_fusion.2), channel_id=1, source_target_pairs={{0,1},{1,2},{2,3},{3,0},{4,5},{5,6},{6,7},{7,4},{8,9},{9,10},{10,1... | collective-permute-start | bytes 2359304 | tf_op jit(solution)/shard_map/ppermute | solution.py:31
  79.1 10.9 %collective-permute-start.17 = (bf16[96,16,128]{2,1,0:T(8,128)(2,1)S(1)}, bf16[96,16,128]{2,1,0:T(8,128)(2,1)S(1)}, u32[]{:S(2)}, u32[]{:S(2)}) collective-permute-start(bf16[96,16,128]{2,1,0:T(8,128)(2,1)S(1)} %collective-permute-done.16), channel_id=1, source_target_pairs={{0,4},{4,8},{8,12},{12,16},{16,20},{20,24},{24,28},{28,0},{1,5},{5... | collective-permute-start | bytes 1179656 | tf_op jit(solution)/shard_map/ppermute | solution.py:31
  79.7 18.7 %collective-permute-start.11 = (bf16[96,16,128]{2,1,0:T(8,128)(2,1)}, bf16[96,16,128]{2,1,0:T(8,128)(2,1)}, u32[]{:S(2)}, u32[]{:S(2)}) collective-permute-start(bf16[96,16,128]{2,1,0:T(8,128)(2,1)} %collective-permute-done.10), channel_id=1, source_target_pairs={{0,4},{4,8},{8,12},{12,16},{16,20},{20,24},{24,28},{28,0},{1,5},{5... | collective-permute-start | bytes 1179656 | tf_op jit(solution)/shard_map/ppermute | solution.py:31
  80.5 17.9 %collective-permute-start.8 = (bf16[96,16,128]{2,1,0:T(8,128)(2,1)}, bf16[96,16,128]{2,1,0:T(8,128)(2,1)}, u32[]{:S(2)}, u32[]{:S(2)}) collective-permute-start(bf16[96,16,128]{2,1,0:T(8,128)(2,1)} %collective-permute-done.7), channel_id=1, source_target_pairs={{0,28},{4,0},{8,4},{12,8},{16,12},{20,16},{24,20},{28,24},{1,29},{... | collective-permute-start | bytes 1179656 | tf_op jit(solution)/shard_map/ppermute | solution.py:31
  98.5 34.4 %collective-permute-start.22 = (bf16[3,96,16,128]{3,2,1,0:T(8,128)(2,1)}, bf16[3,96,16,128]{3,2,1,0:T(8,128)(2,1)}, u32[]{:S(2)}, u32[]{:S(2)}) collective-permute-start(bf16[3,96,16,128]{3,2,1,0:T(8,128)(2,1)} %pad_maximum_fusion), channel_id=1, source_target_pairs={{0,3},{1,0},{2,1},{3,2},{4,7},{5,4},{6,5},{7,6},{8,11},{9,8},{10,9... | collective-permute-start | bytes 3538952 | tf_op jit(solution)/shard_map/ppermute | solution.py:31
  103.2 29.6 %collective-permute-start.21 = (bf16[3,96,16,128]{3,2,1,0:T(8,128)(2,1)}, bf16[3,96,16,128]{3,2,1,0:T(8,128)(2,1)}, u32[]{:S(2)}, u32[]{:S(2)}) collective-permute-start(bf16[3,96,16,128]{3,2,1,0:T(8,128)(2,1)} %pad_maximum_fusion), channel_id=1, source_target_pairs={{0,1},{1,2},{2,3},{3,0},{4,5},{5,6},{6,7},{7,4},{8,9},{9,10},{10,1... | collective-permute-start | bytes 3538952 | tf_op jit(solution)/shard_map/ppermute | solution.py:31
  105.9 27.0 %all-to-all-start.2 = ((f32[32,16,128]{2,1,0:T(8,128)}), f32[32,16,128]{2,1,0:T(8,128)}, u32[]{:S(2)}, u32[]{:S(2)}) async-start(f32[32,16,128]{2,1,0:T(8,128)} %broadcast_in_dim.65), calls=%async_computation.2 | async-start | bytes 524288 | tf_op jit(solution)/shard_map/all_to_all | solution.py:263
  112.3 15.4 %collective-permute-start.12 = (bf16[96,16,128]{2,1,0:T(8,128)(2,1)}, bf16[96,16,128]{2,1,0:T(8,128)(2,1)}, u32[]{:S(2)}, u32[]{:S(2)}) collective-permute-start(bf16[96,16,128]{2,1,0:T(8,128)(2,1)} %collective-permute-done.11), channel_id=1, source_target_pairs={{0,4},{4,8},{8,12},{12,16},{16,20},{20,24},{24,28},{28,0},{1,5},{5... | collective-permute-start | bytes 1179656 | tf_op jit(solution)/shard_map/ppermute | solution.py:31
  113.5 19.3 %collective-permute-start.18 = (bf16[96,16,128]{2,1,0:T(8,128)(2,1)}, bf16[96,16,128]{2,1,0:T(8,128)(2,1)}, u32[]{:S(2)}, u32[]{:S(2)}) collective-permute-start(bf16[96,16,128]{2,1,0:T(8,128)(2,1)} %collective-permute-done.9), channel_id=1, source_target_pairs={{0,28},{4,0},{8,4},{12,8},{16,12},{20,16},{24,20},{28,24},{1,29},{... | collective-permute-start | bytes 1179656 | tf_op jit(solution)/shard_map/ppermute | solution.py:31
  165.8 15.8 %collective-permute-start.23 = (s16[4,2528,128]{2,1,0:T(8,128)(2,1)}, s16[4,2528,128]{2,1,0:T(8,128)(2,1)S(1)}, u32[]{:S(2)}, u32[]{:S(2)}) collective-permute-start(s16[4,2528,128]{2,1,0:T(8,128)(2,1)} %get-tuple-element.32), channel_id=1, source_target_pairs={{0,32},{32,0},{1,33},{33,1},{2,34},{34,2},{3,35},{35,3},{4,36},{36... | collective-permute-start | bytes 7766024 | tf_op jit(solution)/shard_map/ppermute | solution.py:31
  169.8 22.3 %collective-permute-start.29 = (f32[8,16,128]{2,1,0:T(8,128)S(1)}, f32[8,16,128]{2,1,0:T(8,128)S(1)}, u32[]{:S(2)}, u32[]{:S(2)}) collective-permute-start(f32[8,16,128]{2,1,0:T(8,128)S(1)} %get-tuple-element.61), channel_id=1, source_target_pairs={{0,3},{1,0},{2,1},{3,2},{4,7},{5,4},{6,5},{7,6},{8,11},{9,8},{10,9... | collective-permute-start | bytes 196616 | tf_op jit(solution)/shard_map/ppermute | solution.py:31
  179.8 12.9 %collective-permute-start.28 = (f32[8,16,128]{2,1,0:T(8,128)S(1)}, f32[8,16,128]{2,1,0:T(8,128)S(1)}, u32[]{:S(2)}, u32[]{:S(2)}) collective-permute-start(f32[8,16,128]{2,1,0:T(8,128)S(1)} %get-tuple-element.62), channel_id=1, source_target_pairs={{0,1},{1,2},{2,3},{3,0},{4,5},{5,6},{6,7},{7,4},{8,9},{9,10},{10,1... | collective-permute-start | bytes 196616 | tf_op jit(solution)/shard_map/ppermute | solution.py:31
  181.3 11.5 %collective-permute-start.27 = (f32[8,16,128]{2,1,0:T(8,128)S(1)}, f32[8,16,128]{2,1,0:T(8,128)S(1)}, u32[]{:S(2)}, u32[]{:S(2)}) collective-permute-start(f32[8,16,128]{2,1,0:T(8,128)S(1)} %get-tuple-element.63), channel_id=1, source_target_pairs={{0,2},{1,3},{2,0},{3,1},{4,6},{5,7},{6,4},{7,5},{8,10},{9,11},{10,... | collective-permute-start | bytes 196616 | tf_op jit(solution)/shard_map/ppermute | solution.py:31
  188.9 21.1 %collective-permute-start.26 = (s16[1792,128]{1,0:T(8,128)(2,1)}, s16[1792,128]{1,0:T(8,128)(2,1)}, u32[]{:S(2)}, u32[]{:S(2)}) collective-permute-start(s16[1792,128]{1,0:T(8,128)(2,1)} %get-tuple-element.52), channel_id=1, source_target_pairs={{0,192},{64,0},{128,64},{192,128},{1,193},{65,1},{129,65},{193,129... | collective-permute-start | bytes 1376264 | tf_op jit(solution)/shard_map/ppermute | solution.py:31
  191.7 18.4 %collective-permute-start.25 = (s16[1792,128]{1,0:T(8,128)(2,1)}, s16[1792,128]{1,0:T(8,128)(2,1)}, u32[]{:S(2)}, u32[]{:S(2)}) collective-permute-start(s16[1792,128]{1,0:T(8,128)(2,1)} %get-tuple-element.53), channel_id=1, source_target_pairs={{0,128},{64,192},{128,0},{192,64},{1,129},{65,193},{129,1},{193,65... | collective-permute-start | bytes 1376264 | tf_op jit(solution)/shard_map/ppermute | solution.py:31
  192.0 23.7 %collective-permute-start.24 = (s16[1792,128]{1,0:T(8,128)(2,1)}, s16[1792,128]{1,0:T(8,128)(2,1)}, u32[]{:S(2)}, u32[]{:S(2)}) collective-permute-start(s16[1792,128]{1,0:T(8,128)(2,1)} %get-tuple-element.54), channel_id=1, source_target_pairs={{0,64},{64,128},{128,192},{192,0},{1,65},{65,129},{129,193},{193,1... | collective-permute-start | bytes 1376264 | tf_op jit(solution)/shard_map/ppermute | solution.py:31
  228.7 11.3 %collective-permute-start.33 = (s16[736,128]{1,0:T(8,128)(2,1)S(1)}, s16[736,128]{1,0:T(8,128)(2,1)S(1)}, u32[]{:S(2)}, u32[]{:S(2)}) collective-permute-start(s16[736,128]{1,0:T(8,128)(2,1)S(1)} %get-tuple-element.57), channel_id=1, source_target_pairs={{0,64},{64,128},{128,192},{192,0},{1,65},{65,129},{129,193},{193,1... | collective-permute-start | bytes 565256 | tf_op jit(solution)/shard_map/ppermute | solution.py:31
  (26 other events, 230.1 us)

commit v2 on v1

--- a/solution.py
+++ b/solution.py
@@ -1,5 +1,3 @@
-import functools
-
 import jax
 import jax.numpy as jnp
 from jax import lax
@@ -24,6 +22,7 @@
 PART_ROWS = CODE_ROWS + 32
 FINE = 256.0
 CUT = 14 * BS
+HALF = 48
 
 
 def shift(axis, size, step):
@@ -58,10 +57,9 @@
 
 
 def main_kernel(
-    counts, rows_ref, where_ref, place_ref, low_ref, weight_ref, factor_ref, up_ref, *rest
+    rows_ref, where_ref, place_ref, low_ref, weight_ref, factor_ref, up_ref, *rest
 ):
-    arrays, rest = rest[: len(counts)], rest[len(counts) :]
-    pieces = [ref.at[i] for ref, n in zip(arrays, counts) for i in range(n)]
+    half_ref, pieces, rest = rest[0], rest[1 : 1 + NX * NZ], rest[1 + NX * NZ :]
     hidden_ref, send_ref, keep_ref, back_ref = rest[:4]
     tok, wide, low_two, codes, levels, sems = rest[4:]
     c = pl.program_id(0)
@@ -69,15 +67,19 @@
 
     @pl.when(c == 0)
     def _():
+        copies = [pltpu.make_async_copy(half_ref, tok.at[:, pl.ds(0, HALF)], sems.at[NX * NZ])]
         for j in range(NX * NZ):
-            pltpu.make_async_copy(pieces[j], tok.at[place_ref[j]], sems.at[j]).start()
+            target = tok.at[place_ref[j], pl.ds(HALF, RB - HALF)]
+            copies.append(pltpu.make_async_copy(pieces[j], target, sems.at[j]))
+        for copy in copies:
+            copy.start()
         high, low = split_two(low_ref[...])
         low_two[:, :BS] = high
         low_two[:, BS:] = low
         wide[(KB + 1) * BS :, BS:] = jnp.zeros((BS, BS), jnp.bfloat16)
         back_ref[...] = jnp.zeros_like(back_ref)
-        for j in range(NX * NZ):
-            pltpu.make_async_copy(pieces[j], tok.at[place_ref[j]], sems.at[j]).wait()
+        for copy in copies:
+            copy.wait()
 
     for i in range(PER_STEP):
         col = c * PER_STEP + i
@@ -229,64 +231,46 @@
     )(near, turns, cols, *backs)
 
 
-def gather_tokens(own, factor):
+def gather_tokens(own):
     z_up, z_down = shift("z", NZ, 1), shift("z", NZ, -1)
-    x_up, x_down, across = shift("x", NX, 1), shift("x", NX, -1), shift("x", NX, 2)
-    after = lambda value, *others: lax.optimization_barrier((value, others))[0]
-    ring, far, sent = {0: own}, {}, {}
-
-    def step(part, a):
-        part[-a] = z_up(part[1 - a])
-        part[a] = z_down(part[a - 1])
-
-    def batch(*which, later=()):
-        block = after(jnp.stack([ring[a] for a in which]), *later)
-        sent[which] = (x_up(block), x_down(block))
-        return sent[which]
-
-    step(ring, 1)
-    far[0] = across(own)
-    side = batch(0)
-    spread = lax.all_to_all(own.reshape(NX * NZ, -1, ROWS, BS), ("z", "x"), 0, 0)
-    step(ring, 2)
-    first = batch(1, -1)
-    own_cols = after(spread, ring[2], ring[-2]).astype(jnp.float32)
-    partial = jnp.einsum("sbtf,bfr->str", own_cols, factor, precision=highest)
-    ring[2], ring[-2] = after((ring[2], ring[-2]), far[0], side, partial)
-    step(ring, 3)
-    step(far, 1)
-    second = batch(2, -2)
-    low_own = jnp.sum(after(lax.all_to_all(partial, ("z", "x"), 0, 0), first), axis=0)
-    ring[3], ring[-3] = after((ring[3], ring[-3]), first, far[1], far[-1], low_own)
-    ring[4] = z_up(ring[-3])
-    step(far, 2)
-    low = lax.all_to_all(
-        jnp.broadcast_to(low_own[None], (NX * NZ, ROWS, BS)), ("z", "x"), 0, 0
-    )
-    batch(3, -3, 4, later=(second, far[2], far[-2]))
-    step(far, 3)
-    low = after(low, far[3], far[-3])
-    far[4] = z_down(far[3])
-    arrays, keys = [], []
-    for b, part in ((0, ring), (2, far)):
-        for a in part:
-            arrays.append(part[a][None])
-            keys.append([(a, b)])
-    for which, pair in sent.items():
-        for b, value in zip((-1, 1), pair):
-            arrays.append(value)
-            keys.append([(a, b) for a in which])
-    return arrays, keys, spread, low
+    x_up, x_down = shift("x", NX, 1), shift("x", NX, -1)
+    across = shift("x", NX, 2)
+    held = {(0, 0): own}
+    held[0, 2] = across(own)
+    for b in (0, 2):
+        for a in (1, 2, 3):
+            held[-a, b] = z_up(held[1 - a, b])
+            held[a, b] = z_down(held[a - 1, b])
+    held[4, 0] = z_up(held[-3, 0])
+    held[4, 2] = z_down(held[3, 2])
+    for a in (0, -1, 1, -2, 2, -3, 3, 4):
+        for b, move in ((-1, x_up), (1, x_down)):
+            if (a, b) in ((1, 1), (-1, -1)):
+                held[a, b] = (z_down if a > 0 else z_up)(held[0, b])
+            else:
+                held[a, b] = move(held[a, 0])
+    return held
 
 
 def per_device(tokens, block_weights, block_rows, block_owners, factor_in, factor_out, upstream):
     own = jnp.transpose(tokens.reshape(ROWS, RB, BS), (1, 0, 2))
     span = NX * NZ
     per = RB // span
-    arrays, keys, spread, low = gather_tokens(own, factor_in.reshape(per, BS, BS))
+    plane = ("z", "x")
+    whole_half = lax.all_gather(own[:HALF], plane, axis=0)
+    held = gather_tokens(own[HALF:])
+    order = sorted(held)
+    arrays = [held[key] for key in order]
+    spread = lax.all_to_all(own.reshape(span, per, ROWS, BS), plane, 0, 0)
+    factor = factor_in.reshape(per, BS, BS)
+    partial = jnp.einsum(
+        "sbtf,bfr->str", spread.astype(jnp.float32), factor, precision=highest
+    )
+    low_own = jnp.sum(lax.all_to_all(partial, plane, 0, 0), axis=0)
+    low = lax.all_to_all(jnp.broadcast_to(low_own[None], (span, ROWS, BS)), plane, 0, 0)
     z, x = lax.axis_index("z"), lax.axis_index("x")
     y, core = lax.axis_index("y"), lax.axis_index("core")
-    place = [((z + a) % NZ) * NX + (x + b) % NX for group in keys for a, b in group]
+    place = [((z + a) % NZ) * NX + (x + b) % NX for a, b in order]
     place = jnp.stack(place).astype(jnp.int32)
     turn_x = lambda step: jnp.asarray((x + step) % NX, jnp.int32)
     x_up, x_down, across = shift("x", NX, 1), shift("x", NX, -1), shift("x", NX, 2)
@@ -325,7 +309,7 @@
     total = span * ROWS
     anywhere = pl.BlockSpec(memory_space=pl.ANY)
     hidden, send, keep, back = pl.pallas_call(
-        functools.partial(main_kernel, [len(g) for g in keys]),
+        main_kernel,
         grid_spec=pltpu.PrefetchScalarGridSpec(
             num_scalar_prefetch=3,
             grid=(COLS // PER_STEP,),
@@ -335,7 +319,7 @@
                 pl.BlockSpec((BS, PER_STEP * BS), lambda c, *_: (0, c)),
                 pl.BlockSpec((total, PER_STEP * BS), lambda c, *_: (0, c)),
             ]
-            + [anywhere] * len(arrays),
+            + [anywhere] * (span + 1),
             out_specs=[
                 pl.BlockSpec((total, PER_STEP * BS), lambda c, *_: (0, c)),
                 anywhere,
@@ -348,7 +332,7 @@
                 pltpu.VMEM((total, 2 * BS), jnp.bfloat16),
                 pltpu.VMEM((2 * NY, PART_ROWS, BS), jnp.int16),
                 pltpu.VMEM((2 * NY, 32, BS), jnp.float32),
-                pltpu.SemaphoreType.DMA((span,)),
+                pltpu.SemaphoreType.DMA((span + 1,)),
             ],
         ),
         out_shape=[
@@ -361,7 +345,7 @@
         name="columns",
     )(
         block_rows.reshape(-1), where, place,
-        low, block_weights, factor_out, upstream, *arrays,
+        low, block_weights, factor_out, upstream, whole_half, *arrays,
     )
 
     got = shift("core", NC, 1)(send)
@@ -388,8 +372,8 @@
     backs = [back_x, x_up(back_x), x_down(back_x), across(back_x)]
     turns = jnp.stack([part_of(jnp.int32(d)) for d in range(GROUPS)]).astype(jnp.int32)
     in_part = in_partial(near, turns, spread, backs)
+    in_part, _ = lax.optimization_barrier((in_part, second_y))
     in_sum = in_part[NY:] + shift("core", NC, 1)(in_part[:NY])
-    in_sum, _ = lax.optimization_barrier((in_sum, second_y))
     in_grad = in_sum[0]
     for step in (1, 2, 3):
         in_grad = in_grad + shift("y", NY, step)(in_sum[step])

time: 254 us -> 260 us (1.024)
  waiting for transfers between devices: 94.9 us -> 63 us
  starting transfers between devices: 93.8 us -> 115 us
  between operations: 1.19 us -> 14.6 us
  local copies, waits for them, and re-layouts: 10.4 us -> 15.8 us
  other arithmetic: 7.63 us -> 3.59 us
    ppermute x40 -> x48, waiting for transfers between devices: 76.8 us -> 50.8 us  [shift(): return lambda value: lax.ppermute(value, axis, pairs)]
    ppermute x40 -> x48, starting transfers between devices: 67.8 us -> 80 us  [shift(): return lambda value: lax.ppermute(value, axis, pairs)]
    all_to_all x3, starting transfers between devices: 22.8 us -> 31.4 us  [the longest x1 11.9 us: per_device(): spread = lax.all_to_all(own.reshape(span, per, ROWS, BS), plane, 0, 0)]
    all_to_all x3, waiting for transfers between devices: 5.13 us -> 0.01 us  [the longest x1 0.01 us: per_device(): spread = lax.all_to_all(own.reshape(span, per, ROWS, BS), plane, 0, 0)]
    another operation x3 -> x0, other arithmetic: 4.07 us -> none  [batch(): block = after(jnp.stack([ring[a] for a in which]), *later)]
    unnamed x27 -> x35, local copies, waits for them, and re-layouts: 6.09 us -> 9.46 us
  transfers between devices with their start and end apart: 46 -> 55, of which waited for: 19 -> 19; matrix products, arithmetic and copies ran while one was open for 5% -> 4% of each run, Pallas kernels for 4% -> 4%
where the time goes in v2:
time: 260 us; the launch traced here: 255 us
  starting transfers between devices  115 us (44%)
  waiting for transfers between devices  63 us (24%)
  Pallas kernels  41.6 us (16%)
  local copies, waits for them, and re-layouts  15.8 us (6%)
  between operations  14.6 us (6%)
  other arithmetic  3.59 us (1%)
    ppermute x48, starting transfers between devices, shift(): return lambda value: lax.ppermute(value, axis, pairs)  80 us
    ppermute x48, waiting for transfers between devices, shift(): return lambda value: lax.ppermute(value, axis, pairs)  50.8 us
    pallas_call x1, Pallas kernels, per_device(): pl.pallas_call(main_kernel, grid_spec=pltpu.PrefetchScalarGridSpec(num_sc...  31.5 us
    ppermute x3, waiting for transfers between devices, flip(): return lambda value: lax.ppermute(value, axis, pairs)  12.1 us
    all_to_all x1, starting transfers between devices, per_device(): spread = lax.all_to_all(own.reshape(span, per, ROWS, BS), plane, 0, 0)  11.9 us
    all_to_all x1, starting transfers between devices, per_device(): low_own = jnp.sum(lax.all_to_all(partial, plane, 0, 0), axis=0)  11 us
    unnamed x35, local copies, waits for them, and re-layouts  9.46 us
    all_to_all x1, starting transfers between devices, per_device(): lax.all_to_all(jnp.broadcast_to(low_own[None], (span, ROWS, BS)), plane,...  8.49 us
  transfers between devices with their start and end apart: 55, of which 19 were waited for; matrix products, arithmetic and copies ran while one was open for 4% of the time, Pallas kernels for 4%

profile of v2, /device:TPU:1, one launch (start us, length us, event | category | flops | bytes accessed | tf_op | source)
XLA Modules:
  0.0 254.7 jit_solution(4376147257624146683)
XLA Ops:
  9.7 11.9 %all-to-all-start = ((bf16[32,3,16,128]{3,2,1,0:T(8,128)(2,1)}), bf16[32,3,16,128]{3,2,1,0:T(8,128)(2,1)S(1)}, u32[]{:S(2)}, u32[]{:S(2)}) async-start(bf16[32,3,16,128]{3,2,1,0:T(8,128)(2,1)} %bitcast.36), calls=%async_computation | async-start | bytes 786432 | tf_op jit(solution)/shard_map/all_to_all | solution.py:264
  21.6 2.6 %collective-permute-start.15 = (bf16[48,16,128]{2,1,0:T(8,128)(2,1)S(1)}, bf16[48,16,128]{2,1,0:T(8,128)(2,1)S(1)}, u32[]{:S(2)}, u32[]{:S(2)}) collective-permute-start(bf16[48,16,128]{2,1,0:T(8,128)(2,1)S(1)} %get-tuple-element.46.rest_14_), channel_id=1, source_target_pairs={{0,28},{4,0},{8,4},{12,8},{16,12},{20,16},{24,20},{28,24},{1,29},{... | collective-permute-start | bytes 589832 | tf_op jit(solution)/shard_map/ppermute | solution.py:30
  28.4 8.9 %collective-permute-done.15.rest_18_ = bf16[48,16,128]{2,1,0:T(8,128)(2,1)S(1)} collective-permute-done((bf16[48,16,128]{2,1,0:T(8,128)(2,1)S(1)}, bf16[48,16,128]{2,1,0:T(8,128)(2,1)S(1)}, u32[]{:S(2)}, u32[]{:S(2)}) %collective-permute-start.15) | collective-permute-done | bytes 196640 | tf_op jit(solution)/shard_map/ppermute | solution.py:30
  39.5 11.0 %all-to-all-start.1 = ((f32[32,16,128]{2,1,0:T(8,128)}), f32[32,16,128]{2,1,0:T(8,128)}, u32[]{:S(2)}, u32[]{:S(2)}) async-start(f32[32,16,128]{2,1,0:T(8,128)} %convolution_bitcast_fusion), calls=%async_computation.1 | async-start | bytes 524288 | tf_op jit(solution)/shard_map/all_to_all | solution.py:269
  51.8 2.5 collective-permute-start.17
  54.3 2.7 %collective-permute-start.18 = (bf16[48,16,128]{2,1,0:T(8,128)(2,1)S(1)}, bf16[48,16,128]{2,1,0:T(8,128)(2,1)S(1)}, u32[]{:S(2)}, u32[]{:S(2)}) collective-permute-start(bf16[48,16,128]{2,1,0:T(8,128)(2,1)S(1)} %collective-permute-done.5.rest_16_), channel_id=1, source_target_pairs={{0,28},{4,0},{8,4},{12,8},{16,12},{20,16},{24,20},{28,24},{1,29},{... | collective-permute-start | bytes 589832 | tf_op jit(solution)/shard_map/ppermute | solution.py:30
  59.2 3.6 %collective-permute-done.17.rest_19_ = bf16[48,16,128]{2,1,0:T(8,128)(2,1)S(1)} collective-permute-done((bf16[48,16,128]{2,1,0:T(8,128)(2,1)S(1)}, bf16[48,16,128]{2,1,0:T(8,128)(2,1)S(1)}, u32[]{:S(2)}, u32[]{:S(2)}) %collective-permute-start.17) | collective-permute-done | bytes 196640 | tf_op jit(solution)/shard_map/ppermute | solution.py:30
  69.9 2.9 %collective-permute-done.1.rest_6_ = bf16[48,16,128]{2,1,0:T(8,128)(2,1)S(1)} collective-permute-done((bf16[48,16,128]{2,1,0:T(8,128)(2,1)S(1)}, bf16[48,16,128]{2,1,0:T(8,128)(2,1)S(1)}, u32[]{:S(2)}, u32[]{:S(2)}) %collective-permute-start.1) | collective-permute-done | bytes 196640 | tf_op jit(solution)/shard_map/ppermute | solution.py:30
  72.8 2.6 %collective-permute-start.10 = (bf16[48,16,128]{2,1,0:T(8,128)(2,1)S(1)}, bf16[48,16,128]{2,1,0:T(8,128)(2,1)}, u32[]{:S(2)}, u32[]{:S(2)}) collective-permute-start(bf16[48,16,128]{2,1,0:T(8,128)(2,1)S(1)} %collective-permute-done.1.rest_6_), channel_id=1, source_target_pairs={{0,3},{1,0},{2,1},{3,2},{4,7},{5,4},{6,5},{7,6},{8,11},{9,8},{10,9... | collective-permute-start | bytes 589832 | tf_op jit(solution)/shard_map/ppermute | solution.py:30
  75.8 2.5 collective-permute-done.21.rest_23_
  83.1 8.5 %all-to-all-start.2 = ((f32[32,16,128]{2,1,0:T(8,128)}), f32[32,16,128]{2,1,0:T(8,128)}, u32[]{:S(2)}, u32[]{:S(2)}) async-start(f32[32,16,128]{2,1,0:T(8,128)} %broadcast_in_dim.11), calls=%async_computation.2 | async-start | bytes 524288 | tf_op jit(solution)/shard_map/all_to_all | solution.py:270
  91.6 2.4 collective-permute-start.25
  94.1 2.6 %collective-permute-start.26 = (bf16[48,16,128]{2,1,0:T(8,128)(2,1)}, bf16[48,16,128]{2,1,0:T(8,128)(2,1)S(1)}, u32[]{:S(2)}, u32[]{:S(2)}) collective-permute-start(bf16[48,16,128]{2,1,0:T(8,128)(2,1)} %collective-permute-done.22.rest_24_), channel_id=1, source_target_pairs={{0,28},{4,0},{8,4},{12,8},{16,12},{20,16},{24,20},{28,24},{1,29},{... | collective-permute-start | bytes 589832 | tf_op jit(solution)/shard_map/ppermute | solution.py:30
  96.8 5.4 %collective-permute-done.25.rest_27_ = bf16[48,16,128]{2,1,0:T(8,128)(2,1)} collective-permute-done((bf16[48,16,128]{2,1,0:T(8,128)(2,1)}, bf16[48,16,128]{2,1,0:T(8,128)(2,1)}, u32[]{:S(2)}, u32[]{:S(2)}) %collective-permute-start.25) | collective-permute-done | bytes 196640 | tf_op jit(solution)/shard_map/ppermute | solution.py:30
  102.2 3.7 %collective-permute-start.4 = (bf16[48,16,128]{2,1,0:T(8,128)(2,1)}, bf16[48,16,128]{2,1,0:T(8,128)(2,1)S(1)}, u32[]{:S(2)}, u32[]{:S(2)}) collective-permute-start(bf16[48,16,128]{2,1,0:T(8,128)(2,1)} %collective-permute-done.2.rest_2_), channel_id=1, source_target_pairs={{0,3},{1,0},{2,1},{3,2},{4,7},{5,4},{6,5},{7,6},{8,11},{9,8},{10,9... | collective-permute-start | bytes 589832 | tf_op jit(solution)/shard_map/ppermute | solution.py:30
  105.9 12.8 %collective-permute-done.27.rest_30_ = bf16[48,16,128]{2,1,0:T(8,128)(2,1)S(1)} collective-permute-done((bf16[48,16,128]{2,1,0:T(8,128)(2,1)}, bf16[48,16,128]{2,1,0:T(8,128)(2,1)S(1)}, u32[]{:S(2)}, u32[]{:S(2)}) %collective-permute-start.27) | collective-permute-done | bytes 196640 | tf_op jit(solution)/shard_map/ppermute | solution.py:30
  118.8 11.1 %collective-permute-start.29 = (bf16[48,16,128]{2,1,0:T(8,128)(2,1)S(1)}, bf16[48,16,128]{2,1,0:T(8,128)(2,1)S(1)}, u32[]{:S(2)}, u32[]{:S(2)}) collective-permute-start(bf16[48,16,128]{2,1,0:T(8,128)(2,1)S(1)} %collective-permute-done.27.rest_30_), channel_id=1, source_target_pairs={{0,3},{1,0},{2,1},{3,2},{4,7},{5,4},{6,5},{7,6},{8,11},{9,8},{10,9... | collective-permute-start | bytes 589832 | tf_op jit(solution)/shard_map/ppermute | solution.py:30
  132.7 2.4 collective-permute-done.30.rest_32_
  139.3 31.5 %columns.1 = (bf16[512,1536]{1,0:T(8,128)(2,1)}, s16[4,2528,128]{2,1,0:T(8,128)(2,1)}, s16[4,2528,128]{2,1,0:T(8,128)(2,1)}, f32[512,128]{1,0:T(8,128)}) custom-call(s32[96]{0:T(128)S(1)} %reshape.175.rows_ref, s32[4,96]{1,0:T(4,128)S(1)} %pad_add_fusion.where_ref, s32[32]{0:T(128)S(1)} %stack.190.place_ref, f32[512,128]{1,0:T(8,128)} %bitcast.41.low_ref, ...), custom_call_target="tpu_custom_call" | custom-call | tf_op jit(solution)/shard_map/columns/pallas_call | solution.py:311
  170.8 8.1 %collective-permute-start.31 = (s16[4,2528,128]{2,1,0:T(8,128)(2,1)}, s16[4,2528,128]{2,1,0:T(8,128)(2,1)S(1)}, u32[]{:S(2)}, u32[]{:S(2)}) collective-permute-start(s16[4,2528,128]{2,1,0:T(8,128)(2,1)} %get-tuple-element.16), channel_id=1, source_target_pairs={{0,32},{32,0},{1,33},{33,1},{2,34},{34,2},{3,35},{35,3},{4,36},{36... | collective-permute-start | bytes 7766024 | tf_op jit(solution)/shard_map/ppermute | solution.py:30
  180.5 2.9 %collective-permute-start.37 = (f32[8,16,128]{2,1,0:T(8,128)S(1)}, f32[8,16,128]{2,1,0:T(8,128)S(1)}, u32[]{:S(2)}, u32[]{:S(2)}) collective-permute-start(f32[8,16,128]{2,1,0:T(8,128)S(1)} %get-tuple-element.50), channel_id=1, source_target_pairs={{0,3},{1,0},{2,1},{3,2},{4,7},{5,4},{6,5},{7,6},{8,11},{9,8},{10,9... | collective-permute-start | bytes 196616 | tf_op jit(solution)/shard_map/ppermute | solution.py:30
  186.1 4.6 %pairs.1.own_ref = s16[4,2528,128]{2,1,0:T(8,128)(2,1)S(1)} custom-call(s16[4,2528,128]{2,1,0:T(8,128)(2,1)} %get-tuple-element.15.keep_ref, s16[4,2528,128]{2,1,0:T(8,128)(2,1)} %copy-done.8), custom_call_target="tpu_custom_call" | custom-call | tf_op jit(solution)/shard_map/pairs/pallas_call | solution.py:352
  191.9 2.9 %collective-permute-start.34 = (s16[1792,128]{1,0:T(8,128)(2,1)}, s16[1792,128]{1,0:T(8,128)(2,1)}, u32[]{:S(2)}, u32[]{:S(2)}) collective-permute-start(s16[1792,128]{1,0:T(8,128)(2,1)} %get-tuple-element.40), channel_id=1, source_target_pairs={{0,192},{64,0},{128,64},{192,128},{1,193},{65,1},{129,65},{193,129... | collective-permute-start | bytes 1376264 | tf_op jit(solution)/shard_map/ppermute | solution.py:30
  196.7 3.5 %collective-permute-done.38 = f32[8,16,128]{2,1,0:T(8,128)S(1)} collective-permute-done((f32[8,16,128]{2,1,0:T(8,128)S(1)}, f32[8,16,128]{2,1,0:T(8,128)S(1)}, u32[]{:S(2)}, u32[]{:S(2)}) %collective-permute-start.38) | collective-permute-done | bytes 65568 | tf_op jit(solution)/shard_map/ppermute | solution.py:35
  201.2 4.0 %collective-permute-done.39 = f32[8,16,128]{2,1,0:T(8,128)S(1)} collective-permute-done((f32[8,16,128]{2,1,0:T(8,128)S(1)}, f32[8,16,128]{2,1,0:T(8,128)S(1)}, u32[]{:S(2)}, u32[]{:S(2)}) %collective-permute-start.39) | collective-permute-done | bytes 65568 | tf_op jit(solution)/shard_map/ppermute | solution.py:35
  207.7 4.6 %collective-permute-done.40 = f32[8,16,128]{2,1,0:T(8,128)S(1)} collective-permute-done((f32[8,16,128]{2,1,0:T(8,128)S(1)}, f32[8,16,128]{2,1,0:T(8,128)S(1)}, u32[]{:S(2)}, u32[]{:S(2)}) %collective-permute-start.40) | collective-permute-done | bytes 65568 | tf_op jit(solution)/shard_map/ppermute | solution.py:35
  214.0 4.8 %collective-permute-done.32.refs_0_ = s16[1792,128]{1,0:T(8,128)(2,1)} collective-permute-done((s16[1792,128]{1,0:T(8,128)(2,1)}, s16[1792,128]{1,0:T(8,128)(2,1)}, u32[]{:S(2)}, u32[]{:S(2)}) %collective-permute-start.32) | collective-permute-done | bytes 458784 | tf_op jit(solution)/shard_map/ppermute | solution.py:30
  223.2 2.7 %collective-permute-start.45 = (f32[8,16,128]{2,1,0:T(8,128)S(1)}, f32[8,16,128]{2,1,0:T(8,128)S(1)}, u32[]{:S(2)}, u32[]{:S(2)}) collective-permute-start(f32[8,16,128]{2,1,0:T(8,128)S(1)} %add.509.rest_0_), channel_id=1, source_target_pairs={{0,3},{1,0},{2,1},{3,2},{4,7},{5,4},{6,5},{7,6},{8,11},{9,8},{10,9... | collective-permute-start | bytes 196616 | tf_op jit(solution)/shard_map/ppermute | solution.py:30
  228.4 2.5 collective-permute-done.44.rest_1_
  232.4 2.5 collective-permute-start.47
  238.6 2.5 collective-permute-start.49
  241.8 4.4 %slots.1 = (f32[18,128,128]{2,1,0:T(8,128)}, f32[128,192]{1,0:T(8,128)S(1)}) custom-call(s32[1]{0:T(128)} %bitcast.43.count_ref, s16[4,2528,128]{2,1,0:T(8,128)(2,1)} %copy-done.1, s16[1792,128]{1,0:T(8,128)(2,1)} %collective-permute-done.32.refs_0_, s16[1792,128]{1,0:T(8,128)(2,1)} %collective-permute-done.33.refs_1_, ...), custom_call_target="tpu_custom_call" | custom-call | tf_op jit(solution)/shard_map/slots/pallas_call | solution.py:382
  (149 shorter events, 58.4 us)
Async XLA Ops:
  7.2 129.3 %all-gather.3.cloned.1.call-start = ((), (), s32[]{:S(2)}) async-start(), calls=%async_computation.3 | async-start | bytes 6488064 | tf_op jit(solution)/shard_map/all_gather | solution.py:260
  9.7 28.6 %all-to-all-start = ((bf16[32,3,16,128]{3,2,1,0:T(8,128)(2,1)}), bf16[32,3,16,128]{3,2,1,0:T(8,128)(2,1)S(1)}, u32[]{:S(2)}, u32[]{:S(2)}) async-start(bf16[32,3,16,128]{3,2,1,0:T(8,128)(2,1)} %bitcast.36), calls=%async_computation | async-start | bytes 786432 | tf_op jit(solution)/shard_map/all_to_all | solution.py:264
  21.6 15.6 %collective-permute-start.15 = (bf16[48,16,128]{2,1,0:T(8,128)(2,1)S(1)}, bf16[48,16,128]{2,1,0:T(8,128)(2,1)S(1)}, u32[]{:S(2)}, u32[]{:S(2)}) collective-permute-start(bf16[48,16,128]{2,1,0:T(8,128)(2,1)S(1)} %get-tuple-element.46.rest_14_), channel_id=1, source_target_pairs={{0,28},{4,0},{8,4},{12,8},{16,12},{20,16},{24,20},{28,24},{1,29},{... | collective-permute-start | bytes 589832 | tf_op jit(solution)/shard_map/ppermute | solution.py:30
  24.2 26.4 %collective-permute-start.14 = (bf16[48,16,128]{2,1,0:T(8,128)(2,1)S(1)}, bf16[48,16,128]{2,1,0:T(8,128)(2,1)S(1)}, u32[]{:S(2)}, u32[]{:S(2)}) collective-permute-start(bf16[48,16,128]{2,1,0:T(8,128)(2,1)S(1)} %get-tuple-element.46.rest_14_), channel_id=1, source_target_pairs={{0,3},{1,0},{2,1},{3,2},{4,7},{5,4},{6,5},{7,6},{8,11},{9,8},{10,9... | collective-permute-start | bytes 589832 | tf_op jit(solution)/shard_map/ppermute | solution.py:30
  26.6 25.2 %collective-permute-start.11 = (bf16[48,16,128]{2,1,0:T(8,128)(2,1)S(1)}, bf16[48,16,128]{2,1,0:T(8,128)(2,1)S(1)}, u32[]{:S(2)}, u32[]{:S(2)}) collective-permute-start(bf16[48,16,128]{2,1,0:T(8,128)(2,1)S(1)} %get-tuple-element.46.rest_14_), channel_id=1, source_target_pairs={{0,1},{1,2},{2,3},{3,0},{4,5},{5,6},{6,7},{7,4},{8,9},{9,10},{10,1... | collective-permute-start | bytes 589832 | tf_op jit(solution)/shard_map/ppermute | solution.py:30
  26.6 27.7 %collective-permute-start.5 = (bf16[48,16,128]{2,1,0:T(8,128)(2,1)S(1)}, bf16[48,16,128]{2,1,0:T(8,128)(2,1)S(1)}, u32[]{:S(2)}, u32[]{:S(2)}) collective-permute-start(bf16[48,16,128]{2,1,0:T(8,128)(2,1)S(1)} %get-tuple-element.46.rest_14_), channel_id=1, source_target_pairs={{0,2},{1,3},{2,0},{3,1},{4,6},{5,7},{6,4},{7,5},{8,10},{9,11},{10,... | collective-permute-start | bytes 589832 | tf_op jit(solution)/shard_map/ppermute | solution.py:30
  28.4 25.9 %collective-permute-start = (bf16[48,16,128]{2,1,0:T(8,128)(2,1)S(1)}, bf16[48,16,128]{2,1,0:T(8,128)(2,1)S(1)}, u32[]{:S(2)}, u32[]{:S(2)}) collective-permute-start(bf16[48,16,128]{2,1,0:T(8,128)(2,1)S(1)} %get-tuple-element.46.rest_14_), channel_id=1, source_target_pairs={{0,4},{4,8},{8,12},{12,16},{16,20},{20,24},{24,28},{28,0},{1,5},{5... | collective-permute-start | bytes 589832 | tf_op jit(solution)/shard_map/ppermute | solution.py:30
  37.3 19.7 %collective-permute-start.19 = (bf16[48,16,128]{2,1,0:T(8,128)(2,1)S(1)}, bf16[48,16,128]{2,1,0:T(8,128)(2,1)}, u32[]{:S(2)}, u32[]{:S(2)}) collective-permute-start(bf16[48,16,128]{2,1,0:T(8,128)(2,1)S(1)} %collective-permute-done.15.rest_18_), channel_id=1, source_target_pairs={{0,28},{4,0},{8,4},{12,8},{16,12},{20,16},{24,20},{28,24},{1,29},{... | collective-permute-start | bytes 589832 | tf_op jit(solution)/shard_map/ppermute | solution.py:30
  39.5 41.8 %all-to-all-start.1 = ((f32[32,16,128]{2,1,0:T(8,128)}), f32[32,16,128]{2,1,0:T(8,128)}, u32[]{:S(2)}, u32[]{:S(2)}) async-start(f32[32,16,128]{2,1,0:T(8,128)} %convolution_bitcast_fusion), calls=%async_computation.1 | async-start | bytes 524288 | tf_op jit(solution)/shard_map/all_to_all | solution.py:269
  54.3 12.6 %collective-permute-start.18 = (bf16[48,16,128]{2,1,0:T(8,128)(2,1)S(1)}, bf16[48,16,128]{2,1,0:T(8,128)(2,1)S(1)}, u32[]{:S(2)}, u32[]{:S(2)}) collective-permute-start(bf16[48,16,128]{2,1,0:T(8,128)(2,1)S(1)} %collective-permute-done.5.rest_16_), channel_id=1, source_target_pairs={{0,28},{4,0},{8,4},{12,8},{16,12},{20,16},{24,20},{28,24},{1,29},{... | collective-permute-start | bytes 589832 | tf_op jit(solution)/shard_map/ppermute | solution.py:30
  57.4 15.4 %collective-permute-start.1 = (bf16[48,16,128]{2,1,0:T(8,128)(2,1)S(1)}, bf16[48,16,128]{2,1,0:T(8,128)(2,1)S(1)}, u32[]{:S(2)}, u32[]{:S(2)}) collective-permute-start(bf16[48,16,128]{2,1,0:T(8,128)(2,1)S(1)} %collective-permute-done.rest_10_), channel_id=1, source_target_pairs={{0,4},{4,8},{8,12},{12,16},{16,20},{20,24},{24,28},{28,0},{1,5},{5... | collective-permute-start | bytes 589832 | tf_op jit(solution)/shard_map/ppermute | solution.py:30
  62.8 12.6 %collective-permute-start.13 = (bf16[48,16,128]{2,1,0:T(8,128)(2,1)S(1)}, bf16[48,16,128]{2,1,0:T(8,128)(2,1)S(1)}, u32[]{:S(2)}, u32[]{:S(2)}) collective-permute-start(bf16[48,16,128]{2,1,0:T(8,128)(2,1)S(1)} %collective-permute-done.rest_10_), channel_id=1, source_target_pairs={{0,3},{1,0},{2,1},{3,2},{4,7},{5,4},{6,5},{7,6},{8,11},{9,8},{10,9... | collective-permute-start | bytes 589832 | tf_op jit(solution)/shard_map/ppermute | solution.py:30
  72.8 21.3 %collective-permute-start.10 = (bf16[48,16,128]{2,1,0:T(8,128)(2,1)S(1)}, bf16[48,16,128]{2,1,0:T(8,128)(2,1)}, u32[]{:S(2)}, u32[]{:S(2)}) collective-permute-start(bf16[48,16,128]{2,1,0:T(8,128)(2,1)S(1)} %collective-permute-done.1.rest_6_), channel_id=1, source_target_pairs={{0,3},{1,0},{2,1},{3,2},{4,7},{5,4},{6,5},{7,6},{8,11},{9,8},{10,9... | collective-permute-start | bytes 589832 | tf_op jit(solution)/shard_map/ppermute | solution.py:30
  75.4 21.3 %collective-permute-start.9 = (bf16[48,16,128]{2,1,0:T(8,128)(2,1)S(1)}, bf16[48,16,128]{2,1,0:T(8,128)(2,1)}, u32[]{:S(2)}, u32[]{:S(2)}) collective-permute-start(bf16[48,16,128]{2,1,0:T(8,128)(2,1)S(1)} %collective-permute-done.1.rest_6_), channel_id=1, source_target_pairs={{0,1},{1,2},{2,3},{3,0},{4,5},{5,6},{6,7},{7,4},{8,9},{9,10},{10,1... | collective-permute-start | bytes 589832 | tf_op jit(solution)/shard_map/ppermute | solution.py:30
  75.4 21.3 %collective-permute-start.2 = (bf16[48,16,128]{2,1,0:T(8,128)(2,1)S(1)}, bf16[48,16,128]{2,1,0:T(8,128)(2,1)}, u32[]{:S(2)}, u32[]{:S(2)}) collective-permute-start(bf16[48,16,128]{2,1,0:T(8,128)(2,1)S(1)} %collective-permute-done.1.rest_6_), channel_id=1, source_target_pairs={{0,4},{4,8},{8,12},{12,16},{16,20},{20,24},{24,28},{28,0},{1,5},{5... | collective-permute-start | bytes 589832 | tf_op jit(solution)/shard_map/ppermute | solution.py:30
  78.4 13.2 %collective-permute-start.22 = (bf16[48,16,128]{2,1,0:T(8,128)(2,1)S(1)}, bf16[48,16,128]{2,1,0:T(8,128)(2,1)}, u32[]{:S(2)}, u32[]{:S(2)}) collective-permute-start(bf16[48,16,128]{2,1,0:T(8,128)(2,1)S(1)} %collective-permute-done.18.rest_20_), channel_id=1, source_target_pairs={{0,28},{4,0},{8,4},{12,8},{16,12},{20,16},{24,20},{28,24},{1,29},{... | collective-permute-start | bytes 589832 | tf_op jit(solution)/shard_map/ppermute | solution.py:30
  80.8 13.3 %collective-permute-start.7 = (bf16[48,16,128]{2,1,0:T(8,128)(2,1)S(1)}, bf16[48,16,128]{2,1,0:T(8,128)(2,1)}, u32[]{:S(2)}, u32[]{:S(2)}) collective-permute-start(bf16[48,16,128]{2,1,0:T(8,128)(2,1)S(1)} %collective-permute-done.6.rest_12_), channel_id=1, source_target_pairs={{0,4},{4,8},{8,12},{12,16},{16,20},{20,24},{24,28},{28,0},{1,5},{5... | collective-permute-start | bytes 589832 | tf_op jit(solution)/shard_map/ppermute | solution.py:30
  83.1 53.4 %all-to-all-start.2 = ((f32[32,16,128]{2,1,0:T(8,128)}), f32[32,16,128]{2,1,0:T(8,128)}, u32[]{:S(2)}, u32[]{:S(2)}) async-start(f32[32,16,128]{2,1,0:T(8,128)} %broadcast_in_dim.11), calls=%async_computation.2 | async-start | bytes 524288 | tf_op jit(solution)/shard_map/all_to_all | solution.py:270
  94.1 35.8 %collective-permute-start.26 = (bf16[48,16,128]{2,1,0:T(8,128)(2,1)}, bf16[48,16,128]{2,1,0:T(8,128)(2,1)S(1)}, u32[]{:S(2)}, u32[]{:S(2)}) collective-permute-start(bf16[48,16,128]{2,1,0:T(8,128)(2,1)} %collective-permute-done.22.rest_24_), channel_id=1, source_target_pairs={{0,28},{4,0},{8,4},{12,8},{16,12},{20,16},{24,20},{28,24},{1,29},{... | collective-permute-start | bytes 589832 | tf_op jit(solution)/shard_map/ppermute | solution.py:30
  96.6 33.3 %collective-permute-start.8 = (bf16[48,16,128]{2,1,0:T(8,128)(2,1)}, bf16[48,16,128]{2,1,0:T(8,128)(2,1)S(1)}, u32[]{:S(2)}, u32[]{:S(2)}) collective-permute-start(bf16[48,16,128]{2,1,0:T(8,128)(2,1)} %collective-permute-done.7.rest_8_), channel_id=1, source_target_pairs={{0,4},{4,8},{8,12},{12,16},{16,20},{20,24},{24,28},{28,0},{1,5},{5... | collective-permute-start | bytes 589832 | tf_op jit(solution)/shard_map/ppermute | solution.py:30
  96.6 22.1 %collective-permute-start.27 = (bf16[48,16,128]{2,1,0:T(8,128)(2,1)}, bf16[48,16,128]{2,1,0:T(8,128)(2,1)S(1)}, u32[]{:S(2)}, u32[]{:S(2)}) collective-permute-start(bf16[48,16,128]{2,1,0:T(8,128)(2,1)} %collective-permute-done.2.rest_2_), channel_id=1, source_target_pairs={{0,4},{4,8},{8,12},{12,16},{16,20},{20,24},{24,28},{28,0},{1,5},{5... | collective-permute-start | bytes 589832 | tf_op jit(solution)/shard_map/ppermute | solution.py:30
  102.2 29.1 %collective-permute-start.4 = (bf16[48,16,128]{2,1,0:T(8,128)(2,1)}, bf16[48,16,128]{2,1,0:T(8,128)(2,1)S(1)}, u32[]{:S(2)}, u32[]{:S(2)}) collective-permute-start(bf16[48,16,128]{2,1,0:T(8,128)(2,1)} %collective-permute-done.2.rest_2_), channel_id=1, source_target_pairs={{0,3},{1,0},{2,1},{3,2},{4,7},{5,4},{6,5},{7,6},{8,11},{9,8},{10,9... | collective-permute-start | bytes 589832 | tf_op jit(solution)/shard_map/ppermute | solution.py:30
  105.9 26.1 %collective-permute-start.3 = (bf16[48,16,128]{2,1,0:T(8,128)(2,1)}, bf16[48,16,128]{2,1,0:T(8,128)(2,1)S(1)}, u32[]{:S(2)}, u32[]{:S(2)}) collective-permute-start(bf16[48,16,128]{2,1,0:T(8,128)(2,1)} %collective-permute-done.2.rest_2_), channel_id=1, source_target_pairs={{0,1},{1,2},{2,3},{3,0},{4,5},{5,6},{6,7},{7,4},{8,9},{9,10},{10,1... | collective-permute-start | bytes 589832 | tf_op jit(solution)/shard_map/ppermute | solution.py:30
  118.8 16.4 %collective-permute-start.29 = (bf16[48,16,128]{2,1,0:T(8,128)(2,1)S(1)}, bf16[48,16,128]{2,1,0:T(8,128)(2,1)S(1)}, u32[]{:S(2)}, u32[]{:S(2)}) collective-permute-start(bf16[48,16,128]{2,1,0:T(8,128)(2,1)S(1)} %collective-permute-done.27.rest_30_), channel_id=1, source_target_pairs={{0,3},{1,0},{2,1},{3,2},{4,7},{5,4},{6,5},{7,6},{8,11},{9,8},{10,9... | collective-permute-start | bytes 589832 | tf_op jit(solution)/shard_map/ppermute | solution.py:30
  170.8 13.8 %collective-permute-start.31 = (s16[4,2528,128]{2,1,0:T(8,128)(2,1)}, s16[4,2528,128]{2,1,0:T(8,128)(2,1)S(1)}, u32[]{:S(2)}, u32[]{:S(2)}) collective-permute-start(s16[4,2528,128]{2,1,0:T(8,128)(2,1)} %get-tuple-element.16), channel_id=1, source_target_pairs={{0,32},{32,0},{1,33},{33,1},{2,34},{34,2},{3,35},{35,3},{4,36},{36... | collective-permute-start | bytes 7766024 | tf_op jit(solution)/shard_map/ppermute | solution.py:30
  180.5 14.7 %collective-permute-start.37 = (f32[8,16,128]{2,1,0:T(8,128)S(1)}, f32[8,16,128]{2,1,0:T(8,128)S(1)}, u32[]{:S(2)}, u32[]{:S(2)}) collective-permute-start(f32[8,16,128]{2,1,0:T(8,128)S(1)} %get-tuple-element.50), channel_id=1, source_target_pairs={{0,3},{1,0},{2,1},{3,2},{4,7},{5,4},{6,5},{7,6},{8,11},{9,8},{10,9... | collective-permute-start | bytes 196616 | tf_op jit(solution)/shard_map/ppermute | solution.py:30
  183.4 12.3 %collective-permute-start.36 = (f32[8,16,128]{2,1,0:T(8,128)}, f32[8,16,128]{2,1,0:T(8,128)S(1)}, u32[]{:S(2)}, u32[]{:S(2)}) collective-permute-start(f32[8,16,128]{2,1,0:T(8,128)} %get-tuple-element.51), channel_id=1, source_target_pairs={{0,1},{1,2},{2,3},{3,0},{4,5},{5,6},{6,7},{7,4},{8,9},{9,10},{10,1... | collective-permute-start | bytes 196616 | tf_op jit(solution)/shard_map/ppermute | solution.py:30
  183.4 12.3 %collective-permute-start.35 = (f32[8,16,128]{2,1,0:T(8,128)}, f32[8,16,128]{2,1,0:T(8,128)}, u32[]{:S(2)}, u32[]{:S(2)}) collective-permute-start(f32[8,16,128]{2,1,0:T(8,128)} %get-tuple-element.52), channel_id=1, source_target_pairs={{0,2},{1,3},{2,0},{3,1},{4,6},{5,7},{6,4},{7,5},{8,10},{9,11},{10,... | collective-permute-start | bytes 196616 | tf_op jit(solution)/shard_map/ppermute | solution.py:30
  191.9 22.2 %collective-permute-start.34 = (s16[1792,128]{1,0:T(8,128)(2,1)}, s16[1792,128]{1,0:T(8,128)(2,1)}, u32[]{:S(2)}, u32[]{:S(2)}) collective-permute-start(s16[1792,128]{1,0:T(8,128)(2,1)} %get-tuple-element.40), channel_id=1, source_target_pairs={{0,192},{64,0},{128,64},{192,128},{1,193},{65,1},{129,65},{193,129... | collective-permute-start | bytes 1376264 | tf_op jit(solution)/shard_map/ppermute | solution.py:30
  194.8 19.3 %collective-permute-start.33 = (s16[1792,128]{1,0:T(8,128)(2,1)}, s16[1792,128]{1,0:T(8,128)(2,1)}, u32[]{:S(2)}, u32[]{:S(2)}) collective-permute-start(s16[1792,128]{1,0:T(8,128)(2,1)} %get-tuple-element.41), channel_id=1, source_target_pairs={{0,128},{64,192},{128,0},{192,64},{1,129},{65,193},{129,1},{193,65... | collective-permute-start | bytes 1376264 | tf_op jit(solution)/shard_map/ppermute | solution.py:30
  195.2 23.7 %collective-permute-start.32 = (s16[1792,128]{1,0:T(8,128)(2,1)}, s16[1792,128]{1,0:T(8,128)(2,1)}, u32[]{:S(2)}, u32[]{:S(2)}) collective-permute-start(s16[1792,128]{1,0:T(8,128)(2,1)} %get-tuple-element.42), channel_id=1, source_target_pairs={{0,64},{64,128},{128,192},{192,0},{1,65},{65,129},{129,193},{193,1... | collective-permute-start | bytes 1376264 | tf_op jit(solution)/shard_map/ppermute | solution.py:30
  219.7 12.2 %collective-permute-start.43 = (s16[736,128]{1,0:T(8,128)(2,1)}, s16[736,128]{1,0:T(8,128)(2,1)S(1)}, u32[]{:S(2)}, u32[]{:S(2)}) collective-permute-start(s16[736,128]{1,0:T(8,128)(2,1)} %get-tuple-element.43), channel_id=1, source_target_pairs={{0,192},{64,0},{128,64},{192,128},{1,193},{65,1},{129,65},{193,129... | collective-permute-start | bytes 565256 | tf_op jit(solution)/shard_map/ppermute | solution.py:30
  (39 other events, 405.8 us)
Sparse Core Ops, SparseCore 0:
  11.2 116.4 all-gather.2

commit v3 on v2

--- a/solution.py
+++ b/solution.py
@@ -1,3 +1,5 @@
+import functools
+
 import jax
 import jax.numpy as jnp
 from jax import lax
@@ -21,17 +23,10 @@
 CODE_ROWS = SLOT_ROWS + FO_ROWS
 PART_ROWS = CODE_ROWS + 32
 FINE = 256.0
-CUT = 14 * BS
-HALF = 48
 
 
 def shift(axis, size, step):
     pairs = [(i, (i + step) % size) for i in range(size)]
-    return lambda value: lax.ppermute(value, axis, pairs)
-
-
-def flip(axis, size, bit):
-    pairs = [(i, i ^ bit) for i in range(size)]
     return lambda value: lax.ppermute(value, axis, pairs)
 
 
@@ -57,9 +52,10 @@
 
 
 def main_kernel(
-    rows_ref, where_ref, place_ref, low_ref, weight_ref, factor_ref, up_ref, *rest
+    counts, rows_ref, where_ref, place_ref, low_ref, weight_ref, factor_ref, up_ref, *rest
 ):
-    half_ref, pieces, rest = rest[0], rest[1 : 1 + NX * NZ], rest[1 + NX * NZ :]
+    arrays, rest = rest[: len(counts)], rest[len(counts) :]
+    pieces = [ref.at[i] for ref, n in zip(arrays, counts) for i in range(n)]
     hidden_ref, send_ref, keep_ref, back_ref = rest[:4]
     tok, wide, low_two, codes, levels, sems = rest[4:]
     c = pl.program_id(0)
@@ -67,10 +63,10 @@
 
     @pl.when(c == 0)
     def _():
-        copies = [pltpu.make_async_copy(half_ref, tok.at[:, pl.ds(0, HALF)], sems.at[NX * NZ])]
-        for j in range(NX * NZ):
-            target = tok.at[place_ref[j], pl.ds(HALF, RB - HALF)]
-            copies.append(pltpu.make_async_copy(pieces[j], target, sems.at[j]))
+        copies = [
+            pltpu.make_async_copy(pieces[j], tok.at[place_ref[j]], sems.at[j])
+            for j in range(NX * NZ)
+        ]
         for copy in copies:
             copy.start()
         high, low = split_two(low_ref[...])
@@ -178,18 +174,14 @@
 
 
 def final_kernel(count_ref, own_ref, *refs):
-    firsts, seconds = refs[: NY - 1], refs[NY - 1 : 2 * NY - 2]
-    slots_ref, outer_ref = refs[2 * NY - 2 :]
-    tails = [own_ref[0, CODE_ROWS:]] + [r[CODE_ROWS - CUT :] for r in seconds]
+    parts, (slots_ref, outer_ref) = refs[: NY - 1], refs[NY - 1 :]
+    tails = [own_ref[0, CODE_ROWS:]] + [r[CODE_ROWS:] for r in parts]
     levels = [t.astype(jnp.int32).astype(jnp.float32) for t in tails]
     count = count_ref[0]
     for start, size, index in blocks_of():
         total = decode(own_ref[0, start : start + size], levels[0][index : index + 1])
         for i in range(NY - 1):
-            if start < CUT:
-                code = firsts[i][start : start + size]
-            else:
-                code = seconds[i][start - CUT : start - CUT + size]
+            code = parts[i][start : start + size]
             total += decode(code, levels[i + 1][index : index + 1])
         if index < CAP:
             slots_ref[index] = jnp.where(index < count, total.T, 0.0)
@@ -198,45 +190,36 @@
             outer_ref[:, h * 64 : (h + 1) * 64] = total.T
 
 
-def in_kernel(near_ref, turns_ref, cols_ref, *rest):
-    backs, (out_ref, full) = rest[:NX], rest[NX:]
-    for j in range(NX):
-        for g in range(NZ):
-            full[g, near_ref[j]] = backs[j][g]
+def in_kernel(cols_ref, back_ref, out_ref):
     total = NZ * NX * ROWS
-    high, low = split_two(full[...].reshape(total, BS).T)
+    high, low = split_two(back_ref[...].reshape(total, BS).T)
     two = jnp.concatenate([high, low], axis=0)
     panel = jnp.concatenate(
         [cols_ref[:, j].reshape(total, BS) for j in range(cols_ref.shape[1])], axis=1
     )
     both = jnp.dot(two, panel, preferred_element_type=jnp.float32)
-    grad = (both[:BS] + both[BS:]).T
-    size = grad.shape[0] // GROUPS
-    for d in range(GROUPS):
-        out_ref[turns_ref[d]] = grad[d * size : (d + 1) * size]
-
-
-def in_partial(near, turns, cols, backs):
-    small = pl.BlockSpec(memory_space=pltpu.SMEM)
+    out_ref[...] = (both[:BS] + both[BS:]).T.reshape(out_ref.shape)
+
+
+def in_partial(cols, back_all):
     whole = pl.BlockSpec(memory_space=pltpu.VMEM)
     size = cols.shape[1] * BS // GROUPS
     return pl.pallas_call(
         in_kernel,
-        in_specs=[small, small, whole] + [whole] * NX,
+        in_specs=[whole, whole],
         out_specs=whole,
         out_shape=jax.ShapeDtypeStruct((GROUPS, size, BS), jnp.float32),
-        scratch_shapes=[pltpu.VMEM((NZ, NX, ROWS, BS), jnp.float32)],
         compiler_params=pltpu.CompilerParams(vmem_limit_bytes=30 * 1024 * 1024),
         name="into",
-    )(near, turns, cols, *backs)
+    )(cols, back_all)
 
 
 def gather_tokens(own):
     z_up, z_down = shift("z", NZ, 1), shift("z", NZ, -1)
     x_up, x_down = shift("x", NX, 1), shift("x", NX, -1)
     across = shift("x", NX, 2)
-    held = {(0, 0): own}
-    held[0, 2] = across(own)
+    held = {(0, 0): own[None]}
+    held[0, 2] = across(own[None])
     for b in (0, 2):
         for a in (1, 2, 3):
             held[-a, b] = z_up(held[1 - a, b])
@@ -249,7 +232,7 @@
                 held[a, b] = (z_down if a > 0 else z_up)(held[0, b])
             else:
                 held[a, b] = move(held[a, 0])
-    return held
+    return list(held.values()), [[key] for key in held]
 
 
 def per_device(tokens, block_weights, block_rows, block_owners, factor_in, factor_out, upstream):
@@ -257,10 +240,7 @@
     span = NX * NZ
     per = RB // span
     plane = ("z", "x")
-    whole_half = lax.all_gather(own[:HALF], plane, axis=0)
-    held = gather_tokens(own[HALF:])
-    order = sorted(held)
-    arrays = [held[key] for key in order]
+    arrays, keys = gather_tokens(own)
     spread = lax.all_to_all(own.reshape(span, per, ROWS, BS), plane, 0, 0)
     factor = factor_in.reshape(per, BS, BS)
     partial = jnp.einsum(
@@ -270,11 +250,8 @@
     low = lax.all_to_all(jnp.broadcast_to(low_own[None], (span, ROWS, BS)), plane, 0, 0)
     z, x = lax.axis_index("z"), lax.axis_index("x")
     y, core = lax.axis_index("y"), lax.axis_index("core")
-    place = [((z + a) % NZ) * NX + (x + b) % NX for a, b in order]
+    place = [((z + a) % NZ) * NX + (x + b) % NX for group in keys for a, b in group]
     place = jnp.stack(place).astype(jnp.int32)
-    turn_x = lambda step: jnp.asarray((x + step) % NX, jnp.int32)
-    x_up, x_down, across = shift("x", NX, 1), shift("x", NX, -1), shift("x", NX, 2)
-    near = jnp.stack([turn_x(b) for b in (0, -1, 1, 2)])
     low = low.reshape(span * ROWS, BS)
 
     owners = block_owners.reshape(-1)
@@ -309,7 +286,7 @@
     total = span * ROWS
     anywhere = pl.BlockSpec(memory_space=pl.ANY)
     hidden, send, keep, back = pl.pallas_call(
-        main_kernel,
+        functools.partial(main_kernel, [len(g) for g in keys]),
         grid_spec=pltpu.PrefetchScalarGridSpec(
             num_scalar_prefetch=3,
             grid=(COLS // PER_STEP,),
@@ -319,7 +296,7 @@
                 pl.BlockSpec((BS, PER_STEP * BS), lambda c, *_: (0, c)),
                 pl.BlockSpec((total, PER_STEP * BS), lambda c, *_: (0, c)),
             ]
-            + [anywhere] * (span + 1),
+            + [anywhere] * len(arrays),
             out_specs=[
                 pl.BlockSpec((total, PER_STEP * BS), lambda c, *_: (0, c)),
                 anywhere,
@@ -332,7 +309,7 @@
                 pltpu.VMEM((total, 2 * BS), jnp.bfloat16),
                 pltpu.VMEM((2 * NY, PART_ROWS, BS), jnp.int16),
                 pltpu.VMEM((2 * NY, 32, BS), jnp.float32),
-                pltpu.SemaphoreType.DMA((span + 1,)),
+                pltpu.SemaphoreType.DMA((span,)),
             ],
         ),
         out_shape=[
@@ -345,10 +322,12 @@
         name="columns",
     )(
         block_rows.reshape(-1), where, place,
-        low, block_weights, factor_out, upstream, whole_half, *arrays,
+        low, block_weights, factor_out, upstream, *arrays,
     )
 
     got = shift("core", NC, 1)(send)
+    back = lax.all_to_all(back.reshape(span, ROWS, BS), plane, 0, 0)
+    got, _ = lax.optimization_barrier((got, back))
     paired = pl.pallas_call(
         pair_kernel,
         grid=(NY,),
@@ -358,30 +337,20 @@
         compiler_params=pltpu.CompilerParams(vmem_limit_bytes=50 * 1024 * 1024),
         name="pairs",
     )(keep, got)
-    first_y = [shift("y", NY, i)(paired[i, :CUT]) for i in (1, 2, 3)]
-
-    back = back.reshape(NZ, NX, ROWS, BS)
-    pick = lambda step: lax.dynamic_index_in_dim(back, turn_x(step), 1, keepdims=False)
-    back_x = (pick(0) + across(pick(2))) + (x_up(pick(1)) + x_down(pick(-1)))
-    back_x = back_x + flip("z", NZ, 1)(back_x)
-    back_x, _ = lax.optimization_barrier((back_x, paired))
-    for bit in (2, 4):
-        back_x = back_x + flip("z", NZ, bit)(back_x)
-    back_x, rest, _ = lax.optimization_barrier((back_x, paired[1:, CUT:], first_y))
-    second_y = [shift("y", NY, i)(rest[i - 1]) for i in (1, 2, 3)]
-    backs = [back_x, x_up(back_x), x_down(back_x), across(back_x)]
-    turns = jnp.stack([part_of(jnp.int32(d)) for d in range(GROUPS)]).astype(jnp.int32)
-    in_part = in_partial(near, turns, spread, backs)
-    in_part, _ = lax.optimization_barrier((in_part, second_y))
-    in_sum = in_part[NY:] + shift("core", NC, 1)(in_part[:NY])
-    in_grad = in_sum[0]
-    for step in (1, 2, 3):
-        in_grad = in_grad + shift("y", NY, step)(in_sum[step])
+    parts = [shift("y", NY, i)(paired[i]) for i in (1, 2, 3)]
+
+    back, _ = lax.optimization_barrier((back, paired))
+    back_own = jnp.sum(back, axis=0)
+    back_all = lax.all_to_all(
+        jnp.broadcast_to(back_own[None], (span, ROWS, BS)), plane, 0, 0
+    )
+    in_part = in_partial(spread, back_all)
+    in_grad = jnp.sum(lax.all_to_all(in_part, ("y", "core"), 0, 0), axis=0)
 
     whole = pl.BlockSpec(memory_space=pltpu.VMEM)
     slots, out_grad = pl.pallas_call(
         final_kernel,
-        in_specs=[pl.BlockSpec(memory_space=pltpu.SMEM)] + [whole] * (2 * NY - 1),
+        in_specs=[pl.BlockSpec(memory_space=pltpu.SMEM)] + [whole] * NY,
         out_specs=[whole, whole],
         out_shape=[
             jax.ShapeDtypeStruct((CAP, BS, BS), jnp.float32),
@@ -389,7 +358,7 @@
         ],
         compiler_params=pltpu.CompilerParams(vmem_limit_bytes=50 * 1024 * 1024),
         name="slots",
-    )(mine, paired, *first_y, *second_y)
+    )(mine, paired, *parts)
     return hidden, slots, in_grad, out_grad
 
 

time: 260 us -> 228 us (0.88); the launches traced: 255 us -> 227 us
  blocking collectives: 0 us -> 19.9 us
  waiting for transfers between devices: 63 us -> 44.9 us
  between operations: 14.6 us -> 0.86 us
  starting transfers between devices: 115 us -> 106 us
  local copies, waits for them, and re-layouts: 15.8 us -> 9.58 us
    all_to_all x0 -> x1, blocking collectives: none -> 19.9 us  [per_device(): back = lax.all_to_all(back.reshape(span, ROWS, BS), plane, 0, 0)]
    ppermute x48 -> x35, waiting for transfers between devices: 50.8 us -> 36.2 us  [shift(): return lambda value: lax.ppermute(value, axis, pairs)]
    all_to_all x0 -> x2, starting transfers between devices: none -> 12.5 us  [the longest x1 7.96 us: per_device(): in_grad = jnp.sum(lax.all_to_all(in_part, ('y', 'core'), 0, 0), axis=0)]
    ppermute x3 -> x0, waiting for transfers between devices: 12.1 us -> none  [flip(): return lambda value: lax.ppermute(value, axis, pairs)]
    ppermute x48 -> x35, starting transfers between devices: 80 us -> 72 us  [shift(): return lambda value: lax.ppermute(value, axis, pairs)]
    all_to_all x0 -> x2, waiting for transfers between devices: none -> 5.46 us  [the longest x1 5.46 us: per_device(): lax.all_to_all(jnp.broadcast_to(back_own[None], (span, ROWS, BS)), plane,...]
    all_to_all x1, starting transfers between devices: 8.49 us -> 3.87 us  [per_device(): lax.all_to_all(jnp.broadcast_to(low_own[None], (span, ROWS, BS)), plane,...]
    unnamed x35 -> x25, local copies, waits for them, and re-layouts: 9.46 us -> 5.58 us
  transfers between devices with their start and end apart: 55 -> 40, of which waited for: 19 -> 12; matrix products, arithmetic and copies ran while one was open for 4% -> 3% of each run, Pallas kernels for 4% -> 3%
where the time goes in v3:
time: 228 us; the launch traced here: 227 us
  starting transfers between devices  106 us (46%)
  waiting for transfers between devices  44.9 us (20%)
  Pallas kernels  40.2 us (18%)
  blocking collectives  19.9 us (9%)
  local copies, waits for them, and re-layouts  9.58 us (4%)
  other arithmetic  2.83 us (1%)
    ppermute x35, starting transfers between devices, shift(): return lambda value: lax.ppermute(value, axis, pairs)  72 us
    ppermute x35, waiting for transfers between devices, shift(): return lambda value: lax.ppermute(value, axis, pairs)  36.2 us
    pallas_call x1, Pallas kernels, per_device(): pl.pallas_call(functools.partial(main_kernel, [len(g) for g in keys]), gr...  29.6 us
    all_to_all x1, blocking collectives, per_device(): back = lax.all_to_all(back.reshape(span, ROWS, BS), plane, 0, 0)  19.9 us
    all_to_all x1, starting transfers between devices, per_device(): spread = lax.all_to_all(own.reshape(span, per, ROWS, BS), plane, 0, 0)  10.1 us
    all_to_all x1, starting transfers between devices, per_device(): in_grad = jnp.sum(lax.all_to_all(in_part, ('y', 'core'), 0, 0), axis=0)  7.96 us
    all_to_all x1, starting transfers between devices, per_device(): low_own = jnp.sum(lax.all_to_all(partial, plane, 0, 0), axis=0)  7.94 us
    unnamed x25, local copies, waits for them, and re-layouts  5.58 us
  transfers between devices with their start and end apart: 40, of which 12 were waited for; matrix products, arithmetic and copies ran while one was open for 3% of the time, Pallas kernels for 3%

profile of v3, /device:TPU:1, one launch (start us, length us, event | category | flops | bytes accessed | tf_op | source)
XLA Modules:
  0.0 226.9 jit_solution(3976979616947264784)
XLA Ops:
  2.5 3.3 %collective-permute-start.16 = (bf16[1,96,16,128]{3,2,1,0:T(8,128)(2,1)S(1)}, bf16[1,96,16,128]{3,2,1,0:T(8,128)(2,1)S(1)}, u32[]{:S(2)}, u32[]{:S(2)}) collective-permute-start(bf16[1,96,16,128]{3,2,1,0:T(8,128)(2,1)S(1)} %get-tuple-element.35.rest_0_), channel_id=1, source_target_pairs={{0,3},{1,0},{2,1},{3,2},{4,7},{5,4},{6,5},{7,6},{8,11},{9,8},{10,9... | collective-permute-start | bytes 1179656 | tf_op jit(solution)/shard_map/ppermute | solution.py:30
  5.8 5.6 %collective-permute-start.2 = (bf16[1,96,16,128]{3,2,1,0:T(8,128)(2,1)S(1)}, bf16[1,96,16,128]{3,2,1,0:T(8,128)(2,1)S(1)}, u32[]{:S(2)}, u32[]{:S(2)}) collective-permute-start(bf16[1,96,16,128]{3,2,1,0:T(8,128)(2,1)S(1)} %get-tuple-element.35.rest_0_), channel_id=1, source_target_pairs={{0,28},{4,0},{8,4},{12,8},{16,12},{20,16},{24,20},{28,24},{1,29},{... | collective-permute-start | bytes 1179656 | tf_op jit(solution)/shard_map/ppermute | solution.py:30
  11.4 1.7 collective-permute-start
  13.6 6.4 %collective-permute-start.20 = (bf16[1,96,16,128]{3,2,1,0:T(8,128)(2,1)S(1)}, bf16[1,96,16,128]{3,2,1,0:T(8,128)(2,1)S(1)}, u32[]{:S(2)}, u32[]{:S(2)}) collective-permute-start(bf16[1,96,16,128]{3,2,1,0:T(8,128)(2,1)S(1)} %collective-permute-done.16.rest_17_), channel_id=1, source_target_pairs={{0,28},{4,0},{8,4},{12,8},{16,12},{20,16},{24,20},{28,24},{1,29},{... | collective-permute-start | bytes 1179656 | tf_op jit(solution)/shard_map/ppermute | solution.py:30
  20.3 1.8 collective-permute-done.1.rest_2_
  24.2 9.6 %collective-permute-start.18 = (bf16[1,96,16,128]{3,2,1,0:T(8,128)(2,1)S(1)}, bf16[1,96,16,128]{3,2,1,0:T(8,128)(2,1)}, u32[]{:S(2)}, u32[]{:S(2)}) collective-permute-start(bf16[1,96,16,128]{3,2,1,0:T(8,128)(2,1)S(1)} %collective-permute-done.1.rest_2_), channel_id=1, source_target_pairs={{0,3},{1,0},{2,1},{3,2},{4,7},{5,4},{6,5},{7,6},{8,11},{9,8},{10,9... | collective-permute-start | bytes 1179656 | tf_op jit(solution)/shard_map/ppermute | solution.py:30
  34.5 10.1 %all-to-all-start = ((bf16[32,3,16,128]{3,2,1,0:T(8,128)(2,1)}), bf16[32,3,16,128]{3,2,1,0:T(8,128)(2,1)S(1)}, u32[]{:S(2)}, u32[]{:S(2)}) async-start(bf16[32,3,16,128]{3,2,1,0:T(8,128)(2,1)} %bitcast.73), calls=%async_computation | async-start | bytes 786432 | tf_op jit(solution)/shard_map/all_to_all | solution.py:244
  44.6 2.6 %collective-permute-start.8 = (bf16[1,96,16,128]{3,2,1,0:T(8,128)(2,1)S(1)}, bf16[1,96,16,128]{3,2,1,0:T(8,128)(2,1)}, u32[]{:S(2)}, u32[]{:S(2)}) collective-permute-start(bf16[1,96,16,128]{3,2,1,0:T(8,128)(2,1)S(1)} %collective-permute-done.rest_1_), channel_id=1, source_target_pairs={{0,28},{4,0},{8,4},{12,8},{16,12},{20,16},{24,20},{28,24},{1,29},{... | collective-permute-start | bytes 1179656 | tf_op jit(solution)/shard_map/ppermute | solution.py:30
  47.2 2.5 %collective-permute-start.24 = (bf16[1,96,16,128]{3,2,1,0:T(8,128)(2,1)S(1)}, bf16[1,96,16,128]{3,2,1,0:T(8,128)(2,1)S(1)}, u32[]{:S(2)}, u32[]{:S(2)}) collective-permute-start(bf16[1,96,16,128]{3,2,1,0:T(8,128)(2,1)S(1)} %collective-permute-done.4.rest_5_), channel_id=1, source_target_pairs={{0,3},{1,0},{2,1},{3,2},{4,7},{5,4},{6,5},{7,6},{8,11},{9,8},{10,9... | collective-permute-start | bytes 1179656 | tf_op jit(solution)/shard_map/ppermute | solution.py:30
  49.7 2.9 %collective-permute-start.6 = (bf16[1,96,16,128]{3,2,1,0:T(8,128)(2,1)S(1)}, bf16[1,96,16,128]{3,2,1,0:T(8,128)(2,1)}, u32[]{:S(2)}, u32[]{:S(2)}) collective-permute-start(bf16[1,96,16,128]{3,2,1,0:T(8,128)(2,1)S(1)} %collective-permute-done.4.rest_5_), channel_id=1, source_target_pairs={{0,28},{4,0},{8,4},{12,8},{16,12},{20,16},{24,20},{28,24},{1,29},{... | collective-permute-start | bytes 1179656 | tf_op jit(solution)/shard_map/ppermute | solution.py:30
  52.5 8.0 %collective-permute-done.8.rest_9_ = bf16[1,96,16,128]{3,2,1,0:T(8,128)(2,1)} collective-permute-done((bf16[1,96,16,128]{3,2,1,0:T(8,128)(2,1)S(1)}, bf16[1,96,16,128]{3,2,1,0:T(8,128)(2,1)}, u32[]{:S(2)}, u32[]{:S(2)}) %collective-permute-start.8) | collective-permute-done | bytes 393248 | tf_op jit(solution)/shard_map/ppermute | solution.py:30
  60.5 2.4 %collective-permute-start.22 = (bf16[1,96,16,128]{3,2,1,0:T(8,128)(2,1)}, bf16[1,96,16,128]{3,2,1,0:T(8,128)(2,1)}, u32[]{:S(2)}, u32[]{:S(2)}) collective-permute-start(bf16[1,96,16,128]{3,2,1,0:T(8,128)(2,1)} %collective-permute-done.3.rest_4_), channel_id=1, source_target_pairs={{0,3},{1,0},{2,1},{3,2},{4,7},{5,4},{6,5},{7,6},{8,11},{9,8},{10,9... | collective-permute-start | bytes 1179656 | tf_op jit(solution)/shard_map/ppermute | solution.py:30
  64.1 2.5 %collective-permute-start.10 = (bf16[1,96,16,128]{3,2,1,0:T(8,128)(2,1)}, bf16[1,96,16,128]{3,2,1,0:T(8,128)(2,1)}, u32[]{:S(2)}, u32[]{:S(2)}) collective-permute-start(bf16[1,96,16,128]{3,2,1,0:T(8,128)(2,1)} %collective-permute-done.8.rest_9_), channel_id=1, source_target_pairs={{0,28},{4,0},{8,4},{12,8},{16,12},{20,16},{24,20},{28,24},{1,29},{... | collective-permute-start | bytes 1179656 | tf_op jit(solution)/shard_map/ppermute | solution.py:30
  66.7 2.4 %collective-permute-done.6.rest_7_ = bf16[1,96,16,128]{3,2,1,0:T(8,128)(2,1)} collective-permute-done((bf16[1,96,16,128]{3,2,1,0:T(8,128)(2,1)S(1)}, bf16[1,96,16,128]{3,2,1,0:T(8,128)(2,1)}, u32[]{:S(2)}, u32[]{:S(2)}) %collective-permute-start.6) | collective-permute-done | bytes 393248 | tf_op jit(solution)/shard_map/ppermute | solution.py:30
  70.2 2.1 convolution_bitcast_fusion
  72.3 7.9 %all-to-all-start.1 = ((f32[32,16,128]{2,1,0:T(8,128)}), f32[32,16,128]{2,1,0:T(8,128)S(1)}, u32[]{:S(2)}, u32[]{:S(2)}) async-start(f32[32,16,128]{2,1,0:T(8,128)} %convolution_bitcast_fusion), calls=%async_computation.1 | async-start | bytes 524288 | tf_op jit(solution)/shard_map/all_to_all | solution.py:249
  80.3 2.5 %collective-permute-start.28 = (bf16[1,96,16,128]{3,2,1,0:T(8,128)(2,1)}, bf16[1,96,16,128]{3,2,1,0:T(8,128)(2,1)}, u32[]{:S(2)}, u32[]{:S(2)}) collective-permute-start(bf16[1,96,16,128]{3,2,1,0:T(8,128)(2,1)} %collective-permute-done.6.rest_7_), channel_id=1, source_target_pairs={{0,3},{1,0},{2,1},{3,2},{4,7},{5,4},{6,5},{7,6},{8,11},{9,8},{10,9... | collective-permute-start | bytes 1179656 | tf_op jit(solution)/shard_map/ppermute | solution.py:30
  84.1 2.6 %collective-permute-start.26 = (bf16[1,96,16,128]{3,2,1,0:T(8,128)(2,1)}, bf16[1,96,16,128]{3,2,1,0:T(8,128)(2,1)}, u32[]{:S(2)}, u32[]{:S(2)}) collective-permute-start(bf16[1,96,16,128]{3,2,1,0:T(8,128)(2,1)} %collective-permute-done.5.rest_6_), channel_id=1, source_target_pairs={{0,3},{1,0},{2,1},{3,2},{4,7},{5,4},{6,5},{7,6},{8,11},{9,8},{10,9... | collective-permute-start | bytes 1179656 | tf_op jit(solution)/shard_map/ppermute | solution.py:30
  88.9 3.3 %all-to-all-done.1 = f32[32,16,128]{2,1,0:T(8,128)S(1)} async-done(((f32[32,16,128]{2,1,0:T(8,128)}), f32[32,16,128]{2,1,0:T(8,128)S(1)}, u32[]{:S(2)}, u32[]{:S(2)}) %all-to-all-start.1) | async-done | bytes 262176 | tf_op jit(solution)/shard_map/all_to_all | solution.py:249
  92.9 3.9 %all-to-all-start.2 = ((f32[32,16,128]{2,1,0:T(8,128)}), f32[32,16,128]{2,1,0:T(8,128)S(1)}, u32[]{:S(2)}, u32[]{:S(2)}) async-start(f32[32,16,128]{2,1,0:T(8,128)} %broadcast_in_dim.17), calls=%async_computation.2 | async-start | bytes 524288 | tf_op jit(solution)/shard_map/all_to_all | solution.py:250
  102.4 3.7 %collective-permute-done.25.rest_26_ = bf16[1,96,16,128]{3,2,1,0:T(8,128)(2,1)S(1)} collective-permute-done((bf16[1,96,16,128]{3,2,1,0:T(8,128)(2,1)}, bf16[1,96,16,128]{3,2,1,0:T(8,128)(2,1)S(1)}, u32[]{:S(2)}, u32[]{:S(2)}) %collective-permute-start.25) | collective-permute-done | bytes 393248 | tf_op jit(solution)/shard_map/ppermute | solution.py:30
  108.5 2.0 collective-permute-done.29.rest_30_
  110.5 29.6 %columns.1 = (bf16[512,1536]{1,0:T(8,128)(2,1)}, s16[4,2528,128]{2,1,0:T(8,128)(2,1)}, s16[4,2528,128]{2,1,0:T(8,128)(2,1)}, f32[512,128]{1,0:T(8,128)S(1)}) custom-call(s32[96]{0:T(128)S(1)} %reshape.176.rows_ref, s32[4,96]{1,0:T(4,128)S(1)} %pad_add_fusion.where_ref, s32[32]{0:T(128)S(1)} %stack.148.place_ref, f32[512,128]{1,0:T(8,128)S(1)} %bitcast.71, ...), custom_call_target="tpu_custom_call" | custom-call | tf_op jit(solution)/shard_map/columns/pallas_call | solution.py:288
  140.1 11.4 %collective-permute-start.31 = (s16[4,2528,128]{2,1,0:T(8,128)(2,1)}, s16[4,2528,128]{2,1,0:T(8,128)(2,1)S(1)}, u32[]{:S(2)}, u32[]{:S(2)}) collective-permute-start(s16[4,2528,128]{2,1,0:T(8,128)(2,1)} %get-tuple-element.14), channel_id=1, source_target_pairs={{0,32},{32,0},{1,33},{33,1},{2,34},{34,2},{3,35},{35,3},{4,36},{36... | collective-permute-start | bytes 7766024 | tf_op jit(solution)/shard_map/ppermute | solution.py:30
  151.5 19.9 %all_to_all.30 = f32[32,16,128]{2,1,0:T(8,128)} all-to-all(f32[32,16,128]{2,1,0:T(8,128)S(1)} %bitcast.72), channel_id=1, replica_groups=mesh['y'=4,'core'=2,'z'=8,'x'=4] {'z','x'}, dimensions={0} | all-to-all | bytes 524288 | tf_op jit(solution)/shard_map/all_to_all | solution.py:329
  173.0 4.6 %pairs.1.own_ref = s16[4,2528,128]{2,1,0:T(8,128)(2,1)S(1)} custom-call(s16[4,2528,128]{2,1,0:T(8,128)(2,1)} %get-tuple-element.13.keep_ref, s16[4,2528,128]{2,1,0:T(8,128)(2,1)} %copy-done.3), custom_call_target="tpu_custom_call" | custom-call | tf_op jit(solution)/shard_map/pairs/pallas_call | solution.py:331
  179.5 4.6 %all-to-all-start.4 = ((f32[32,16,128]{2,1,0:T(8,128)}), f32[32,16,128]{2,1,0:T(8,128)}, u32[]{:S(2)}, u32[]{:S(2)}) async-start(f32[32,16,128]{2,1,0:T(8,128)} %broadcast_in_dim.21), calls=%async_computation.4 | async-start | bytes 524288 | tf_op jit(solution)/shard_map/all_to_all | solution.py:344
  185.4 2.7 %collective-permute-start.34 = (s16[2528,128]{1,0:T(8,128)(2,1)}, s16[2528,128]{1,0:T(8,128)(2,1)}, u32[]{:S(2)}, u32[]{:S(2)}) collective-permute-start(s16[2528,128]{1,0:T(8,128)(2,1)} %get-tuple-element.32), channel_id=1, source_target_pairs={{0,192},{64,0},{128,64},{192,128},{1,193},{65,1},{129,65},{193,129... | collective-permute-start | bytes 1941512 | tf_op jit(solution)/shard_map/ppermute | solution.py:30
  189.2 5.5 %all-to-all-done.4.back_ref = f32[32,16,128]{2,1,0:T(8,128)} async-done(((f32[32,16,128]{2,1,0:T(8,128)}), f32[32,16,128]{2,1,0:T(8,128)}, u32[]{:S(2)}, u32[]{:S(2)}) %all-to-all-start.4) | async-done | bytes 262176 | tf_op jit(solution)/shard_map/all_to_all | solution.py:344
  196.7 8.0 %all-to-all-start.5 = ((f32[8,48,128]{2,1,0:T(8,128)}), f32[8,48,128]{2,1,0:T(8,128)S(1)}, u32[]{:S(2)}, u32[]{:S(2)}) async-start(f32[8,48,128]{2,1,0:T(8,128)} %copy-done.2), calls=%async_computation.5 | async-start | bytes 393216 | tf_op jit(solution)/shard_map/all_to_all | solution.py:348
  205.5 15.4 %collective-permute-done.32.refs_0_ = s16[2528,128]{1,0:T(8,128)(2,1)} collective-permute-done((s16[2528,128]{1,0:T(8,128)(2,1)}, s16[2528,128]{1,0:T(8,128)(2,1)}, u32[]{:S(2)}, u32[]{:S(2)}) %collective-permute-start.32) | collective-permute-done | bytes 647200 | tf_op jit(solution)/shard_map/ppermute | solution.py:30
  220.9 4.6 %slots.1 = (f32[18,128,128]{2,1,0:T(8,128)}, f32[128,192]{1,0:T(8,128)S(1)}) custom-call(s32[1]{0:T(128)} %bitcast.44.count_ref, s16[4,2528,128]{2,1,0:T(8,128)(2,1)} %copy-done.1, s16[2528,128]{1,0:T(8,128)(2,1)} %collective-permute-done.32.refs_0_, s16[2528,128]{1,0:T(8,128)(2,1)} %collective-permute-done.33.refs_1_, ...), custom_call_target="tpu_custom_call" | custom-call | tf_op jit(solution)/shard_map/slots/pallas_call | solution.py:351
  (98 shorter events, 30.2 us)
Async XLA Ops:
  5.8 14.2 %collective-permute-start.15 = (bf16[1,96,16,128]{3,2,1,0:T(8,128)(2,1)S(1)}, bf16[1,96,16,128]{3,2,1,0:T(8,128)(2,1)}, u32[]{:S(2)}, u32[]{:S(2)}) collective-permute-start(bf16[1,96,16,128]{3,2,1,0:T(8,128)(2,1)S(1)} %get-tuple-element.35.rest_0_), channel_id=1, source_target_pairs={{0,1},{1,2},{2,3},{3,0},{4,5},{5,6},{6,7},{7,4},{8,9},{9,10},{10,1... | collective-permute-start | bytes 1179656 | tf_op jit(solution)/shard_map/ppermute | solution.py:30
  5.8 14.2 %collective-permute-start.2 = (bf16[1,96,16,128]{3,2,1,0:T(8,128)(2,1)S(1)}, bf16[1,96,16,128]{3,2,1,0:T(8,128)(2,1)S(1)}, u32[]{:S(2)}, u32[]{:S(2)}) collective-permute-start(bf16[1,96,16,128]{3,2,1,0:T(8,128)(2,1)S(1)} %get-tuple-element.35.rest_0_), channel_id=1, source_target_pairs={{0,28},{4,0},{8,4},{12,8},{16,12},{20,16},{24,20},{28,24},{1,29},{... | collective-permute-start | bytes 1179656 | tf_op jit(solution)/shard_map/ppermute | solution.py:30
  13.6 20.2 %collective-permute-start.20 = (bf16[1,96,16,128]{3,2,1,0:T(8,128)(2,1)S(1)}, bf16[1,96,16,128]{3,2,1,0:T(8,128)(2,1)S(1)}, u32[]{:S(2)}, u32[]{:S(2)}) collective-permute-start(bf16[1,96,16,128]{3,2,1,0:T(8,128)(2,1)S(1)} %collective-permute-done.16.rest_17_), channel_id=1, source_target_pairs={{0,28},{4,0},{8,4},{12,8},{16,12},{20,16},{24,20},{28,24},{1,29},{... | collective-permute-start | bytes 1179656 | tf_op jit(solution)/shard_map/ppermute | solution.py:30
  19.9 24.6 %collective-permute-start.17 = (bf16[1,96,16,128]{3,2,1,0:T(8,128)(2,1)}, bf16[1,96,16,128]{3,2,1,0:T(8,128)(2,1)}, u32[]{:S(2)}, u32[]{:S(2)}) collective-permute-start(bf16[1,96,16,128]{3,2,1,0:T(8,128)(2,1)} %collective-permute-done.15.rest_16_), channel_id=1, source_target_pairs={{0,4},{4,8},{8,12},{12,16},{16,20},{20,24},{24,28},{28,0},{1,5},{5... | collective-permute-start | bytes 1179656 | tf_op jit(solution)/shard_map/ppermute | solution.py:30
  20.0 27.2 %collective-permute-start.19 = (bf16[1,96,16,128]{3,2,1,0:T(8,128)(2,1)S(1)}, bf16[1,96,16,128]{3,2,1,0:T(8,128)(2,1)}, u32[]{:S(2)}, u32[]{:S(2)}) collective-permute-start(bf16[1,96,16,128]{3,2,1,0:T(8,128)(2,1)S(1)} %collective-permute-done.2.rest_3_), channel_id=1, source_target_pairs={{0,1},{1,2},{2,3},{3,0},{4,5},{5,6},{6,7},{7,4},{8,9},{9,10},{10,1... | collective-permute-start | bytes 1179656 | tf_op jit(solution)/shard_map/ppermute | solution.py:30
  22.1 25.1 %collective-permute-start.4 = (bf16[1,96,16,128]{3,2,1,0:T(8,128)(2,1)S(1)}, bf16[1,96,16,128]{3,2,1,0:T(8,128)(2,1)S(1)}, u32[]{:S(2)}, u32[]{:S(2)}) collective-permute-start(bf16[1,96,16,128]{3,2,1,0:T(8,128)(2,1)S(1)} %collective-permute-done.2.rest_3_), channel_id=1, source_target_pairs={{0,28},{4,0},{8,4},{12,8},{16,12},{20,16},{24,20},{28,24},{1,29},{... | collective-permute-start | bytes 1179656 | tf_op jit(solution)/shard_map/ppermute | solution.py:30
  24.2 25.5 %collective-permute-start.18 = (bf16[1,96,16,128]{3,2,1,0:T(8,128)(2,1)S(1)}, bf16[1,96,16,128]{3,2,1,0:T(8,128)(2,1)}, u32[]{:S(2)}, u32[]{:S(2)}) collective-permute-start(bf16[1,96,16,128]{3,2,1,0:T(8,128)(2,1)S(1)} %collective-permute-done.1.rest_2_), channel_id=1, source_target_pairs={{0,3},{1,0},{2,1},{3,2},{4,7},{5,4},{6,5},{7,6},{8,11},{9,8},{10,9... | collective-permute-start | bytes 1179656 | tf_op jit(solution)/shard_map/ppermute | solution.py:30
  34.5 15.2 %collective-permute-start.3 = (bf16[1,96,16,128]{3,2,1,0:T(8,128)(2,1)S(1)}, bf16[1,96,16,128]{3,2,1,0:T(8,128)(2,1)}, u32[]{:S(2)}, u32[]{:S(2)}) collective-permute-start(bf16[1,96,16,128]{3,2,1,0:T(8,128)(2,1)S(1)} %collective-permute-done.1.rest_2_), channel_id=1, source_target_pairs={{0,4},{4,8},{8,12},{12,16},{16,20},{20,24},{24,28},{28,0},{1,5},{5... | collective-permute-start | bytes 1179656 | tf_op jit(solution)/shard_map/ppermute | solution.py:30
  34.5 35.7 %all-to-all-start = ((bf16[32,3,16,128]{3,2,1,0:T(8,128)(2,1)}), bf16[32,3,16,128]{3,2,1,0:T(8,128)(2,1)S(1)}, u32[]{:S(2)}, u32[]{:S(2)}) async-start(bf16[32,3,16,128]{3,2,1,0:T(8,128)(2,1)} %bitcast.73), calls=%async_computation | async-start | bytes 786432 | tf_op jit(solution)/shard_map/all_to_all | solution.py:244
  44.6 15.9 %collective-permute-start.8 = (bf16[1,96,16,128]{3,2,1,0:T(8,128)(2,1)S(1)}, bf16[1,96,16,128]{3,2,1,0:T(8,128)(2,1)}, u32[]{:S(2)}, u32[]{:S(2)}) collective-permute-start(bf16[1,96,16,128]{3,2,1,0:T(8,128)(2,1)S(1)} %collective-permute-done.rest_1_), channel_id=1, source_target_pairs={{0,28},{4,0},{8,4},{12,8},{16,12},{20,16},{24,20},{28,24},{1,29},{... | collective-permute-start | bytes 1179656 | tf_op jit(solution)/shard_map/ppermute | solution.py:30
  47.2 15.7 %collective-permute-start.7 = (bf16[1,96,16,128]{3,2,1,0:T(8,128)(2,1)S(1)}, bf16[1,96,16,128]{3,2,1,0:T(8,128)(2,1)}, u32[]{:S(2)}, u32[]{:S(2)}) collective-permute-start(bf16[1,96,16,128]{3,2,1,0:T(8,128)(2,1)S(1)} %collective-permute-done.rest_1_), channel_id=1, source_target_pairs={{0,4},{4,8},{8,12},{12,16},{16,20},{20,24},{24,28},{28,0},{1,5},{5... | collective-permute-start | bytes 1179656 | tf_op jit(solution)/shard_map/ppermute | solution.py:30
  47.2 16.1 %collective-permute-start.24 = (bf16[1,96,16,128]{3,2,1,0:T(8,128)(2,1)S(1)}, bf16[1,96,16,128]{3,2,1,0:T(8,128)(2,1)S(1)}, u32[]{:S(2)}, u32[]{:S(2)}) collective-permute-start(bf16[1,96,16,128]{3,2,1,0:T(8,128)(2,1)S(1)} %collective-permute-done.4.rest_5_), channel_id=1, source_target_pairs={{0,3},{1,0},{2,1},{3,2},{4,7},{5,4},{6,5},{7,6},{8,11},{9,8},{10,9... | collective-permute-start | bytes 1179656 | tf_op jit(solution)/shard_map/ppermute | solution.py:30
  49.7 14.4 %collective-permute-start.23 = (bf16[1,96,16,128]{3,2,1,0:T(8,128)(2,1)S(1)}, bf16[1,96,16,128]{3,2,1,0:T(8,128)(2,1)S(1)}, u32[]{:S(2)}, u32[]{:S(2)}) collective-permute-start(bf16[1,96,16,128]{3,2,1,0:T(8,128)(2,1)S(1)} %collective-permute-done.4.rest_5_), channel_id=1, source_target_pairs={{0,1},{1,2},{2,3},{3,0},{4,5},{5,6},{6,7},{7,4},{8,9},{9,10},{10,1... | collective-permute-start | bytes 1179656 | tf_op jit(solution)/shard_map/ppermute | solution.py:30
  49.7 19.3 %collective-permute-start.6 = (bf16[1,96,16,128]{3,2,1,0:T(8,128)(2,1)S(1)}, bf16[1,96,16,128]{3,2,1,0:T(8,128)(2,1)}, u32[]{:S(2)}, u32[]{:S(2)}) collective-permute-start(bf16[1,96,16,128]{3,2,1,0:T(8,128)(2,1)S(1)} %collective-permute-done.4.rest_5_), channel_id=1, source_target_pairs={{0,28},{4,0},{8,4},{12,8},{16,12},{20,16},{24,20},{28,24},{1,29},{... | collective-permute-start | bytes 1179656 | tf_op jit(solution)/shard_map/ppermute | solution.py:30
  60.5 19.7 %collective-permute-start.22 = (bf16[1,96,16,128]{3,2,1,0:T(8,128)(2,1)}, bf16[1,96,16,128]{3,2,1,0:T(8,128)(2,1)}, u32[]{:S(2)}, u32[]{:S(2)}) collective-permute-start(bf16[1,96,16,128]{3,2,1,0:T(8,128)(2,1)} %collective-permute-done.3.rest_4_), channel_id=1, source_target_pairs={{0,3},{1,0},{2,1},{3,2},{4,7},{5,4},{6,5},{7,6},{8,11},{9,8},{10,9... | collective-permute-start | bytes 1179656 | tf_op jit(solution)/shard_map/ppermute | solution.py:30
  62.9 19.9 %collective-permute-start.21 = (bf16[1,96,16,128]{3,2,1,0:T(8,128)(2,1)}, bf16[1,96,16,128]{3,2,1,0:T(8,128)(2,1)}, u32[]{:S(2)}, u32[]{:S(2)}) collective-permute-start(bf16[1,96,16,128]{3,2,1,0:T(8,128)(2,1)} %collective-permute-done.3.rest_4_), channel_id=1, source_target_pairs={{0,1},{1,2},{2,3},{3,0},{4,5},{5,6},{6,7},{7,4},{8,9},{9,10},{10,1... | collective-permute-start | bytes 1179656 | tf_op jit(solution)/shard_map/ppermute | solution.py:30
  63.3 19.5 %collective-permute-start.5 = (bf16[1,96,16,128]{3,2,1,0:T(8,128)(2,1)}, bf16[1,96,16,128]{3,2,1,0:T(8,128)(2,1)}, u32[]{:S(2)}, u32[]{:S(2)}) collective-permute-start(bf16[1,96,16,128]{3,2,1,0:T(8,128)(2,1)} %collective-permute-done.3.rest_4_), channel_id=1, source_target_pairs={{0,4},{4,8},{8,12},{12,16},{16,20},{20,24},{24,28},{28,0},{1,5},{5... | collective-permute-start | bytes 1179656 | tf_op jit(solution)/shard_map/ppermute | solution.py:30
  64.1 19.9 %collective-permute-start.10 = (bf16[1,96,16,128]{3,2,1,0:T(8,128)(2,1)}, bf16[1,96,16,128]{3,2,1,0:T(8,128)(2,1)}, u32[]{:S(2)}, u32[]{:S(2)}) collective-permute-start(bf16[1,96,16,128]{3,2,1,0:T(8,128)(2,1)} %collective-permute-done.8.rest_9_), channel_id=1, source_target_pairs={{0,28},{4,0},{8,4},{12,8},{16,12},{20,16},{24,20},{28,24},{1,29},{... | collective-permute-start | bytes 1179656 | tf_op jit(solution)/shard_map/ppermute | solution.py:30
  69.0 17.6 %collective-permute-start.9 = (bf16[1,96,16,128]{3,2,1,0:T(8,128)(2,1)}, bf16[1,96,16,128]{3,2,1,0:T(8,128)(2,1)}, u32[]{:S(2)}, u32[]{:S(2)}) collective-permute-start(bf16[1,96,16,128]{3,2,1,0:T(8,128)(2,1)} %collective-permute-done.7.rest_8_), channel_id=1, source_target_pairs={{0,4},{4,8},{8,12},{12,16},{16,20},{20,24},{24,28},{28,0},{1,5},{5... | collective-permute-start | bytes 1179656 | tf_op jit(solution)/shard_map/ppermute | solution.py:30
  72.3 19.8 %all-to-all-start.1 = ((f32[32,16,128]{2,1,0:T(8,128)}), f32[32,16,128]{2,1,0:T(8,128)S(1)}, u32[]{:S(2)}, u32[]{:S(2)}) async-start(f32[32,16,128]{2,1,0:T(8,128)} %convolution_bitcast_fusion), calls=%async_computation.1 | async-start | bytes 524288 | tf_op jit(solution)/shard_map/all_to_all | solution.py:249
  80.3 16.6 %collective-permute-start.28 = (bf16[1,96,16,128]{3,2,1,0:T(8,128)(2,1)}, bf16[1,96,16,128]{3,2,1,0:T(8,128)(2,1)}, u32[]{:S(2)}, u32[]{:S(2)}) collective-permute-start(bf16[1,96,16,128]{3,2,1,0:T(8,128)(2,1)} %collective-permute-done.6.rest_7_), channel_id=1, source_target_pairs={{0,3},{1,0},{2,1},{3,2},{4,7},{5,4},{6,5},{7,6},{8,11},{9,8},{10,9... | collective-permute-start | bytes 1179656 | tf_op jit(solution)/shard_map/ppermute | solution.py:30
  82.8 15.2 %collective-permute-start.27 = (bf16[1,96,16,128]{3,2,1,0:T(8,128)(2,1)}, bf16[1,96,16,128]{3,2,1,0:T(8,128)(2,1)}, u32[]{:S(2)}, u32[]{:S(2)}) collective-permute-start(bf16[1,96,16,128]{3,2,1,0:T(8,128)(2,1)} %collective-permute-done.6.rest_7_), channel_id=1, source_target_pairs={{0,1},{1,2},{2,3},{3,0},{4,5},{5,6},{6,7},{7,4},{8,9},{9,10},{10,1... | collective-permute-start | bytes 1179656 | tf_op jit(solution)/shard_map/ppermute | solution.py:30
  82.8 16.5 %collective-permute-start.13 = (bf16[1,96,16,128]{3,2,1,0:T(8,128)(2,1)}, bf16[1,96,16,128]{3,2,1,0:T(8,128)(2,1)}, u32[]{:S(2)}, u32[]{:S(2)}) collective-permute-start(bf16[1,96,16,128]{3,2,1,0:T(8,128)(2,1)} %collective-permute-done.5.rest_6_), channel_id=1, source_target_pairs={{0,4},{4,8},{8,12},{12,16},{16,20},{20,24},{24,28},{28,0},{1,5},{5... | collective-permute-start | bytes 1179656 | tf_op jit(solution)/shard_map/ppermute | solution.py:30
  84.1 16.7 %collective-permute-start.26 = (bf16[1,96,16,128]{3,2,1,0:T(8,128)(2,1)}, bf16[1,96,16,128]{3,2,1,0:T(8,128)(2,1)}, u32[]{:S(2)}, u32[]{:S(2)}) collective-permute-start(bf16[1,96,16,128]{3,2,1,0:T(8,128)(2,1)} %collective-permute-done.5.rest_6_), channel_id=1, source_target_pairs={{0,3},{1,0},{2,1},{3,2},{4,7},{5,4},{6,5},{7,6},{8,11},{9,8},{10,9... | collective-permute-start | bytes 1179656 | tf_op jit(solution)/shard_map/ppermute | solution.py:30
  86.7 14.1 %collective-permute-start.12 = (bf16[1,96,16,128]{3,2,1,0:T(8,128)(2,1)}, bf16[1,96,16,128]{3,2,1,0:T(8,128)(2,1)}, u32[]{:S(2)}, u32[]{:S(2)}) collective-permute-start(bf16[1,96,16,128]{3,2,1,0:T(8,128)(2,1)} %collective-permute-done.10.rest_11_), channel_id=1, source_target_pairs={{0,28},{4,0},{8,4},{12,8},{16,12},{20,16},{24,20},{28,24},{1,29},{... | collective-permute-start | bytes 1179656 | tf_op jit(solution)/shard_map/ppermute | solution.py:30
  92.9 14.6 %all-to-all-start.2 = ((f32[32,16,128]{2,1,0:T(8,128)}), f32[32,16,128]{2,1,0:T(8,128)S(1)}, u32[]{:S(2)}, u32[]{:S(2)}) async-start(f32[32,16,128]{2,1,0:T(8,128)} %broadcast_in_dim.17), calls=%async_computation.2 | async-start | bytes 524288 | tf_op jit(solution)/shard_map/all_to_all | solution.py:250
  140.1 31.3 %collective-permute-start.31 = (s16[4,2528,128]{2,1,0:T(8,128)(2,1)}, s16[4,2528,128]{2,1,0:T(8,128)(2,1)S(1)}, u32[]{:S(2)}, u32[]{:S(2)}) collective-permute-start(s16[4,2528,128]{2,1,0:T(8,128)(2,1)} %get-tuple-element.14), channel_id=1, source_target_pairs={{0,32},{32,0},{1,33},{33,1},{2,34},{34,2},{3,35},{35,3},{4,36},{36... | collective-permute-start | bytes 7766024 | tf_op jit(solution)/shard_map/ppermute | solution.py:30
  179.5 15.2 %all-to-all-start.4 = ((f32[32,16,128]{2,1,0:T(8,128)}), f32[32,16,128]{2,1,0:T(8,128)}, u32[]{:S(2)}, u32[]{:S(2)}) async-start(f32[32,16,128]{2,1,0:T(8,128)} %broadcast_in_dim.21), calls=%async_computation.4 | async-start | bytes 524288 | tf_op jit(solution)/shard_map/all_to_all | solution.py:344
  185.4 20.0 %collective-permute-start.34 = (s16[2528,128]{1,0:T(8,128)(2,1)}, s16[2528,128]{1,0:T(8,128)(2,1)}, u32[]{:S(2)}, u32[]{:S(2)}) collective-permute-start(s16[2528,128]{1,0:T(8,128)(2,1)} %get-tuple-element.32), channel_id=1, source_target_pairs={{0,192},{64,0},{128,64},{192,128},{1,193},{65,1},{129,65},{193,129... | collective-permute-start | bytes 1941512 | tf_op jit(solution)/shard_map/ppermute | solution.py:30
  188.2 17.3 %collective-permute-start.33 = (s16[2528,128]{1,0:T(8,128)(2,1)}, s16[2528,128]{1,0:T(8,128)(2,1)}, u32[]{:S(2)}, u32[]{:S(2)}) collective-permute-start(s16[2528,128]{1,0:T(8,128)(2,1)} %get-tuple-element.33), channel_id=1, source_target_pairs={{0,128},{64,192},{128,0},{192,64},{1,129},{65,193},{129,1},{193,65... | collective-permute-start | bytes 1941512 | tf_op jit(solution)/shard_map/ppermute | solution.py:30
  188.5 32.3 %collective-permute-start.32 = (s16[2528,128]{1,0:T(8,128)(2,1)}, s16[2528,128]{1,0:T(8,128)(2,1)}, u32[]{:S(2)}, u32[]{:S(2)}) collective-permute-start(s16[2528,128]{1,0:T(8,128)(2,1)} %get-tuple-element.34), channel_id=1, source_target_pairs={{0,64},{64,128},{128,192},{192,0},{1,65},{65,129},{129,193},{193,1... | collective-permute-start | bytes 1941512 | tf_op jit(solution)/shard_map/ppermute | solution.py:30
  196.7 29.5 %all-to-all-start.5 = ((f32[8,48,128]{2,1,0:T(8,128)}), f32[8,48,128]{2,1,0:T(8,128)S(1)}, u32[]{:S(2)}, u32[]{:S(2)}) async-start(f32[8,48,128]{2,1,0:T(8,128)} %copy-done.2), calls=%async_computation.5 | async-start | bytes 393216 | tf_op jit(solution)/shard_map/all_to_all | solution.py:348
  (19 other events, 311.4 us)

commit v4 on v3

--- a/solution.py
+++ b/solution.py
@@ -327,7 +327,6 @@
 
     got = shift("core", NC, 1)(send)
     back = lax.all_to_all(back.reshape(span, ROWS, BS), plane, 0, 0)
-    got, _ = lax.optimization_barrier((got, back))
     paired = pl.pallas_call(
         pair_kernel,
         grid=(NY,),
@@ -337,9 +336,10 @@
         compiler_params=pltpu.CompilerParams(vmem_limit_bytes=50 * 1024 * 1024),
         name="pairs",
     )(keep, got)
-    parts = [shift("y", NY, i)(paired[i]) for i in (1, 2, 3)]
-
-    back, _ = lax.optimization_barrier((back, paired))
+    outward = [paired[i] for i in (1, 2, 3)]
+    parts = [shift("y", NY, i)(outward[i - 1]) for i in (1, 2, 3)]
+
+    back, _ = lax.optimization_barrier((back, outward))
     back_own = jnp.sum(back, axis=0)
     back_all = lax.all_to_all(
         jnp.broadcast_to(back_own[None], (span, ROWS, BS)), plane, 0, 0

time: 228 us -> 221 us (0.969)
  blocking collectives: 19.9 us -> 0 us
  starting transfers between devices: 106 us -> 115 us
  waiting for transfers between devices: 44.9 us -> 49.4 us
    all_to_all x1 -> x0, blocking collectives: 19.9 us -> none  [per_device(): back = lax.all_to_all(back.reshape(span, ROWS, BS), plane, 0, 0)]
    all_to_all x0 -> x1, starting transfers between devices: none -> 8.2 us  [per_device(): back = lax.all_to_all(back.reshape(span, ROWS, BS), plane, 0, 0)]
    all_to_all x0 -> x1, waiting for transfers between devices: none -> 4.49 us  [per_device(): back = lax.all_to_all(back.reshape(span, ROWS, BS), plane, 0, 0)]
  transfers between devices with their start and end apart: 40 -> 41, of which waited for: 12 -> 13; matrix products, arithmetic and copies ran while one was open for 3% -> 3% of each run, Pallas kernels for 3% -> 5%
where the time goes in v4:
time: 221 us; the launch traced here: 220 us
  starting transfers between devices  115 us (52%)
  waiting for transfers between devices  49.4 us (22%)
  Pallas kernels  40.3 us (18%)
  local copies, waits for them, and re-layouts  9.59 us (4%)
  other arithmetic  2.63 us (1%)
    ppermute x35, starting transfers between devices, shift(): return lambda value: lax.ppermute(value, axis, pairs)  72.1 us
    ppermute x35, waiting for transfers between devices, shift(): return lambda value: lax.ppermute(value, axis, pairs)  35.1 us
    pallas_call x1, Pallas kernels, per_device(): pl.pallas_call(functools.partial(main_kernel, [len(g) for g in keys]), gr...  29.7 us
    all_to_all x1, starting transfers between devices, per_device(): spread = lax.all_to_all(own.reshape(span, per, ROWS, BS), plane, 0, 0)  10.1 us
    all_to_all x1, starting transfers between devices, per_device(): back = lax.all_to_all(back.reshape(span, ROWS, BS), plane, 0, 0)  8.2 us
    all_to_all x1, starting transfers between devices, per_device(): in_grad = jnp.sum(lax.all_to_all(in_part, ('y', 'core'), 0, 0), axis=0)  7.94 us
    all_to_all x1, starting transfers between devices, per_device(): low_own = jnp.sum(lax.all_to_all(partial, plane, 0, 0), axis=0)  7.94 us
    all_to_all x1, waiting for transfers between devices, per_device(): lax.all_to_all(jnp.broadcast_to(back_own[None], (span, ROWS, BS)), plane,...  6.55 us
  transfers between devices with their start and end apart: 41, of which 13 were waited for; matrix products, arithmetic and copies ran while one was open for 3% of the time, Pallas kernels for 5%

profile of v4, /device:TPU:1, one launch (start us, length us, event | category | flops | bytes accessed | tf_op | source)
XLA Modules:
  0.0 219.9 jit_solution(13068217435256334402)
XLA Ops:
  2.5 3.3 %collective-permute-start.16 = (bf16[1,96,16,128]{3,2,1,0:T(8,128)(2,1)S(1)}, bf16[1,96,16,128]{3,2,1,0:T(8,128)(2,1)S(1)}, u32[]{:S(2)}, u32[]{:S(2)}) collective-permute-start(bf16[1,96,16,128]{3,2,1,0:T(8,128)(2,1)S(1)} %get-tuple-element.33.rest_0_), channel_id=1, source_target_pairs={{0,3},{1,0},{2,1},{3,2},{4,7},{5,4},{6,5},{7,6},{8,11},{9,8},{10,9... | collective-permute-start | bytes 1179656 | tf_op jit(solution)/shard_map/ppermute | solution.py:30
  5.8 5.6 %collective-permute-start.2 = (bf16[1,96,16,128]{3,2,1,0:T(8,128)(2,1)S(1)}, bf16[1,96,16,128]{3,2,1,0:T(8,128)(2,1)S(1)}, u32[]{:S(2)}, u32[]{:S(2)}) collective-permute-start(bf16[1,96,16,128]{3,2,1,0:T(8,128)(2,1)S(1)} %get-tuple-element.33.rest_0_), channel_id=1, source_target_pairs={{0,28},{4,0},{8,4},{12,8},{16,12},{20,16},{24,20},{28,24},{1,29},{... | collective-permute-start | bytes 1179656 | tf_op jit(solution)/shard_map/ppermute | solution.py:30
  13.6 6.4 %collective-permute-start.20 = (bf16[1,96,16,128]{3,2,1,0:T(8,128)(2,1)S(1)}, bf16[1,96,16,128]{3,2,1,0:T(8,128)(2,1)S(1)}, u32[]{:S(2)}, u32[]{:S(2)}) collective-permute-start(bf16[1,96,16,128]{3,2,1,0:T(8,128)(2,1)S(1)} %collective-permute-done.16.rest_17_), channel_id=1, source_target_pairs={{0,28},{4,0},{8,4},{12,8},{16,12},{20,16},{24,20},{28,24},{1,29},{... | collective-permute-start | bytes 1179656 | tf_op jit(solution)/shard_map/ppermute | solution.py:30
  20.3 1.8 collective-permute-done.1.rest_2_
  24.2 9.6 %collective-permute-start.18 = (bf16[1,96,16,128]{3,2,1,0:T(8,128)(2,1)S(1)}, bf16[1,96,16,128]{3,2,1,0:T(8,128)(2,1)}, u32[]{:S(2)}, u32[]{:S(2)}) collective-permute-start(bf16[1,96,16,128]{3,2,1,0:T(8,128)(2,1)S(1)} %collective-permute-done.1.rest_2_), channel_id=1, source_target_pairs={{0,3},{1,0},{2,1},{3,2},{4,7},{5,4},{6,5},{7,6},{8,11},{9,8},{10,9... | collective-permute-start | bytes 1179656 | tf_op jit(solution)/shard_map/ppermute | solution.py:30
  34.5 10.1 %all-to-all-start = ((bf16[32,3,16,128]{3,2,1,0:T(8,128)(2,1)}), bf16[32,3,16,128]{3,2,1,0:T(8,128)(2,1)S(1)}, u32[]{:S(2)}, u32[]{:S(2)}) async-start(bf16[32,3,16,128]{3,2,1,0:T(8,128)(2,1)} %bitcast.72), calls=%async_computation | async-start | bytes 786432 | tf_op jit(solution)/shard_map/all_to_all | solution.py:244
  44.6 2.6 %collective-permute-start.8 = (bf16[1,96,16,128]{3,2,1,0:T(8,128)(2,1)S(1)}, bf16[1,96,16,128]{3,2,1,0:T(8,128)(2,1)}, u32[]{:S(2)}, u32[]{:S(2)}) collective-permute-start(bf16[1,96,16,128]{3,2,1,0:T(8,128)(2,1)S(1)} %collective-permute-done.rest_1_), channel_id=1, source_target_pairs={{0,28},{4,0},{8,4},{12,8},{16,12},{20,16},{24,20},{28,24},{1,29},{... | collective-permute-start | bytes 1179656 | tf_op jit(solution)/shard_map/ppermute | solution.py:30
  47.2 2.5 %collective-permute-start.24 = (bf16[1,96,16,128]{3,2,1,0:T(8,128)(2,1)S(1)}, bf16[1,96,16,128]{3,2,1,0:T(8,128)(2,1)S(1)}, u32[]{:S(2)}, u32[]{:S(2)}) collective-permute-start(bf16[1,96,16,128]{3,2,1,0:T(8,128)(2,1)S(1)} %collective-permute-done.4.rest_5_), channel_id=1, source_target_pairs={{0,3},{1,0},{2,1},{3,2},{4,7},{5,4},{6,5},{7,6},{8,11},{9,8},{10,9... | collective-permute-start | bytes 1179656 | tf_op jit(solution)/shard_map/ppermute | solution.py:30
  49.7 2.9 %collective-permute-start.6 = (bf16[1,96,16,128]{3,2,1,0:T(8,128)(2,1)S(1)}, bf16[1,96,16,128]{3,2,1,0:T(8,128)(2,1)}, u32[]{:S(2)}, u32[]{:S(2)}) collective-permute-start(bf16[1,96,16,128]{3,2,1,0:T(8,128)(2,1)S(1)} %collective-permute-done.4.rest_5_), channel_id=1, source_target_pairs={{0,28},{4,0},{8,4},{12,8},{16,12},{20,16},{24,20},{28,24},{1,29},{... | collective-permute-start | bytes 1179656 | tf_op jit(solution)/shard_map/ppermute | solution.py:30
  52.5 8.0 %collective-permute-done.8.rest_9_ = bf16[1,96,16,128]{3,2,1,0:T(8,128)(2,1)} collective-permute-done((bf16[1,96,16,128]{3,2,1,0:T(8,128)(2,1)S(1)}, bf16[1,96,16,128]{3,2,1,0:T(8,128)(2,1)}, u32[]{:S(2)}, u32[]{:S(2)}) %collective-permute-start.8) | collective-permute-done | bytes 393248 | tf_op jit(solution)/shard_map/ppermute | solution.py:30
  60.5 2.4 %collective-permute-start.22 = (bf16[1,96,16,128]{3,2,1,0:T(8,128)(2,1)}, bf16[1,96,16,128]{3,2,1,0:T(8,128)(2,1)}, u32[]{:S(2)}, u32[]{:S(2)}) collective-permute-start(bf16[1,96,16,128]{3,2,1,0:T(8,128)(2,1)} %collective-permute-done.3.rest_4_), channel_id=1, source_target_pairs={{0,3},{1,0},{2,1},{3,2},{4,7},{5,4},{6,5},{7,6},{8,11},{9,8},{10,9... | collective-permute-start | bytes 1179656 | tf_op jit(solution)/shard_map/ppermute | solution.py:30
  64.1 2.5 %collective-permute-start.10 = (bf16[1,96,16,128]{3,2,1,0:T(8,128)(2,1)}, bf16[1,96,16,128]{3,2,1,0:T(8,128)(2,1)}, u32[]{:S(2)}, u32[]{:S(2)}) collective-permute-start(bf16[1,96,16,128]{3,2,1,0:T(8,128)(2,1)} %collective-permute-done.8.rest_9_), channel_id=1, source_target_pairs={{0,28},{4,0},{8,4},{12,8},{16,12},{20,16},{24,20},{28,24},{1,29},{... | collective-permute-start | bytes 1179656 | tf_op jit(solution)/shard_map/ppermute | solution.py:30
  66.7 2.4 %collective-permute-done.6.rest_7_ = bf16[1,96,16,128]{3,2,1,0:T(8,128)(2,1)} collective-permute-done((bf16[1,96,16,128]{3,2,1,0:T(8,128)(2,1)S(1)}, bf16[1,96,16,128]{3,2,1,0:T(8,128)(2,1)}, u32[]{:S(2)}, u32[]{:S(2)}) %collective-permute-start.6) | collective-permute-done | bytes 393248 | tf_op jit(solution)/shard_map/ppermute | solution.py:30
  70.2 2.1 convolution_bitcast_fusion
  72.3 7.9 %all-to-all-start.1 = ((f32[32,16,128]{2,1,0:T(8,128)}), f32[32,16,128]{2,1,0:T(8,128)S(1)}, u32[]{:S(2)}, u32[]{:S(2)}) async-start(f32[32,16,128]{2,1,0:T(8,128)} %convolution_bitcast_fusion), calls=%async_computation.1 | async-start | bytes 524288 | tf_op jit(solution)/shard_map/all_to_all | solution.py:249
  80.3 2.5 %collective-permute-start.28 = (bf16[1,96,16,128]{3,2,1,0:T(8,128)(2,1)}, bf16[1,96,16,128]{3,2,1,0:T(8,128)(2,1)}, u32[]{:S(2)}, u32[]{:S(2)}) collective-permute-start(bf16[1,96,16,128]{3,2,1,0:T(8,128)(2,1)} %collective-permute-done.6.rest_7_), channel_id=1, source_target_pairs={{0,3},{1,0},{2,1},{3,2},{4,7},{5,4},{6,5},{7,6},{8,11},{9,8},{10,9... | collective-permute-start | bytes 1179656 | tf_op jit(solution)/shard_map/ppermute | solution.py:30
  84.1 2.6 %collective-permute-start.26 = (bf16[1,96,16,128]{3,2,1,0:T(8,128)(2,1)}, bf16[1,96,16,128]{3,2,1,0:T(8,128)(2,1)}, u32[]{:S(2)}, u32[]{:S(2)}) collective-permute-start(bf16[1,96,16,128]{3,2,1,0:T(8,128)(2,1)} %collective-permute-done.5.rest_6_), channel_id=1, source_target_pairs={{0,3},{1,0},{2,1},{3,2},{4,7},{5,4},{6,5},{7,6},{8,11},{9,8},{10,9... | collective-permute-start | bytes 1179656 | tf_op jit(solution)/shard_map/ppermute | solution.py:30
  88.9 3.3 %all-to-all-done.1 = f32[32,16,128]{2,1,0:T(8,128)S(1)} async-done(((f32[32,16,128]{2,1,0:T(8,128)}), f32[32,16,128]{2,1,0:T(8,128)S(1)}, u32[]{:S(2)}, u32[]{:S(2)}) %all-to-all-start.1) | async-done | bytes 262176 | tf_op jit(solution)/shard_map/all_to_all | solution.py:249
  92.9 3.9 %all-to-all-start.2 = ((f32[32,16,128]{2,1,0:T(8,128)}), f32[32,16,128]{2,1,0:T(8,128)S(1)}, u32[]{:S(2)}, u32[]{:S(2)}) async-start(f32[32,16,128]{2,1,0:T(8,128)} %broadcast_in_dim.17), calls=%async_computation.2 | async-start | bytes 524288 | tf_op jit(solution)/shard_map/all_to_all | solution.py:250
  102.4 3.7 %collective-permute-done.25.rest_26_ = bf16[1,96,16,128]{3,2,1,0:T(8,128)(2,1)S(1)} collective-permute-done((bf16[1,96,16,128]{3,2,1,0:T(8,128)(2,1)}, bf16[1,96,16,128]{3,2,1,0:T(8,128)(2,1)S(1)}, u32[]{:S(2)}, u32[]{:S(2)}) %collective-permute-start.25) | collective-permute-done | bytes 393248 | tf_op jit(solution)/shard_map/ppermute | solution.py:30
  108.5 2.0 collective-permute-done.29.rest_30_
  110.5 29.7 %columns.1 = (bf16[512,1536]{1,0:T(8,128)(2,1)}, s16[4,2528,128]{2,1,0:T(8,128)(2,1)}, s16[4,2528,128]{2,1,0:T(8,128)(2,1)}, f32[512,128]{1,0:T(8,128)}) custom-call(s32[96]{0:T(128)S(1)} %reshape.176.rows_ref, s32[4,96]{1,0:T(4,128)S(1)} %pad_add_fusion.where_ref, s32[32]{0:T(128)S(1)} %stack.148.place_ref, f32[512,128]{1,0:T(8,128)S(1)} %bitcast.71, ...), custom_call_target="tpu_custom_call" | custom-call | tf_op jit(solution)/shard_map/columns/pallas_call | solution.py:288
  140.2 11.4 %collective-permute-start.31 = (s16[4,2528,128]{2,1,0:T(8,128)(2,1)}, s16[4,2528,128]{2,1,0:T(8,128)(2,1)S(1)}, u32[]{:S(2)}, u32[]{:S(2)}) collective-permute-start(s16[4,2528,128]{2,1,0:T(8,128)(2,1)} %get-tuple-element.13), channel_id=1, source_target_pairs={{0,32},{32,0},{1,33},{33,1},{2,34},{34,2},{3,35},{35,3},{4,36},{36... | collective-permute-start | bytes 7766024 | tf_op jit(solution)/shard_map/ppermute | solution.py:30
  151.6 8.2 %all-to-all-start.3 = ((f32[32,16,128]{2,1,0:T(8,128)}), f32[32,16,128]{2,1,0:T(8,128)}, u32[]{:S(2)}, u32[]{:S(2)}) async-start(f32[32,16,128]{2,1,0:T(8,128)} %bitcast.48), calls=%async_computation.3 | async-start | bytes 524288 | tf_op jit(solution)/shard_map/all_to_all | solution.py:329
  161.3 4.6 %pairs.1.own_ref = s16[4,2528,128]{2,1,0:T(8,128)(2,1)S(1)} custom-call(s16[4,2528,128]{2,1,0:T(8,128)(2,1)} %get-tuple-element.12.keep_ref, s16[4,2528,128]{2,1,0:T(8,128)(2,1)} %copy-done.3), custom_call_target="tpu_custom_call" | custom-call | tf_op jit(solution)/shard_map/pairs/pallas_call | solution.py:330
  167.3 4.5 %all-to-all-done.3 = f32[32,16,128]{2,1,0:T(8,128)} async-done(((f32[32,16,128]{2,1,0:T(8,128)}), f32[32,16,128]{2,1,0:T(8,128)}, u32[]{:S(2)}, u32[]{:S(2)}) %all-to-all-start.3) | async-done | bytes 262176 | tf_op jit(solution)/shard_map/all_to_all | solution.py:329
  173.5 4.9 %all-to-all-start.4 = ((f32[32,16,128]{2,1,0:T(8,128)}), f32[32,16,128]{2,1,0:T(8,128)}, u32[]{:S(2)}, u32[]{:S(2)}) async-start(f32[32,16,128]{2,1,0:T(8,128)} %broadcast_in_dim.21), calls=%async_computation.4 | async-start | bytes 524288 | tf_op jit(solution)/shard_map/all_to_all | solution.py:344
  178.4 2.8 %collective-permute-start.34 = (s16[2528,128]{1,0:T(8,128)(2,1)}, s16[2528,128]{1,0:T(8,128)(2,1)}, u32[]{:S(2)}, u32[]{:S(2)}) collective-permute-start(s16[2528,128]{1,0:T(8,128)(2,1)} %get-tuple-element.30), channel_id=1, source_target_pairs={{0,192},{64,0},{128,64},{192,128},{1,193},{65,1},{129,65},{193,129... | collective-permute-start | bytes 1941512 | tf_op jit(solution)/shard_map/ppermute | solution.py:30
  182.3 6.5 %all-to-all-done.4.back_ref = f32[32,16,128]{2,1,0:T(8,128)} async-done(((f32[32,16,128]{2,1,0:T(8,128)}), f32[32,16,128]{2,1,0:T(8,128)}, u32[]{:S(2)}, u32[]{:S(2)}) %all-to-all-start.4) | async-done | bytes 262176 | tf_op jit(solution)/shard_map/all_to_all | solution.py:344
  190.9 7.9 %all-to-all-start.5 = ((f32[8,48,128]{2,1,0:T(8,128)}), f32[8,48,128]{2,1,0:T(8,128)S(1)}, u32[]{:S(2)}, u32[]{:S(2)}) async-start(f32[8,48,128]{2,1,0:T(8,128)} %copy-done.2), calls=%async_computation.5 | async-start | bytes 393216 | tf_op jit(solution)/shard_map/all_to_all | solution.py:348
  199.6 14.3 %collective-permute-done.32.refs_0_ = s16[2528,128]{1,0:T(8,128)(2,1)} collective-permute-done((s16[2528,128]{1,0:T(8,128)(2,1)}, s16[2528,128]{1,0:T(8,128)(2,1)}, u32[]{:S(2)}, u32[]{:S(2)}) %collective-permute-start.32) | collective-permute-done | bytes 647200 | tf_op jit(solution)/shard_map/ppermute | solution.py:30
  213.9 4.6 %slots.1 = (f32[18,128,128]{2,1,0:T(8,128)}, f32[128,192]{1,0:T(8,128)S(1)}) custom-call(s32[1]{0:T(128)} %bitcast.44.count_ref, s16[4,2528,128]{2,1,0:T(8,128)(2,1)} %copy-done.1, s16[2528,128]{1,0:T(8,128)(2,1)} %collective-permute-done.32.refs_0_, s16[2528,128]{1,0:T(8,128)(2,1)} %collective-permute-done.33.refs_1_, ...), custom_call_target="tpu_custom_call" | custom-call | tf_op jit(solution)/shard_map/slots/pallas_call | solution.py:351
  (99 shorter events, 31.7 us)
Async XLA Ops:
  5.8 14.2 %collective-permute-start.15 = (bf16[1,96,16,128]{3,2,1,0:T(8,128)(2,1)S(1)}, bf16[1,96,16,128]{3,2,1,0:T(8,128)(2,1)}, u32[]{:S(2)}, u32[]{:S(2)}) collective-permute-start(bf16[1,96,16,128]{3,2,1,0:T(8,128)(2,1)S(1)} %get-tuple-element.33.rest_0_), channel_id=1, source_target_pairs={{0,1},{1,2},{2,3},{3,0},{4,5},{5,6},{6,7},{7,4},{8,9},{9,10},{10,1... | collective-permute-start | bytes 1179656 | tf_op jit(solution)/shard_map/ppermute | solution.py:30
  5.8 14.2 %collective-permute-start.2 = (bf16[1,96,16,128]{3,2,1,0:T(8,128)(2,1)S(1)}, bf16[1,96,16,128]{3,2,1,0:T(8,128)(2,1)S(1)}, u32[]{:S(2)}, u32[]{:S(2)}) collective-permute-start(bf16[1,96,16,128]{3,2,1,0:T(8,128)(2,1)S(1)} %get-tuple-element.33.rest_0_), channel_id=1, source_target_pairs={{0,28},{4,0},{8,4},{12,8},{16,12},{20,16},{24,20},{28,24},{1,29},{... | collective-permute-start | bytes 1179656 | tf_op jit(solution)/shard_map/ppermute | solution.py:30
  13.6 20.2 %collective-permute-start.20 = (bf16[1,96,16,128]{3,2,1,0:T(8,128)(2,1)S(1)}, bf16[1,96,16,128]{3,2,1,0:T(8,128)(2,1)S(1)}, u32[]{:S(2)}, u32[]{:S(2)}) collective-permute-start(bf16[1,96,16,128]{3,2,1,0:T(8,128)(2,1)S(1)} %collective-permute-done.16.rest_17_), channel_id=1, source_target_pairs={{0,28},{4,0},{8,4},{12,8},{16,12},{20,16},{24,20},{28,24},{1,29},{... | collective-permute-start | bytes 1179656 | tf_op jit(solution)/shard_map/ppermute | solution.py:30
  19.9 24.6 %collective-permute-start.17 = (bf16[1,96,16,128]{3,2,1,0:T(8,128)(2,1)}, bf16[1,96,16,128]{3,2,1,0:T(8,128)(2,1)}, u32[]{:S(2)}, u32[]{:S(2)}) collective-permute-start(bf16[1,96,16,128]{3,2,1,0:T(8,128)(2,1)} %collective-permute-done.15.rest_16_), channel_id=1, source_target_pairs={{0,4},{4,8},{8,12},{12,16},{16,20},{20,24},{24,28},{28,0},{1,5},{5... | collective-permute-start | bytes 1179656 | tf_op jit(solution)/shard_map/ppermute | solution.py:30
  20.0 27.2 %collective-permute-start.19 = (bf16[1,96,16,128]{3,2,1,0:T(8,128)(2,1)S(1)}, bf16[1,96,16,128]{3,2,1,0:T(8,128)(2,1)}, u32[]{:S(2)}, u32[]{:S(2)}) collective-permute-start(bf16[1,96,16,128]{3,2,1,0:T(8,128)(2,1)S(1)} %collective-permute-done.2.rest_3_), channel_id=1, source_target_pairs={{0,1},{1,2},{2,3},{3,0},{4,5},{5,6},{6,7},{7,4},{8,9},{9,10},{10,1... | collective-permute-start | bytes 1179656 | tf_op jit(solution)/shard_map/ppermute | solution.py:30
  22.1 25.1 %collective-permute-start.4 = (bf16[1,96,16,128]{3,2,1,0:T(8,128)(2,1)S(1)}, bf16[1,96,16,128]{3,2,1,0:T(8,128)(2,1)S(1)}, u32[]{:S(2)}, u32[]{:S(2)}) collective-permute-start(bf16[1,96,16,128]{3,2,1,0:T(8,128)(2,1)S(1)} %collective-permute-done.2.rest_3_), channel_id=1, source_target_pairs={{0,28},{4,0},{8,4},{12,8},{16,12},{20,16},{24,20},{28,24},{1,29},{... | collective-permute-start | bytes 1179656 | tf_op jit(solution)/shard_map/ppermute | solution.py:30
  24.2 25.5 %collective-permute-start.18 = (bf16[1,96,16,128]{3,2,1,0:T(8,128)(2,1)S(1)}, bf16[1,96,16,128]{3,2,1,0:T(8,128)(2,1)}, u32[]{:S(2)}, u32[]{:S(2)}) collective-permute-start(bf16[1,96,16,128]{3,2,1,0:T(8,128)(2,1)S(1)} %collective-permute-done.1.rest_2_), channel_id=1, source_target_pairs={{0,3},{1,0},{2,1},{3,2},{4,7},{5,4},{6,5},{7,6},{8,11},{9,8},{10,9... | collective-permute-start | bytes 1179656 | tf_op jit(solution)/shard_map/ppermute | solution.py:30
  34.5 15.2 %collective-permute-start.3 = (bf16[1,96,16,128]{3,2,1,0:T(8,128)(2,1)S(1)}, bf16[1,96,16,128]{3,2,1,0:T(8,128)(2,1)}, u32[]{:S(2)}, u32[]{:S(2)}) collective-permute-start(bf16[1,96,16,128]{3,2,1,0:T(8,128)(2,1)S(1)} %collective-permute-done.1.rest_2_), channel_id=1, source_target_pairs={{0,4},{4,8},{8,12},{12,16},{16,20},{20,24},{24,28},{28,0},{1,5},{5... | collective-permute-start | bytes 1179656 | tf_op jit(solution)/shard_map/ppermute | solution.py:30
  34.5 35.7 %all-to-all-start = ((bf16[32,3,16,128]{3,2,1,0:T(8,128)(2,1)}), bf16[32,3,16,128]{3,2,1,0:T(8,128)(2,1)S(1)}, u32[]{:S(2)}, u32[]{:S(2)}) async-start(bf16[32,3,16,128]{3,2,1,0:T(8,128)(2,1)} %bitcast.72), calls=%async_computation | async-start | bytes 786432 | tf_op jit(solution)/shard_map/all_to_all | solution.py:244
  44.6 15.9 %collective-permute-start.8 = (bf16[1,96,16,128]{3,2,1,0:T(8,128)(2,1)S(1)}, bf16[1,96,16,128]{3,2,1,0:T(8,128)(2,1)}, u32[]{:S(2)}, u32[]{:S(2)}) collective-permute-start(bf16[1,96,16,128]{3,2,1,0:T(8,128)(2,1)S(1)} %collective-permute-done.rest_1_), channel_id=1, source_target_pairs={{0,28},{4,0},{8,4},{12,8},{16,12},{20,16},{24,20},{28,24},{1,29},{... | collective-permute-start | bytes 1179656 | tf_op jit(solution)/shard_map/ppermute | solution.py:30
  47.2 15.7 %collective-permute-start.7 = (bf16[1,96,16,128]{3,2,1,0:T(8,128)(2,1)S(1)}, bf16[1,96,16,128]{3,2,1,0:T(8,128)(2,1)}, u32[]{:S(2)}, u32[]{:S(2)}) collective-permute-start(bf16[1,96,16,128]{3,2,1,0:T(8,128)(2,1)S(1)} %collective-permute-done.rest_1_), channel_id=1, source_target_pairs={{0,4},{4,8},{8,12},{12,16},{16,20},{20,24},{24,28},{28,0},{1,5},{5... | collective-permute-start | bytes 1179656 | tf_op jit(solution)/shard_map/ppermute | solution.py:30
  47.2 16.1 %collective-permute-start.24 = (bf16[1,96,16,128]{3,2,1,0:T(8,128)(2,1)S(1)}, bf16[1,96,16,128]{3,2,1,0:T(8,128)(2,1)S(1)}, u32[]{:S(2)}, u32[]{:S(2)}) collective-permute-start(bf16[1,96,16,128]{3,2,1,0:T(8,128)(2,1)S(1)} %collective-permute-done.4.rest_5_), channel_id=1, source_target_pairs={{0,3},{1,0},{2,1},{3,2},{4,7},{5,4},{6,5},{7,6},{8,11},{9,8},{10,9... | collective-permute-start | bytes 1179656 | tf_op jit(solution)/shard_map/ppermute | solution.py:30
  49.7 14.4 %collective-permute-start.23 = (bf16[1,96,16,128]{3,2,1,0:T(8,128)(2,1)S(1)}, bf16[1,96,16,128]{3,2,1,0:T(8,128)(2,1)S(1)}, u32[]{:S(2)}, u32[]{:S(2)}) collective-permute-start(bf16[1,96,16,128]{3,2,1,0:T(8,128)(2,1)S(1)} %collective-permute-done.4.rest_5_), channel_id=1, source_target_pairs={{0,1},{1,2},{2,3},{3,0},{4,5},{5,6},{6,7},{7,4},{8,9},{9,10},{10,1... | collective-permute-start | bytes 1179656 | tf_op jit(solution)/shard_map/ppermute | solution.py:30
  49.7 19.3 %collective-permute-start.6 = (bf16[1,96,16,128]{3,2,1,0:T(8,128)(2,1)S(1)}, bf16[1,96,16,128]{3,2,1,0:T(8,128)(2,1)}, u32[]{:S(2)}, u32[]{:S(2)}) collective-permute-start(bf16[1,96,16,128]{3,2,1,0:T(8,128)(2,1)S(1)} %collective-permute-done.4.rest_5_), channel_id=1, source_target_pairs={{0,28},{4,0},{8,4},{12,8},{16,12},{20,16},{24,20},{28,24},{1,29},{... | collective-permute-start | bytes 1179656 | tf_op jit(solution)/shard_map/ppermute | solution.py:30
  60.5 19.7 %collective-permute-start.22 = (bf16[1,96,16,128]{3,2,1,0:T(8,128)(2,1)}, bf16[1,96,16,128]{3,2,1,0:T(8,128)(2,1)}, u32[]{:S(2)}, u32[]{:S(2)}) collective-permute-start(bf16[1,96,16,128]{3,2,1,0:T(8,128)(2,1)} %collective-permute-done.3.rest_4_), channel_id=1, source_target_pairs={{0,3},{1,0},{2,1},{3,2},{4,7},{5,4},{6,5},{7,6},{8,11},{9,8},{10,9... | collective-permute-start | bytes 1179656 | tf_op jit(solution)/shard_map/ppermute | solution.py:30
  62.9 19.9 %collective-permute-start.21 = (bf16[1,96,16,128]{3,2,1,0:T(8,128)(2,1)}, bf16[1,96,16,128]{3,2,1,0:T(8,128)(2,1)}, u32[]{:S(2)}, u32[]{:S(2)}) collective-permute-start(bf16[1,96,16,128]{3,2,1,0:T(8,128)(2,1)} %collective-permute-done.3.rest_4_), channel_id=1, source_target_pairs={{0,1},{1,2},{2,3},{3,0},{4,5},{5,6},{6,7},{7,4},{8,9},{9,10},{10,1... | collective-permute-start | bytes 1179656 | tf_op jit(solution)/shard_map/ppermute | solution.py:30
  63.3 19.5 %collective-permute-start.5 = (bf16[1,96,16,128]{3,2,1,0:T(8,128)(2,1)}, bf16[1,96,16,128]{3,2,1,0:T(8,128)(2,1)}, u32[]{:S(2)}, u32[]{:S(2)}) collective-permute-start(bf16[1,96,16,128]{3,2,1,0:T(8,128)(2,1)} %collective-permute-done.3.rest_4_), channel_id=1, source_target_pairs={{0,4},{4,8},{8,12},{12,16},{16,20},{20,24},{24,28},{28,0},{1,5},{5... | collective-permute-start | bytes 1179656 | tf_op jit(solution)/shard_map/ppermute | solution.py:30
  64.1 19.9 %collective-permute-start.10 = (bf16[1,96,16,128]{3,2,1,0:T(8,128)(2,1)}, bf16[1,96,16,128]{3,2,1,0:T(8,128)(2,1)}, u32[]{:S(2)}, u32[]{:S(2)}) collective-permute-start(bf16[1,96,16,128]{3,2,1,0:T(8,128)(2,1)} %collective-permute-done.8.rest_9_), channel_id=1, source_target_pairs={{0,28},{4,0},{8,4},{12,8},{16,12},{20,16},{24,20},{28,24},{1,29},{... | collective-permute-start | bytes 1179656 | tf_op jit(solution)/shard_map/ppermute | solution.py:30
  69.0 17.6 %collective-permute-start.9 = (bf16[1,96,16,128]{3,2,1,0:T(8,128)(2,1)}, bf16[1,96,16,128]{3,2,1,0:T(8,128)(2,1)}, u32[]{:S(2)}, u32[]{:S(2)}) collective-permute-start(bf16[1,96,16,128]{3,2,1,0:T(8,128)(2,1)} %collective-permute-done.7.rest_8_), channel_id=1, source_target_pairs={{0,4},{4,8},{8,12},{12,16},{16,20},{20,24},{24,28},{28,0},{1,5},{5... | collective-permute-start | bytes 1179656 | tf_op jit(solution)/shard_map/ppermute | solution.py:30
  72.3 19.9 %all-to-all-start.1 = ((f32[32,16,128]{2,1,0:T(8,128)}), f32[32,16,128]{2,1,0:T(8,128)S(1)}, u32[]{:S(2)}, u32[]{:S(2)}) async-start(f32[32,16,128]{2,1,0:T(8,128)} %convolution_bitcast_fusion), calls=%async_computation.1 | async-start | bytes 524288 | tf_op jit(solution)/shard_map/all_to_all | solution.py:249
  80.3 16.6 %collective-permute-start.28 = (bf16[1,96,16,128]{3,2,1,0:T(8,128)(2,1)}, bf16[1,96,16,128]{3,2,1,0:T(8,128)(2,1)}, u32[]{:S(2)}, u32[]{:S(2)}) collective-permute-start(bf16[1,96,16,128]{3,2,1,0:T(8,128)(2,1)} %collective-permute-done.6.rest_7_), channel_id=1, source_target_pairs={{0,3},{1,0},{2,1},{3,2},{4,7},{5,4},{6,5},{7,6},{8,11},{9,8},{10,9... | collective-permute-start | bytes 1179656 | tf_op jit(solution)/shard_map/ppermute | solution.py:30
  82.8 15.3 %collective-permute-start.27 = (bf16[1,96,16,128]{3,2,1,0:T(8,128)(2,1)}, bf16[1,96,16,128]{3,2,1,0:T(8,128)(2,1)}, u32[]{:S(2)}, u32[]{:S(2)}) collective-permute-start(bf16[1,96,16,128]{3,2,1,0:T(8,128)(2,1)} %collective-permute-done.6.rest_7_), channel_id=1, source_target_pairs={{0,1},{1,2},{2,3},{3,0},{4,5},{5,6},{6,7},{7,4},{8,9},{9,10},{10,1... | collective-permute-start | bytes 1179656 | tf_op jit(solution)/shard_map/ppermute | solution.py:30
  82.8 16.5 %collective-permute-start.13 = (bf16[1,96,16,128]{3,2,1,0:T(8,128)(2,1)}, bf16[1,96,16,128]{3,2,1,0:T(8,128)(2,1)}, u32[]{:S(2)}, u32[]{:S(2)}) collective-permute-start(bf16[1,96,16,128]{3,2,1,0:T(8,128)(2,1)} %collective-permute-done.5.rest_6_), channel_id=1, source_target_pairs={{0,4},{4,8},{8,12},{12,16},{16,20},{20,24},{24,28},{28,0},{1,5},{5... | collective-permute-start | bytes 1179656 | tf_op jit(solution)/shard_map/ppermute | solution.py:30
  84.1 16.7 %collective-permute-start.26 = (bf16[1,96,16,128]{3,2,1,0:T(8,128)(2,1)}, bf16[1,96,16,128]{3,2,1,0:T(8,128)(2,1)}, u32[]{:S(2)}, u32[]{:S(2)}) collective-permute-start(bf16[1,96,16,128]{3,2,1,0:T(8,128)(2,1)} %collective-permute-done.5.rest_6_), channel_id=1, source_target_pairs={{0,3},{1,0},{2,1},{3,2},{4,7},{5,4},{6,5},{7,6},{8,11},{9,8},{10,9... | collective-permute-start | bytes 1179656 | tf_op jit(solution)/shard_map/ppermute | solution.py:30
  92.9 14.6 %all-to-all-start.2 = ((f32[32,16,128]{2,1,0:T(8,128)}), f32[32,16,128]{2,1,0:T(8,128)S(1)}, u32[]{:S(2)}, u32[]{:S(2)}) async-start(f32[32,16,128]{2,1,0:T(8,128)} %broadcast_in_dim.17), calls=%async_computation.2 | async-start | bytes 524288 | tf_op jit(solution)/shard_map/all_to_all | solution.py:250
  140.2 19.6 %collective-permute-start.31 = (s16[4,2528,128]{2,1,0:T(8,128)(2,1)}, s16[4,2528,128]{2,1,0:T(8,128)(2,1)S(1)}, u32[]{:S(2)}, u32[]{:S(2)}) collective-permute-start(s16[4,2528,128]{2,1,0:T(8,128)(2,1)} %get-tuple-element.13), channel_id=1, source_target_pairs={{0,32},{32,0},{1,33},{33,1},{2,34},{34,2},{3,35},{35,3},{4,36},{36... | collective-permute-start | bytes 7766024 | tf_op jit(solution)/shard_map/ppermute | solution.py:30
  151.6 20.2 %all-to-all-start.3 = ((f32[32,16,128]{2,1,0:T(8,128)}), f32[32,16,128]{2,1,0:T(8,128)}, u32[]{:S(2)}, u32[]{:S(2)}) async-start(f32[32,16,128]{2,1,0:T(8,128)} %bitcast.48), calls=%async_computation.3 | async-start | bytes 524288 | tf_op jit(solution)/shard_map/all_to_all | solution.py:329
  173.5 15.3 %all-to-all-start.4 = ((f32[32,16,128]{2,1,0:T(8,128)}), f32[32,16,128]{2,1,0:T(8,128)}, u32[]{:S(2)}, u32[]{:S(2)}) async-start(f32[32,16,128]{2,1,0:T(8,128)} %broadcast_in_dim.21), calls=%async_computation.4 | async-start | bytes 524288 | tf_op jit(solution)/shard_map/all_to_all | solution.py:344
  178.4 21.2 %collective-permute-start.34 = (s16[2528,128]{1,0:T(8,128)(2,1)}, s16[2528,128]{1,0:T(8,128)(2,1)}, u32[]{:S(2)}, u32[]{:S(2)}) collective-permute-start(s16[2528,128]{1,0:T(8,128)(2,1)} %get-tuple-element.30), channel_id=1, source_target_pairs={{0,192},{64,0},{128,64},{192,128},{1,193},{65,1},{129,65},{193,129... | collective-permute-start | bytes 1941512 | tf_op jit(solution)/shard_map/ppermute | solution.py:30
  181.3 18.4 %collective-permute-start.33 = (s16[2528,128]{1,0:T(8,128)(2,1)}, s16[2528,128]{1,0:T(8,128)(2,1)}, u32[]{:S(2)}, u32[]{:S(2)}) collective-permute-start(s16[2528,128]{1,0:T(8,128)(2,1)} %get-tuple-element.31), channel_id=1, source_target_pairs={{0,128},{64,192},{128,0},{192,64},{1,129},{65,193},{129,1},{193,65... | collective-permute-start | bytes 1941512 | tf_op jit(solution)/shard_map/ppermute | solution.py:30
  181.6 32.3 %collective-permute-start.32 = (s16[2528,128]{1,0:T(8,128)(2,1)}, s16[2528,128]{1,0:T(8,128)(2,1)}, u32[]{:S(2)}, u32[]{:S(2)}) collective-permute-start(s16[2528,128]{1,0:T(8,128)(2,1)} %get-tuple-element.32), channel_id=1, source_target_pairs={{0,64},{64,128},{128,192},{192,0},{1,65},{65,129},{129,193},{193,1... | collective-permute-start | bytes 1941512 | tf_op jit(solution)/shard_map/ppermute | solution.py:30
  190.9 28.4 %all-to-all-start.5 = ((f32[8,48,128]{2,1,0:T(8,128)}), f32[8,48,128]{2,1,0:T(8,128)S(1)}, u32[]{:S(2)}, u32[]{:S(2)}) async-start(f32[8,48,128]{2,1,0:T(8,128)} %copy-done.2), calls=%async_computation.5 | async-start | bytes 393216 | tf_op jit(solution)/shard_map/all_to_all | solution.py:348
  (20 other events, 331.3 us)

commit v5 on v4

--- a/solution.py
+++ b/solution.py
@@ -23,6 +23,7 @@
 CODE_ROWS = SLOT_ROWS + FO_ROWS
 PART_ROWS = CODE_ROWS + 32
 FINE = 256.0
+CUT = 10 * BS
 
 
 def shift(axis, size, step):
@@ -173,16 +174,61 @@
     out_ref[0, CODE_ROWS:] = fresh.astype(jnp.int32).astype(jnp.int16)
 
 
+def levels_in(rows):
+    return rows.astype(jnp.int32).astype(jnp.float32)
+
+
+def relay_kernel(up_ref, down_ref, above_ref, below_ref, up_out, down_out):
+    for own, got, out, first in (
+        (up_ref, above_ref, up_out, True),
+        (down_ref, below_ref, down_out, False),
+    ):
+        own_levels = levels_in(own[0, CODE_ROWS:])
+        got_levels = levels_in(got[CUT:] if first else got[CODE_ROWS - CUT :])
+        fresh = []
+        for start, size, index in blocks_of():
+            span = slice(start, start + size)
+            level = own_levels[index : index + 1]
+            if (start < CUT) == first:
+                offset = start if first else start - CUT
+                total = decode(own[0, span], level)
+                total += decode(got[offset : offset + size], got_levels[index : index + 1])
+                level = level_of(total)
+                out[span] = encode(total, level)
+            else:
+                out[span] = own[0, span]
+            fresh.append(level)
+        fresh.append(jnp.zeros((32 - len(fresh), BS), jnp.float32))
+        fresh = jnp.concatenate(fresh, axis=0)
+        out[CODE_ROWS:] = fresh.astype(jnp.int32).astype(jnp.int16)
+
+
+def relay(paired, above, below):
+    one = lambda i: pl.BlockSpec((1, PART_ROWS, BS), lambda _: (i, 0, 0))
+    flat = lambda rows: pl.BlockSpec((rows, BS), lambda _: (0, 0))
+    return pl.pallas_call(
+        relay_kernel,
+        grid=(1,),
+        in_specs=[one(1), one(3), flat(above.shape[0]), flat(below.shape[0])],
+        out_specs=[flat(PART_ROWS)] * 2,
+        out_shape=[jax.ShapeDtypeStruct((PART_ROWS, BS), jnp.int16)] * 2,
+        compiler_params=pltpu.CompilerParams(vmem_limit_bytes=30 * 1024 * 1024),
+        cost_estimate=pl.CostEstimate(
+            flops=40_000_000, bytes_accessed=40_000_000, transcendentals=0
+        ),
+        name="relay",
+    )(paired, paired, above, below)
+
+
 def final_kernel(count_ref, own_ref, *refs):
-    parts, (slots_ref, outer_ref) = refs[: NY - 1], refs[NY - 1 :]
-    tails = [own_ref[0, CODE_ROWS:]] + [r[CODE_ROWS:] for r in parts]
-    levels = [t.astype(jnp.int32).astype(jnp.float32) for t in tails]
+    parts, (slots_ref, outer_ref) = refs[:2], refs[2:]
+    levels = [levels_in(own_ref[0, CODE_ROWS:])] + [levels_in(r[CODE_ROWS:]) for r in parts]
     count = count_ref[0]
     for start, size, index in blocks_of():
-        total = decode(own_ref[0, start : start + size], levels[0][index : index + 1])
-        for i in range(NY - 1):
-            code = parts[i][start : start + size]
-            total += decode(code, levels[i + 1][index : index + 1])
+        span = slice(start, start + size)
+        total = decode(own_ref[0, span], levels[0][index : index + 1])
+        for i in range(2):
+            total += decode(parts[i][span], levels[i + 1][index : index + 1])
         if index < CAP:
             slots_ref[index] = jnp.where(index < count, total.T, 0.0)
         else:
@@ -336,10 +382,13 @@
         compiler_params=pltpu.CompilerParams(vmem_limit_bytes=50 * 1024 * 1024),
         name="pairs",
     )(keep, got)
-    outward = [paired[i] for i in (1, 2, 3)]
-    parts = [shift("y", NY, i)(outward[i - 1]) for i in (1, 2, 3)]
-
-    back, _ = lax.optimization_barrier((back, outward))
+    y_up, y_down = shift("y", NY, 1), shift("y", NY, -1)
+    above = jnp.concatenate([paired[2, :CUT], paired[2, CODE_ROWS:]])
+    below = paired[2, CUT:]
+    parts = relay(paired, y_up(above), y_down(below))
+    parts = [y_up(parts[0]), y_down(parts[1])]
+
+    back, _ = lax.optimization_barrier((back, (above, below)))
     back_own = jnp.sum(back, axis=0)
     back_all = lax.all_to_all(
         jnp.broadcast_to(back_own[None], (span, ROWS, BS)), plane, 0, 0
@@ -350,13 +399,16 @@
     whole = pl.BlockSpec(memory_space=pltpu.VMEM)
     slots, out_grad = pl.pallas_call(
         final_kernel,
-        in_specs=[pl.BlockSpec(memory_space=pltpu.SMEM)] + [whole] * NY,
+        in_specs=[pl.BlockSpec(memory_space=pltpu.SMEM)] + [whole] * 3,
         out_specs=[whole, whole],
         out_shape=[
             jax.ShapeDtypeStruct((CAP, BS, BS), jnp.float32),
             jax.ShapeDtypeStruct((BS, FO_ROWS), jnp.float32),
         ],
         compiler_params=pltpu.CompilerParams(vmem_limit_bytes=50 * 1024 * 1024),
+        cost_estimate=pl.CostEstimate(
+            flops=10_000_000, bytes_accessed=16_000_000, transcendentals=0
+        ),
         name="slots",
     )(mine, paired, *parts)
     return hidden, slots, in_grad, out_grad

time: 221 us -> 212 us (0.959)
  waiting for transfers between devices: 49.4 us -> 35.8 us
  starting transfers between devices: 115 us -> 118 us
    ppermute x35 -> x36, waiting for transfers between devices: 35.1 us -> 20.8 us  [shift(): return lambda value: lax.ppermute(value, axis, pairs)]
    all_to_all x1, waiting for transfers between devices: 0.01 us -> 5.16 us  [per_device(): in_grad = jnp.sum(lax.all_to_all(in_part, ('y', 'core'), 0, 0), axis=0)]
    all_to_all x1, waiting for transfers between devices: 4.49 us -> 1.58 us  [per_device(): back = lax.all_to_all(back.reshape(span, ROWS, BS), plane, 0, 0)]
    all_to_all x1, starting transfers between devices: 4.94 us -> 7.69 us  [per_device(): lax.all_to_all(jnp.broadcast_to(back_own[None], (span, ROWS, BS)), plane,...]
    pallas_call x0 -> x1, Pallas kernels: none -> 2.7 us  [relay(): pl.pallas_call(relay_kernel, grid=(1,), in_specs=[one(1), one(3), flat(ab...]
    ppermute x35 -> x36, starting transfers between devices: 72.1 us -> 73.7 us  [shift(): return lambda value: lax.ppermute(value, axis, pairs)]
    unnamed x25 -> x23, local copies, waits for them, and re-layouts: 5.57 us -> 5.58 us
  transfers between devices with their start and end apart: 41 -> 42, of which waited for: 13 -> 13; matrix products, arithmetic and copies ran while one was open for 3% -> 4% of each run, Pallas kernels for 5% -> 4%
where the time goes in v5:
time: 212 us; the launch traced here: 211 us
  starting transfers between devices  118 us (56%)
  Pallas kernels  41.8 us (20%)
  waiting for transfers between devices  35.8 us (17%)
  local copies, waits for them, and re-layouts  9.01 us (4%)
  other arithmetic  3.38 us (2%)
    ppermute x36, starting transfers between devices, shift(): return lambda value: lax.ppermute(value, axis, pairs)  73.7 us
    pallas_call x1, Pallas kernels, per_device(): pl.pallas_call(functools.partial(main_kernel, [len(g) for g in keys]), gr...  29.7 us
    ppermute x36, waiting for transfers between devices, shift(): return lambda value: lax.ppermute(value, axis, pairs)  20.8 us
    all_to_all x1, starting transfers between devices, per_device(): spread = lax.all_to_all(own.reshape(span, per, ROWS, BS), plane, 0, 0)  10.1 us
    all_to_all x1, starting transfers between devices, per_device(): back = lax.all_to_all(back.reshape(span, ROWS, BS), plane, 0, 0)  8.2 us
    all_to_all x1, starting transfers between devices, per_device(): low_own = jnp.sum(lax.all_to_all(partial, plane, 0, 0), axis=0)  7.94 us
    all_to_all x1, starting transfers between devices, per_device(): lax.all_to_all(jnp.broadcast_to(back_own[None], (span, ROWS, BS)), plane,...  7.69 us
    all_to_all x1, starting transfers between devices, per_device(): in_grad = jnp.sum(lax.all_to_all(in_part, ('y', 'core'), 0, 0), axis=0)  6.73 us
  transfers between devices with their start and end apart: 42, of which 13 were waited for; matrix products, arithmetic and copies ran while one was open for 4% of the time, Pallas kernels for 4%

profile of v5, /device:TPU:1, one launch (start us, length us, event | category | flops | bytes accessed | tf_op | source)
XLA Modules:
  0.0 211.2 jit_solution(7140203774352082893)
XLA Ops:
  2.5 3.3 %collective-permute-start.16 = (bf16[1,96,16,128]{3,2,1,0:T(8,128)(2,1)S(1)}, bf16[1,96,16,128]{3,2,1,0:T(8,128)(2,1)S(1)}, u32[]{:S(2)}, u32[]{:S(2)}) collective-permute-start(bf16[1,96,16,128]{3,2,1,0:T(8,128)(2,1)S(1)} %get-tuple-element.34.rest_0_), channel_id=1, source_target_pairs={{0,3},{1,0},{2,1},{3,2},{4,7},{5,4},{6,5},{7,6},{8,11},{9,8},{10,9... | collective-permute-start | bytes 1179656 | tf_op jit(solution)/shard_map/ppermute | solution.py:31
  5.8 5.6 %collective-permute-start.2 = (bf16[1,96,16,128]{3,2,1,0:T(8,128)(2,1)S(1)}, bf16[1,96,16,128]{3,2,1,0:T(8,128)(2,1)S(1)}, u32[]{:S(2)}, u32[]{:S(2)}) collective-permute-start(bf16[1,96,16,128]{3,2,1,0:T(8,128)(2,1)S(1)} %get-tuple-element.34.rest_0_), channel_id=1, source_target_pairs={{0,28},{4,0},{8,4},{12,8},{16,12},{20,16},{24,20},{28,24},{1,29},{... | collective-permute-start | bytes 1179656 | tf_op jit(solution)/shard_map/ppermute | solution.py:31
  13.6 6.4 %collective-permute-start.20 = (bf16[1,96,16,128]{3,2,1,0:T(8,128)(2,1)S(1)}, bf16[1,96,16,128]{3,2,1,0:T(8,128)(2,1)S(1)}, u32[]{:S(2)}, u32[]{:S(2)}) collective-permute-start(bf16[1,96,16,128]{3,2,1,0:T(8,128)(2,1)S(1)} %collective-permute-done.16.rest_17_), channel_id=1, source_target_pairs={{0,28},{4,0},{8,4},{12,8},{16,12},{20,16},{24,20},{28,24},{1,29},{... | collective-permute-start | bytes 1179656 | tf_op jit(solution)/shard_map/ppermute | solution.py:31
  20.3 1.8 collective-permute-done.1.rest_2_
  24.2 9.6 %collective-permute-start.18 = (bf16[1,96,16,128]{3,2,1,0:T(8,128)(2,1)S(1)}, bf16[1,96,16,128]{3,2,1,0:T(8,128)(2,1)}, u32[]{:S(2)}, u32[]{:S(2)}) collective-permute-start(bf16[1,96,16,128]{3,2,1,0:T(8,128)(2,1)S(1)} %collective-permute-done.1.rest_2_), channel_id=1, source_target_pairs={{0,3},{1,0},{2,1},{3,2},{4,7},{5,4},{6,5},{7,6},{8,11},{9,8},{10,9... | collective-permute-start | bytes 1179656 | tf_op jit(solution)/shard_map/ppermute | solution.py:31
  34.5 10.1 %all-to-all-start = ((bf16[32,3,16,128]{3,2,1,0:T(8,128)(2,1)}), bf16[32,3,16,128]{3,2,1,0:T(8,128)(2,1)S(1)}, u32[]{:S(2)}, u32[]{:S(2)}) async-start(bf16[32,3,16,128]{3,2,1,0:T(8,128)(2,1)} %bitcast.72), calls=%async_computation | async-start | bytes 786432 | tf_op jit(solution)/shard_map/all_to_all | solution.py:290
  44.6 2.6 %collective-permute-start.8 = (bf16[1,96,16,128]{3,2,1,0:T(8,128)(2,1)S(1)}, bf16[1,96,16,128]{3,2,1,0:T(8,128)(2,1)}, u32[]{:S(2)}, u32[]{:S(2)}) collective-permute-start(bf16[1,96,16,128]{3,2,1,0:T(8,128)(2,1)S(1)} %collective-permute-done.rest_1_), channel_id=1, source_target_pairs={{0,28},{4,0},{8,4},{12,8},{16,12},{20,16},{24,20},{28,24},{1,29},{... | collective-permute-start | bytes 1179656 | tf_op jit(solution)/shard_map/ppermute | solution.py:31
  47.2 2.5 %collective-permute-start.24 = (bf16[1,96,16,128]{3,2,1,0:T(8,128)(2,1)S(1)}, bf16[1,96,16,128]{3,2,1,0:T(8,128)(2,1)S(1)}, u32[]{:S(2)}, u32[]{:S(2)}) collective-permute-start(bf16[1,96,16,128]{3,2,1,0:T(8,128)(2,1)S(1)} %collective-permute-done.4.rest_5_), channel_id=1, source_target_pairs={{0,3},{1,0},{2,1},{3,2},{4,7},{5,4},{6,5},{7,6},{8,11},{9,8},{10,9... | collective-permute-start | bytes 1179656 | tf_op jit(solution)/shard_map/ppermute | solution.py:31
  49.7 2.9 %collective-permute-start.6 = (bf16[1,96,16,128]{3,2,1,0:T(8,128)(2,1)S(1)}, bf16[1,96,16,128]{3,2,1,0:T(8,128)(2,1)}, u32[]{:S(2)}, u32[]{:S(2)}) collective-permute-start(bf16[1,96,16,128]{3,2,1,0:T(8,128)(2,1)S(1)} %collective-permute-done.4.rest_5_), channel_id=1, source_target_pairs={{0,28},{4,0},{8,4},{12,8},{16,12},{20,16},{24,20},{28,24},{1,29},{... | collective-permute-start | bytes 1179656 | tf_op jit(solution)/shard_map/ppermute | solution.py:31
  52.5 8.0 %collective-permute-done.8.rest_9_ = bf16[1,96,16,128]{3,2,1,0:T(8,128)(2,1)} collective-permute-done((bf16[1,96,16,128]{3,2,1,0:T(8,128)(2,1)S(1)}, bf16[1,96,16,128]{3,2,1,0:T(8,128)(2,1)}, u32[]{:S(2)}, u32[]{:S(2)}) %collective-permute-start.8) | collective-permute-done | bytes 393248 | tf_op jit(solution)/shard_map/ppermute | solution.py:31
  60.5 2.4 %collective-permute-start.22 = (bf16[1,96,16,128]{3,2,1,0:T(8,128)(2,1)}, bf16[1,96,16,128]{3,2,1,0:T(8,128)(2,1)}, u32[]{:S(2)}, u32[]{:S(2)}) collective-permute-start(bf16[1,96,16,128]{3,2,1,0:T(8,128)(2,1)} %collective-permute-done.3.rest_4_), channel_id=1, source_target_pairs={{0,3},{1,0},{2,1},{3,2},{4,7},{5,4},{6,5},{7,6},{8,11},{9,8},{10,9... | collective-permute-start | bytes 1179656 | tf_op jit(solution)/shard_map/ppermute | solution.py:31
  64.1 2.5 %collective-permute-start.10 = (bf16[1,96,16,128]{3,2,1,0:T(8,128)(2,1)}, bf16[1,96,16,128]{3,2,1,0:T(8,128)(2,1)}, u32[]{:S(2)}, u32[]{:S(2)}) collective-permute-start(bf16[1,96,16,128]{3,2,1,0:T(8,128)(2,1)} %collective-permute-done.8.rest_9_), channel_id=1, source_target_pairs={{0,28},{4,0},{8,4},{12,8},{16,12},{20,16},{24,20},{28,24},{1,29},{... | collective-permute-start | bytes 1179656 | tf_op jit(solution)/shard_map/ppermute | solution.py:31
  66.7 2.4 %collective-permute-done.6.rest_7_ = bf16[1,96,16,128]{3,2,1,0:T(8,128)(2,1)} collective-permute-done((bf16[1,96,16,128]{3,2,1,0:T(8,128)(2,1)S(1)}, bf16[1,96,16,128]{3,2,1,0:T(8,128)(2,1)}, u32[]{:S(2)}, u32[]{:S(2)}) %collective-permute-start.6) | collective-permute-done | bytes 393248 | tf_op jit(solution)/shard_map/ppermute | solution.py:31
  70.2 2.1 convolution_bitcast_fusion
  72.3 7.9 %all-to-all-start.1 = ((f32[32,16,128]{2,1,0:T(8,128)}), f32[32,16,128]{2,1,0:T(8,128)S(1)}, u32[]{:S(2)}, u32[]{:S(2)}) async-start(f32[32,16,128]{2,1,0:T(8,128)} %convolution_bitcast_fusion), calls=%async_computation.1 | async-start | bytes 524288 | tf_op jit(solution)/shard_map/all_to_all | solution.py:295
  80.3 2.5 %collective-permute-start.28 = (bf16[1,96,16,128]{3,2,1,0:T(8,128)(2,1)}, bf16[1,96,16,128]{3,2,1,0:T(8,128)(2,1)}, u32[]{:S(2)}, u32[]{:S(2)}) collective-permute-start(bf16[1,96,16,128]{3,2,1,0:T(8,128)(2,1)} %collective-permute-done.6.rest_7_), channel_id=1, source_target_pairs={{0,3},{1,0},{2,1},{3,2},{4,7},{5,4},{6,5},{7,6},{8,11},{9,8},{10,9... | collective-permute-start | bytes 1179656 | tf_op jit(solution)/shard_map/ppermute | solution.py:31
  84.1 2.6 %collective-permute-start.26 = (bf16[1,96,16,128]{3,2,1,0:T(8,128)(2,1)}, bf16[1,96,16,128]{3,2,1,0:T(8,128)(2,1)}, u32[]{:S(2)}, u32[]{:S(2)}) collective-permute-start(bf16[1,96,16,128]{3,2,1,0:T(8,128)(2,1)} %collective-permute-done.5.rest_6_), channel_id=1, source_target_pairs={{0,3},{1,0},{2,1},{3,2},{4,7},{5,4},{6,5},{7,6},{8,11},{9,8},{10,9... | collective-permute-start | bytes 1179656 | tf_op jit(solution)/shard_map/ppermute | solution.py:31
  88.9 3.3 %all-to-all-done.1 = f32[32,16,128]{2,1,0:T(8,128)S(1)} async-done(((f32[32,16,128]{2,1,0:T(8,128)}), f32[32,16,128]{2,1,0:T(8,128)S(1)}, u32[]{:S(2)}, u32[]{:S(2)}) %all-to-all-start.1) | async-done | bytes 262176 | tf_op jit(solution)/shard_map/all_to_all | solution.py:295
  92.9 3.9 %all-to-all-start.2 = ((f32[32,16,128]{2,1,0:T(8,128)}), f32[32,16,128]{2,1,0:T(8,128)S(1)}, u32[]{:S(2)}, u32[]{:S(2)}) async-start(f32[32,16,128]{2,1,0:T(8,128)} %broadcast_in_dim.17), calls=%async_computation.2 | async-start | bytes 524288 | tf_op jit(solution)/shard_map/all_to_all | solution.py:296
  102.4 3.7 %collective-permute-done.25.rest_26_ = bf16[1,96,16,128]{3,2,1,0:T(8,128)(2,1)S(1)} collective-permute-done((bf16[1,96,16,128]{3,2,1,0:T(8,128)(2,1)}, bf16[1,96,16,128]{3,2,1,0:T(8,128)(2,1)S(1)}, u32[]{:S(2)}, u32[]{:S(2)}) %collective-permute-start.25) | collective-permute-done | bytes 393248 | tf_op jit(solution)/shard_map/ppermute | solution.py:31
  108.5 2.0 collective-permute-done.29.rest_30_
  110.5 29.7 %columns.1 = (bf16[512,1536]{1,0:T(8,128)(2,1)}, s16[4,2528,128]{2,1,0:T(8,128)(2,1)}, s16[4,2528,128]{2,1,0:T(8,128)(2,1)}, f32[512,128]{1,0:T(8,128)}) custom-call(s32[96]{0:T(128)S(1)} %reshape.176.rows_ref, s32[4,96]{1,0:T(4,128)S(1)} %pad_add_fusion.1.where_ref, s32[32]{0:T(128)S(1)} %stack.148.place_ref, f32[512,128]{1,0:T(8,128)S(1)} %bitcast.71, ...), custom_call_target="tpu_custom_call" | custom-call | tf_op jit(solution)/shard_map/columns/pallas_call | solution.py:334
  140.2 11.4 %collective-permute-start.31 = (s16[4,2528,128]{2,1,0:T(8,128)(2,1)}, s16[4,2528,128]{2,1,0:T(8,128)(2,1)S(1)}, u32[]{:S(2)}, u32[]{:S(2)}) collective-permute-start(s16[4,2528,128]{2,1,0:T(8,128)(2,1)} %get-tuple-element.15), channel_id=1, source_target_pairs={{0,32},{32,0},{1,33},{33,1},{2,34},{34,2},{3,35},{35,3},{4,36},{36... | collective-permute-start | bytes 7766024 | tf_op jit(solution)/shard_map/ppermute | solution.py:31
  151.6 8.2 %all-to-all-start.3 = ((f32[32,16,128]{2,1,0:T(8,128)}), f32[32,16,128]{2,1,0:T(8,128)}, u32[]{:S(2)}, u32[]{:S(2)}) async-start(f32[32,16,128]{2,1,0:T(8,128)} %bitcast.48), calls=%async_computation.3 | async-start | bytes 524288 | tf_op jit(solution)/shard_map/all_to_all | solution.py:375
  161.3 4.6 %pairs.1.up_ref.down_ref.own_ref = s16[4,2528,128]{2,1,0:T(8,128)(2,1)S(1)} custom-call(s16[4,2528,128]{2,1,0:T(8,128)(2,1)} %get-tuple-element.14.keep_ref, s16[4,2528,128]{2,1,0:T(8,128)(2,1)} %copy-done.2), custom_call_target="tpu_custom_call" | custom-call | tf_op jit(solution)/shard_map/pairs/pallas_call | solution.py:376
  173.5 7.7 %all-to-all-start.4 = ((f32[32,16,128]{2,1,0:T(8,128)}), f32[32,16,128]{2,1,0:T(8,128)}, u32[]{:S(2)}, u32[]{:S(2)}) async-start(f32[32,16,128]{2,1,0:T(8,128)} %broadcast_in_dim.21), calls=%async_computation.4 | async-start | bytes 524288 | tf_op jit(solution)/shard_map/all_to_all | solution.py:393
  181.2 2.7 %relay.1 = (s16[2528,128]{1,0:T(8,128)(2,1)}, s16[2528,128]{1,0:T(8,128)(2,1)}) custom-call(s16[4,2528,128]{2,1,0:T(8,128)(2,1)S(1)} %pairs.1.up_ref.down_ref.own_ref, s16[4,2528,128]{2,1,0:T(8,128)(2,1)S(1)} %pairs.1.up_ref.down_ref.own_ref, s16[1312,128]{1,0:T(8,128)(2,1)} %collective-permute-done.32.above_ref, ...), custom_call_target="tpu_custom_call" | custom-call | flops 40000000 | bytes 40000000 | tf_op jit(solution)/shard_map/relay/pallas_call | solution.py:209
  183.9 2.6 %collective-permute-start.35 = (s16[2528,128]{1,0:T(8,128)(2,1)}, s16[2528,128]{1,0:T(8,128)(2,1)}, u32[]{:S(2)}, u32[]{:S(2)}) collective-permute-start(s16[2528,128]{1,0:T(8,128)(2,1)} %get-tuple-element.17), channel_id=1, source_target_pairs={{0,192},{64,0},{128,64},{192,128},{1,193},{65,1},{129,65},{193,129... | collective-permute-start | bytes 1941512 | tf_op jit(solution)/shard_map/ppermute | solution.py:31
  186.6 5.0 %all-to-all-done.4.back_ref = f32[32,16,128]{2,1,0:T(8,128)} async-done(((f32[32,16,128]{2,1,0:T(8,128)}), f32[32,16,128]{2,1,0:T(8,128)}, u32[]{:S(2)}, u32[]{:S(2)}) %all-to-all-start.4) | async-done | bytes 262176 | tf_op jit(solution)/shard_map/all_to_all | solution.py:393
  193.7 6.7 %all-to-all-start.5 = ((f32[8,48,128]{2,1,0:T(8,128)}), f32[8,48,128]{2,1,0:T(8,128)S(1)}, u32[]{:S(2)}, u32[]{:S(2)}) async-start(f32[8,48,128]{2,1,0:T(8,128)} %copy-done.1), calls=%async_computation.5 | async-start | bytes 393216 | tf_op jit(solution)/shard_map/all_to_all | solution.py:397
  201.2 5.2 %all-to-all-done.5 = f32[8,48,128]{2,1,0:T(8,128)S(1)} async-done(((f32[8,48,128]{2,1,0:T(8,128)}), f32[8,48,128]{2,1,0:T(8,128)S(1)}, u32[]{:S(2)}, u32[]{:S(2)}) %all-to-all-start.5) | async-done | bytes 196640 | tf_op jit(solution)/shard_map/all_to_all | solution.py:397
  206.9 3.5 %slots.1 = (f32[18,128,128]{2,1,0:T(8,128)}, f32[128,192]{1,0:T(8,128)S(1)}) custom-call(s32[1]{0:T(128)} %bitcast.44.count_ref, s16[4,2528,128]{2,1,0:T(8,128)(2,1)S(1)} %pairs.1.up_ref.down_ref.own_ref, s16[2528,128]{1,0:T(8,128)(2,1)} %collective-permute-done.34.refs_0_, s16[2528,128]{1,0:T(8,128)(2,1)} %collective-permute-done.35.refs_1_), custom_call_target="tpu_custom_call" | custom-call | flops 10000000 | bytes 16000000 | tf_op jit(solution)/shard_map/slots/pallas_call | solution.py:400
  (103 shorter events, 35.2 us)
Async XLA Ops:
  5.8 14.2 %collective-permute-start.15 = (bf16[1,96,16,128]{3,2,1,0:T(8,128)(2,1)S(1)}, bf16[1,96,16,128]{3,2,1,0:T(8,128)(2,1)}, u32[]{:S(2)}, u32[]{:S(2)}) collective-permute-start(bf16[1,96,16,128]{3,2,1,0:T(8,128)(2,1)S(1)} %get-tuple-element.34.rest_0_), channel_id=1, source_target_pairs={{0,1},{1,2},{2,3},{3,0},{4,5},{5,6},{6,7},{7,4},{8,9},{9,10},{10,1... | collective-permute-start | bytes 1179656 | tf_op jit(solution)/shard_map/ppermute | solution.py:31
  5.8 14.2 %collective-permute-start.2 = (bf16[1,96,16,128]{3,2,1,0:T(8,128)(2,1)S(1)}, bf16[1,96,16,128]{3,2,1,0:T(8,128)(2,1)S(1)}, u32[]{:S(2)}, u32[]{:S(2)}) collective-permute-start(bf16[1,96,16,128]{3,2,1,0:T(8,128)(2,1)S(1)} %get-tuple-element.34.rest_0_), channel_id=1, source_target_pairs={{0,28},{4,0},{8,4},{12,8},{16,12},{20,16},{24,20},{28,24},{1,29},{... | collective-permute-start | bytes 1179656 | tf_op jit(solution)/shard_map/ppermute | solution.py:31
  13.6 20.2 %collective-permute-start.20 = (bf16[1,96,16,128]{3,2,1,0:T(8,128)(2,1)S(1)}, bf16[1,96,16,128]{3,2,1,0:T(8,128)(2,1)S(1)}, u32[]{:S(2)}, u32[]{:S(2)}) collective-permute-start(bf16[1,96,16,128]{3,2,1,0:T(8,128)(2,1)S(1)} %collective-permute-done.16.rest_17_), channel_id=1, source_target_pairs={{0,28},{4,0},{8,4},{12,8},{16,12},{20,16},{24,20},{28,24},{1,29},{... | collective-permute-start | bytes 1179656 | tf_op jit(solution)/shard_map/ppermute | solution.py:31
  19.9 24.6 %collective-permute-start.17 = (bf16[1,96,16,128]{3,2,1,0:T(8,128)(2,1)}, bf16[1,96,16,128]{3,2,1,0:T(8,128)(2,1)}, u32[]{:S(2)}, u32[]{:S(2)}) collective-permute-start(bf16[1,96,16,128]{3,2,1,0:T(8,128)(2,1)} %collective-permute-done.15.rest_16_), channel_id=1, source_target_pairs={{0,4},{4,8},{8,12},{12,16},{16,20},{20,24},{24,28},{28,0},{1,5},{5... | collective-permute-start | bytes 1179656 | tf_op jit(solution)/shard_map/ppermute | solution.py:31
  20.0 27.2 %collective-permute-start.19 = (bf16[1,96,16,128]{3,2,1,0:T(8,128)(2,1)S(1)}, bf16[1,96,16,128]{3,2,1,0:T(8,128)(2,1)}, u32[]{:S(2)}, u32[]{:S(2)}) collective-permute-start(bf16[1,96,16,128]{3,2,1,0:T(8,128)(2,1)S(1)} %collective-permute-done.2.rest_3_), channel_id=1, source_target_pairs={{0,1},{1,2},{2,3},{3,0},{4,5},{5,6},{6,7},{7,4},{8,9},{9,10},{10,1... | collective-permute-start | bytes 1179656 | tf_op jit(solution)/shard_map/ppermute | solution.py:31
  22.1 25.1 %collective-permute-start.4 = (bf16[1,96,16,128]{3,2,1,0:T(8,128)(2,1)S(1)}, bf16[1,96,16,128]{3,2,1,0:T(8,128)(2,1)S(1)}, u32[]{:S(2)}, u32[]{:S(2)}) collective-permute-start(bf16[1,96,16,128]{3,2,1,0:T(8,128)(2,1)S(1)} %collective-permute-done.2.rest_3_), channel_id=1, source_target_pairs={{0,28},{4,0},{8,4},{12,8},{16,12},{20,16},{24,20},{28,24},{1,29},{... | collective-permute-start | bytes 1179656 | tf_op jit(solution)/shard_map/ppermute | solution.py:31
  24.2 25.5 %collective-permute-start.18 = (bf16[1,96,16,128]{3,2,1,0:T(8,128)(2,1)S(1)}, bf16[1,96,16,128]{3,2,1,0:T(8,128)(2,1)}, u32[]{:S(2)}, u32[]{:S(2)}) collective-permute-start(bf16[1,96,16,128]{3,2,1,0:T(8,128)(2,1)S(1)} %collective-permute-done.1.rest_2_), channel_id=1, source_target_pairs={{0,3},{1,0},{2,1},{3,2},{4,7},{5,4},{6,5},{7,6},{8,11},{9,8},{10,9... | collective-permute-start | bytes 1179656 | tf_op jit(solution)/shard_map/ppermute | solution.py:31
  34.5 15.2 %collective-permute-start.3 = (bf16[1,96,16,128]{3,2,1,0:T(8,128)(2,1)S(1)}, bf16[1,96,16,128]{3,2,1,0:T(8,128)(2,1)}, u32[]{:S(2)}, u32[]{:S(2)}) collective-permute-start(bf16[1,96,16,128]{3,2,1,0:T(8,128)(2,1)S(1)} %collective-permute-done.1.rest_2_), channel_id=1, source_target_pairs={{0,4},{4,8},{8,12},{12,16},{16,20},{20,24},{24,28},{28,0},{1,5},{5... | collective-permute-start | bytes 1179656 | tf_op jit(solution)/shard_map/ppermute | solution.py:31
  34.5 35.7 %all-to-all-start = ((bf16[32,3,16,128]{3,2,1,0:T(8,128)(2,1)}), bf16[32,3,16,128]{3,2,1,0:T(8,128)(2,1)S(1)}, u32[]{:S(2)}, u32[]{:S(2)}) async-start(bf16[32,3,16,128]{3,2,1,0:T(8,128)(2,1)} %bitcast.72), calls=%async_computation | async-start | bytes 786432 | tf_op jit(solution)/shard_map/all_to_all | solution.py:290
  44.6 15.9 %collective-permute-start.8 = (bf16[1,96,16,128]{3,2,1,0:T(8,128)(2,1)S(1)}, bf16[1,96,16,128]{3,2,1,0:T(8,128)(2,1)}, u32[]{:S(2)}, u32[]{:S(2)}) collective-permute-start(bf16[1,96,16,128]{3,2,1,0:T(8,128)(2,1)S(1)} %collective-permute-done.rest_1_), channel_id=1, source_target_pairs={{0,28},{4,0},{8,4},{12,8},{16,12},{20,16},{24,20},{28,24},{1,29},{... | collective-permute-start | bytes 1179656 | tf_op jit(solution)/shard_map/ppermute | solution.py:31
  47.2 15.7 %collective-permute-start.7 = (bf16[1,96,16,128]{3,2,1,0:T(8,128)(2,1)S(1)}, bf16[1,96,16,128]{3,2,1,0:T(8,128)(2,1)}, u32[]{:S(2)}, u32[]{:S(2)}) collective-permute-start(bf16[1,96,16,128]{3,2,1,0:T(8,128)(2,1)S(1)} %collective-permute-done.rest_1_), channel_id=1, source_target_pairs={{0,4},{4,8},{8,12},{12,16},{16,20},{20,24},{24,28},{28,0},{1,5},{5... | collective-permute-start | bytes 1179656 | tf_op jit(solution)/shard_map/ppermute | solution.py:31
  47.2 16.1 %collective-permute-start.24 = (bf16[1,96,16,128]{3,2,1,0:T(8,128)(2,1)S(1)}, bf16[1,96,16,128]{3,2,1,0:T(8,128)(2,1)S(1)}, u32[]{:S(2)}, u32[]{:S(2)}) collective-permute-start(bf16[1,96,16,128]{3,2,1,0:T(8,128)(2,1)S(1)} %collective-permute-done.4.rest_5_), channel_id=1, source_target_pairs={{0,3},{1,0},{2,1},{3,2},{4,7},{5,4},{6,5},{7,6},{8,11},{9,8},{10,9... | collective-permute-start | bytes 1179656 | tf_op jit(solution)/shard_map/ppermute | solution.py:31
  49.7 14.4 %collective-permute-start.23 = (bf16[1,96,16,128]{3,2,1,0:T(8,128)(2,1)S(1)}, bf16[1,96,16,128]{3,2,1,0:T(8,128)(2,1)S(1)}, u32[]{:S(2)}, u32[]{:S(2)}) collective-permute-start(bf16[1,96,16,128]{3,2,1,0:T(8,128)(2,1)S(1)} %collective-permute-done.4.rest_5_), channel_id=1, source_target_pairs={{0,1},{1,2},{2,3},{3,0},{4,5},{5,6},{6,7},{7,4},{8,9},{9,10},{10,1... | collective-permute-start | bytes 1179656 | tf_op jit(solution)/shard_map/ppermute | solution.py:31
  49.7 19.3 %collective-permute-start.6 = (bf16[1,96,16,128]{3,2,1,0:T(8,128)(2,1)S(1)}, bf16[1,96,16,128]{3,2,1,0:T(8,128)(2,1)}, u32[]{:S(2)}, u32[]{:S(2)}) collective-permute-start(bf16[1,96,16,128]{3,2,1,0:T(8,128)(2,1)S(1)} %collective-permute-done.4.rest_5_), channel_id=1, source_target_pairs={{0,28},{4,0},{8,4},{12,8},{16,12},{20,16},{24,20},{28,24},{1,29},{... | collective-permute-start | bytes 1179656 | tf_op jit(solution)/shard_map/ppermute | solution.py:31
  60.5 19.7 %collective-permute-start.22 = (bf16[1,96,16,128]{3,2,1,0:T(8,128)(2,1)}, bf16[1,96,16,128]{3,2,1,0:T(8,128)(2,1)}, u32[]{:S(2)}, u32[]{:S(2)}) collective-permute-start(bf16[1,96,16,128]{3,2,1,0:T(8,128)(2,1)} %collective-permute-done.3.rest_4_), channel_id=1, source_target_pairs={{0,3},{1,0},{2,1},{3,2},{4,7},{5,4},{6,5},{7,6},{8,11},{9,8},{10,9... | collective-permute-start | bytes 1179656 | tf_op jit(solution)/shard_map/ppermute | solution.py:31
  62.9 19.9 %collective-permute-start.21 = (bf16[1,96,16,128]{3,2,1,0:T(8,128)(2,1)}, bf16[1,96,16,128]{3,2,1,0:T(8,128)(2,1)}, u32[]{:S(2)}, u32[]{:S(2)}) collective-permute-start(bf16[1,96,16,128]{3,2,1,0:T(8,128)(2,1)} %collective-permute-done.3.rest_4_), channel_id=1, source_target_pairs={{0,1},{1,2},{2,3},{3,0},{4,5},{5,6},{6,7},{7,4},{8,9},{9,10},{10,1... | collective-permute-start | bytes 1179656 | tf_op jit(solution)/shard_map/ppermute | solution.py:31
  63.3 19.5 %collective-permute-start.5 = (bf16[1,96,16,128]{3,2,1,0:T(8,128)(2,1)}, bf16[1,96,16,128]{3,2,1,0:T(8,128)(2,1)}, u32[]{:S(2)}, u32[]{:S(2)}) collective-permute-start(bf16[1,96,16,128]{3,2,1,0:T(8,128)(2,1)} %collective-permute-done.3.rest_4_), channel_id=1, source_target_pairs={{0,4},{4,8},{8,12},{12,16},{16,20},{20,24},{24,28},{28,0},{1,5},{5... | collective-permute-start | bytes 1179656 | tf_op jit(solution)/shard_map/ppermute | solution.py:31
  64.1 19.9 %collective-permute-start.10 = (bf16[1,96,16,128]{3,2,1,0:T(8,128)(2,1)}, bf16[1,96,16,128]{3,2,1,0:T(8,128)(2,1)}, u32[]{:S(2)}, u32[]{:S(2)}) collective-permute-start(bf16[1,96,16,128]{3,2,1,0:T(8,128)(2,1)} %collective-permute-done.8.rest_9_), channel_id=1, source_target_pairs={{0,28},{4,0},{8,4},{12,8},{16,12},{20,16},{24,20},{28,24},{1,29},{... | collective-permute-start | bytes 1179656 | tf_op jit(solution)/shard_map/ppermute | solution.py:31
  69.0 17.6 %collective-permute-start.9 = (bf16[1,96,16,128]{3,2,1,0:T(8,128)(2,1)}, bf16[1,96,16,128]{3,2,1,0:T(8,128)(2,1)}, u32[]{:S(2)}, u32[]{:S(2)}) collective-permute-start(bf16[1,96,16,128]{3,2,1,0:T(8,128)(2,1)} %collective-permute-done.7.rest_8_), channel_id=1, source_target_pairs={{0,4},{4,8},{8,12},{12,16},{16,20},{20,24},{24,28},{28,0},{1,5},{5... | collective-permute-start | bytes 1179656 | tf_op jit(solution)/shard_map/ppermute | solution.py:31
  72.3 19.9 %all-to-all-start.1 = ((f32[32,16,128]{2,1,0:T(8,128)}), f32[32,16,128]{2,1,0:T(8,128)S(1)}, u32[]{:S(2)}, u32[]{:S(2)}) async-start(f32[32,16,128]{2,1,0:T(8,128)} %convolution_bitcast_fusion), calls=%async_computation.1 | async-start | bytes 524288 | tf_op jit(solution)/shard_map/all_to_all | solution.py:295
  80.3 16.6 %collective-permute-start.28 = (bf16[1,96,16,128]{3,2,1,0:T(8,128)(2,1)}, bf16[1,96,16,128]{3,2,1,0:T(8,128)(2,1)}, u32[]{:S(2)}, u32[]{:S(2)}) collective-permute-start(bf16[1,96,16,128]{3,2,1,0:T(8,128)(2,1)} %collective-permute-done.6.rest_7_), channel_id=1, source_target_pairs={{0,3},{1,0},{2,1},{3,2},{4,7},{5,4},{6,5},{7,6},{8,11},{9,8},{10,9... | collective-permute-start | bytes 1179656 | tf_op jit(solution)/shard_map/ppermute | solution.py:31
  82.8 15.3 %collective-permute-start.27 = (bf16[1,96,16,128]{3,2,1,0:T(8,128)(2,1)}, bf16[1,96,16,128]{3,2,1,0:T(8,128)(2,1)}, u32[]{:S(2)}, u32[]{:S(2)}) collective-permute-start(bf16[1,96,16,128]{3,2,1,0:T(8,128)(2,1)} %collective-permute-done.6.rest_7_), channel_id=1, source_target_pairs={{0,1},{1,2},{2,3},{3,0},{4,5},{5,6},{6,7},{7,4},{8,9},{9,10},{10,1... | collective-permute-start | bytes 1179656 | tf_op jit(solution)/shard_map/ppermute | solution.py:31
  82.8 16.5 %collective-permute-start.13 = (bf16[1,96,16,128]{3,2,1,0:T(8,128)(2,1)}, bf16[1,96,16,128]{3,2,1,0:T(8,128)(2,1)}, u32[]{:S(2)}, u32[]{:S(2)}) collective-permute-start(bf16[1,96,16,128]{3,2,1,0:T(8,128)(2,1)} %collective-permute-done.5.rest_6_), channel_id=1, source_target_pairs={{0,4},{4,8},{8,12},{12,16},{16,20},{20,24},{24,28},{28,0},{1,5},{5... | collective-permute-start | bytes 1179656 | tf_op jit(solution)/shard_map/ppermute | solution.py:31
  84.1 16.7 %collective-permute-start.26 = (bf16[1,96,16,128]{3,2,1,0:T(8,128)(2,1)}, bf16[1,96,16,128]{3,2,1,0:T(8,128)(2,1)}, u32[]{:S(2)}, u32[]{:S(2)}) collective-permute-start(bf16[1,96,16,128]{3,2,1,0:T(8,128)(2,1)} %collective-permute-done.5.rest_6_), channel_id=1, source_target_pairs={{0,3},{1,0},{2,1},{3,2},{4,7},{5,4},{6,5},{7,6},{8,11},{9,8},{10,9... | collective-permute-start | bytes 1179656 | tf_op jit(solution)/shard_map/ppermute | solution.py:31
  86.7 14.1 %collective-permute-start.12 = (bf16[1,96,16,128]{3,2,1,0:T(8,128)(2,1)}, bf16[1,96,16,128]{3,2,1,0:T(8,128)(2,1)}, u32[]{:S(2)}, u32[]{:S(2)}) collective-permute-start(bf16[1,96,16,128]{3,2,1,0:T(8,128)(2,1)} %collective-permute-done.10.rest_11_), channel_id=1, source_target_pairs={{0,28},{4,0},{8,4},{12,8},{16,12},{20,16},{24,20},{28,24},{1,29},{... | collective-permute-start | bytes 1179656 | tf_op jit(solution)/shard_map/ppermute | solution.py:31
  92.9 14.6 %all-to-all-start.2 = ((f32[32,16,128]{2,1,0:T(8,128)}), f32[32,16,128]{2,1,0:T(8,128)S(1)}, u32[]{:S(2)}, u32[]{:S(2)}) async-start(f32[32,16,128]{2,1,0:T(8,128)} %broadcast_in_dim.17), calls=%async_computation.2 | async-start | bytes 524288 | tf_op jit(solution)/shard_map/all_to_all | solution.py:296
  140.2 19.6 %collective-permute-start.31 = (s16[4,2528,128]{2,1,0:T(8,128)(2,1)}, s16[4,2528,128]{2,1,0:T(8,128)(2,1)S(1)}, u32[]{:S(2)}, u32[]{:S(2)}) collective-permute-start(s16[4,2528,128]{2,1,0:T(8,128)(2,1)} %get-tuple-element.15), channel_id=1, source_target_pairs={{0,32},{32,0},{1,33},{33,1},{2,34},{34,2},{3,35},{35,3},{4,36},{36... | collective-permute-start | bytes 7766024 | tf_op jit(solution)/shard_map/ppermute | solution.py:31
  151.6 20.2 %all-to-all-start.3 = ((f32[32,16,128]{2,1,0:T(8,128)}), f32[32,16,128]{2,1,0:T(8,128)}, u32[]{:S(2)}, u32[]{:S(2)}) async-start(f32[32,16,128]{2,1,0:T(8,128)} %bitcast.48), calls=%async_computation.3 | async-start | bytes 524288 | tf_op jit(solution)/shard_map/all_to_all | solution.py:375
  166.7 14.5 %collective-permute-start.32 = (s16[1312,128]{1,0:T(8,128)(2,1)}, s16[1312,128]{1,0:T(8,128)(2,1)}, u32[]{:S(2)}, u32[]{:S(2)}) collective-permute-start(s16[1312,128]{1,0:T(8,128)(2,1)} %pad_add_fusion), channel_id=1, source_target_pairs={{0,64},{64,128},{128,192},{192,0},{1,65},{65,129},{129,193},{193,1... | collective-permute-start | bytes 1007624 | tf_op jit(solution)/shard_map/ppermute | solution.py:31
  173.5 18.1 %all-to-all-start.4 = ((f32[32,16,128]{2,1,0:T(8,128)}), f32[32,16,128]{2,1,0:T(8,128)}, u32[]{:S(2)}, u32[]{:S(2)}) async-start(f32[32,16,128]{2,1,0:T(8,128)} %broadcast_in_dim.21), calls=%async_computation.4 | async-start | bytes 524288 | tf_op jit(solution)/shard_map/all_to_all | solution.py:393
  183.9 23.0 %collective-permute-start.34 = (s16[2528,128]{1,0:T(8,128)(2,1)}, s16[2528,128]{1,0:T(8,128)(2,1)}, u32[]{:S(2)}, u32[]{:S(2)}) collective-permute-start(s16[2528,128]{1,0:T(8,128)(2,1)} %get-tuple-element.16), channel_id=1, source_target_pairs={{0,64},{64,128},{128,192},{192,0},{1,65},{65,129},{129,193},{193,1... | collective-permute-start | bytes 1941512 | tf_op jit(solution)/shard_map/ppermute | solution.py:31
  183.9 23.0 %collective-permute-start.35 = (s16[2528,128]{1,0:T(8,128)(2,1)}, s16[2528,128]{1,0:T(8,128)(2,1)}, u32[]{:S(2)}, u32[]{:S(2)}) collective-permute-start(s16[2528,128]{1,0:T(8,128)(2,1)} %get-tuple-element.17), channel_id=1, source_target_pairs={{0,192},{64,0},{128,64},{192,128},{1,193},{65,1},{129,65},{193,129... | collective-permute-start | bytes 1941512 | tf_op jit(solution)/shard_map/ppermute | solution.py:31
  (20 other events, 318.0 us)

commit v6 on v5

--- a/solution.py
+++ b/solution.py
@@ -233,7 +233,7 @@
             slots_ref[index] = jnp.where(index < count, total.T, 0.0)
         else:
             h = index - CAP
-            outer_ref[:, h * 64 : (h + 1) * 64] = total.T
+            outer_ref[h * 64 : (h + 1) * 64] = total
 
 
 def in_kernel(cols_ref, back_ref, out_ref):
@@ -260,25 +260,39 @@
     )(cols, back_all)
 
 
-def gather_tokens(own):
+def gather_tokens(own, x):
     z_up, z_down = shift("z", NZ, 1), shift("z", NZ, -1)
     x_up, x_down = shift("x", NX, 1), shift("x", NX, -1)
-    across = shift("x", NX, 2)
+    arrays, keys = [], []
+
+    def around(a):
+        copies = jnp.broadcast_to(held[a, 0], (NX,) + own.shape)
+        row = lax.all_to_all(copies, "x", 0, 0)
+        arrays.append(row)
+        keys.append([(a, g - x) for g in range(NX)])
+        return row
+
     held = {(0, 0): own[None]}
-    held[0, 2] = across(own[None])
-    for b in (0, 2):
-        for a in (1, 2, 3):
+    row = around(0)
+    for b in (-1, 1, 2):
+        held[0, b] = lax.dynamic_slice_in_dim(row, lax.rem(x + b + NX, NX), 1, 0)
+    for a in (1, 2, 3):
+        for b in (0, 2):
             held[-a, b] = z_up(held[1 - a, b])
             held[a, b] = z_down(held[a - 1, b])
     held[4, 0] = z_up(held[-3, 0])
-    held[4, 2] = z_down(held[3, 2])
-    for a in (0, -1, 1, -2, 2, -3, 3, 4):
+    for a in (-1, 1, -2, 2, -3, 3):
         for b, move in ((-1, x_up), (1, x_down)):
-            if (a, b) in ((1, 1), (-1, -1)):
+            if a == b:
                 held[a, b] = (z_down if a > 0 else z_up)(held[0, b])
             else:
                 held[a, b] = move(held[a, 0])
-    return list(held.values()), [[key] for key in held]
+    around(4)
+    for (a, b), value in held.items():
+        if a not in (0, 4):
+            arrays.append(value)
+            keys.append([(a, b)])
+    return arrays, keys
 
 
 def per_device(tokens, block_weights, block_rows, block_owners, factor_in, factor_out, upstream):
@@ -286,7 +300,8 @@
     span = NX * NZ
     per = RB // span
     plane = ("z", "x")
-    arrays, keys = gather_tokens(own)
+    z, x = lax.axis_index("z"), lax.axis_index("x")
+    arrays, keys = gather_tokens(own, x)
     spread = lax.all_to_all(own.reshape(span, per, ROWS, BS), plane, 0, 0)
     factor = factor_in.reshape(per, BS, BS)
     partial = jnp.einsum(
@@ -294,9 +309,8 @@
     )
     low_own = jnp.sum(lax.all_to_all(partial, plane, 0, 0), axis=0)
     low = lax.all_to_all(jnp.broadcast_to(low_own[None], (span, ROWS, BS)), plane, 0, 0)
-    z, x = lax.axis_index("z"), lax.axis_index("x")
     y, core = lax.axis_index("y"), lax.axis_index("core")
-    place = [((z + a) % NZ) * NX + (x + b) % NX for group in keys for a, b in group]
+    place = [((z + a) % NZ) * NX + (x + b + NX) % NX for group in keys for a, b in group]
     place = jnp.stack(place).astype(jnp.int32)
     low = low.reshape(span * ROWS, BS)
 
@@ -403,7 +417,7 @@
         out_specs=[whole, whole],
         out_shape=[
             jax.ShapeDtypeStruct((CAP, BS, BS), jnp.float32),
-            jax.ShapeDtypeStruct((BS, FO_ROWS), jnp.float32),
+            jax.ShapeDtypeStruct((FO_ROWS, BS), jnp.float32),
         ],
         compiler_params=pltpu.CompilerParams(vmem_limit_bytes=50 * 1024 * 1024),
         cost_estimate=pl.CostEstimate(
@@ -411,7 +425,7 @@
         ),
         name="slots",
     )(mine, paired, *parts)
-    return hidden, slots, in_grad, out_grad
+    return hidden, slots, in_grad, out_grad.T
 
 
 def solution(mesh):

time: 212 us -> 244 us (1.15)
  blocking collectives: 0 us -> 40.7 us
  starting transfers between devices: 118 us -> 83.4 us
  waiting for transfers between devices: 35.8 us -> 59.4 us
  local copies, waits for them, and re-layouts: 9.01 us -> 12.8 us
    all_to_all x0 -> x2, blocking collectives: none -> 40.7 us  [the longest x1 25.5 us: per_device(): spread = lax.all_to_all(own.reshape(span, per, ROWS, BS), plane, 0, 0)]
    ppermute x36 -> x30, starting transfers between devices: 73.7 us -> 44.1 us  [shift(): return lambda value: lax.ppermute(value, axis, pairs)]
    ppermute x36 -> x30, waiting for transfers between devices: 20.8 us -> 47.7 us  [shift(): return lambda value: lax.ppermute(value, axis, pairs)]
    all_to_all x2, starting transfers between devices: 18 us -> 8.76 us  [around(): row = lax.all_to_all(copies, 'x', 0, 0)]
    broadcast_in_dim x0 -> x2, local copies, waits for them, and re-layouts: none -> 3.7 us  [around(): copies = jnp.broadcast_to(held[a, 0], (NX,) + own.shape)]
    all_to_all x2, waiting for transfers between devices: 3.26 us -> 0.01 us  [around(): row = lax.all_to_all(copies, 'x', 0, 0)]
    all_to_all x1, starting transfers between devices: 3.87 us -> 6.61 us  [per_device(): lax.all_to_all(jnp.broadcast_to(low_own[None], (span, ROWS, BS)), plane,...]
    unnamed x23 -> x14, local copies, waits for them, and re-layouts: 5.58 us -> 4.11 us
  transfers between devices with their start and end apart: 42 -> 36, of which waited for: 13 -> 12; matrix products, arithmetic and copies ran while one was open for 4% -> 4% of each run, Pallas kernels for 4% -> 4%
where the time goes in v6:
time: 244 us; the launch traced here: 243 us
  starting transfers between devices  83.4 us (34%)
  waiting for transfers between devices  59.4 us (24%)
  Pallas kernels  41.2 us (17%)
  blocking collectives  40.7 us (17%)
  local copies, waits for them, and re-layouts  12.8 us (5%)
  other arithmetic  3.38 us (1%)
    ppermute x30, waiting for transfers between devices, shift(): return lambda value: lax.ppermute(value, axis, pairs)  47.7 us
    ppermute x30, starting transfers between devices, shift(): return lambda value: lax.ppermute(value, axis, pairs)  44.1 us
    pallas_call x1, Pallas kernels, per_device(): pl.pallas_call(functools.partial(main_kernel, [len(g) for g in keys]), gr...  29.1 us
    all_to_all x1, blocking collectives, per_device(): spread = lax.all_to_all(own.reshape(span, per, ROWS, BS), plane, 0, 0)  25.5 us
    all_to_all x1, blocking collectives, per_device(): low_own = jnp.sum(lax.all_to_all(partial, plane, 0, 0), axis=0)  15.2 us
    all_to_all x1, starting transfers between devices, per_device(): back = lax.all_to_all(back.reshape(span, ROWS, BS), plane, 0, 0)  9.45 us
    all_to_all x2, starting transfers between devices, around(): row = lax.all_to_all(copies, 'x', 0, 0)  8.76 us
    all_to_all x1, starting transfers between devices, per_device(): lax.all_to_all(jnp.broadcast_to(back_own[None], (span, ROWS, BS)), plane,...  7.73 us
  transfers between devices with their start and end apart: 36, of which 12 were waited for; matrix products, arithmetic and copies ran while one was open for 4% of the time, Pallas kernels for 4%

profile of v6, /device:TPU:1, one launch (start us, length us, event | category | flops | bytes accessed | tf_op | source)
XLA Modules:
  0.0 243.2 jit_solution(5761824350358932296)
XLA Ops:
  1.8 25.5 %all_to_all.40.cols_ref = bf16[32,3,16,128]{3,2,1,0:T(8,128)(2,1)S(1)} all-to-all(bf16[32,3,16,128]{3,2,1,0:T(8,128)(2,1)S(1)} %bitcast.77), channel_id=1, replica_groups=mesh['y'=4,'core'=2,'z'=8,'x'=4] {'z','x'}, dimensions={0} | all-to-all | bytes 786432 | tf_op jit(solution)/shard_map/all_to_all | solution.py:305
  28.6 15.2 %all_to_all.41 = f32[32,16,128]{2,1,0:T(8,128)S(1)} all-to-all(f32[32,16,128]{2,1,0:T(8,128)S(1)} %convolution_bitcast_fusion), channel_id=1, replica_groups=mesh['y'=4,'core'=2,'z'=8,'x'=4] {'z','x'}, dimensions={0} | all-to-all | bytes 524288 | tf_op jit(solution)/shard_map/all_to_all | solution.py:310
  45.2 4.3 %all-to-all-start.3 = ((bf16[4,96,16,128]{3,2,1,0:T(8,128)(2,1)}), bf16[4,96,16,128]{3,2,1,0:T(8,128)(2,1)}, u32[]{:S(2)}, u32[]{:S(2)}) async-start(bf16[4,96,16,128]{3,2,1,0:T(8,128)(2,1)} %broadcast_in_dim.25), calls=%async_computation.3 | async-start | bytes 3145728 | tf_op jit(solution)/shard_map/all_to_all | solution.py:270
  50.4 1.9 collective-permute-start.4
  52.3 5.2 %collective-permute-done.rest_2_ = bf16[1,96,16,128]{3,2,1,0:T(8,128)(2,1)S(1)} collective-permute-done((bf16[1,96,16,128]{3,2,1,0:T(8,128)(2,1)S(1)}, bf16[1,96,16,128]{3,2,1,0:T(8,128)(2,1)S(1)}, u32[]{:S(2)}, u32[]{:S(2)}) %collective-permute-start) | collective-permute-done | bytes 393248 | tf_op jit(solution)/shard_map/ppermute | solution.py:31
  57.7 2.9 %collective-permute-start.7 = (bf16[1,96,16,128]{3,2,1,0:T(8,128)(2,1)S(1)}, bf16[1,96,16,128]{3,2,1,0:T(8,128)(2,1)S(1)}, u32[]{:S(2)}, u32[]{:S(2)}) collective-permute-start(bf16[1,96,16,128]{3,2,1,0:T(8,128)(2,1)S(1)} %collective-permute-done.4.rest_3_), channel_id=1, source_target_pairs={{0,28},{4,0},{8,4},{12,8},{16,12},{20,16},{24,20},{28,24},{1,29},{... | collective-permute-start | bytes 1179656 | tf_op jit(solution)/shard_map/ppermute | solution.py:31
  60.5 5.6 %collective-permute-done.1.rest_6_ = bf16[1,96,16,128]{3,2,1,0:T(8,128)(2,1)S(1)} collective-permute-done((bf16[1,96,16,128]{3,2,1,0:T(8,128)(2,1)S(1)}, bf16[1,96,16,128]{3,2,1,0:T(8,128)(2,1)S(1)}, u32[]{:S(2)}, u32[]{:S(2)}) %collective-permute-start.1) | collective-permute-done | bytes 393248 | tf_op jit(solution)/shard_map/ppermute | solution.py:31
  68.5 6.6 %all-to-all-start.2 = ((f32[32,16,128]{2,1,0:T(8,128)}), f32[32,16,128]{2,1,0:T(8,128)S(1)}, u32[]{:S(2)}, u32[]{:S(2)}) async-start(f32[32,16,128]{2,1,0:T(8,128)} %broadcast_in_dim.24), calls=%async_computation.2 | async-start | bytes 524288 | tf_op jit(solution)/shard_map/all_to_all | solution.py:311
  75.2 2.5 %collective-permute-start.14 = (bf16[1,96,16,128]{3,2,1,0:T(8,128)(2,1)S(1)}, bf16[1,96,16,128]{3,2,1,0:T(8,128)(2,1)}, u32[]{:S(2)}, u32[]{:S(2)}) collective-permute-start(bf16[1,96,16,128]{3,2,1,0:T(8,128)(2,1)S(1)} %collective-permute-done.rest_2_), channel_id=1, source_target_pairs={{0,3},{1,0},{2,1},{3,2},{4,7},{5,4},{6,5},{7,6},{8,11},{9,8},{10,9... | collective-permute-start | bytes 1179656 | tf_op jit(solution)/shard_map/ppermute | solution.py:31
  81.8 2.3 constant_dynamic-slice_fusion
  84.1 2.8 %collective-permute-start.18 = (bf16[1,96,16,128]{3,2,1,0:T(8,128)(2,1)S(1)}, bf16[1,96,16,128]{3,2,1,0:T(8,128)(2,1)}, u32[]{:S(2)}, u32[]{:S(2)}) collective-permute-start(bf16[1,96,16,128]{3,2,1,0:T(8,128)(2,1)S(1)} %collective-permute-done.1.rest_6_), channel_id=1, source_target_pairs={{0,3},{1,0},{2,1},{3,2},{4,7},{5,4},{6,5},{7,6},{8,11},{9,8},{10,9... | collective-permute-start | bytes 1179656 | tf_op jit(solution)/shard_map/ppermute | solution.py:31
  86.9 3.7 %collective-permute-done.20.rest_21_ = bf16[1,96,16,128]{3,2,1,0:T(8,128)(2,1)} collective-permute-done((bf16[1,96,16,128]{3,2,1,0:T(8,128)(2,1)S(1)}, bf16[1,96,16,128]{3,2,1,0:T(8,128)(2,1)}, u32[]{:S(2)}, u32[]{:S(2)}) %collective-permute-start.20) | collective-permute-done | bytes 393248 | tf_op jit(solution)/shard_map/ppermute | solution.py:31
  91.5 2.9 %collective-permute-start.6 = (bf16[1,96,16,128]{3,2,1,0:T(8,128)(2,1)}, bf16[1,96,16,128]{3,2,1,0:T(8,128)(2,1)}, u32[]{:S(2)}, u32[]{:S(2)}) collective-permute-start(bf16[1,96,16,128]{3,2,1,0:T(8,128)(2,1)} %get-tuple-element.24), channel_id=1, source_target_pairs={{0,28},{4,0},{8,4},{12,8},{16,12},{20,16},{24,20},{28,24},{1,29},{... | collective-permute-start | bytes 1179656 | tf_op jit(solution)/shard_map/ppermute | solution.py:31
  94.4 2.4 broadcast_in_dim.46
  96.8 4.4 %all-to-all-start.4 = ((bf16[4,96,16,128]{3,2,1,0:T(8,128)(2,1)}), bf16[4,96,16,128]{3,2,1,0:T(8,128)(2,1)}, u32[]{:S(2)}, u32[]{:S(2)}) async-start(bf16[4,96,16,128]{3,2,1,0:T(8,128)(2,1)} %broadcast_in_dim.46), calls=%async_computation.4 | async-start | bytes 3145728 | tf_op jit(solution)/shard_map/all_to_all | solution.py:270
  101.2 2.7 %collective-permute-start.24 = (bf16[1,96,16,128]{3,2,1,0:T(8,128)(2,1)}, bf16[1,96,16,128]{3,2,1,0:T(8,128)(2,1)}, u32[]{:S(2)}, u32[]{:S(2)}) collective-permute-start(bf16[1,96,16,128]{3,2,1,0:T(8,128)(2,1)} %collective-permute-done.10.rest_11_), channel_id=1, source_target_pairs={{0,3},{1,0},{2,1},{3,2},{4,7},{5,4},{6,5},{7,6},{8,11},{9,8},{10,9... | collective-permute-start | bytes 1179656 | tf_op jit(solution)/shard_map/ppermute | solution.py:31
  103.9 2.7 %collective-permute-start.22 = (bf16[1,96,16,128]{3,2,1,0:T(8,128)(2,1)S(1)}, bf16[1,96,16,128]{3,2,1,0:T(8,128)(2,1)}, u32[]{:S(2)}, u32[]{:S(2)}) collective-permute-start(bf16[1,96,16,128]{3,2,1,0:T(8,128)(2,1)S(1)} %collective-permute-done.2.rest_10_), channel_id=1, source_target_pairs={{0,3},{1,0},{2,1},{3,2},{4,7},{5,4},{6,5},{7,6},{8,11},{9,8},{10,9... | collective-permute-start | bytes 1179656 | tf_op jit(solution)/shard_map/ppermute | solution.py:31
  106.6 2.7 %collective-permute-start.9 = (bf16[1,96,16,128]{3,2,1,0:T(8,128)(2,1)}, bf16[1,96,16,128]{3,2,1,0:T(8,128)(2,1)}, u32[]{:S(2)}, u32[]{:S(2)}) collective-permute-start(bf16[1,96,16,128]{3,2,1,0:T(8,128)(2,1)} %collective-permute-done.6.rest_5_), channel_id=1, source_target_pairs={{0,28},{4,0},{8,4},{12,8},{16,12},{20,16},{24,20},{28,24},{1,29},{... | collective-permute-start | bytes 1179656 | tf_op jit(solution)/shard_map/ppermute | solution.py:31
  110.0 12.8 %collective-permute-done.24.rest_25_ = bf16[1,96,16,128]{3,2,1,0:T(8,128)(2,1)} collective-permute-done((bf16[1,96,16,128]{3,2,1,0:T(8,128)(2,1)}, bf16[1,96,16,128]{3,2,1,0:T(8,128)(2,1)}, u32[]{:S(2)}, u32[]{:S(2)}) %collective-permute-start.24) | collective-permute-done | bytes 393248 | tf_op jit(solution)/shard_map/ppermute | solution.py:31
  124.7 10.7 %collective-permute-done.22.rest_23_ = bf16[1,96,16,128]{3,2,1,0:T(8,128)(2,1)} collective-permute-done((bf16[1,96,16,128]{3,2,1,0:T(8,128)(2,1)S(1)}, bf16[1,96,16,128]{3,2,1,0:T(8,128)(2,1)}, u32[]{:S(2)}, u32[]{:S(2)}) %collective-permute-start.22) | collective-permute-done | bytes 393248 | tf_op jit(solution)/shard_map/ppermute | solution.py:31
  136.9 7.6 %collective-permute-done.21.rest_22_ = bf16[1,96,16,128]{3,2,1,0:T(8,128)(2,1)S(1)} collective-permute-done((bf16[1,96,16,128]{3,2,1,0:T(8,128)(2,1)S(1)}, bf16[1,96,16,128]{3,2,1,0:T(8,128)(2,1)S(1)}, u32[]{:S(2)}, u32[]{:S(2)}) %collective-permute-start.21) | collective-permute-done | bytes 393248 | tf_op jit(solution)/shard_map/ppermute | solution.py:31
  146.9 29.1 %columns.1 = (bf16[512,1536]{1,0:T(8,128)(2,1)}, s16[4,2528,128]{2,1,0:T(8,128)(2,1)}, s16[4,2528,128]{2,1,0:T(8,128)(2,1)}, f32[512,128]{1,0:T(8,128)}) custom-call(s32[96]{0:T(128)S(1)} %reshape.177.rows_ref, s32[4,96]{1,0:T(4,128)S(1)} %pad_add_fusion.1.where_ref, s32[32]{0:T(128)S(1)} %stack.148.place_ref, f32[512,128]{1,0:T(8,128)S(1)} %bitcast.76, ...), custom_call_target="tpu_custom_call" | custom-call | tf_op jit(solution)/shard_map/columns/pallas_call | solution.py:348
  176.0 7.2 %collective-permute-start.25 = (s16[4,2528,128]{2,1,0:T(8,128)(2,1)}, s16[4,2528,128]{2,1,0:T(8,128)(2,1)S(1)}, u32[]{:S(2)}, u32[]{:S(2)}) collective-permute-start(s16[4,2528,128]{2,1,0:T(8,128)(2,1)} %get-tuple-element.15), channel_id=1, source_target_pairs={{0,32},{32,0},{1,33},{33,1},{2,34},{34,2},{3,35},{35,3},{4,36},{36... | collective-permute-start | bytes 7766024 | tf_op jit(solution)/shard_map/ppermute | solution.py:31
  183.2 9.5 %all-to-all-start.5 = ((f32[32,16,128]{2,1,0:T(8,128)}), f32[32,16,128]{2,1,0:T(8,128)}, u32[]{:S(2)}, u32[]{:S(2)}) async-start(f32[32,16,128]{2,1,0:T(8,128)} %bitcast.49), calls=%async_computation.5 | async-start | bytes 524288 | tf_op jit(solution)/shard_map/all_to_all | solution.py:389
  194.2 4.6 %pairs.1.up_ref.down_ref.own_ref = s16[4,2528,128]{2,1,0:T(8,128)(2,1)S(1)} custom-call(s16[4,2528,128]{2,1,0:T(8,128)(2,1)} %get-tuple-element.14.keep_ref, s16[4,2528,128]{2,1,0:T(8,128)(2,1)} %copy-done.2), custom_call_target="tpu_custom_call" | custom-call | tf_op jit(solution)/shard_map/pairs/pallas_call | solution.py:390
  206.3 7.7 %all-to-all-start.6 = ((f32[32,16,128]{2,1,0:T(8,128)}), f32[32,16,128]{2,1,0:T(8,128)}, u32[]{:S(2)}, u32[]{:S(2)}) async-start(f32[32,16,128]{2,1,0:T(8,128)} %broadcast_in_dim.48), calls=%async_computation.6 | async-start | bytes 524288 | tf_op jit(solution)/shard_map/all_to_all | solution.py:407
  214.0 2.7 %relay.1 = (s16[2528,128]{1,0:T(8,128)(2,1)}, s16[2528,128]{1,0:T(8,128)(2,1)}) custom-call(s16[4,2528,128]{2,1,0:T(8,128)(2,1)S(1)} %pairs.1.up_ref.down_ref.own_ref, s16[4,2528,128]{2,1,0:T(8,128)(2,1)S(1)} %pairs.1.up_ref.down_ref.own_ref, s16[1312,128]{1,0:T(8,128)(2,1)} %collective-permute-done.26.above_ref, ...), custom_call_target="tpu_custom_call" | custom-call | flops 40000000 | bytes 40000000 | tf_op jit(solution)/shard_map/relay/pallas_call | solution.py:209
  216.8 2.7 %collective-permute-start.29 = (s16[2528,128]{1,0:T(8,128)(2,1)}, s16[2528,128]{1,0:T(8,128)(2,1)}, u32[]{:S(2)}, u32[]{:S(2)}) collective-permute-start(s16[2528,128]{1,0:T(8,128)(2,1)} %get-tuple-element.17), channel_id=1, source_target_pairs={{0,192},{64,0},{128,64},{192,128},{1,193},{65,1},{129,65},{193,129... | collective-permute-start | bytes 1941512 | tf_op jit(solution)/shard_map/ppermute | solution.py:31
  219.4 5.0 %all-to-all-done.6.back_ref = f32[32,16,128]{2,1,0:T(8,128)} async-done(((f32[32,16,128]{2,1,0:T(8,128)}), f32[32,16,128]{2,1,0:T(8,128)}, u32[]{:S(2)}, u32[]{:S(2)}) %all-to-all-start.6) | async-done | bytes 262176 | tf_op jit(solution)/shard_map/all_to_all | solution.py:407
  226.5 6.7 %all-to-all-start.7 = ((f32[8,48,128]{2,1,0:T(8,128)}), f32[8,48,128]{2,1,0:T(8,128)S(1)}, u32[]{:S(2)}, u32[]{:S(2)}) async-start(f32[8,48,128]{2,1,0:T(8,128)} %copy-done.1), calls=%async_computation.7 | async-start | bytes 393216 | tf_op jit(solution)/shard_map/all_to_all | solution.py:411
  234.0 5.2 %all-to-all-done.7 = f32[8,48,128]{2,1,0:T(8,128)S(1)} async-done(((f32[8,48,128]{2,1,0:T(8,128)}), f32[8,48,128]{2,1,0:T(8,128)S(1)}, u32[]{:S(2)}, u32[]{:S(2)}) %all-to-all-start.7) | async-done | bytes 196640 | tf_op jit(solution)/shard_map/all_to_all | solution.py:411
  239.8 3.4 %slots.1 = (f32[18,128,128]{2,1,0:T(8,128)}, f32[192,128]{1,0:T(8,128)}) custom-call(s32[1]{0:T(128)} %bitcast.45.count_ref, s16[4,2528,128]{2,1,0:T(8,128)(2,1)S(1)} %pairs.1.up_ref.down_ref.own_ref, s16[2528,128]{1,0:T(8,128)(2,1)} %collective-permute-done.28.refs_0_, s16[2528,128]{1,0:T(8,128)(2,1)} %collective-permute-done.29.refs_1_), custom_call_target="tpu_custom_call" | custom-call | flops 10000000 | bytes 16000000 | tf_op jit(solution)/shard_map/slots/pallas_call | solution.py:414
  (87 shorter events, 31.4 us)
Async XLA Ops:
  45.2 22.6 %all-to-all-start.3 = ((bf16[4,96,16,128]{3,2,1,0:T(8,128)(2,1)}), bf16[4,96,16,128]{3,2,1,0:T(8,128)(2,1)}, u32[]{:S(2)}, u32[]{:S(2)}) async-start(bf16[4,96,16,128]{3,2,1,0:T(8,128)(2,1)} %broadcast_in_dim.25), calls=%async_computation.3 | async-start | bytes 3145728 | tf_op jit(solution)/shard_map/all_to_all | solution.py:270
  57.7 20.0 %collective-permute-start.7 = (bf16[1,96,16,128]{3,2,1,0:T(8,128)(2,1)S(1)}, bf16[1,96,16,128]{3,2,1,0:T(8,128)(2,1)S(1)}, u32[]{:S(2)}, u32[]{:S(2)}) collective-permute-start(bf16[1,96,16,128]{3,2,1,0:T(8,128)(2,1)S(1)} %collective-permute-done.4.rest_3_), channel_id=1, source_target_pairs={{0,28},{4,0},{8,4},{12,8},{16,12},{20,16},{24,20},{28,24},{1,29},{... | collective-permute-start | bytes 1179656 | tf_op jit(solution)/shard_map/ppermute | solution.py:31
  66.2 13.0 %collective-permute-start.2 = (bf16[1,96,16,128]{3,2,1,0:T(8,128)(2,1)S(1)}, bf16[1,96,16,128]{3,2,1,0:T(8,128)(2,1)S(1)}, u32[]{:S(2)}, u32[]{:S(2)}) collective-permute-start(bf16[1,96,16,128]{3,2,1,0:T(8,128)(2,1)S(1)} %collective-permute-done.1.rest_6_), channel_id=1, source_target_pairs={{0,4},{4,8},{8,12},{12,16},{16,20},{20,24},{24,28},{28,0},{1,5},{5... | collective-permute-start | bytes 1179656 | tf_op jit(solution)/shard_map/ppermute | solution.py:31
  66.2 14.2 %collective-permute-start.15 = (bf16[1,96,16,128]{3,2,1,0:T(8,128)(2,1)S(1)}, bf16[1,96,16,128]{3,2,1,0:T(8,128)(2,1)}, u32[]{:S(2)}, u32[]{:S(2)}) collective-permute-start(bf16[1,96,16,128]{3,2,1,0:T(8,128)(2,1)S(1)} %collective-permute-done.4.rest_3_), channel_id=1, source_target_pairs={{0,1},{1,2},{2,3},{3,0},{4,5},{5,6},{6,7},{7,4},{8,9},{9,10},{10,1... | collective-permute-start | bytes 1179656 | tf_op jit(solution)/shard_map/ppermute | solution.py:31
  68.5 25.9 %all-to-all-start.2 = ((f32[32,16,128]{2,1,0:T(8,128)}), f32[32,16,128]{2,1,0:T(8,128)S(1)}, u32[]{:S(2)}, u32[]{:S(2)}) async-start(f32[32,16,128]{2,1,0:T(8,128)} %broadcast_in_dim.24), calls=%async_computation.2 | async-start | bytes 524288 | tf_op jit(solution)/shard_map/all_to_all | solution.py:311
  77.7 12.8 %collective-permute-start.20 = (bf16[1,96,16,128]{3,2,1,0:T(8,128)(2,1)S(1)}, bf16[1,96,16,128]{3,2,1,0:T(8,128)(2,1)}, u32[]{:S(2)}, u32[]{:S(2)}) collective-permute-start(bf16[1,96,16,128]{3,2,1,0:T(8,128)(2,1)S(1)} %collective-permute-done.7.rest_7_), channel_id=1, source_target_pairs={{0,3},{1,0},{2,1},{3,2},{4,7},{5,4},{6,5},{7,6},{8,11},{9,8},{10,9... | collective-permute-start | bytes 1179656 | tf_op jit(solution)/shard_map/ppermute | solution.py:31
  78.3 13.2 %collective-permute-start.19 = (bf16[1,96,16,128]{3,2,1,0:T(8,128)(2,1)S(1)}, bf16[1,96,16,128]{3,2,1,0:T(8,128)(2,1)}, u32[]{:S(2)}, u32[]{:S(2)}) collective-permute-start(bf16[1,96,16,128]{3,2,1,0:T(8,128)(2,1)S(1)} %collective-permute-done.7.rest_7_), channel_id=1, source_target_pairs={{0,1},{1,2},{2,3},{3,0},{4,5},{5,6},{6,7},{7,4},{8,9},{9,10},{10,1... | collective-permute-start | bytes 1179656 | tf_op jit(solution)/shard_map/ppermute | solution.py:31
  79.2 15.2 %collective-permute-start.3 = (bf16[1,96,16,128]{3,2,1,0:T(8,128)(2,1)S(1)}, bf16[1,96,16,128]{3,2,1,0:T(8,128)(2,1)}, u32[]{:S(2)}, u32[]{:S(2)}) collective-permute-start(bf16[1,96,16,128]{3,2,1,0:T(8,128)(2,1)S(1)} %collective-permute-done.2.rest_10_), channel_id=1, source_target_pairs={{0,4},{4,8},{8,12},{12,16},{16,20},{20,24},{24,28},{28,0},{1,5},{5... | collective-permute-start | bytes 1179656 | tf_op jit(solution)/shard_map/ppermute | solution.py:31
  80.3 20.9 %collective-permute-start.10 = (bf16[1,96,16,128]{3,2,1,0:T(8,128)(2,1)S(1)}, bf16[1,96,16,128]{3,2,1,0:T(8,128)(2,1)}, u32[]{:S(2)}, u32[]{:S(2)}) collective-permute-start(bf16[1,96,16,128]{3,2,1,0:T(8,128)(2,1)S(1)} %collective-permute-done.7.rest_7_), channel_id=1, source_target_pairs={{0,28},{4,0},{8,4},{12,8},{16,12},{20,16},{24,20},{28,24},{1,29},{... | collective-permute-start | bytes 1179656 | tf_op jit(solution)/shard_map/ppermute | solution.py:31
  84.1 19.8 %collective-permute-start.18 = (bf16[1,96,16,128]{3,2,1,0:T(8,128)(2,1)S(1)}, bf16[1,96,16,128]{3,2,1,0:T(8,128)(2,1)}, u32[]{:S(2)}, u32[]{:S(2)}) collective-permute-start(bf16[1,96,16,128]{3,2,1,0:T(8,128)(2,1)S(1)} %collective-permute-done.1.rest_6_), channel_id=1, source_target_pairs={{0,3},{1,0},{2,1},{3,2},{4,7},{5,4},{6,5},{7,6},{8,11},{9,8},{10,9... | collective-permute-start | bytes 1179656 | tf_op jit(solution)/shard_map/ppermute | solution.py:31
  90.5 13.3 %collective-permute-start.17 = (bf16[1,96,16,128]{3,2,1,0:T(8,128)(2,1)S(1)}, bf16[1,96,16,128]{3,2,1,0:T(8,128)(2,1)}, u32[]{:S(2)}, u32[]{:S(2)}) collective-permute-start(bf16[1,96,16,128]{3,2,1,0:T(8,128)(2,1)S(1)} %collective-permute-done.1.rest_6_), channel_id=1, source_target_pairs={{0,1},{1,2},{2,3},{3,0},{4,5},{5,6},{6,7},{7,4},{8,9},{9,10},{10,1... | collective-permute-start | bytes 1179656 | tf_op jit(solution)/shard_map/ppermute | solution.py:31
  91.5 15.1 %collective-permute-start.6 = (bf16[1,96,16,128]{3,2,1,0:T(8,128)(2,1)}, bf16[1,96,16,128]{3,2,1,0:T(8,128)(2,1)}, u32[]{:S(2)}, u32[]{:S(2)}) collective-permute-start(bf16[1,96,16,128]{3,2,1,0:T(8,128)(2,1)} %get-tuple-element.24), channel_id=1, source_target_pairs={{0,28},{4,0},{8,4},{12,8},{16,12},{20,16},{24,20},{28,24},{1,29},{... | collective-permute-start | bytes 1179656 | tf_op jit(solution)/shard_map/ppermute | solution.py:31
  94.4 14.8 %collective-permute-start.5 = (bf16[1,96,16,128]{3,2,1,0:T(8,128)(2,1)}, bf16[1,96,16,128]{3,2,1,0:T(8,128)(2,1)}, u32[]{:S(2)}, u32[]{:S(2)}) collective-permute-start(bf16[1,96,16,128]{3,2,1,0:T(8,128)(2,1)} %get-tuple-element.24), channel_id=1, source_target_pairs={{0,4},{4,8},{8,12},{12,16},{16,20},{20,24},{24,28},{28,0},{1,5},{5... | collective-permute-start | bytes 1179656 | tf_op jit(solution)/shard_map/ppermute | solution.py:31
  96.8 50.1 %all-to-all-start.4 = ((bf16[4,96,16,128]{3,2,1,0:T(8,128)(2,1)}), bf16[4,96,16,128]{3,2,1,0:T(8,128)(2,1)}, u32[]{:S(2)}, u32[]{:S(2)}) async-start(bf16[4,96,16,128]{3,2,1,0:T(8,128)(2,1)} %broadcast_in_dim.46), calls=%async_computation.4 | async-start | bytes 3145728 | tf_op jit(solution)/shard_map/all_to_all | solution.py:270
  101.2 21.6 %collective-permute-start.24 = (bf16[1,96,16,128]{3,2,1,0:T(8,128)(2,1)}, bf16[1,96,16,128]{3,2,1,0:T(8,128)(2,1)}, u32[]{:S(2)}, u32[]{:S(2)}) collective-permute-start(bf16[1,96,16,128]{3,2,1,0:T(8,128)(2,1)} %collective-permute-done.10.rest_11_), channel_id=1, source_target_pairs={{0,3},{1,0},{2,1},{3,2},{4,7},{5,4},{6,5},{7,6},{8,11},{9,8},{10,9... | collective-permute-start | bytes 1179656 | tf_op jit(solution)/shard_map/ppermute | solution.py:31
  103.9 20.8 %collective-permute-start.23 = (bf16[1,96,16,128]{3,2,1,0:T(8,128)(2,1)}, bf16[1,96,16,128]{3,2,1,0:T(8,128)(2,1)}, u32[]{:S(2)}, u32[]{:S(2)}) collective-permute-start(bf16[1,96,16,128]{3,2,1,0:T(8,128)(2,1)} %collective-permute-done.10.rest_11_), channel_id=1, source_target_pairs={{0,1},{1,2},{2,3},{3,0},{4,5},{5,6},{6,7},{7,4},{8,9},{9,10},{10,1... | collective-permute-start | bytes 1179656 | tf_op jit(solution)/shard_map/ppermute | solution.py:31
  103.9 31.5 %collective-permute-start.22 = (bf16[1,96,16,128]{3,2,1,0:T(8,128)(2,1)S(1)}, bf16[1,96,16,128]{3,2,1,0:T(8,128)(2,1)}, u32[]{:S(2)}, u32[]{:S(2)}) collective-permute-start(bf16[1,96,16,128]{3,2,1,0:T(8,128)(2,1)S(1)} %collective-permute-done.2.rest_10_), channel_id=1, source_target_pairs={{0,3},{1,0},{2,1},{3,2},{4,7},{5,4},{6,5},{7,6},{8,11},{9,8},{10,9... | collective-permute-start | bytes 1179656 | tf_op jit(solution)/shard_map/ppermute | solution.py:31
  106.6 28.8 %collective-permute-start.9 = (bf16[1,96,16,128]{3,2,1,0:T(8,128)(2,1)}, bf16[1,96,16,128]{3,2,1,0:T(8,128)(2,1)}, u32[]{:S(2)}, u32[]{:S(2)}) collective-permute-start(bf16[1,96,16,128]{3,2,1,0:T(8,128)(2,1)} %collective-permute-done.6.rest_5_), channel_id=1, source_target_pairs={{0,28},{4,0},{8,4},{12,8},{16,12},{20,16},{24,20},{28,24},{1,29},{... | collective-permute-start | bytes 1179656 | tf_op jit(solution)/shard_map/ppermute | solution.py:31
  109.2 27.5 %collective-permute-start.8 = (bf16[1,96,16,128]{3,2,1,0:T(8,128)(2,1)}, bf16[1,96,16,128]{3,2,1,0:T(8,128)(2,1)}, u32[]{:S(2)}, u32[]{:S(2)}) collective-permute-start(bf16[1,96,16,128]{3,2,1,0:T(8,128)(2,1)} %collective-permute-done.5.rest_4_), channel_id=1, source_target_pairs={{0,4},{4,8},{8,12},{12,16},{16,20},{20,24},{24,28},{28,0},{1,5},{5... | collective-permute-start | bytes 1179656 | tf_op jit(solution)/shard_map/ppermute | solution.py:31
  122.8 22.4 %collective-permute-start.16 = (bf16[1,96,16,128]{3,2,1,0:T(8,128)(2,1)}, bf16[1,96,16,128]{3,2,1,0:T(8,128)(2,1)}, u32[]{:S(2)}, u32[]{:S(2)}) collective-permute-start(bf16[1,96,16,128]{3,2,1,0:T(8,128)(2,1)} %get-tuple-element.22), channel_id=1, source_target_pairs={{0,28},{4,0},{8,4},{12,8},{16,12},{20,16},{24,20},{28,24},{1,29},{... | collective-permute-start | bytes 1179656 | tf_op jit(solution)/shard_map/ppermute | solution.py:31
  124.7 20.5 %collective-permute-start.13 = (bf16[1,96,16,128]{3,2,1,0:T(8,128)(2,1)}, bf16[1,96,16,128]{3,2,1,0:T(8,128)(2,1)}, u32[]{:S(2)}, u32[]{:S(2)}) collective-permute-start(bf16[1,96,16,128]{3,2,1,0:T(8,128)(2,1)} %get-tuple-element.23), channel_id=1, source_target_pairs={{0,4},{4,8},{8,12},{12,16},{16,20},{20,24},{24,28},{28,0},{1,5},{5... | collective-permute-start | bytes 1179656 | tf_op jit(solution)/shard_map/ppermute | solution.py:31
  135.4 9.1 %collective-permute-start.21 = (bf16[1,96,16,128]{3,2,1,0:T(8,128)(2,1)S(1)}, bf16[1,96,16,128]{3,2,1,0:T(8,128)(2,1)S(1)}, u32[]{:S(2)}, u32[]{:S(2)}) collective-permute-start(bf16[1,96,16,128]{3,2,1,0:T(8,128)(2,1)S(1)} %collective-permute-done.2.rest_10_), channel_id=1, source_target_pairs={{0,1},{1,2},{2,3},{3,0},{4,5},{5,6},{6,7},{7,4},{8,9},{9,10},{10,1... | collective-permute-start | bytes 1179656 | tf_op jit(solution)/shard_map/ppermute | solution.py:31
  135.4 10.4 %collective-permute-start.12 = (bf16[1,96,16,128]{3,2,1,0:T(8,128)(2,1)}, bf16[1,96,16,128]{3,2,1,0:T(8,128)(2,1)}, u32[]{:S(2)}, u32[]{:S(2)}) collective-permute-start(bf16[1,96,16,128]{3,2,1,0:T(8,128)(2,1)} %collective-permute-done.9.rest_9_), channel_id=1, source_target_pairs={{0,28},{4,0},{8,4},{12,8},{16,12},{20,16},{24,20},{28,24},{1,29},{... | collective-permute-start | bytes 1179656 | tf_op jit(solution)/shard_map/ppermute | solution.py:31
  136.7 10.2 %collective-permute-start.11 = (bf16[1,96,16,128]{3,2,1,0:T(8,128)(2,1)}, bf16[1,96,16,128]{3,2,1,0:T(8,128)(2,1)}, u32[]{:S(2)}, u32[]{:S(2)}) collective-permute-start(bf16[1,96,16,128]{3,2,1,0:T(8,128)(2,1)} %collective-permute-done.8.rest_8_), channel_id=1, source_target_pairs={{0,4},{4,8},{8,12},{12,16},{16,20},{20,24},{24,28},{28,0},{1,5},{5... | collective-permute-start | bytes 1179656 | tf_op jit(solution)/shard_map/ppermute | solution.py:31
  176.0 16.7 %collective-permute-start.25 = (s16[4,2528,128]{2,1,0:T(8,128)(2,1)}, s16[4,2528,128]{2,1,0:T(8,128)(2,1)S(1)}, u32[]{:S(2)}, u32[]{:S(2)}) collective-permute-start(s16[4,2528,128]{2,1,0:T(8,128)(2,1)} %get-tuple-element.15), channel_id=1, source_target_pairs={{0,32},{32,0},{1,33},{33,1},{2,34},{34,2},{3,35},{35,3},{4,36},{36... | collective-permute-start | bytes 7766024 | tf_op jit(solution)/shard_map/ppermute | solution.py:31
  183.2 21.4 %all-to-all-start.5 = ((f32[32,16,128]{2,1,0:T(8,128)}), f32[32,16,128]{2,1,0:T(8,128)}, u32[]{:S(2)}, u32[]{:S(2)}) async-start(f32[32,16,128]{2,1,0:T(8,128)} %bitcast.49), calls=%async_computation.5 | async-start | bytes 524288 | tf_op jit(solution)/shard_map/all_to_all | solution.py:389
  199.5 14.5 %collective-permute-start.26 = (s16[1312,128]{1,0:T(8,128)(2,1)}, s16[1312,128]{1,0:T(8,128)(2,1)}, u32[]{:S(2)}, u32[]{:S(2)}) collective-permute-start(s16[1312,128]{1,0:T(8,128)(2,1)} %pad_add_fusion), channel_id=1, source_target_pairs={{0,64},{64,128},{128,192},{192,0},{1,65},{65,129},{129,193},{193,1... | collective-permute-start | bytes 1007624 | tf_op jit(solution)/shard_map/ppermute | solution.py:31
  201.6 12.4 %collective-permute-start.27 = (s16[1248,128]{1,0:T(8,128)(2,1)}, s16[1248,128]{1,0:T(8,128)(2,1)}, u32[]{:S(2)}, u32[]{:S(2)}) collective-permute-start(s16[1248,128]{1,0:T(8,128)(2,1)} %slice_bitcast_fusion.1), channel_id=1, source_target_pairs={{0,192},{64,0},{128,64},{192,128},{1,193},{65,1},{129,65},{193,129... | collective-permute-start | bytes 958472 | tf_op jit(solution)/shard_map/ppermute | solution.py:31
  206.3 18.1 %all-to-all-start.6 = ((f32[32,16,128]{2,1,0:T(8,128)}), f32[32,16,128]{2,1,0:T(8,128)}, u32[]{:S(2)}, u32[]{:S(2)}) async-start(f32[32,16,128]{2,1,0:T(8,128)} %broadcast_in_dim.48), calls=%async_computation.6 | async-start | bytes 524288 | tf_op jit(solution)/shard_map/all_to_all | solution.py:407
  216.8 23.0 %collective-permute-start.28 = (s16[2528,128]{1,0:T(8,128)(2,1)}, s16[2528,128]{1,0:T(8,128)(2,1)}, u32[]{:S(2)}, u32[]{:S(2)}) collective-permute-start(s16[2528,128]{1,0:T(8,128)(2,1)} %get-tuple-element.16), channel_id=1, source_target_pairs={{0,64},{64,128},{128,192},{192,0},{1,65},{65,129},{129,193},{193,1... | collective-permute-start | bytes 1941512 | tf_op jit(solution)/shard_map/ppermute | solution.py:31
  216.8 23.0 %collective-permute-start.29 = (s16[2528,128]{1,0:T(8,128)(2,1)}, s16[2528,128]{1,0:T(8,128)(2,1)}, u32[]{:S(2)}, u32[]{:S(2)}) collective-permute-start(s16[2528,128]{1,0:T(8,128)(2,1)} %get-tuple-element.17), channel_id=1, source_target_pairs={{0,192},{64,0},{128,64},{192,128},{1,193},{65,1},{129,65},{193,129... | collective-permute-start | bytes 1941512 | tf_op jit(solution)/shard_map/ppermute | solution.py:31
  226.5 12.6 %all-to-all-start.7 = ((f32[8,48,128]{2,1,0:T(8,128)}), f32[8,48,128]{2,1,0:T(8,128)S(1)}, u32[]{:S(2)}, u32[]{:S(2)}) async-start(f32[8,48,128]{2,1,0:T(8,128)} %copy-done.1), calls=%async_computation.7 | async-start | bytes 393216 | tf_op jit(solution)/shard_map/all_to_all | solution.py:411
  (10 other events, 66.7 us)

commit v7 on v5

--- a/solution.py
+++ b/solution.py
@@ -23,6 +23,39 @@
 CODE_ROWS = SLOT_ROWS + FO_ROWS
 PART_ROWS = CODE_ROWS + 32
 FINE = 256.0
+ORDER = (
+    ("across", (0, 0), (0, 2)),
+    ("z_up", (0, 0), (-1, 0)),
+    ("z_up", (-1, 0), (-2, 0)),
+    ("z_down", (0, 0), (1, 0)),
+    ("z_down", (1, 0), (2, 0)),
+    ("x_up", (1, 0), (1, -1)),
+    ("z_up", (0, 2), (-1, 2)),
+    ("x_down", (0, 0), (0, 1)),
+    ("x_up", (0, 0), (0, -1)),
+    ("x_down", (-1, 0), (-1, 1)),
+    ("x_up", (2, 0), (2, -1)),
+    ("z_down", (0, 2), (1, 2)),
+    ("x_up", (-2, 0), (-2, -1)),
+    ("z_down", (0, 1), (1, 1)),
+    ("z_up", (-2, 0), (-3, 0)),
+    ("z_down", (2, 0), (3, 0)),
+    ("x_up", (3, 0), (3, -1)),
+    ("x_down", (-2, 0), (-2, 1)),
+    ("z_up", (0, -1), (-1, -1)),
+    ("x_down", (-3, 0), (-3, 1)),
+    ("x_up", (-3, 0), (-3, -1)),
+    ("x_down", (2, 0), (2, 1)),
+    ("z_up", (-1, 2), (-2, 2)),
+    ("z_up", (-2, 2), (-3, 2)),
+    ("z_down", (1, 2), (2, 2)),
+    ("z_up", (-3, 0), (4, 0)),
+    ("z_down", (2, 2), (3, 2)),
+    ("x_down", (3, 0), (3, 1)),
+    ("x_up", (4, 0), (4, -1)),
+    ("x_down", (4, 0), (4, 1)),
+    ("z_down", (3, 2), (4, 2)),
+)
 CUT = 10 * BS
 
 
@@ -233,7 +266,7 @@
             slots_ref[index] = jnp.where(index < count, total.T, 0.0)
         else:
             h = index - CAP
-            outer_ref[:, h * 64 : (h + 1) * 64] = total.T
+            outer_ref[h * 64 : (h + 1) * 64] = total
 
 
 def in_kernel(cols_ref, back_ref, out_ref):
@@ -261,23 +294,16 @@
 
 
 def gather_tokens(own):
-    z_up, z_down = shift("z", NZ, 1), shift("z", NZ, -1)
-    x_up, x_down = shift("x", NX, 1), shift("x", NX, -1)
-    across = shift("x", NX, 2)
+    moves = {
+        "z_up": shift("z", NZ, 1),
+        "z_down": shift("z", NZ, -1),
+        "x_up": shift("x", NX, 1),
+        "x_down": shift("x", NX, -1),
+        "across": shift("x", NX, 2),
+    }
     held = {(0, 0): own[None]}
-    held[0, 2] = across(own[None])
-    for b in (0, 2):
-        for a in (1, 2, 3):
-            held[-a, b] = z_up(held[1 - a, b])
-            held[a, b] = z_down(held[a - 1, b])
-    held[4, 0] = z_up(held[-3, 0])
-    held[4, 2] = z_down(held[3, 2])
-    for a in (0, -1, 1, -2, 2, -3, 3, 4):
-        for b, move in ((-1, x_up), (1, x_down)):
-            if (a, b) in ((1, 1), (-1, -1)):
-                held[a, b] = (z_down if a > 0 else z_up)(held[0, b])
-            else:
-                held[a, b] = move(held[a, 0])
+    for name, source, target in ORDER:
+        held[target] = moves[name](held[source])
     return list(held.values()), [[key] for key in held]
 
 
@@ -403,7 +429,7 @@
         out_specs=[whole, whole],
         out_shape=[
             jax.ShapeDtypeStruct((CAP, BS, BS), jnp.float32),
-            jax.ShapeDtypeStruct((BS, FO_ROWS), jnp.float32),
+            jax.ShapeDtypeStruct((FO_ROWS, BS), jnp.float32),
         ],
         compiler_params=pltpu.CompilerParams(vmem_limit_bytes=50 * 1024 * 1024),
         cost_estimate=pl.CostEstimate(
@@ -411,7 +437,7 @@
         ),
         name="slots",
     )(mine, paired, *parts)
-    return hidden, slots, in_grad, out_grad
+    return hidden, slots, in_grad, out_grad.T
 
 
 def solution(mesh):

time: 212 us -> 206 us (0.972)
  starting transfers between devices: 118 us -> 99.6 us
  waiting for transfers between devices: 35.8 us -> 48.6 us
    ppermute x36, starting transfers between devices: 73.7 us -> 57.6 us  [shift(): return lambda value: lax.ppermute(value, axis, pairs)]
    ppermute x36, waiting for transfers between devices: 20.8 us -> 32.7 us  [shift(): return lambda value: lax.ppermute(value, axis, pairs)]
    all_to_all x1, starting transfers between devices: 10.1 us -> 5.59 us  [per_device(): spread = lax.all_to_all(own.reshape(span, per, ROWS, BS), plane, 0, 0)]
    unnamed x23 -> x22, local copies, waits for them, and re-layouts: 5.58 us -> 5.63 us
  transfers between devices with their start and end apart: 42 -> 42, of which waited for: 13 -> 14; matrix products, arithmetic and copies ran while one was open for 4% -> 4% of each run, Pallas kernels for 4% -> 4%
where the time goes in v7:
time: 206 us; the launch traced here: 205 us
  starting transfers between devices  99.6 us (48%)
  waiting for transfers between devices  48.6 us (24%)
  Pallas kernels  41.7 us (20%)
  local copies, waits for them, and re-layouts  9.07 us (4%)
  other arithmetic  3.44 us (2%)
  matrix products  2.09 us (1%)
    ppermute x36, starting transfers between devices, shift(): return lambda value: lax.ppermute(value, axis, pairs)  57.6 us
    ppermute x36, waiting for transfers between devices, shift(): return lambda value: lax.ppermute(value, axis, pairs)  32.7 us
    pallas_call x1, Pallas kernels, per_device(): pl.pallas_call(functools.partial(main_kernel, [len(g) for g in keys]), gr...  29.6 us
    all_to_all x1, starting transfers between devices, per_device(): back = lax.all_to_all(back.reshape(span, ROWS, BS), plane, 0, 0)  9.19 us
    all_to_all x1, starting transfers between devices, per_device(): lax.all_to_all(jnp.broadcast_to(back_own[None], (span, ROWS, BS)), plane,...  7.69 us
    all_to_all x1, starting transfers between devices, per_device(): low_own = jnp.sum(lax.all_to_all(partial, plane, 0, 0), axis=0)  6.87 us
    all_to_all x1, starting transfers between devices, per_device(): in_grad = jnp.sum(lax.all_to_all(in_part, ('y', 'core'), 0, 0), axis=0)  6.72 us
    all_to_all x1, starting transfers between devices, per_device(): lax.all_to_all(jnp.broadcast_to(low_own[None], (span, ROWS, BS)), plane,...  5.92 us
  transfers between devices with their start and end apart: 42, of which 14 were waited for; matrix products, arithmetic and copies ran while one was open for 4% of the time, Pallas kernels for 4%

profile of v7, /device:TPU:1, one launch (start us, length us, event | category | flops | bytes accessed | tf_op | source)
XLA Modules:
  0.0 205.4 jit_solution(7545621749968564824)
XLA Ops:
  2.5 2.0 collective-permute-start.8
  5.8 5.8 %collective-permute-start.3 = (bf16[1,96,16,128]{3,2,1,0:T(8,128)(2,1)S(1)}, bf16[1,96,16,128]{3,2,1,0:T(8,128)(2,1)S(1)}, u32[]{:S(2)}, u32[]{:S(2)}) collective-permute-start(bf16[1,96,16,128]{3,2,1,0:T(8,128)(2,1)S(1)} %get-tuple-element.22.rest_0_), channel_id=1, source_target_pairs={{0,28},{4,0},{8,4},{12,8},{16,12},{20,16},{24,20},{28,24},{1,29},{... | collective-permute-start | bytes 1179656 | tf_op jit(solution)/shard_map/ppermute | solution.py:64
  13.1 3.0 %collective-permute-start.18 = (bf16[1,96,16,128]{3,2,1,0:T(8,128)(2,1)S(1)}, bf16[1,96,16,128]{3,2,1,0:T(8,128)(2,1)S(1)}, u32[]{:S(2)}, u32[]{:S(2)}) collective-permute-start(bf16[1,96,16,128]{3,2,1,0:T(8,128)(2,1)S(1)} %collective-permute-done.8.rest_9_), channel_id=1, source_target_pairs={{0,4},{4,8},{8,12},{12,16},{16,20},{20,24},{24,28},{28,0},{1,5},{5... | collective-permute-start | bytes 1179656 | tf_op jit(solution)/shard_map/ppermute | solution.py:64
  16.1 4.0 %collective-permute-start.13 = (bf16[1,96,16,128]{3,2,1,0:T(8,128)(2,1)S(1)}, bf16[1,96,16,128]{3,2,1,0:T(8,128)(2,1)}, u32[]{:S(2)}, u32[]{:S(2)}) collective-permute-start(bf16[1,96,16,128]{3,2,1,0:T(8,128)(2,1)S(1)} %collective-permute-done.7.rest_8_), channel_id=1, source_target_pairs={{0,28},{4,0},{8,4},{12,8},{16,12},{20,16},{24,20},{28,24},{1,29},{... | collective-permute-start | bytes 1179656 | tf_op jit(solution)/shard_map/ppermute | solution.py:64
  25.5 4.8 %collective-permute-done.18.rest_19_ = bf16[1,96,16,128]{3,2,1,0:T(8,128)(2,1)S(1)} collective-permute-done((bf16[1,96,16,128]{3,2,1,0:T(8,128)(2,1)S(1)}, bf16[1,96,16,128]{3,2,1,0:T(8,128)(2,1)S(1)}, u32[]{:S(2)}, u32[]{:S(2)}) %collective-permute-start.18) | collective-permute-done | bytes 393248 | tf_op jit(solution)/shard_map/ppermute | solution.py:64
  31.0 5.6 %all-to-all-start = ((bf16[32,3,16,128]{3,2,1,0:T(8,128)(2,1)}), bf16[32,3,16,128]{3,2,1,0:T(8,128)(2,1)S(1)}, u32[]{:S(2)}, u32[]{:S(2)}) async-start(bf16[32,3,16,128]{3,2,1,0:T(8,128)(2,1)} %bitcast.73), calls=%async_computation | async-start | bytes 786432 | tf_op jit(solution)/shard_map/all_to_all | solution.py:316
  36.6 2.6 %collective-permute-start.11 = (bf16[1,96,16,128]{3,2,1,0:T(8,128)(2,1)S(1)}, bf16[1,96,16,128]{3,2,1,0:T(8,128)(2,1)}, u32[]{:S(2)}, u32[]{:S(2)}) collective-permute-start(bf16[1,96,16,128]{3,2,1,0:T(8,128)(2,1)S(1)} %collective-permute-done.rest_1_), channel_id=1, source_target_pairs={{0,28},{4,0},{8,4},{12,8},{16,12},{20,16},{24,20},{28,24},{1,29},{... | collective-permute-start | bytes 1179656 | tf_op jit(solution)/shard_map/ppermute | solution.py:64
  39.2 2.5 %collective-permute-start.21 = (bf16[1,96,16,128]{3,2,1,0:T(8,128)(2,1)}, bf16[1,96,16,128]{3,2,1,0:T(8,128)(2,1)S(1)}, u32[]{:S(2)}, u32[]{:S(2)}) collective-permute-start(bf16[1,96,16,128]{3,2,1,0:T(8,128)(2,1)} %collective-permute-done.4.rest_5_), channel_id=1, source_target_pairs={{0,3},{1,0},{2,1},{3,2},{4,7},{5,4},{6,5},{7,6},{8,11},{9,8},{10,9... | collective-permute-start | bytes 1179656 | tf_op jit(solution)/shard_map/ppermute | solution.py:64
  41.7 2.6 %collective-permute-start.15 = (bf16[1,96,16,128]{3,2,1,0:T(8,128)(2,1)}, bf16[1,96,16,128]{3,2,1,0:T(8,128)(2,1)}, u32[]{:S(2)}, u32[]{:S(2)}) collective-permute-start(bf16[1,96,16,128]{3,2,1,0:T(8,128)(2,1)} %collective-permute-done.4.rest_5_), channel_id=1, source_target_pairs={{0,28},{4,0},{8,4},{12,8},{16,12},{20,16},{24,20},{28,24},{1,29},{... | collective-permute-start | bytes 1179656 | tf_op jit(solution)/shard_map/ppermute | solution.py:64
  44.3 9.7 %collective-permute-done.11.rest_12_ = bf16[1,96,16,128]{3,2,1,0:T(8,128)(2,1)} collective-permute-done((bf16[1,96,16,128]{3,2,1,0:T(8,128)(2,1)S(1)}, bf16[1,96,16,128]{3,2,1,0:T(8,128)(2,1)}, u32[]{:S(2)}, u32[]{:S(2)}) %collective-permute-start.11) | collective-permute-done | bytes 393248 | tf_op jit(solution)/shard_map/ppermute | solution.py:64
  54.0 2.6 %collective-permute-start.17 = (bf16[1,96,16,128]{3,2,1,0:T(8,128)(2,1)}, bf16[1,96,16,128]{3,2,1,0:T(8,128)(2,1)}, u32[]{:S(2)}, u32[]{:S(2)}) collective-permute-start(bf16[1,96,16,128]{3,2,1,0:T(8,128)(2,1)} %collective-permute-done.2.rest_3_), channel_id=1, source_target_pairs={{0,3},{1,0},{2,1},{3,2},{4,7},{5,4},{6,5},{7,6},{8,11},{9,8},{10,9... | collective-permute-start | bytes 1179656 | tf_op jit(solution)/shard_map/ppermute | solution.py:64
  58.8 3.8 %collective-permute-done.15.rest_16_ = bf16[1,96,16,128]{3,2,1,0:T(8,128)(2,1)} collective-permute-done((bf16[1,96,16,128]{3,2,1,0:T(8,128)(2,1)}, bf16[1,96,16,128]{3,2,1,0:T(8,128)(2,1)}, u32[]{:S(2)}, u32[]{:S(2)}) %collective-permute-start.15) | collective-permute-done | bytes 393248 | tf_op jit(solution)/shard_map/ppermute | solution.py:64
  62.6 3.4 %collective-permute-start.24 = (bf16[1,96,16,128]{3,2,1,0:T(8,128)(2,1)}, bf16[1,96,16,128]{3,2,1,0:T(8,128)(2,1)}, u32[]{:S(2)}, u32[]{:S(2)}) collective-permute-start(bf16[1,96,16,128]{3,2,1,0:T(8,128)(2,1)} %collective-permute-done.11.rest_12_), channel_id=1, source_target_pairs={{0,28},{4,0},{8,4},{12,8},{16,12},{20,16},{24,20},{28,24},{1,29},{... | collective-permute-start | bytes 1179656 | tf_op jit(solution)/shard_map/ppermute | solution.py:64
  66.8 2.1 %convolution_bitcast_fusion = f32[32,16,128]{2,1,0:T(8,128)} fusion(bf16[32,3,16,128]{3,2,1,0:T(8,128)(2,1)S(1)} %all-to-all-done.cols_ref, f32[3,128,128,1]{2,1,0,3:T(8,128)} %bitcast.74), kind=kOutput, calls=%fused_computation | convolution fusion | flops 301989888 | bytes 851968 | tf_op jit(solution)/shard_map/sbtf,bfr->str/dot_general | solution.py:318
  68.9 6.9 %all-to-all-start.1 = ((f32[32,16,128]{2,1,0:T(8,128)}), f32[32,16,128]{2,1,0:T(8,128)S(1)}, u32[]{:S(2)}, u32[]{:S(2)}) async-start(f32[32,16,128]{2,1,0:T(8,128)} %convolution_bitcast_fusion), calls=%async_computation.1 | async-start | bytes 524288 | tf_op jit(solution)/shard_map/all_to_all | solution.py:321
  75.8 2.5 %collective-permute-start.27 = (bf16[1,96,16,128]{3,2,1,0:T(8,128)(2,1)}, bf16[1,96,16,128]{3,2,1,0:T(8,128)(2,1)}, u32[]{:S(2)}, u32[]{:S(2)}) collective-permute-start(bf16[1,96,16,128]{3,2,1,0:T(8,128)(2,1)} %collective-permute-done.15.rest_16_), channel_id=1, source_target_pairs={{0,3},{1,0},{2,1},{3,2},{4,7},{5,4},{6,5},{7,6},{8,11},{9,8},{10,9... | collective-permute-start | bytes 1179656 | tf_op jit(solution)/shard_map/ppermute | solution.py:64
  82.0 4.2 %all-to-all-done.1 = f32[32,16,128]{2,1,0:T(8,128)S(1)} async-done(((f32[32,16,128]{2,1,0:T(8,128)}), f32[32,16,128]{2,1,0:T(8,128)S(1)}, u32[]{:S(2)}, u32[]{:S(2)}) %all-to-all-start.1) | async-done | bytes 262176 | tf_op jit(solution)/shard_map/all_to_all | solution.py:321
  86.9 5.9 %all-to-all-start.2 = ((f32[32,16,128]{2,1,0:T(8,128)}), f32[32,16,128]{2,1,0:T(8,128)S(1)}, u32[]{:S(2)}, u32[]{:S(2)}) async-start(f32[32,16,128]{2,1,0:T(8,128)} %broadcast_in_dim.18), calls=%async_computation.2 | async-start | bytes 524288 | tf_op jit(solution)/shard_map/all_to_all | solution.py:322
  92.9 2.5 %collective-permute-start.19 = (bf16[1,96,16,128]{3,2,1,0:T(8,128)(2,1)}, bf16[1,96,16,128]{3,2,1,0:T(8,128)(2,1)S(1)}, u32[]{:S(2)}, u32[]{:S(2)}) collective-permute-start(bf16[1,96,16,128]{3,2,1,0:T(8,128)(2,1)} %collective-permute-done.14.rest_15_), channel_id=1, source_target_pairs={{0,3},{1,0},{2,1},{3,2},{4,7},{5,4},{6,5},{7,6},{8,11},{9,8},{10,9... | collective-permute-start | bytes 1179656 | tf_op jit(solution)/shard_map/ppermute | solution.py:64
  102.4 3.6 %collective-permute-done.23.rest_24_ = bf16[1,96,16,128]{3,2,1,0:T(8,128)(2,1)} collective-permute-done((bf16[1,96,16,128]{3,2,1,0:T(8,128)(2,1)}, bf16[1,96,16,128]{3,2,1,0:T(8,128)(2,1)}, u32[]{:S(2)}, u32[]{:S(2)}) %collective-permute-start.23) | collective-permute-done | bytes 393248 | tf_op jit(solution)/shard_map/ppermute | solution.py:64
  106.0 4.5 %collective-permute-done.29.rest_30_ = bf16[1,96,16,128]{3,2,1,0:T(8,128)(2,1)} collective-permute-done((bf16[1,96,16,128]{3,2,1,0:T(8,128)(2,1)}, bf16[1,96,16,128]{3,2,1,0:T(8,128)(2,1)}, u32[]{:S(2)}, u32[]{:S(2)}) %collective-permute-start.29) | collective-permute-done | bytes 393248 | tf_op jit(solution)/shard_map/ppermute | solution.py:64
  110.5 29.6 %columns.1 = (bf16[512,1536]{1,0:T(8,128)(2,1)}, s16[4,2528,128]{2,1,0:T(8,128)(2,1)}, s16[4,2528,128]{2,1,0:T(8,128)(2,1)}, f32[512,128]{1,0:T(8,128)}) custom-call(s32[96]{0:T(128)S(1)} %reshape.176.rows_ref, s32[4,96]{1,0:T(4,128)S(1)} %pad_add_fusion.1.where_ref, s32[32]{0:T(128)S(1)} %stack.148.place_ref, f32[512,128]{1,0:T(8,128)S(1)} %bitcast.72, ...), custom_call_target="tpu_custom_call" | custom-call | tf_op jit(solution)/shard_map/columns/pallas_call | solution.py:360
  140.1 5.5 %collective-permute-start.31 = (s16[4,2528,128]{2,1,0:T(8,128)(2,1)}, s16[4,2528,128]{2,1,0:T(8,128)(2,1)S(1)}, u32[]{:S(2)}, u32[]{:S(2)}) collective-permute-start(s16[4,2528,128]{2,1,0:T(8,128)(2,1)} %get-tuple-element.15), channel_id=1, source_target_pairs={{0,32},{32,0},{1,33},{33,1},{2,34},{34,2},{3,35},{35,3},{4,36},{36... | collective-permute-start | bytes 7766024 | tf_op jit(solution)/shard_map/ppermute | solution.py:64
  145.6 9.2 %all-to-all-start.3 = ((f32[32,16,128]{2,1,0:T(8,128)}), f32[32,16,128]{2,1,0:T(8,128)}, u32[]{:S(2)}, u32[]{:S(2)}) async-start(f32[32,16,128]{2,1,0:T(8,128)} %bitcast.48), calls=%async_computation.3 | async-start | bytes 524288 | tf_op jit(solution)/shard_map/all_to_all | solution.py:401
  156.3 4.6 %pairs.1.up_ref.down_ref.own_ref = s16[4,2528,128]{2,1,0:T(8,128)(2,1)S(1)} custom-call(s16[4,2528,128]{2,1,0:T(8,128)(2,1)} %get-tuple-element.14.keep_ref, s16[4,2528,128]{2,1,0:T(8,128)(2,1)} %copy-done.2), custom_call_target="tpu_custom_call" | custom-call | tf_op jit(solution)/shard_map/pairs/pallas_call | solution.py:402
  168.4 7.7 %all-to-all-start.4 = ((f32[32,16,128]{2,1,0:T(8,128)}), f32[32,16,128]{2,1,0:T(8,128)}, u32[]{:S(2)}, u32[]{:S(2)}) async-start(f32[32,16,128]{2,1,0:T(8,128)} %broadcast_in_dim.21), calls=%async_computation.4 | async-start | bytes 524288 | tf_op jit(solution)/shard_map/all_to_all | solution.py:419
  176.2 2.7 %relay.1 = (s16[2528,128]{1,0:T(8,128)(2,1)}, s16[2528,128]{1,0:T(8,128)(2,1)}) custom-call(s16[4,2528,128]{2,1,0:T(8,128)(2,1)S(1)} %pairs.1.up_ref.down_ref.own_ref, s16[4,2528,128]{2,1,0:T(8,128)(2,1)S(1)} %pairs.1.up_ref.down_ref.own_ref, s16[1312,128]{1,0:T(8,128)(2,1)} %collective-permute-done.32.above_ref, ...), custom_call_target="tpu_custom_call" | custom-call | flops 40000000 | bytes 40000000 | tf_op jit(solution)/shard_map/relay/pallas_call | solution.py:242
  178.9 2.6 %collective-permute-start.35 = (s16[2528,128]{1,0:T(8,128)(2,1)}, s16[2528,128]{1,0:T(8,128)(2,1)}, u32[]{:S(2)}, u32[]{:S(2)}) collective-permute-start(s16[2528,128]{1,0:T(8,128)(2,1)} %get-tuple-element.17), channel_id=1, source_target_pairs={{0,192},{64,0},{128,64},{192,128},{1,193},{65,1},{129,65},{193,129... | collective-permute-start | bytes 1941512 | tf_op jit(solution)/shard_map/ppermute | solution.py:64
  181.5 5.0 %all-to-all-done.4.back_ref = f32[32,16,128]{2,1,0:T(8,128)} async-done(((f32[32,16,128]{2,1,0:T(8,128)}), f32[32,16,128]{2,1,0:T(8,128)}, u32[]{:S(2)}, u32[]{:S(2)}) %all-to-all-start.4) | async-done | bytes 262176 | tf_op jit(solution)/shard_map/all_to_all | solution.py:419
  188.6 6.7 %all-to-all-start.5 = ((f32[8,48,128]{2,1,0:T(8,128)}), f32[8,48,128]{2,1,0:T(8,128)S(1)}, u32[]{:S(2)}, u32[]{:S(2)}) async-start(f32[8,48,128]{2,1,0:T(8,128)} %copy-done.1), calls=%async_computation.5 | async-start | bytes 393216 | tf_op jit(solution)/shard_map/all_to_all | solution.py:423
  196.2 5.1 %all-to-all-done.5 = f32[8,48,128]{2,1,0:T(8,128)S(1)} async-done(((f32[8,48,128]{2,1,0:T(8,128)}), f32[8,48,128]{2,1,0:T(8,128)S(1)}, u32[]{:S(2)}, u32[]{:S(2)}) %all-to-all-start.5) | async-done | bytes 196640 | tf_op jit(solution)/shard_map/all_to_all | solution.py:423
  201.9 3.5 %slots.1 = (f32[18,128,128]{2,1,0:T(8,128)}, f32[192,128]{1,0:T(8,128)}) custom-call(s32[1]{0:T(128)} %bitcast.44.count_ref, s16[4,2528,128]{2,1,0:T(8,128)(2,1)S(1)} %pairs.1.up_ref.down_ref.own_ref, s16[2528,128]{1,0:T(8,128)(2,1)} %collective-permute-done.34.refs_0_, s16[2528,128]{1,0:T(8,128)(2,1)} %collective-permute-done.35.refs_1_), custom_call_target="tpu_custom_call" | custom-call | flops 10000000 | bytes 16000000 | tf_op jit(solution)/shard_map/slots/pallas_call | solution.py:426
  (102 shorter events, 37.7 us)
Async XLA Ops:
  5.8 14.4 %collective-permute-start.3 = (bf16[1,96,16,128]{3,2,1,0:T(8,128)(2,1)S(1)}, bf16[1,96,16,128]{3,2,1,0:T(8,128)(2,1)S(1)}, u32[]{:S(2)}, u32[]{:S(2)}) collective-permute-start(bf16[1,96,16,128]{3,2,1,0:T(8,128)(2,1)S(1)} %get-tuple-element.22.rest_0_), channel_id=1, source_target_pairs={{0,28},{4,0},{8,4},{12,8},{16,12},{20,16},{24,20},{28,24},{1,29},{... | collective-permute-start | bytes 1179656 | tf_op jit(solution)/shard_map/ppermute | solution.py:64
  13.1 17.2 %collective-permute-start.18 = (bf16[1,96,16,128]{3,2,1,0:T(8,128)(2,1)S(1)}, bf16[1,96,16,128]{3,2,1,0:T(8,128)(2,1)S(1)}, u32[]{:S(2)}, u32[]{:S(2)}) collective-permute-start(bf16[1,96,16,128]{3,2,1,0:T(8,128)(2,1)S(1)} %collective-permute-done.8.rest_9_), channel_id=1, source_target_pairs={{0,4},{4,8},{8,12},{12,16},{16,20},{20,24},{24,28},{28,0},{1,5},{5... | collective-permute-start | bytes 1179656 | tf_op jit(solution)/shard_map/ppermute | solution.py:64
  16.1 20.5 %collective-permute-start.13 = (bf16[1,96,16,128]{3,2,1,0:T(8,128)(2,1)S(1)}, bf16[1,96,16,128]{3,2,1,0:T(8,128)(2,1)}, u32[]{:S(2)}, u32[]{:S(2)}) collective-permute-start(bf16[1,96,16,128]{3,2,1,0:T(8,128)(2,1)S(1)} %collective-permute-done.7.rest_8_), channel_id=1, source_target_pairs={{0,28},{4,0},{8,4},{12,8},{16,12},{20,16},{24,20},{28,24},{1,29},{... | collective-permute-start | bytes 1179656 | tf_op jit(solution)/shard_map/ppermute | solution.py:64
  20.2 19.1 %collective-permute-start.5 = (bf16[1,96,16,128]{3,2,1,0:T(8,128)(2,1)S(1)}, bf16[1,96,16,128]{3,2,1,0:T(8,128)(2,1)}, u32[]{:S(2)}, u32[]{:S(2)}) collective-permute-start(bf16[1,96,16,128]{3,2,1,0:T(8,128)(2,1)S(1)} %collective-permute-done.3.rest_4_), channel_id=1, source_target_pairs={{0,1},{1,2},{2,3},{3,0},{4,5},{5,6},{6,7},{7,4},{8,9},{9,10},{10,1... | collective-permute-start | bytes 1179656 | tf_op jit(solution)/shard_map/ppermute | solution.py:64
  21.9 17.4 %collective-permute-start.4 = (bf16[1,96,16,128]{3,2,1,0:T(8,128)(2,1)S(1)}, bf16[1,96,16,128]{3,2,1,0:T(8,128)(2,1)}, u32[]{:S(2)}, u32[]{:S(2)}) collective-permute-start(bf16[1,96,16,128]{3,2,1,0:T(8,128)(2,1)S(1)} %collective-permute-done.3.rest_4_), channel_id=1, source_target_pairs={{0,28},{4,0},{8,4},{12,8},{16,12},{20,16},{24,20},{28,24},{1,29},{... | collective-permute-start | bytes 1179656 | tf_op jit(solution)/shard_map/ppermute | solution.py:64
  23.9 17.9 %collective-permute-start.9 = (bf16[1,96,16,128]{3,2,1,0:T(8,128)(2,1)S(1)}, bf16[1,96,16,128]{3,2,1,0:T(8,128)(2,1)}, u32[]{:S(2)}, u32[]{:S(2)}) collective-permute-start(bf16[1,96,16,128]{3,2,1,0:T(8,128)(2,1)S(1)} %collective-permute-done.1.rest_2_), channel_id=1, source_target_pairs={{0,3},{1,0},{2,1},{3,2},{4,7},{5,4},{6,5},{7,6},{8,11},{9,8},{10,9... | collective-permute-start | bytes 1179656 | tf_op jit(solution)/shard_map/ppermute | solution.py:64
  31.0 13.3 %collective-permute-start.2 = (bf16[1,96,16,128]{3,2,1,0:T(8,128)(2,1)S(1)}, bf16[1,96,16,128]{3,2,1,0:T(8,128)(2,1)}, u32[]{:S(2)}, u32[]{:S(2)}) collective-permute-start(bf16[1,96,16,128]{3,2,1,0:T(8,128)(2,1)S(1)} %collective-permute-done.1.rest_2_), channel_id=1, source_target_pairs={{0,4},{4,8},{8,12},{12,16},{16,20},{20,24},{24,28},{28,0},{1,5},{5... | collective-permute-start | bytes 1179656 | tf_op jit(solution)/shard_map/ppermute | solution.py:64
  31.0 35.7 %all-to-all-start = ((bf16[32,3,16,128]{3,2,1,0:T(8,128)(2,1)}), bf16[32,3,16,128]{3,2,1,0:T(8,128)(2,1)S(1)}, u32[]{:S(2)}, u32[]{:S(2)}) async-start(bf16[32,3,16,128]{3,2,1,0:T(8,128)(2,1)} %bitcast.73), calls=%async_computation | async-start | bytes 786432 | tf_op jit(solution)/shard_map/all_to_all | solution.py:316
  36.6 17.4 %collective-permute-start.11 = (bf16[1,96,16,128]{3,2,1,0:T(8,128)(2,1)S(1)}, bf16[1,96,16,128]{3,2,1,0:T(8,128)(2,1)}, u32[]{:S(2)}, u32[]{:S(2)}) collective-permute-start(bf16[1,96,16,128]{3,2,1,0:T(8,128)(2,1)S(1)} %collective-permute-done.rest_1_), channel_id=1, source_target_pairs={{0,28},{4,0},{8,4},{12,8},{16,12},{20,16},{24,20},{28,24},{1,29},{... | collective-permute-start | bytes 1179656 | tf_op jit(solution)/shard_map/ppermute | solution.py:64
  39.2 18.2 %collective-permute-start.6 = (bf16[1,96,16,128]{3,2,1,0:T(8,128)(2,1)S(1)}, bf16[1,96,16,128]{3,2,1,0:T(8,128)(2,1)}, u32[]{:S(2)}, u32[]{:S(2)}) collective-permute-start(bf16[1,96,16,128]{3,2,1,0:T(8,128)(2,1)S(1)} %collective-permute-done.rest_1_), channel_id=1, source_target_pairs={{0,4},{4,8},{8,12},{12,16},{16,20},{20,24},{24,28},{28,0},{1,5},{5... | collective-permute-start | bytes 1179656 | tf_op jit(solution)/shard_map/ppermute | solution.py:64
  39.2 18.2 %collective-permute-start.21 = (bf16[1,96,16,128]{3,2,1,0:T(8,128)(2,1)}, bf16[1,96,16,128]{3,2,1,0:T(8,128)(2,1)S(1)}, u32[]{:S(2)}, u32[]{:S(2)}) collective-permute-start(bf16[1,96,16,128]{3,2,1,0:T(8,128)(2,1)} %collective-permute-done.4.rest_5_), channel_id=1, source_target_pairs={{0,3},{1,0},{2,1},{3,2},{4,7},{5,4},{6,5},{7,6},{8,11},{9,8},{10,9... | collective-permute-start | bytes 1179656 | tf_op jit(solution)/shard_map/ppermute | solution.py:64
  41.7 20.8 %collective-permute-start.15 = (bf16[1,96,16,128]{3,2,1,0:T(8,128)(2,1)}, bf16[1,96,16,128]{3,2,1,0:T(8,128)(2,1)}, u32[]{:S(2)}, u32[]{:S(2)}) collective-permute-start(bf16[1,96,16,128]{3,2,1,0:T(8,128)(2,1)} %collective-permute-done.4.rest_5_), channel_id=1, source_target_pairs={{0,28},{4,0},{8,4},{12,8},{16,12},{20,16},{24,20},{28,24},{1,29},{... | collective-permute-start | bytes 1179656 | tf_op jit(solution)/shard_map/ppermute | solution.py:64
  44.3 21.6 %collective-permute-start.10 = (bf16[1,96,16,128]{3,2,1,0:T(8,128)(2,1)}, bf16[1,96,16,128]{3,2,1,0:T(8,128)(2,1)S(1)}, u32[]{:S(2)}, u32[]{:S(2)}) collective-permute-start(bf16[1,96,16,128]{3,2,1,0:T(8,128)(2,1)} %collective-permute-done.4.rest_5_), channel_id=1, source_target_pairs={{0,1},{1,2},{2,3},{3,0},{4,5},{5,6},{6,7},{7,4},{8,9},{9,10},{10,1... | collective-permute-start | bytes 1179656 | tf_op jit(solution)/shard_map/ppermute | solution.py:64
  54.0 21.7 %collective-permute-start.17 = (bf16[1,96,16,128]{3,2,1,0:T(8,128)(2,1)}, bf16[1,96,16,128]{3,2,1,0:T(8,128)(2,1)}, u32[]{:S(2)}, u32[]{:S(2)}) collective-permute-start(bf16[1,96,16,128]{3,2,1,0:T(8,128)(2,1)} %collective-permute-done.2.rest_3_), channel_id=1, source_target_pairs={{0,3},{1,0},{2,1},{3,2},{4,7},{5,4},{6,5},{7,6},{8,11},{9,8},{10,9... | collective-permute-start | bytes 1179656 | tf_op jit(solution)/shard_map/ppermute | solution.py:64
  57.4 20.8 %collective-permute-start.14 = (bf16[1,96,16,128]{3,2,1,0:T(8,128)(2,1)}, bf16[1,96,16,128]{3,2,1,0:T(8,128)(2,1)}, u32[]{:S(2)}, u32[]{:S(2)}) collective-permute-start(bf16[1,96,16,128]{3,2,1,0:T(8,128)(2,1)} %collective-permute-done.2.rest_3_), channel_id=1, source_target_pairs={{0,4},{4,8},{8,12},{12,16},{16,20},{20,24},{24,28},{28,0},{1,5},{5... | collective-permute-start | bytes 1179656 | tf_op jit(solution)/shard_map/ppermute | solution.py:64
  57.4 20.8 %collective-permute-start.12 = (bf16[1,96,16,128]{3,2,1,0:T(8,128)(2,1)}, bf16[1,96,16,128]{3,2,1,0:T(8,128)(2,1)}, u32[]{:S(2)}, u32[]{:S(2)}) collective-permute-start(bf16[1,96,16,128]{3,2,1,0:T(8,128)(2,1)} %collective-permute-done.2.rest_3_), channel_id=1, source_target_pairs={{0,1},{1,2},{2,3},{3,0},{4,5},{5,6},{6,7},{7,4},{8,9},{9,10},{10,1... | collective-permute-start | bytes 1179656 | tf_op jit(solution)/shard_map/ppermute | solution.py:64
  62.6 17.0 %collective-permute-start.24 = (bf16[1,96,16,128]{3,2,1,0:T(8,128)(2,1)}, bf16[1,96,16,128]{3,2,1,0:T(8,128)(2,1)}, u32[]{:S(2)}, u32[]{:S(2)}) collective-permute-start(bf16[1,96,16,128]{3,2,1,0:T(8,128)(2,1)} %collective-permute-done.11.rest_12_), channel_id=1, source_target_pairs={{0,28},{4,0},{8,4},{12,8},{16,12},{20,16},{24,20},{28,24},{1,29},{... | collective-permute-start | bytes 1179656 | tf_op jit(solution)/shard_map/ppermute | solution.py:64
  66.8 13.0 %collective-permute-start.22 = (bf16[1,96,16,128]{3,2,1,0:T(8,128)(2,1)}, bf16[1,96,16,128]{3,2,1,0:T(8,128)(2,1)}, u32[]{:S(2)}, u32[]{:S(2)}) collective-permute-start(bf16[1,96,16,128]{3,2,1,0:T(8,128)(2,1)} %collective-permute-done.6.rest_7_), channel_id=1, source_target_pairs={{0,4},{4,8},{8,12},{12,16},{16,20},{20,24},{24,28},{28,0},{1,5},{5... | collective-permute-start | bytes 1179656 | tf_op jit(solution)/shard_map/ppermute | solution.py:64
  68.9 17.3 %all-to-all-start.1 = ((f32[32,16,128]{2,1,0:T(8,128)}), f32[32,16,128]{2,1,0:T(8,128)S(1)}, u32[]{:S(2)}, u32[]{:S(2)}) async-start(f32[32,16,128]{2,1,0:T(8,128)} %convolution_bitcast_fusion), calls=%async_computation.1 | async-start | bytes 524288 | tf_op jit(solution)/shard_map/all_to_all | solution.py:321
  75.8 17.1 %collective-permute-start.27 = (bf16[1,96,16,128]{3,2,1,0:T(8,128)(2,1)}, bf16[1,96,16,128]{3,2,1,0:T(8,128)(2,1)}, u32[]{:S(2)}, u32[]{:S(2)}) collective-permute-start(bf16[1,96,16,128]{3,2,1,0:T(8,128)(2,1)} %collective-permute-done.15.rest_16_), channel_id=1, source_target_pairs={{0,3},{1,0},{2,1},{3,2},{4,7},{5,4},{6,5},{7,6},{8,11},{9,8},{10,9... | collective-permute-start | bytes 1179656 | tf_op jit(solution)/shard_map/ppermute | solution.py:64
  78.3 17.1 %collective-permute-start.16 = (bf16[1,96,16,128]{3,2,1,0:T(8,128)(2,1)}, bf16[1,96,16,128]{3,2,1,0:T(8,128)(2,1)}, u32[]{:S(2)}, u32[]{:S(2)}) collective-permute-start(bf16[1,96,16,128]{3,2,1,0:T(8,128)(2,1)} %collective-permute-done.15.rest_16_), channel_id=1, source_target_pairs={{0,1},{1,2},{2,3},{3,0},{4,5},{5,6},{6,7},{7,4},{8,9},{9,10},{10,1... | collective-permute-start | bytes 1179656 | tf_op jit(solution)/shard_map/ppermute | solution.py:64
  78.3 18.3 %collective-permute-start.25 = (bf16[1,96,16,128]{3,2,1,0:T(8,128)(2,1)}, bf16[1,96,16,128]{3,2,1,0:T(8,128)(2,1)}, u32[]{:S(2)}, u32[]{:S(2)}) collective-permute-start(bf16[1,96,16,128]{3,2,1,0:T(8,128)(2,1)} %collective-permute-done.14.rest_15_), channel_id=1, source_target_pairs={{0,4},{4,8},{8,12},{12,16},{16,20},{20,24},{24,28},{28,0},{1,5},{5... | collective-permute-start | bytes 1179656 | tf_op jit(solution)/shard_map/ppermute | solution.py:64
  79.6 18.7 %collective-permute-start.20 = (bf16[1,96,16,128]{3,2,1,0:T(8,128)(2,1)}, bf16[1,96,16,128]{3,2,1,0:T(8,128)(2,1)}, u32[]{:S(2)}, u32[]{:S(2)}) collective-permute-start(bf16[1,96,16,128]{3,2,1,0:T(8,128)(2,1)} %collective-permute-done.14.rest_15_), channel_id=1, source_target_pairs={{0,1},{1,2},{2,3},{3,0},{4,5},{5,6},{6,7},{7,4},{8,9},{9,10},{10,1... | collective-permute-start | bytes 1179656 | tf_op jit(solution)/shard_map/ppermute | solution.py:64
  79.7 18.5 %collective-permute-start.26 = (bf16[1,96,16,128]{3,2,1,0:T(8,128)(2,1)}, bf16[1,96,16,128]{3,2,1,0:T(8,128)(2,1)}, u32[]{:S(2)}, u32[]{:S(2)}) collective-permute-start(bf16[1,96,16,128]{3,2,1,0:T(8,128)(2,1)} %collective-permute-done.24.rest_25_), channel_id=1, source_target_pairs={{0,28},{4,0},{8,4},{12,8},{16,12},{20,16},{24,20},{28,24},{1,29},{... | collective-permute-start | bytes 1179656 | tf_op jit(solution)/shard_map/ppermute | solution.py:64
  86.9 19.1 %all-to-all-start.2 = ((f32[32,16,128]{2,1,0:T(8,128)}), f32[32,16,128]{2,1,0:T(8,128)S(1)}, u32[]{:S(2)}, u32[]{:S(2)}) async-start(f32[32,16,128]{2,1,0:T(8,128)} %broadcast_in_dim.18), calls=%async_computation.2 | async-start | bytes 524288 | tf_op jit(solution)/shard_map/all_to_all | solution.py:322
  96.6 13.9 %collective-permute-start.29 = (bf16[1,96,16,128]{3,2,1,0:T(8,128)(2,1)}, bf16[1,96,16,128]{3,2,1,0:T(8,128)(2,1)}, u32[]{:S(2)}, u32[]{:S(2)}) collective-permute-start(bf16[1,96,16,128]{3,2,1,0:T(8,128)(2,1)} %collective-permute-done.25.rest_26_), channel_id=1, source_target_pairs={{0,3},{1,0},{2,1},{3,2},{4,7},{5,4},{6,5},{7,6},{8,11},{9,8},{10,9... | collective-permute-start | bytes 1179656 | tf_op jit(solution)/shard_map/ppermute | solution.py:64
  140.1 14.7 %collective-permute-start.31 = (s16[4,2528,128]{2,1,0:T(8,128)(2,1)}, s16[4,2528,128]{2,1,0:T(8,128)(2,1)S(1)}, u32[]{:S(2)}, u32[]{:S(2)}) collective-permute-start(s16[4,2528,128]{2,1,0:T(8,128)(2,1)} %get-tuple-element.15), channel_id=1, source_target_pairs={{0,32},{32,0},{1,33},{33,1},{2,34},{34,2},{3,35},{35,3},{4,36},{36... | collective-permute-start | bytes 7766024 | tf_op jit(solution)/shard_map/ppermute | solution.py:64
  145.6 21.2 %all-to-all-start.3 = ((f32[32,16,128]{2,1,0:T(8,128)}), f32[32,16,128]{2,1,0:T(8,128)}, u32[]{:S(2)}, u32[]{:S(2)}) async-start(f32[32,16,128]{2,1,0:T(8,128)} %bitcast.48), calls=%async_computation.3 | async-start | bytes 524288 | tf_op jit(solution)/shard_map/all_to_all | solution.py:401
  161.7 14.5 %collective-permute-start.32 = (s16[1312,128]{1,0:T(8,128)(2,1)}, s16[1312,128]{1,0:T(8,128)(2,1)}, u32[]{:S(2)}, u32[]{:S(2)}) collective-permute-start(s16[1312,128]{1,0:T(8,128)(2,1)} %pad_add_fusion), channel_id=1, source_target_pairs={{0,64},{64,128},{128,192},{192,0},{1,65},{65,129},{129,193},{193,1... | collective-permute-start | bytes 1007624 | tf_op jit(solution)/shard_map/ppermute | solution.py:64
  168.4 18.1 %all-to-all-start.4 = ((f32[32,16,128]{2,1,0:T(8,128)}), f32[32,16,128]{2,1,0:T(8,128)}, u32[]{:S(2)}, u32[]{:S(2)}) async-start(f32[32,16,128]{2,1,0:T(8,128)} %broadcast_in_dim.21), calls=%async_computation.4 | async-start | bytes 524288 | tf_op jit(solution)/shard_map/all_to_all | solution.py:419
  178.9 23.0 %collective-permute-start.34 = (s16[2528,128]{1,0:T(8,128)(2,1)}, s16[2528,128]{1,0:T(8,128)(2,1)}, u32[]{:S(2)}, u32[]{:S(2)}) collective-permute-start(s16[2528,128]{1,0:T(8,128)(2,1)} %get-tuple-element.16), channel_id=1, source_target_pairs={{0,64},{64,128},{128,192},{192,0},{1,65},{65,129},{129,193},{193,1... | collective-permute-start | bytes 1941512 | tf_op jit(solution)/shard_map/ppermute | solution.py:64
  178.9 23.0 %collective-permute-start.35 = (s16[2528,128]{1,0:T(8,128)(2,1)}, s16[2528,128]{1,0:T(8,128)(2,1)}, u32[]{:S(2)}, u32[]{:S(2)}) collective-permute-start(s16[2528,128]{1,0:T(8,128)(2,1)} %get-tuple-element.17), channel_id=1, source_target_pairs={{0,192},{64,0},{128,64},{192,128},{1,193},{65,1},{129,65},{193,129... | collective-permute-start | bytes 1941512 | tf_op jit(solution)/shard_map/ppermute | solution.py:64
  (20 other events, 301.5 us)

commit v8 on v7

--- a/solution.py
+++ b/solution.py
@@ -191,7 +191,7 @@
     return spans + [(SLOT_ROWS + h * 64, 64, CAP + h) for h in range(FO_ROWS // 64)]
 
 
-def pair_kernel(keep_ref, got_ref, out_ref):
+def pair_kernel(keep_ref, got_ref, out_ref, above_ref, below_ref):
     keep_levels = keep_ref[0, CODE_ROWS:].astype(jnp.int32).astype(jnp.float32)
     got_levels = got_ref[0, CODE_ROWS:].astype(jnp.int32).astype(jnp.float32)
     fresh = []
@@ -205,6 +205,12 @@
     fresh.append(jnp.zeros((32 - len(fresh), BS), jnp.float32))
     fresh = jnp.concatenate(fresh, axis=0)
     out_ref[0, CODE_ROWS:] = fresh.astype(jnp.int32).astype(jnp.int16)
+
+    @pl.when(pl.program_id(0) == 2)
+    def _():
+        above_ref[:CUT] = out_ref[0, :CUT]
+        above_ref[CUT:] = out_ref[0, CODE_ROWS:]
+        below_ref[...] = out_ref[0, CUT:]
 
 
 def levels_in(rows):
@@ -399,18 +405,20 @@
 
     got = shift("core", NC, 1)(send)
     back = lax.all_to_all(back.reshape(span, ROWS, BS), plane, 0, 0)
-    paired = pl.pallas_call(
+    flat = lambda rows: pl.BlockSpec((rows, BS), lambda i: (0, 0))
+    heights = (CUT + PART_ROWS - CODE_ROWS, PART_ROWS - CUT)
+    paired, above, below = pl.pallas_call(
         pair_kernel,
         grid=(NY,),
         in_specs=[pl.BlockSpec((1, PART_ROWS, BS), lambda i: (i, 0, 0))] * 2,
-        out_specs=pl.BlockSpec((1, PART_ROWS, BS), lambda i: (i, 0, 0)),
-        out_shape=jax.ShapeDtypeStruct((NY, PART_ROWS, BS), jnp.int16),
+        out_specs=[pl.BlockSpec((1, PART_ROWS, BS), lambda i: (i, 0, 0))]
+        + [flat(rows) for rows in heights],
+        out_shape=[jax.ShapeDtypeStruct((NY, PART_ROWS, BS), jnp.int16)]
+        + [jax.ShapeDtypeStruct((rows, BS), jnp.int16) for rows in heights],
         compiler_params=pltpu.CompilerParams(vmem_limit_bytes=50 * 1024 * 1024),
         name="pairs",
     )(keep, got)
     y_up, y_down = shift("y", NY, 1), shift("y", NY, -1)
-    above = jnp.concatenate([paired[2, :CUT], paired[2, CODE_ROWS:]])
-    below = paired[2, CUT:]
     parts = relay(paired, y_up(above), y_down(below))
     parts = [y_up(parts[0]), y_down(parts[1])]
 

time: 206 us -> 206 us (level)
  transfers between devices with their start and end apart: 42 -> 42, of which waited for: 14 -> 14; matrix products, arithmetic and copies ran while one was open for 4% -> 3% of each run, Pallas kernels for 4% -> 5%
where the time goes in v8:
time: 206 us; the launch traced here: 205 us
  starting transfers between devices  98.9 us (48%)
  waiting for transfers between devices  49.3 us (24%)
  Pallas kernels  42.6 us (21%)
  local copies, waits for them, and re-layouts  8.29 us (4%)
  other arithmetic  2.65 us (1%)
  matrix products  2.09 us (1%)
    ppermute x36, starting transfers between devices, shift(): return lambda value: lax.ppermute(value, axis, pairs)  57.6 us
    ppermute x36, waiting for transfers between devices, shift(): return lambda value: lax.ppermute(value, axis, pairs)  32.7 us
    pallas_call x1, Pallas kernels, per_device(): pl.pallas_call(functools.partial(main_kernel, [len(g) for g in keys]), gr...  29.6 us
    all_to_all x1, starting transfers between devices, per_device(): back = lax.all_to_all(back.reshape(span, ROWS, BS), plane, 0, 0)  9.2 us
    all_to_all x1, starting transfers between devices, per_device(): lax.all_to_all(jnp.broadcast_to(back_own[None], (span, ROWS, BS)), plane,...  6.98 us
    all_to_all x1, starting transfers between devices, per_device(): low_own = jnp.sum(lax.all_to_all(partial, plane, 0, 0), axis=0)  6.87 us
    all_to_all x1, starting transfers between devices, per_device(): in_grad = jnp.sum(lax.all_to_all(in_part, ('y', 'core'), 0, 0), axis=0)  6.73 us
    all_to_all x1, starting transfers between devices, per_device(): lax.all_to_all(jnp.broadcast_to(low_own[None], (span, ROWS, BS)), plane,...  5.92 us
  transfers between devices with their start and end apart: 42, of which 14 were waited for; matrix products, arithmetic and copies ran while one was open for 3% of the time, Pallas kernels for 5%

profile of v8, /device:TPU:1, one launch (start us, length us, event | category | flops | bytes accessed | tf_op | source)
XLA Modules:
  0.0 204.7 jit_solution(7639831834373066797)
XLA Ops:
  5.8 5.8 %collective-permute-start.3 = (bf16[1,96,16,128]{3,2,1,0:T(8,128)(2,1)S(1)}, bf16[1,96,16,128]{3,2,1,0:T(8,128)(2,1)S(1)}, u32[]{:S(2)}, u32[]{:S(2)}) collective-permute-start(bf16[1,96,16,128]{3,2,1,0:T(8,128)(2,1)S(1)} %get-tuple-element.28.rest_0_), channel_id=1, source_target_pairs={{0,28},{4,0},{8,4},{12,8},{16,12},{20,16},{24,20},{28,24},{1,29},{... | collective-permute-start | bytes 1179656 | tf_op jit(solution)/shard_map/ppermute | solution.py:64
  13.1 3.0 %collective-permute-start.18 = (bf16[1,96,16,128]{3,2,1,0:T(8,128)(2,1)S(1)}, bf16[1,96,16,128]{3,2,1,0:T(8,128)(2,1)S(1)}, u32[]{:S(2)}, u32[]{:S(2)}) collective-permute-start(bf16[1,96,16,128]{3,2,1,0:T(8,128)(2,1)S(1)} %collective-permute-done.8.rest_9_), channel_id=1, source_target_pairs={{0,4},{4,8},{8,12},{12,16},{16,20},{20,24},{24,28},{28,0},{1,5},{5... | collective-permute-start | bytes 1179656 | tf_op jit(solution)/shard_map/ppermute | solution.py:64
  16.1 4.0 %collective-permute-start.13 = (bf16[1,96,16,128]{3,2,1,0:T(8,128)(2,1)S(1)}, bf16[1,96,16,128]{3,2,1,0:T(8,128)(2,1)}, u32[]{:S(2)}, u32[]{:S(2)}) collective-permute-start(bf16[1,96,16,128]{3,2,1,0:T(8,128)(2,1)S(1)} %collective-permute-done.7.rest_8_), channel_id=1, source_target_pairs={{0,28},{4,0},{8,4},{12,8},{16,12},{20,16},{24,20},{28,24},{1,29},{... | collective-permute-start | bytes 1179656 | tf_op jit(solution)/shard_map/ppermute | solution.py:64
  25.5 4.8 %collective-permute-done.18.rest_19_ = bf16[1,96,16,128]{3,2,1,0:T(8,128)(2,1)S(1)} collective-permute-done((bf16[1,96,16,128]{3,2,1,0:T(8,128)(2,1)S(1)}, bf16[1,96,16,128]{3,2,1,0:T(8,128)(2,1)S(1)}, u32[]{:S(2)}, u32[]{:S(2)}) %collective-permute-start.18) | collective-permute-done | bytes 393248 | tf_op jit(solution)/shard_map/ppermute | solution.py:64
  31.0 5.6 %all-to-all-start = ((bf16[32,3,16,128]{3,2,1,0:T(8,128)(2,1)}), bf16[32,3,16,128]{3,2,1,0:T(8,128)(2,1)S(1)}, u32[]{:S(2)}, u32[]{:S(2)}) async-start(bf16[32,3,16,128]{3,2,1,0:T(8,128)(2,1)} %bitcast.67), calls=%async_computation | async-start | bytes 786432 | tf_op jit(solution)/shard_map/all_to_all | solution.py:322
  36.6 2.6 %collective-permute-start.11 = (bf16[1,96,16,128]{3,2,1,0:T(8,128)(2,1)S(1)}, bf16[1,96,16,128]{3,2,1,0:T(8,128)(2,1)}, u32[]{:S(2)}, u32[]{:S(2)}) collective-permute-start(bf16[1,96,16,128]{3,2,1,0:T(8,128)(2,1)S(1)} %collective-permute-done.rest_1_), channel_id=1, source_target_pairs={{0,28},{4,0},{8,4},{12,8},{16,12},{20,16},{24,20},{28,24},{1,29},{... | collective-permute-start | bytes 1179656 | tf_op jit(solution)/shard_map/ppermute | solution.py:64
  39.3 2.5 %collective-permute-start.21 = (bf16[1,96,16,128]{3,2,1,0:T(8,128)(2,1)}, bf16[1,96,16,128]{3,2,1,0:T(8,128)(2,1)S(1)}, u32[]{:S(2)}, u32[]{:S(2)}) collective-permute-start(bf16[1,96,16,128]{3,2,1,0:T(8,128)(2,1)} %collective-permute-done.4.rest_5_), channel_id=1, source_target_pairs={{0,3},{1,0},{2,1},{3,2},{4,7},{5,4},{6,5},{7,6},{8,11},{9,8},{10,9... | collective-permute-start | bytes 1179656 | tf_op jit(solution)/shard_map/ppermute | solution.py:64
  41.7 2.6 %collective-permute-start.15 = (bf16[1,96,16,128]{3,2,1,0:T(8,128)(2,1)}, bf16[1,96,16,128]{3,2,1,0:T(8,128)(2,1)}, u32[]{:S(2)}, u32[]{:S(2)}) collective-permute-start(bf16[1,96,16,128]{3,2,1,0:T(8,128)(2,1)} %collective-permute-done.4.rest_5_), channel_id=1, source_target_pairs={{0,28},{4,0},{8,4},{12,8},{16,12},{20,16},{24,20},{28,24},{1,29},{... | collective-permute-start | bytes 1179656 | tf_op jit(solution)/shard_map/ppermute | solution.py:64
  44.3 9.7 %collective-permute-done.11.rest_12_ = bf16[1,96,16,128]{3,2,1,0:T(8,128)(2,1)} collective-permute-done((bf16[1,96,16,128]{3,2,1,0:T(8,128)(2,1)S(1)}, bf16[1,96,16,128]{3,2,1,0:T(8,128)(2,1)}, u32[]{:S(2)}, u32[]{:S(2)}) %collective-permute-start.11) | collective-permute-done | bytes 393248 | tf_op jit(solution)/shard_map/ppermute | solution.py:64
  54.0 2.6 %collective-permute-start.17 = (bf16[1,96,16,128]{3,2,1,0:T(8,128)(2,1)}, bf16[1,96,16,128]{3,2,1,0:T(8,128)(2,1)}, u32[]{:S(2)}, u32[]{:S(2)}) collective-permute-start(bf16[1,96,16,128]{3,2,1,0:T(8,128)(2,1)} %collective-permute-done.2.rest_3_), channel_id=1, source_target_pairs={{0,3},{1,0},{2,1},{3,2},{4,7},{5,4},{6,5},{7,6},{8,11},{9,8},{10,9... | collective-permute-start | bytes 1179656 | tf_op jit(solution)/shard_map/ppermute | solution.py:64
  58.8 3.8 %collective-permute-done.15.rest_16_ = bf16[1,96,16,128]{3,2,1,0:T(8,128)(2,1)} collective-permute-done((bf16[1,96,16,128]{3,2,1,0:T(8,128)(2,1)}, bf16[1,96,16,128]{3,2,1,0:T(8,128)(2,1)}, u32[]{:S(2)}, u32[]{:S(2)}) %collective-permute-start.15) | collective-permute-done | bytes 393248 | tf_op jit(solution)/shard_map/ppermute | solution.py:64
  62.6 3.4 %collective-permute-start.24 = (bf16[1,96,16,128]{3,2,1,0:T(8,128)(2,1)}, bf16[1,96,16,128]{3,2,1,0:T(8,128)(2,1)}, u32[]{:S(2)}, u32[]{:S(2)}) collective-permute-start(bf16[1,96,16,128]{3,2,1,0:T(8,128)(2,1)} %collective-permute-done.11.rest_12_), channel_id=1, source_target_pairs={{0,28},{4,0},{8,4},{12,8},{16,12},{20,16},{24,20},{28,24},{1,29},{... | collective-permute-start | bytes 1179656 | tf_op jit(solution)/shard_map/ppermute | solution.py:64
  66.8 2.1 %convolution_bitcast_fusion = f32[32,16,128]{2,1,0:T(8,128)} fusion(bf16[32,3,16,128]{3,2,1,0:T(8,128)(2,1)S(1)} %all-to-all-done.cols_ref, f32[3,128,128,1]{2,1,0,3:T(8,128)} %bitcast.68), kind=kOutput, calls=%fused_computation | convolution fusion | flops 301989888 | bytes 851968 | tf_op jit(solution)/shard_map/sbtf,bfr->str/dot_general | solution.py:324
  68.9 6.9 %all-to-all-start.1 = ((f32[32,16,128]{2,1,0:T(8,128)}), f32[32,16,128]{2,1,0:T(8,128)S(1)}, u32[]{:S(2)}, u32[]{:S(2)}) async-start(f32[32,16,128]{2,1,0:T(8,128)} %convolution_bitcast_fusion), calls=%async_computation.1 | async-start | bytes 524288 | tf_op jit(solution)/shard_map/all_to_all | solution.py:327
  75.7 2.5 %collective-permute-start.27 = (bf16[1,96,16,128]{3,2,1,0:T(8,128)(2,1)}, bf16[1,96,16,128]{3,2,1,0:T(8,128)(2,1)}, u32[]{:S(2)}, u32[]{:S(2)}) collective-permute-start(bf16[1,96,16,128]{3,2,1,0:T(8,128)(2,1)} %collective-permute-done.15.rest_16_), channel_id=1, source_target_pairs={{0,3},{1,0},{2,1},{3,2},{4,7},{5,4},{6,5},{7,6},{8,11},{9,8},{10,9... | collective-permute-start | bytes 1179656 | tf_op jit(solution)/shard_map/ppermute | solution.py:64
  82.0 4.2 %all-to-all-done.1 = f32[32,16,128]{2,1,0:T(8,128)S(1)} async-done(((f32[32,16,128]{2,1,0:T(8,128)}), f32[32,16,128]{2,1,0:T(8,128)S(1)}, u32[]{:S(2)}, u32[]{:S(2)}) %all-to-all-start.1) | async-done | bytes 262176 | tf_op jit(solution)/shard_map/all_to_all | solution.py:327
  86.9 5.9 %all-to-all-start.2 = ((f32[32,16,128]{2,1,0:T(8,128)}), f32[32,16,128]{2,1,0:T(8,128)S(1)}, u32[]{:S(2)}, u32[]{:S(2)}) async-start(f32[32,16,128]{2,1,0:T(8,128)} %broadcast_in_dim.18), calls=%async_computation.2 | async-start | bytes 524288 | tf_op jit(solution)/shard_map/all_to_all | solution.py:328
  92.9 2.5 %collective-permute-start.19 = (bf16[1,96,16,128]{3,2,1,0:T(8,128)(2,1)}, bf16[1,96,16,128]{3,2,1,0:T(8,128)(2,1)S(1)}, u32[]{:S(2)}, u32[]{:S(2)}) collective-permute-start(bf16[1,96,16,128]{3,2,1,0:T(8,128)(2,1)} %collective-permute-done.14.rest_15_), channel_id=1, source_target_pairs={{0,3},{1,0},{2,1},{3,2},{4,7},{5,4},{6,5},{7,6},{8,11},{9,8},{10,9... | collective-permute-start | bytes 1179656 | tf_op jit(solution)/shard_map/ppermute | solution.py:64
  102.4 3.6 %collective-permute-done.23.rest_24_ = bf16[1,96,16,128]{3,2,1,0:T(8,128)(2,1)} collective-permute-done((bf16[1,96,16,128]{3,2,1,0:T(8,128)(2,1)}, bf16[1,96,16,128]{3,2,1,0:T(8,128)(2,1)}, u32[]{:S(2)}, u32[]{:S(2)}) %collective-permute-start.23) | collective-permute-done | bytes 393248 | tf_op jit(solution)/shard_map/ppermute | solution.py:64
  106.0 4.5 %collective-permute-done.29.rest_30_ = bf16[1,96,16,128]{3,2,1,0:T(8,128)(2,1)} collective-permute-done((bf16[1,96,16,128]{3,2,1,0:T(8,128)(2,1)}, bf16[1,96,16,128]{3,2,1,0:T(8,128)(2,1)}, u32[]{:S(2)}, u32[]{:S(2)}) %collective-permute-start.29) | collective-permute-done | bytes 393248 | tf_op jit(solution)/shard_map/ppermute | solution.py:64
  110.5 29.6 %columns.1 = (bf16[512,1536]{1,0:T(8,128)(2,1)}, s16[4,2528,128]{2,1,0:T(8,128)(2,1)}, s16[4,2528,128]{2,1,0:T(8,128)(2,1)}, f32[512,128]{1,0:T(8,128)}) custom-call(s32[96]{0:T(128)S(1)} %reshape.176.rows_ref, s32[4,96]{1,0:T(4,128)S(1)} %pad_add_fusion.where_ref, s32[32]{0:T(128)S(1)} %stack.148.place_ref, f32[512,128]{1,0:T(8,128)S(1)} %bitcast.66, ...), custom_call_target="tpu_custom_call" | custom-call | tf_op jit(solution)/shard_map/columns/pallas_call | solution.py:366
  140.1 5.5 %collective-permute-start.31 = (s16[4,2528,128]{2,1,0:T(8,128)(2,1)}, s16[4,2528,128]{2,1,0:T(8,128)(2,1)S(1)}, u32[]{:S(2)}, u32[]{:S(2)}) collective-permute-start(s16[4,2528,128]{2,1,0:T(8,128)(2,1)} %get-tuple-element.18), channel_id=1, source_target_pairs={{0,32},{32,0},{1,33},{33,1},{2,34},{34,2},{3,35},{35,3},{4,36},{36... | collective-permute-start | bytes 7766024 | tf_op jit(solution)/shard_map/ppermute | solution.py:64
  145.5 9.2 %all-to-all-start.3 = ((f32[32,16,128]{2,1,0:T(8,128)}), f32[32,16,128]{2,1,0:T(8,128)}, u32[]{:S(2)}, u32[]{:S(2)}) async-start(f32[32,16,128]{2,1,0:T(8,128)} %bitcast.45), calls=%async_computation.3 | async-start | bytes 524288 | tf_op jit(solution)/shard_map/all_to_all | solution.py:407
  156.3 5.4 %pairs.1 = (s16[4,2528,128]{2,1,0:T(8,128)(2,1)S(1)}, s16[1312,128]{1,0:T(8,128)(2,1)}, s16[1248,128]{1,0:T(8,128)(2,1)}) custom-call(s16[4,2528,128]{2,1,0:T(8,128)(2,1)} %get-tuple-element.17.keep_ref, s16[4,2528,128]{2,1,0:T(8,128)(2,1)} %copy-done.2), custom_call_target="tpu_custom_call" | custom-call | tf_op jit(solution)/shard_map/pairs/pallas_call | solution.py:410
  164.4 2.3 %all-to-all-done.3 = f32[32,16,128]{2,1,0:T(8,128)} async-done(((f32[32,16,128]{2,1,0:T(8,128)}), f32[32,16,128]{2,1,0:T(8,128)}, u32[]{:S(2)}, u32[]{:S(2)}) %all-to-all-start.3) | async-done | bytes 262176 | tf_op jit(solution)/shard_map/all_to_all | solution.py:407
  168.4 7.0 %all-to-all-start.4 = ((f32[32,16,128]{2,1,0:T(8,128)}), f32[32,16,128]{2,1,0:T(8,128)}, u32[]{:S(2)}, u32[]{:S(2)}) async-start(f32[32,16,128]{2,1,0:T(8,128)} %broadcast_in_dim.21), calls=%async_computation.4 | async-start | bytes 524288 | tf_op jit(solution)/shard_map/all_to_all | solution.py:427
  175.5 2.7 %relay.1 = (s16[2528,128]{1,0:T(8,128)(2,1)}, s16[2528,128]{1,0:T(8,128)(2,1)}) custom-call(s16[4,2528,128]{2,1,0:T(8,128)(2,1)S(1)} %get-tuple-element.19.up_ref.down_ref.own_ref, s16[4,2528,128]{2,1,0:T(8,128)(2,1)S(1)} %get-tuple-element.19.up_ref.down_ref.own_ref, s16[1312,128]{1,0:T(8,128)(2,1)} %collective-permute-done.32.above_ref, ...), custom_call_target="tpu_custom_call" | custom-call | flops 40000000 | bytes 40000000 | tf_op jit(solution)/shard_map/relay/pallas_call | solution.py:248
  178.2 2.6 %collective-permute-start.35 = (s16[2528,128]{1,0:T(8,128)(2,1)}, s16[2528,128]{1,0:T(8,128)(2,1)}, u32[]{:S(2)}, u32[]{:S(2)}) collective-permute-start(s16[2528,128]{1,0:T(8,128)(2,1)} %get-tuple-element.23), channel_id=1, source_target_pairs={{0,192},{64,0},{128,64},{192,128},{1,193},{65,1},{129,65},{193,129... | collective-permute-start | bytes 1941512 | tf_op jit(solution)/shard_map/ppermute | solution.py:64
  180.8 5.0 %all-to-all-done.4.back_ref = f32[32,16,128]{2,1,0:T(8,128)} async-done(((f32[32,16,128]{2,1,0:T(8,128)}), f32[32,16,128]{2,1,0:T(8,128)}, u32[]{:S(2)}, u32[]{:S(2)}) %all-to-all-start.4) | async-done | bytes 262176 | tf_op jit(solution)/shard_map/all_to_all | solution.py:427
  187.9 6.7 %all-to-all-start.5 = ((f32[8,48,128]{2,1,0:T(8,128)}), f32[8,48,128]{2,1,0:T(8,128)S(1)}, u32[]{:S(2)}, u32[]{:S(2)}) async-start(f32[8,48,128]{2,1,0:T(8,128)} %copy-done.1), calls=%async_computation.5 | async-start | bytes 393216 | tf_op jit(solution)/shard_map/all_to_all | solution.py:431
  195.4 5.1 %all-to-all-done.5 = f32[8,48,128]{2,1,0:T(8,128)S(1)} async-done(((f32[8,48,128]{2,1,0:T(8,128)}), f32[8,48,128]{2,1,0:T(8,128)S(1)}, u32[]{:S(2)}, u32[]{:S(2)}) %all-to-all-start.5) | async-done | bytes 196640 | tf_op jit(solution)/shard_map/all_to_all | solution.py:431
  201.2 3.5 %slots.1 = (f32[18,128,128]{2,1,0:T(8,128)}, f32[192,128]{1,0:T(8,128)}) custom-call(s32[1]{0:T(128)} %bitcast.44.count_ref, s16[4,2528,128]{2,1,0:T(8,128)(2,1)S(1)} %get-tuple-element.19.up_ref.down_ref.own_ref, s16[2528,128]{1,0:T(8,128)(2,1)} %collective-permute-done.34.refs_0_, s16[2528,128]{1,0:T(8,128)(2,1)} %collective-permute-done.35.refs_1_), custom_call_target="tpu_custom_call" | custom-call | flops 10000000 | bytes 16000000 | tf_op jit(solution)/shard_map/slots/pallas_call | solution.py:434
  (98 shorter events, 36.6 us)
Async XLA Ops:
  5.8 14.4 %collective-permute-start.3 = (bf16[1,96,16,128]{3,2,1,0:T(8,128)(2,1)S(1)}, bf16[1,96,16,128]{3,2,1,0:T(8,128)(2,1)S(1)}, u32[]{:S(2)}, u32[]{:S(2)}) collective-permute-start(bf16[1,96,16,128]{3,2,1,0:T(8,128)(2,1)S(1)} %get-tuple-element.28.rest_0_), channel_id=1, source_target_pairs={{0,28},{4,0},{8,4},{12,8},{16,12},{20,16},{24,20},{28,24},{1,29},{... | collective-permute-start | bytes 1179656 | tf_op jit(solution)/shard_map/ppermute | solution.py:64
  13.1 17.2 %collective-permute-start.18 = (bf16[1,96,16,128]{3,2,1,0:T(8,128)(2,1)S(1)}, bf16[1,96,16,128]{3,2,1,0:T(8,128)(2,1)S(1)}, u32[]{:S(2)}, u32[]{:S(2)}) collective-permute-start(bf16[1,96,16,128]{3,2,1,0:T(8,128)(2,1)S(1)} %collective-permute-done.8.rest_9_), channel_id=1, source_target_pairs={{0,4},{4,8},{8,12},{12,16},{16,20},{20,24},{24,28},{28,0},{1,5},{5... | collective-permute-start | bytes 1179656 | tf_op jit(solution)/shard_map/ppermute | solution.py:64
  16.1 20.5 %collective-permute-start.13 = (bf16[1,96,16,128]{3,2,1,0:T(8,128)(2,1)S(1)}, bf16[1,96,16,128]{3,2,1,0:T(8,128)(2,1)}, u32[]{:S(2)}, u32[]{:S(2)}) collective-permute-start(bf16[1,96,16,128]{3,2,1,0:T(8,128)(2,1)S(1)} %collective-permute-done.7.rest_8_), channel_id=1, source_target_pairs={{0,28},{4,0},{8,4},{12,8},{16,12},{20,16},{24,20},{28,24},{1,29},{... | collective-permute-start | bytes 1179656 | tf_op jit(solution)/shard_map/ppermute | solution.py:64
  20.2 19.1 %collective-permute-start.5 = (bf16[1,96,16,128]{3,2,1,0:T(8,128)(2,1)S(1)}, bf16[1,96,16,128]{3,2,1,0:T(8,128)(2,1)}, u32[]{:S(2)}, u32[]{:S(2)}) collective-permute-start(bf16[1,96,16,128]{3,2,1,0:T(8,128)(2,1)S(1)} %collective-permute-done.3.rest_4_), channel_id=1, source_target_pairs={{0,1},{1,2},{2,3},{3,0},{4,5},{5,6},{6,7},{7,4},{8,9},{9,10},{10,1... | collective-permute-start | bytes 1179656 | tf_op jit(solution)/shard_map/ppermute | solution.py:64
  21.9 17.4 %collective-permute-start.4 = (bf16[1,96,16,128]{3,2,1,0:T(8,128)(2,1)S(1)}, bf16[1,96,16,128]{3,2,1,0:T(8,128)(2,1)}, u32[]{:S(2)}, u32[]{:S(2)}) collective-permute-start(bf16[1,96,16,128]{3,2,1,0:T(8,128)(2,1)S(1)} %collective-permute-done.3.rest_4_), channel_id=1, source_target_pairs={{0,28},{4,0},{8,4},{12,8},{16,12},{20,16},{24,20},{28,24},{1,29},{... | collective-permute-start | bytes 1179656 | tf_op jit(solution)/shard_map/ppermute | solution.py:64
  23.9 17.9 %collective-permute-start.9 = (bf16[1,96,16,128]{3,2,1,0:T(8,128)(2,1)S(1)}, bf16[1,96,16,128]{3,2,1,0:T(8,128)(2,1)}, u32[]{:S(2)}, u32[]{:S(2)}) collective-permute-start(bf16[1,96,16,128]{3,2,1,0:T(8,128)(2,1)S(1)} %collective-permute-done.1.rest_2_), channel_id=1, source_target_pairs={{0,3},{1,0},{2,1},{3,2},{4,7},{5,4},{6,5},{7,6},{8,11},{9,8},{10,9... | collective-permute-start | bytes 1179656 | tf_op jit(solution)/shard_map/ppermute | solution.py:64
  31.0 13.3 %collective-permute-start.2 = (bf16[1,96,16,128]{3,2,1,0:T(8,128)(2,1)S(1)}, bf16[1,96,16,128]{3,2,1,0:T(8,128)(2,1)}, u32[]{:S(2)}, u32[]{:S(2)}) collective-permute-start(bf16[1,96,16,128]{3,2,1,0:T(8,128)(2,1)S(1)} %collective-permute-done.1.rest_2_), channel_id=1, source_target_pairs={{0,4},{4,8},{8,12},{12,16},{16,20},{20,24},{24,28},{28,0},{1,5},{5... | collective-permute-start | bytes 1179656 | tf_op jit(solution)/shard_map/ppermute | solution.py:64
  31.0 35.7 %all-to-all-start = ((bf16[32,3,16,128]{3,2,1,0:T(8,128)(2,1)}), bf16[32,3,16,128]{3,2,1,0:T(8,128)(2,1)S(1)}, u32[]{:S(2)}, u32[]{:S(2)}) async-start(bf16[32,3,16,128]{3,2,1,0:T(8,128)(2,1)} %bitcast.67), calls=%async_computation | async-start | bytes 786432 | tf_op jit(solution)/shard_map/all_to_all | solution.py:322
  36.6 17.4 %collective-permute-start.11 = (bf16[1,96,16,128]{3,2,1,0:T(8,128)(2,1)S(1)}, bf16[1,96,16,128]{3,2,1,0:T(8,128)(2,1)}, u32[]{:S(2)}, u32[]{:S(2)}) collective-permute-start(bf16[1,96,16,128]{3,2,1,0:T(8,128)(2,1)S(1)} %collective-permute-done.rest_1_), channel_id=1, source_target_pairs={{0,28},{4,0},{8,4},{12,8},{16,12},{20,16},{24,20},{28,24},{1,29},{... | collective-permute-start | bytes 1179656 | tf_op jit(solution)/shard_map/ppermute | solution.py:64
  39.2 18.2 %collective-permute-start.6 = (bf16[1,96,16,128]{3,2,1,0:T(8,128)(2,1)S(1)}, bf16[1,96,16,128]{3,2,1,0:T(8,128)(2,1)}, u32[]{:S(2)}, u32[]{:S(2)}) collective-permute-start(bf16[1,96,16,128]{3,2,1,0:T(8,128)(2,1)S(1)} %collective-permute-done.rest_1_), channel_id=1, source_target_pairs={{0,4},{4,8},{8,12},{12,16},{16,20},{20,24},{24,28},{28,0},{1,5},{5... | collective-permute-start | bytes 1179656 | tf_op jit(solution)/shard_map/ppermute | solution.py:64
  39.3 18.2 %collective-permute-start.21 = (bf16[1,96,16,128]{3,2,1,0:T(8,128)(2,1)}, bf16[1,96,16,128]{3,2,1,0:T(8,128)(2,1)S(1)}, u32[]{:S(2)}, u32[]{:S(2)}) collective-permute-start(bf16[1,96,16,128]{3,2,1,0:T(8,128)(2,1)} %collective-permute-done.4.rest_5_), channel_id=1, source_target_pairs={{0,3},{1,0},{2,1},{3,2},{4,7},{5,4},{6,5},{7,6},{8,11},{9,8},{10,9... | collective-permute-start | bytes 1179656 | tf_op jit(solution)/shard_map/ppermute | solution.py:64
  41.7 20.8 %collective-permute-start.15 = (bf16[1,96,16,128]{3,2,1,0:T(8,128)(2,1)}, bf16[1,96,16,128]{3,2,1,0:T(8,128)(2,1)}, u32[]{:S(2)}, u32[]{:S(2)}) collective-permute-start(bf16[1,96,16,128]{3,2,1,0:T(8,128)(2,1)} %collective-permute-done.4.rest_5_), channel_id=1, source_target_pairs={{0,28},{4,0},{8,4},{12,8},{16,12},{20,16},{24,20},{28,24},{1,29},{... | collective-permute-start | bytes 1179656 | tf_op jit(solution)/shard_map/ppermute | solution.py:64
  44.3 21.6 %collective-permute-start.10 = (bf16[1,96,16,128]{3,2,1,0:T(8,128)(2,1)}, bf16[1,96,16,128]{3,2,1,0:T(8,128)(2,1)S(1)}, u32[]{:S(2)}, u32[]{:S(2)}) collective-permute-start(bf16[1,96,16,128]{3,2,1,0:T(8,128)(2,1)} %collective-permute-done.4.rest_5_), channel_id=1, source_target_pairs={{0,1},{1,2},{2,3},{3,0},{4,5},{5,6},{6,7},{7,4},{8,9},{9,10},{10,1... | collective-permute-start | bytes 1179656 | tf_op jit(solution)/shard_map/ppermute | solution.py:64
  54.0 21.7 %collective-permute-start.17 = (bf16[1,96,16,128]{3,2,1,0:T(8,128)(2,1)}, bf16[1,96,16,128]{3,2,1,0:T(8,128)(2,1)}, u32[]{:S(2)}, u32[]{:S(2)}) collective-permute-start(bf16[1,96,16,128]{3,2,1,0:T(8,128)(2,1)} %collective-permute-done.2.rest_3_), channel_id=1, source_target_pairs={{0,3},{1,0},{2,1},{3,2},{4,7},{5,4},{6,5},{7,6},{8,11},{9,8},{10,9... | collective-permute-start | bytes 1179656 | tf_op jit(solution)/shard_map/ppermute | solution.py:64
  57.4 20.8 %collective-permute-start.14 = (bf16[1,96,16,128]{3,2,1,0:T(8,128)(2,1)}, bf16[1,96,16,128]{3,2,1,0:T(8,128)(2,1)}, u32[]{:S(2)}, u32[]{:S(2)}) collective-permute-start(bf16[1,96,16,128]{3,2,1,0:T(8,128)(2,1)} %collective-permute-done.2.rest_3_), channel_id=1, source_target_pairs={{0,4},{4,8},{8,12},{12,16},{16,20},{20,24},{24,28},{28,0},{1,5},{5... | collective-permute-start | bytes 1179656 | tf_op jit(solution)/shard_map/ppermute | solution.py:64
  57.5 20.8 %collective-permute-start.12 = (bf16[1,96,16,128]{3,2,1,0:T(8,128)(2,1)}, bf16[1,96,16,128]{3,2,1,0:T(8,128)(2,1)}, u32[]{:S(2)}, u32[]{:S(2)}) collective-permute-start(bf16[1,96,16,128]{3,2,1,0:T(8,128)(2,1)} %collective-permute-done.2.rest_3_), channel_id=1, source_target_pairs={{0,1},{1,2},{2,3},{3,0},{4,5},{5,6},{6,7},{7,4},{8,9},{9,10},{10,1... | collective-permute-start | bytes 1179656 | tf_op jit(solution)/shard_map/ppermute | solution.py:64
  62.6 17.0 %collective-permute-start.24 = (bf16[1,96,16,128]{3,2,1,0:T(8,128)(2,1)}, bf16[1,96,16,128]{3,2,1,0:T(8,128)(2,1)}, u32[]{:S(2)}, u32[]{:S(2)}) collective-permute-start(bf16[1,96,16,128]{3,2,1,0:T(8,128)(2,1)} %collective-permute-done.11.rest_12_), channel_id=1, source_target_pairs={{0,28},{4,0},{8,4},{12,8},{16,12},{20,16},{24,20},{28,24},{1,29},{... | collective-permute-start | bytes 1179656 | tf_op jit(solution)/shard_map/ppermute | solution.py:64
  66.8 13.0 %collective-permute-start.22 = (bf16[1,96,16,128]{3,2,1,0:T(8,128)(2,1)}, bf16[1,96,16,128]{3,2,1,0:T(8,128)(2,1)}, u32[]{:S(2)}, u32[]{:S(2)}) collective-permute-start(bf16[1,96,16,128]{3,2,1,0:T(8,128)(2,1)} %collective-permute-done.6.rest_7_), channel_id=1, source_target_pairs={{0,4},{4,8},{8,12},{12,16},{16,20},{20,24},{24,28},{28,0},{1,5},{5... | collective-permute-start | bytes 1179656 | tf_op jit(solution)/shard_map/ppermute | solution.py:64
  68.9 17.3 %all-to-all-start.1 = ((f32[32,16,128]{2,1,0:T(8,128)}), f32[32,16,128]{2,1,0:T(8,128)S(1)}, u32[]{:S(2)}, u32[]{:S(2)}) async-start(f32[32,16,128]{2,1,0:T(8,128)} %convolution_bitcast_fusion), calls=%async_computation.1 | async-start | bytes 524288 | tf_op jit(solution)/shard_map/all_to_all | solution.py:327
  75.7 17.1 %collective-permute-start.27 = (bf16[1,96,16,128]{3,2,1,0:T(8,128)(2,1)}, bf16[1,96,16,128]{3,2,1,0:T(8,128)(2,1)}, u32[]{:S(2)}, u32[]{:S(2)}) collective-permute-start(bf16[1,96,16,128]{3,2,1,0:T(8,128)(2,1)} %collective-permute-done.15.rest_16_), channel_id=1, source_target_pairs={{0,3},{1,0},{2,1},{3,2},{4,7},{5,4},{6,5},{7,6},{8,11},{9,8},{10,9... | collective-permute-start | bytes 1179656 | tf_op jit(solution)/shard_map/ppermute | solution.py:64
  78.3 17.1 %collective-permute-start.16 = (bf16[1,96,16,128]{3,2,1,0:T(8,128)(2,1)}, bf16[1,96,16,128]{3,2,1,0:T(8,128)(2,1)}, u32[]{:S(2)}, u32[]{:S(2)}) collective-permute-start(bf16[1,96,16,128]{3,2,1,0:T(8,128)(2,1)} %collective-permute-done.15.rest_16_), channel_id=1, source_target_pairs={{0,1},{1,2},{2,3},{3,0},{4,5},{5,6},{6,7},{7,4},{8,9},{9,10},{10,1... | collective-permute-start | bytes 1179656 | tf_op jit(solution)/shard_map/ppermute | solution.py:64
  78.3 18.3 %collective-permute-start.25 = (bf16[1,96,16,128]{3,2,1,0:T(8,128)(2,1)}, bf16[1,96,16,128]{3,2,1,0:T(8,128)(2,1)}, u32[]{:S(2)}, u32[]{:S(2)}) collective-permute-start(bf16[1,96,16,128]{3,2,1,0:T(8,128)(2,1)} %collective-permute-done.14.rest_15_), channel_id=1, source_target_pairs={{0,4},{4,8},{8,12},{12,16},{16,20},{20,24},{24,28},{28,0},{1,5},{5... | collective-permute-start | bytes 1179656 | tf_op jit(solution)/shard_map/ppermute | solution.py:64
  79.5 18.7 %collective-permute-start.20 = (bf16[1,96,16,128]{3,2,1,0:T(8,128)(2,1)}, bf16[1,96,16,128]{3,2,1,0:T(8,128)(2,1)}, u32[]{:S(2)}, u32[]{:S(2)}) collective-permute-start(bf16[1,96,16,128]{3,2,1,0:T(8,128)(2,1)} %collective-permute-done.14.rest_15_), channel_id=1, source_target_pairs={{0,1},{1,2},{2,3},{3,0},{4,5},{5,6},{6,7},{7,4},{8,9},{9,10},{10,1... | collective-permute-start | bytes 1179656 | tf_op jit(solution)/shard_map/ppermute | solution.py:64
  79.7 18.5 %collective-permute-start.26 = (bf16[1,96,16,128]{3,2,1,0:T(8,128)(2,1)}, bf16[1,96,16,128]{3,2,1,0:T(8,128)(2,1)}, u32[]{:S(2)}, u32[]{:S(2)}) collective-permute-start(bf16[1,96,16,128]{3,2,1,0:T(8,128)(2,1)} %collective-permute-done.24.rest_25_), channel_id=1, source_target_pairs={{0,28},{4,0},{8,4},{12,8},{16,12},{20,16},{24,20},{28,24},{1,29},{... | collective-permute-start | bytes 1179656 | tf_op jit(solution)/shard_map/ppermute | solution.py:64
  86.9 19.1 %all-to-all-start.2 = ((f32[32,16,128]{2,1,0:T(8,128)}), f32[32,16,128]{2,1,0:T(8,128)S(1)}, u32[]{:S(2)}, u32[]{:S(2)}) async-start(f32[32,16,128]{2,1,0:T(8,128)} %broadcast_in_dim.18), calls=%async_computation.2 | async-start | bytes 524288 | tf_op jit(solution)/shard_map/all_to_all | solution.py:328
  96.6 13.9 %collective-permute-start.29 = (bf16[1,96,16,128]{3,2,1,0:T(8,128)(2,1)}, bf16[1,96,16,128]{3,2,1,0:T(8,128)(2,1)}, u32[]{:S(2)}, u32[]{:S(2)}) collective-permute-start(bf16[1,96,16,128]{3,2,1,0:T(8,128)(2,1)} %collective-permute-done.25.rest_26_), channel_id=1, source_target_pairs={{0,3},{1,0},{2,1},{3,2},{4,7},{5,4},{6,5},{7,6},{8,11},{9,8},{10,9... | collective-permute-start | bytes 1179656 | tf_op jit(solution)/shard_map/ppermute | solution.py:64
  140.1 14.7 %collective-permute-start.31 = (s16[4,2528,128]{2,1,0:T(8,128)(2,1)}, s16[4,2528,128]{2,1,0:T(8,128)(2,1)S(1)}, u32[]{:S(2)}, u32[]{:S(2)}) collective-permute-start(s16[4,2528,128]{2,1,0:T(8,128)(2,1)} %get-tuple-element.18), channel_id=1, source_target_pairs={{0,32},{32,0},{1,33},{33,1},{2,34},{34,2},{3,35},{35,3},{4,36},{36... | collective-permute-start | bytes 7766024 | tf_op jit(solution)/shard_map/ppermute | solution.py:64
  145.5 21.2 %all-to-all-start.3 = ((f32[32,16,128]{2,1,0:T(8,128)}), f32[32,16,128]{2,1,0:T(8,128)}, u32[]{:S(2)}, u32[]{:S(2)}) async-start(f32[32,16,128]{2,1,0:T(8,128)} %bitcast.45), calls=%async_computation.3 | async-start | bytes 524288 | tf_op jit(solution)/shard_map/all_to_all | solution.py:407
  161.7 13.8 %collective-permute-start.32 = (s16[1312,128]{1,0:T(8,128)(2,1)}, s16[1312,128]{1,0:T(8,128)(2,1)}, u32[]{:S(2)}, u32[]{:S(2)}) collective-permute-start(s16[1312,128]{1,0:T(8,128)(2,1)} %get-tuple-element.20), channel_id=1, source_target_pairs={{0,64},{64,128},{128,192},{192,0},{1,65},{65,129},{129,193},{193,1... | collective-permute-start | bytes 1007624 | tf_op jit(solution)/shard_map/ppermute | solution.py:64
  168.4 17.4 %all-to-all-start.4 = ((f32[32,16,128]{2,1,0:T(8,128)}), f32[32,16,128]{2,1,0:T(8,128)}, u32[]{:S(2)}, u32[]{:S(2)}) async-start(f32[32,16,128]{2,1,0:T(8,128)} %broadcast_in_dim.21), calls=%async_computation.4 | async-start | bytes 524288 | tf_op jit(solution)/shard_map/all_to_all | solution.py:427
  178.2 23.0 %collective-permute-start.34 = (s16[2528,128]{1,0:T(8,128)(2,1)}, s16[2528,128]{1,0:T(8,128)(2,1)}, u32[]{:S(2)}, u32[]{:S(2)}) collective-permute-start(s16[2528,128]{1,0:T(8,128)(2,1)} %get-tuple-element.22), channel_id=1, source_target_pairs={{0,64},{64,128},{128,192},{192,0},{1,65},{65,129},{129,193},{193,1... | collective-permute-start | bytes 1941512 | tf_op jit(solution)/shard_map/ppermute | solution.py:64
  178.2 23.0 %collective-permute-start.35 = (s16[2528,128]{1,0:T(8,128)(2,1)}, s16[2528,128]{1,0:T(8,128)(2,1)}, u32[]{:S(2)}, u32[]{:S(2)}) collective-permute-start(s16[2528,128]{1,0:T(8,128)(2,1)} %get-tuple-element.23), channel_id=1, source_target_pairs={{0,192},{64,0},{128,64},{192,128},{1,193},{65,1},{129,65},{193,129... | collective-permute-start | bytes 1941512 | tf_op jit(solution)/shard_map/ppermute | solution.py:64
  (20 other events, 301.5 us)
